TPU v7x, 32 devices: a whole 2x2x4 slice. The times are simulated.
32 devices in a mesh: atom: 8 (over y, x, core), mode: 4 (over z).
Axes of the slice: x: 2, y: 2, z: 4, core: 2. Of those that a mesh axis runs over, the one named last changes fastest.
Arguments:
- eigvec: bfloat16 [3, 2048, 1024], P(None, 'atom', 'mode'), may hold values from -0.078125 to 0.078125
- force: float32 [3, 3, 16, 2048], P(None, None, None, 'atom'), may hold values from -12 to 12
- bond: float32 [3, 16, 2048], P(None, None, 'atom'), may hold values from -6 to 6
- nbr: int32 [16, 2048], P(None, 'atom'), may hold values from 0 to 2047, as said below
- band: int32 [2, 1024], P(None, 'mode'), may hold values from 0 to 1024, as said below
- freq: float32 [1024], P('mode'), may hold values from 0.5 to 4, as said below
Outputs:
- diffusivity: float32 [1024], P('mode')
- conductivity: float32 [1024], P('mode')
Inputs may be any that keep to these rules, and one draw needn't show every extreme that they name: `nbr`: each entry is an atom whose position in atom order differs from that of its own atom by 1 to 128, counted cyclically over the 2048 atoms; the distance 128 occurs in every draw. For every mode i: max(0, i - 128) <= band[0, i] <= i < band[1, i] <= min(1024, i + 129); both outer limits are reached at some mode. `freq`: strictly increasing along the modes.
All inputs are finite; a program needn't handle non-finite values.
Results may differ from a plain program's by a relative error of at most 0.00057.
Values may be sent and summed in bfloat16 or wider, within the bound.
No kernel may reach another device: no remote copies, remote signals or barrier semaphores. Data moves between devices by JAX's collectives and lax.ppermute only.
A program may use at most 64 MiB of HBM per device.

v0:
```python
import math

import jax
import jax.numpy as jnp
from jax import lax
from jax.sharding import PartitionSpec as P

ATOM_DEV = 256
MODE_DEV = 256
RIM = 128
HALF = 128
BROAD = 128


def extended(shard, sides, width, wrap):
    for axis, dim in sides:
        size, length = (lax.axis_size(axis), shard.shape[dim])
        up = [(i, (i + 1) % size) for i in range(size if wrap else size - 1)]
        down = [(j, i) for i, j in up]
        last = lax.slice_in_dim(shard, length - width, length, axis=dim)
        first = lax.slice_in_dim(shard, 0, width, axis=dim)
        before = lax.ppermute(last, axis, up)
        after = lax.ppermute(first, axis, down)
        shard = jnp.concatenate([before, shard, after], axis=dim)
    return shard


def prefix(part, axis, combine, identity):
    place = lax.axis_index(axis)
    gathered = lax.all_gather(part, axis)
    state = jnp.zeros_like(part) + jnp.asarray(identity, part.dtype)

    def one(lap, state):
        return combine(state, lax.dynamic_index_in_dim(gathered, lap, 0, False))

    return lax.fori_loop(0, place, one, state)


def capacity_of(spectral):
    return spectral * spectral * jnp.exp(spectral) / jnp.expm1(spectral) ** 2


def pair_weight(own_freq, partner_freq, own_ids, partner_ids, lower_end, upper_end, broaden):
    inside = (
        (partner_ids[:, None] >= lower_end[None, :])
        & (partner_ids[:, None] < upper_end[None, :])
        & (partner_ids[:, None] != own_ids[None, :])
    )
    detune = own_freq[None, :] - partner_freq[:, None]
    lorentz = broaden / math.pi / (detune * detune + broaden * broaden)
    factor = (own_freq[None, :] + partner_freq[:, None]) ** 2 / (
        4.0 * own_freq[None, :] * partner_freq[:, None]
    )
    return jnp.where(inside, lorentz * factor, 0.0)


def add_totals(earlier, later):
    return earlier + later


def body(eigvec, force, bond, nbr, band, freq):
    atom_count = ATOM_DEV * lax.axis_size("atom")
    mode_count = MODE_DEV * lax.axis_size("mode")
    partner_span = MODE_DEV + 2 * HALF
    spectrum = lax.all_gather(freq, "mode", axis=0, tiled=True)
    atom_rows = extended(eigvec, (("atom", 1),), RIM, True)
    band_rows = extended(eigvec, (("mode", 2),), HALF, False)
    row_major = jnp.transpose(atom_rows, (1, 0, 2))
    domain = lax.axis_index("atom")
    local_ids = (nbr - domain * ATOM_DEV + RIM + atom_count) % atom_count
    block_size = min(512, ATOM_DEV)
    gathered = jnp.take(row_major, local_ids, axis=0)
    coupling = (bond[:, None, None, :, 0:block_size] * force[None, :, :, :, 0:block_size]).astype(
        jnp.bfloat16
    )
    block_image = jnp.einsum(
        "kcdna,nadi->kcai", coupling, gathered, preferred_element_type=jnp.float32
    )
    pieces = block_image.astype(jnp.bfloat16)
    pair_terms = jnp.einsum("caj,kcai->kji", band_rows, pieces, preferred_element_type=jnp.float32)
    mode_block = lax.axis_index("mode")
    mode_start = mode_block * MODE_DEV
    broaden = BROAD * (jnp.max(spectrum) - jnp.min(spectrum)) / (mode_count - 1)
    padded_freq = jnp.pad(spectrum, (HALF, HALF), constant_values=1.0)
    partner_freq = lax.dynamic_slice_in_dim(padded_freq, mode_start, partner_span)
    partner_ids = mode_start - HALF + jnp.arange(partner_span, dtype=jnp.int32)
    own_ids = mode_start + jnp.arange(MODE_DEV, dtype=jnp.int32)
    weight = pair_weight(freq, partner_freq, own_ids, partner_ids, band[0], band[1], broaden)
    summed_pair = lax.psum(pair_terms, "atom")
    strength = jnp.sum(summed_pair * summed_pair, axis=0)
    row_sums = jnp.sum(weight * strength, axis=0)
    diffusivity = math.pi / (3.0 * freq * freq) * row_sums
    running = jnp.cumsum(capacity_of(freq) * diffusivity)
    device_total = running[-1]
    earlier_sum = prefix(device_total, "mode", add_totals, jnp.float32(0.0))
    conductivity = (earlier_sum + running) / MODE_DEV
    return (diffusivity, conductivity)


def solution(mesh):
    in_specs = (
        P(None, "atom", "mode"),
        P(None, None, None, "atom"),
        P(None, None, "atom"),
        P(None, "atom"),
        P(None, "mode"),
        P("mode"),
    )
    out_specs = (P("mode"), P("mode"))
    return jax.shard_map(body, mesh=mesh, in_specs=in_specs, out_specs=out_specs, check_vma=False)
```

profile of v0, /device:TPU:0, one launch (start us, length us, event | category | flops | bytes accessed | tf_op | source)
XLA Modules:
  0.0 158.0 jit_solution(6767578995563934164)
XLA Ops:
  7.2 0.0 copy-start
  7.2 0.0 copy-start.3
  7.2 0.0 copy-start.2
  7.2 0.0 all-reduce.4.cloned.1.call-start
  7.2 1.4 copy.12
  8.6 0.0 copy-start.4
  8.6 0.2 fusion.21
  8.8 3.4 %collective-permute-start.1 = (bf16[3,128,256]{2,0,1:T(4,128)(2,1)S(1)}, bf16[3,128,256]{2,0,1:T(4,128)(2,1)}, u32[]{:S(2)}, u32[]{:S(2)}) collective-permute-start(bf16[3,128,256]{2,0,1:T(4,128)(2,1)S(1)} %get-tuple-element.39), channel_id=1, source_target_pairs={{4,0},{8,4},{12,8},{16,12},{20,16},{24,20},{28,24},{0,28},{5,1},{9... | collective-permute-start | bytes 589832 | tf_op jit(solution)/shard_map/ppermute | solution.py:23
  12.2 0.0 collective-permute-start
  12.2 0.0 copy-done
  12.2 0.8 fusion.22
  13.1 1.3 collective-permute-start.3
  14.3 5.2 %collective-permute-start.2 = (bf16[3,256,128]{2,1,0:T(8,128)(2,1)}, bf16[3,256,128]{2,1,0:T(8,128)(2,1)}, u32[]{:S(2)}, u32[]{:S(2)}) collective-permute-start(bf16[3,256,128]{2,1,0:T(8,128)(2,1)} %get-tuple-element.40), channel_id=1, source_target_pairs={{0,1},{1,2},{2,3},{4,5},{5,6},{6,7},{8,9},{9,10},{10,11},{12,13},{... | collective-permute-start | bytes 589832 | tf_op jit(solution)/shard_map/ppermute | solution.py:22
  19.6 0.0 copy-done.3
  19.6 0.0 copy-done.2
  19.6 0.7 copy.17
  20.4 0.0 copy-done.4
  20.4 1.1 copy.16
  21.5 0.7 copy.11
  22.2 0.0 copy-done.6
  22.2 9.4 %all-gather = f32[4,1,256]{2,1,0:T(1,128)} all-gather(f32[1,1,256]{2,1,0:T(1,128)S(1)} %bitcast.45), channel_id=1, replica_groups=mesh['atom'=8,'mode'=4] {'mode'}, dimensions={0}, use_global_device_ids=true | all-gather | bytes 5120 | tf_op jit(solution)/shard_map/all_gather | solution.py:65
  31.6 0.0 collective-permute-done.1
  31.6 0.0 collective-permute-done
  31.6 1.8 %maximum_bitcast_fusion = bf16[512,3,256]{2,1,0:T(4,128)(2,1)S(1)} fusion(bf16[3,128,256]{2,0,1:T(4,128)(2,1)} %collective-permute-done.1, bf16[3,256,256]{2,0,1:T(4,128)(2,1)S(1)} %copy.12, bf16[3,128,256]{2,0,1:T(4,128)(2,1)} %collective-permute-done), kind=kLoop, calls=%fused_computation.14 | loop fusion | flops 786432 | bytes 1572864 | tf_op jit(solution)/shard_map/transpose | solution.py:68
  33.3 0.0 copy-start.1
  33.4 32.8 %gather_fusion = bf16[4096,3,256]{2,1,0:T(4,128)(2,1)} fusion(bf16[512,3,256]{2,1,0:T(4,128)(2,1)S(1)} %maximum_bitcast_fusion, s32[4096]{0:T(1024)S(1)} %broadcast_clamp_fusion), kind=kCustom, calls=%fused_computation | custom fusion | bytes 12599296 | tf_op jit(solution)/shard_map/jit(_take)/gather | solution.py:72
  66.1 9.2 %fusion.8 = bf16[3,3,256,256]{3,1,0,2:T(4,128)(2,1)S(1)} fusion(f32[3,3,16,256]{2,0,1,3:T(4,128)S(1)} %copy.17, f32[3,16,256]{1,0,2:T(4,128)S(1)} %copy-done.1, bf16[16,256,3,256]{3,2,1,0:T(4,128)(2,1)} %bitcast.42, pred[16,256]{0,1:T(8,128)(4,1)} %copy.11), kind=kOutput, calls=%fused_computation.11 | convolution fusion | flops 60579840 | bytes 7671808 | tf_op jit(solution)/shard_map/kcdna,nadi->kcai/dot_general | solution.py:76
  75.4 0.0 collective-permute-done.3
  75.4 0.0 collective-permute-done.2
  75.4 3.0 %convolution_bitcast_fusion = f32[3,512,256]{1,2,0:T(8,128)} fusion(bf16[3,3,256,256]{3,1,0,2:T(4,128)(2,1)S(1)} %fusion.8, bf16[3,256,128]{2,1,0:T(8,128)(2,1)} %collective-permute-done.3, bf16[3,256,256]{2,1,0:T(8,128)(2,1)S(1)} %copy-done, bf16[3,256,128]{2,1,0:T(8,128)(2,1)} %collective-permute-done.2), kind=kOutput, calls=%fused_computation.12 | convolution fusion | flops 606339072 | bytes 3538944 | tf_op jit(solution)/shard_map/caj,kcai->kji/dot_general | solution.py:80
  78.4 0.0 all-reduce.4.cloned.1.call-update
  78.4 0.6 copy-done.5
  79.1 0.6 fusion.20
  81.0 0.0 copy-done.9
  81.0 0.6 dynamic-slice
  81.6 0.1 pad_dynamic-slice_fusion
  81.7 0.0 copy-done.7
  81.7 52.9 %all-reduce.4.cloned.1.call-done = f32[3,512,256]{1,2,0:T(8,128)} async-done(((f32[3,512,256]{1,2,0:T(8,128)}), f32[3,512,256]{1,2,0:T(8,128)}) %all-reduce.4.cloned.1.call-update) | async-done | bytes 1572880 | tf_op jit(solution)/shard_map/psum | solution.py:89
  134.6 1.6 %multiply_reduce_fusion = f32[512,256]{0,1:T(8,128)S(1)} fusion(f32[3,512,256]{1,2,0:T(8,128)} %all-reduce.4.cloned.1.call-done), kind=kLoop, calls=%fused_computation.10 | loop fusion | flops 655360 | bytes 2097152 | tf_op jit(solution)/shard_map/reduce_sum | solution.py:90
  136.3 0.5 multiply_reduce_fusion.1
  136.8 0.6 multiply_bitcast_fusion
  137.4 0.3 reduce-window.9
  137.7 0.1 slice.34
  137.8 0.1 slice_reduce_fusion
  137.9 0.1 add_bitcast_fusion
  138.0 0.8 slice_dynamic-update-slice_fusion
  138.8 11.8 %all-reduce.1 = f32[4]{0:T(128)S(1)} all-reduce(f32[4]{0:T(128)S(1)} %slice_dynamic-update-slice_fusion), channel_id=1, replica_groups=mesh['atom'=8,'mode'=4] {'mode'}, use_global_device_ids=true, to_apply=%add.1 | all-reduce | flops 4 | bytes 32
  150.6 0.6 add_multiply_fusion
  (18 shorter events, 0.1 us)
Async XLA Ops:
  7.2 5.1 %copy-start = (bf16[3,256,256]{2,1,0:T(8,128)(2,1)S(1)}, bf16[3,256,256]{2,1,0:T(8,128)(2,1)}, u32[]{:S(2)}) copy-start(bf16[3,256,256]{2,1,0:T(8,128)(2,1)} %param.8) | copy-start | bytes 1179652
  7.2 12.4 %copy-start.3 = (s32[16,256]{1,0:T(8,128)S(1)}, s32[16,256]{1,0:T(8,128)}, u32[]{:S(2)}) copy-start(s32[16,256]{1,0:T(8,128)} %param.11) | copy-start | bytes 49156
  7.2 12.4 %copy-start.2 = (f32[3,3,16,256]{3,2,1,0:T(8,128)S(1)}, f32[3,3,16,256]{3,2,1,0:T(8,128)}, u32[]{:S(2)}) copy-start(f32[3,3,16,256]{3,2,1,0:T(8,128)} %param.9) | copy-start | bytes 442372
  7.2 127.4 %all-reduce.4.cloned.1.call-start = ((), (), s32[]{:S(2)}) async-start(), calls=%async_computation | async-start | bytes 3145728 | tf_op jit(solution)/shard_map/psum | solution.py:89
  8.6 11.8 %copy-start.4 = (f32[3,16,256]{2,1,0:T(8,128)S(1)}, f32[3,16,256]{2,1,0:T(8,128)}, u32[]{:S(2)}) copy-start(f32[3,16,256]{2,1,0:T(8,128)} %param.10) | copy-start | bytes 147460
  8.8 22.7 %collective-permute-start.1 = (bf16[3,128,256]{2,0,1:T(4,128)(2,1)S(1)}, bf16[3,128,256]{2,0,1:T(4,128)(2,1)}, u32[]{:S(2)}, u32[]{:S(2)}) collective-permute-start(bf16[3,128,256]{2,0,1:T(4,128)(2,1)S(1)} %get-tuple-element.39), channel_id=1, source_target_pairs={{4,0},{8,4},{12,8},{16,12},{20,16},{24,20},{28,24},{0,28},{5,1},{9... | collective-permute-start | bytes 589832 | tf_op jit(solution)/shard_map/ppermute | solution.py:23
  12.2 10.0 %copy-start.6 = (f32[256]{0:T(256)S(1)}, f32[256]{0:T(256)}, u32[]{:S(2)}) copy-start(f32[256]{0:T(256)} %param.13) | copy-start | bytes 3076
  12.2 19.4 %collective-permute-start = (bf16[3,128,256]{2,0,1:T(4,128)(2,1)S(1)}, bf16[3,128,256]{2,0,1:T(4,128)(2,1)}, u32[]{:S(2)}, u32[]{:S(2)}) collective-permute-start(bf16[3,128,256]{2,0,1:T(4,128)(2,1)S(1)} %get-tuple-element.38), channel_id=1, source_target_pairs={{0,4},{4,8},{8,12},{12,16},{16,20},{20,24},{24,28},{28,0},{1,5},{5... | collective-permute-start | bytes 589832 | tf_op jit(solution)/shard_map/ppermute | solution.py:22
  13.1 62.3 %collective-permute-start.3 = (bf16[3,256,128]{2,1,0:T(8,128)(2,1)}, bf16[3,256,128]{2,1,0:T(8,128)(2,1)}, u32[]{:S(2)}, u32[]{:S(2)}) collective-permute-start(bf16[3,256,128]{2,1,0:T(8,128)(2,1)} %get-tuple-element.41), channel_id=1, source_target_pairs={{1,0},{2,1},{3,2},{5,4},{6,5},{7,6},{9,8},{10,9},{11,10},{13,12},{... | collective-permute-start | bytes 589832 | tf_op jit(solution)/shard_map/ppermute | solution.py:23
  14.3 61.1 %collective-permute-start.2 = (bf16[3,256,128]{2,1,0:T(8,128)(2,1)}, bf16[3,256,128]{2,1,0:T(8,128)(2,1)}, u32[]{:S(2)}, u32[]{:S(2)}) collective-permute-start(bf16[3,256,128]{2,1,0:T(8,128)(2,1)} %get-tuple-element.40), channel_id=1, source_target_pairs={{0,1},{1,2},{2,3},{4,5},{5,6},{6,7},{8,9},{9,10},{10,11},{12,13},{... | collective-permute-start | bytes 589832 | tf_op jit(solution)/shard_map/ppermute | solution.py:22
  33.3 32.8 %copy-start.1 = (f32[3,16,256]{1,0,2:T(4,128)S(1)}, f32[3,16,256]{1,0,2:T(4,128)}, u32[]{:S(2)}) copy-start(f32[3,16,256]{1,0,2:T(4,128)} %copy.16) | copy-start | bytes 147460
  78.4 0.7 copy-start.5
  78.4 2.6 %copy-start.9 = (u32[32]{0:T(128)S(1)}, u32[32]{0:T(128)}, u32[]{:S(2)}) copy-start(u32[32]{0:T(128)} %constant.93) | copy-start | bytes 388
  78.4 3.3 %copy-start.7 = (f32[256]{0:T(256)S(1)}, f32[256]{0:T(256)}, u32[]{:S(2)}) copy-start(f32[256]{0:T(256)} %param.13) | copy-start | bytes 3076
  78.4 3.3 %copy-start.8 = (s32[2,256]{1,0:T(2,128)S(1)}, s32[2,256]{1,0:T(2,128)}, u32[]{:S(2)}) copy-start(s32[2,256]{1,0:T(2,128)} %param.12) | copy-start | bytes 6148
Sparse Core Ops, SparseCore 0:
  78.6 56.0 all-reduce.3
where the time goes:
time: 158 us
  waiting for transfers between devices  52.9 us (33%)
  local copies, waits for them, and re-layouts  40 us (25%)
  blocking collectives  21.2 us (13%)
  between operations  15.5 us (10%)
  matrix products  12.2 us (8%)
  starting transfers between devices  9.95 us (6%)
  other arithmetic  6.14 us (4%)
    psum x1, waiting for transfers between devices, body(): summed_pair = lax.psum(pair_terms, 'atom')  52.9 us
    gather x1, local copies, waits for them, and re-layouts, body(): gathered = jnp.take(row_major, local_ids, axis=0)  32.8 us
    unnamed x1, blocking collectives  11.8 us
    all_gather x1, blocking collectives, body(): spectrum = lax.all_gather(freq, 'mode', axis=0, tiled=True)  9.39 us
    dot_general x1, matrix products, body(): jnp.einsum('kcdna,nadi->kcai', coupling, gathered, preferred_element_type...  9.23 us
    ppermute x2, starting transfers between devices, extended(): before = lax.ppermute(last, axis, up)  5.24 us
    unnamed x27, local copies, waits for them, and re-layouts  5.24 us
    ppermute x2, starting transfers between devices, extended(): after = lax.ppermute(first, axis, down)  4.67 us
  transfers between devices with their start and end apart: 5, of which 1 were waited for; matrix products, arithmetic and copies ran while one was open for 31% of the time, Pallas kernels for 0%

commit v1 on v0

v1 whole, which is shorter than its diff:
```python
import functools
import math

import jax
import jax.numpy as jnp
from jax import lax
from jax.experimental import pallas as pl
from jax.experimental.pallas import tpu as pltpu
from jax.sharding import PartitionSpec as P

RIM = 128
HALF = 128
BROAD = 128
GROUP = 16
EXTRA = 16
F32 = jnp.float32
BF16 = jnp.bfloat16
VMEM = pl.BlockSpec(memory_space=pltpu.VMEM)


def iota(shape, dim):
    return lax.broadcasted_iota(jnp.int32, shape, dim)


def coupling_kernel(atoms, force_ref, bond_ref, nbr_ref, out_ref, cpl_ref):
    comps, _, slots, own = force_ref.shape
    wide = slots * GROUP
    span = own + RIM
    start = lax.axis_index("atom") * own
    offset = nbr_ref[...] - start
    offset = jnp.where(offset < -RIM, offset + atoms, offset)
    offset = jnp.where(offset >= own + RIM, offset - atoms, offset)
    place = jnp.transpose((offset - RIM).astype(F32)).astype(BF16)
    spread = jnp.where(iota((slots, wide), 1) // GROUP == iota((slots, wide), 0), 1.0, 0.0).astype(BF16)
    same = iota((GROUP, wide), 0) == iota((GROUP, wide), 1) % GROUP
    placed = jnp.dot(place, spread, preferred_element_type=F32)
    bonds = [jnp.transpose(bond_ref[k]) for k in range(comps)]
    for c in range(comps):
        for d in range(comps):
            column = jnp.transpose(force_ref[c, d])
            for k in range(comps):
                cpl_ref[(k * comps + c) * comps + d] = (bonds[k] * column).astype(BF16)
    own_ids = iota((own, wide), 0) - RIM
    halves = own // RIM
    for h in range(halves):
        rim_ids = iota((RIM, wide), 0) + (-2 * RIM if h == 0 else own - RIM)
        ids = jnp.concatenate([own_ids, rim_ids], axis=0)
        for g in range(RIM // GROUP):
            base = h * RIM + g * GROUP
            row = jnp.sum(jnp.where(same, placed[base : base + GROUP], 0.0), axis=0, keepdims=True)
            hot = jnp.where(ids == row.astype(jnp.int32), 1.0, 0.0).astype(BF16)
            part = cpl_ref[:, base : base + GROUP, :].reshape(comps**3 * GROUP, slots)
            diag = jnp.dot(part, spread, preferred_element_type=F32).reshape(comps**3, GROUP, wide)
            diag = jnp.where(same[None], diag, 0.0).astype(BF16).reshape(comps**3 * GROUP, wide)
            block = lax.dot_general(diag, hot, (((1,), (1,)), ((), ())), preferred_element_type=F32)
            block = block.astype(BF16)
            for kc in range(comps * comps):
                rows = slice(kc * RIM + g * GROUP, kc * RIM + (g + 1) * GROUP)
                for d in range(comps):
                    top = (kc * comps + d) * GROUP
                    piece = block[top : top + GROUP]
                    out_ref[h, rows, d * own : (d + 1) * own] = piece[:, :own]
                    left = comps * own + d * RIM
                    out_ref[h, rows, left : left + RIM] = piece[:, own:span]


def coupling_matrix(force, bond, nbr, atoms):
    comps, _, slots, own = force.shape
    size = comps * (own + RIM)
    return pl.pallas_call(
        functools.partial(coupling_kernel, atoms),
        out_shape=jax.ShapeDtypeStruct((own // RIM, comps * comps * RIM, size), BF16),
        in_specs=[VMEM] * 3,
        out_specs=VMEM,
        scratch_shapes=[pltpu.VMEM((comps**3, own, slots), BF16)],
        compiler_params=pltpu.CompilerParams(vmem_limit_bytes=40 * 2**20),
        cost_estimate=pl.CostEstimate(flops=4 * 10**9, bytes_accessed=6 * 10**6, transcendentals=0),
    )(force, bond, nbr)


def pair_kernel(cpl_ref, own_ref, rim_one, rim_two, halo_one, halo_two, keep_ref, send_ref, rows_ref, flux_ref):
    comps, own, modes = own_ref.shape
    depth = comps * own
    place = lax.axis_index("atom")
    odd = lax.rem(place, 2) == 1
    high = lax.rem(lax.axis_index("mode"), 2) == 1
    for h in range(2):
        rows_ref[h, 0:depth] = own_ref[...].reshape(depth, modes)
    one = rim_one[...].reshape(comps * RIM, modes)
    two = rim_two[...].reshape(comps * RIM, modes)
    rows_ref[0, depth:] = jnp.where(odd, one, two)
    rows_ref[1, depth:] = jnp.where(odd, two, one)
    for h in range(2):
        image = jnp.dot(cpl_ref[h], rows_ref[h], preferred_element_type=F32).astype(BF16)
        for k in range(comps):
            for c in range(comps):
                top = (k * comps + c) * RIM
                flux_ref[c, h * RIM : (h + 1) * RIM, k * modes : (k + 1) * modes] = image[top : top + RIM]
    flux = flux_ref[...].reshape(depth, comps * modes)
    contract = (((0,), (0,)), ((), ()))
    pairs = lax.dot_general(own_ref[...].reshape(depth, modes), flux, contract, preferred_element_type=F32)
    first = halo_one[...].reshape(depth, HALF)
    second = halo_two[...].reshape(depth, HALF)
    before = jnp.where(high, first, second)
    after = jnp.where(high, second, first)
    low_flux = jnp.concatenate([flux[:, k * modes : k * modes + HALF] for k in range(comps)], axis=1)
    high_flux = jnp.concatenate([flux[:, k * modes + HALF : (k + 1) * modes] for k in range(comps)], axis=1)
    below = lax.dot_general(before, low_flux, contract, preferred_element_type=F32)
    above = lax.dot_general(after, high_flux, contract, preferred_element_type=F32)
    lower = iota((HALF, HALF), 0) > iota((HALF, HALF), 1)
    equal = iota((HALF, HALF), 0) == iota((HALF, HALF), 1)
    second_core = odd
    for k in range(comps):
        left, middle, right = k * modes, k * modes + HALF, (k + 1) * modes
        sets = []
        for part in range(2):
            if part == 0:
                main = pairs[0:HALF, left:middle]
                low = below[:, k * HALF : (k + 1) * HALF]
                up = pairs[HALF : 2 * HALF, left:middle]
            else:
                main = pairs[HALF : 2 * HALF, middle:right]
                low = pairs[0:HALF, middle:right]
                up = above[:, k * HALF : (k + 1) * HALF]
            edge = jnp.sum(jnp.where(equal, low, 0.0), axis=0, keepdims=True)
            edge = jnp.broadcast_to(edge, (EXTRA, HALF))
            sets.append(jnp.concatenate([main, jnp.where(lower, low, up), edge], axis=0))
        keep_ref[k] = jnp.where(second_core, sets[1], sets[0])
        send_ref[k] = jnp.where(second_core, sets[0], sets[1]).astype(BF16)


def pair_parts(matrix, eigvec, rim_one, rim_two, halo_one, halo_two):
    comps, own, modes = eigvec.shape
    shape = (comps, 2 * HALF + EXTRA, HALF)
    return pl.pallas_call(
        pair_kernel,
        out_shape=(jax.ShapeDtypeStruct(shape, F32), jax.ShapeDtypeStruct(shape, BF16)),
        in_specs=[VMEM] * 6,
        out_specs=(VMEM, VMEM),
        scratch_shapes=[
            pltpu.VMEM((own // RIM, comps * (own + RIM), modes), BF16),
            pltpu.VMEM((comps, own, comps * modes), BF16),
        ],
        compiler_params=pltpu.CompilerParams(vmem_limit_bytes=40 * 2**20),
        cost_estimate=pl.CostEstimate(flops=2 * 10**9, bytes_accessed=6 * 10**6, transcendentals=0),
    )(matrix, eigvec, rim_one, rim_two, halo_one, halo_two)


def weigh_kernel(modes, count, table_ref, eta_ref, band_ref, main_one, main_two, side_one, side_two, out_ref):
    part = lax.rem(lax.axis_index("atom"), 2)
    block = lax.axis_index("mode")
    base = block * (modes // HALF) + part
    start = block * modes + part * HALF
    prev = table_ref[pl.ds(base, 1), :]
    freq = table_ref[pl.ds(base + 1, 1), :]
    following = table_ref[pl.ds(base + 2, 1), :]
    low_end = band_ref[pl.ds(part, 1), :]
    high_end = band_ref[pl.ds(part + 2, 1), :]
    eta = eta_ref[0:1, :]

    def column(row):
        return jnp.transpose(jnp.broadcast_to(row, (HALF, HALF)))

    def weight(partner_freq, partner_ids, own_ids):
        inside = (partner_ids >= low_end) & (partner_ids < high_end) & (partner_ids != own_ids)
        detune = freq - partner_freq
        lorentz = (eta / math.pi) / (detune * detune + eta * eta)
        total = freq + partner_freq
        factor = total * total / (4.0 * freq * partner_freq)
        return jnp.where(inside, lorentz * factor, 0.0)

    rows = iota((HALF, HALF), 0)
    own_ids = start + iota((HALF, HALF), 1)
    lower = rows > iota((HALF, HALF), 1)
    main_weight = weight(column(freq), start + rows, own_ids)
    side_freq = jnp.where(lower, column(prev), column(following))
    side_weight = weight(side_freq, start + rows + jnp.where(lower, -HALF, HALF), own_ids)
    edge_own = start + iota((1, HALF), 1)
    edge_weight = weight(prev, edge_own - HALF, edge_own)
    comps = main_one.shape[0]
    main_strength = jnp.zeros((HALF, HALF), F32)
    side_strength = jnp.zeros((HALF, HALF), F32)
    edge_strength = jnp.zeros((1, HALF), F32)
    for k in range(comps):
        main = main_one[k].astype(F32) + main_two[k].astype(F32)
        side = side_one[k].astype(F32) + side_two[k].astype(F32)
        main_strength += main * main
        side_strength += side[:HALF] * side[:HALF]
        edge = side[HALF : HALF + 1]
        edge_strength += edge * edge
    total = jnp.sum(main_weight * main_strength + side_weight * side_strength, axis=0, keepdims=True)
    total += edge_weight * edge_strength
    out_ref[...] = math.pi / (3.0 * freq * freq) * total


def weigh(table, eta, band, main_one, main_two, side_one, side_two, modes, count):
    return pl.pallas_call(
        functools.partial(weigh_kernel, modes, count),
        out_shape=jax.ShapeDtypeStruct((1, HALF), F32),
        in_specs=[VMEM] * 7,
        out_specs=VMEM,
        cost_estimate=pl.CostEstimate(flops=10**6, bytes_accessed=10**6, transcendentals=0),
    )(table, eta, band, main_one, main_two, side_one, side_two)


def running_kernel(own_ref, other_ref, capacity_ref, diff_ref, run_ref, total_ref):
    modes = capacity_ref.shape[1]
    odd = lax.rem(lax.axis_index("atom"), 2) == 1
    own, other = own_ref[...], other_ref[...]
    diff = jnp.concatenate([jnp.where(odd, other, own), jnp.where(odd, own, other)], axis=1)
    diff_ref[...] = diff
    carried = capacity_ref[...] * diff
    until = jnp.where(iota((modes, modes), 0) <= iota((modes, modes), 1), 1.0, 0.0)
    running = jnp.dot(
        jnp.broadcast_to(carried, (8, modes)), until, precision=lax.Precision.HIGHEST, preferred_element_type=F32
    )
    run_ref[...] = running[0:1]
    total_ref[...] = jnp.broadcast_to(running[0:1, modes - 1 : modes], total_ref.shape)


def running_sum(own, other, capacity):
    modes = capacity.shape[1]
    row = jax.ShapeDtypeStruct((1, modes), F32)
    return pl.pallas_call(
        running_kernel,
        out_shape=(row, row, jax.ShapeDtypeStruct((1, HALF), F32)),
        in_specs=[VMEM] * 3,
        out_specs=(VMEM,) * 3,
    )(own, other, capacity)


def swap(x, axis, bit):
    return lax.ppermute(x, axis, [(i, i ^ bit) for i in range(lax.axis_size(axis))])


def bits_of(axis):
    return [1 << b for b in range(lax.axis_size(axis).bit_length() - 1)]


def rounded_sum(own, other):
    total = own.astype(F32) + other.astype(F32)
    return lax.reduce_precision(total, 8, 7).astype(BF16)


def body(eigvec, force, bond, nbr, band, freq):
    domains, blocks = lax.axis_size("atom"), lax.axis_size("mode")
    comps, own, modes = eigvec.shape
    atoms, count = own * domains, modes * blocks
    place, block = lax.axis_index("atom"), lax.axis_index("mode")
    odd, high = lax.rem(place, 2), lax.rem(block, 2)

    inner = [(i, i ^ 1) for i in range(domains)]
    outer = [(i, (i + 1) % domains if i % 2 else (i - 1) % domains) for i in range(domains)]
    rim_two = lax.ppermute(lax.dynamic_slice_in_dim(eigvec, (own - RIM) * odd, RIM, 1), "atom", outer)
    rim_one = lax.ppermute(lax.dynamic_slice_in_dim(eigvec, (own - RIM) * (1 - odd), RIM, 1), "atom", inner)
    near = [(i, i ^ 1) for i in range(blocks)]
    far = [(i, i + 1 if i % 2 else i - 1) for i in range(1, blocks - 1)]
    halo_one = lax.ppermute(lax.dynamic_slice_in_dim(eigvec, (modes - HALF) * (1 - high), HALF, 2), "mode", near)
    halo_two = lax.ppermute(lax.dynamic_slice_in_dim(eigvec, (modes - HALF) * high, HALF, 2), "mode", far)

    matrix = coupling_matrix(force, bond, nbr, atoms)
    keep, send = pair_parts(matrix, eigvec, rim_one, rim_two, halo_one, halo_two)

    spectrum = freq.reshape(1, modes)
    for bit in bits_of("mode"):
        other = swap(spectrum, "mode", bit)
        upper = (block & bit) != 0
        spectrum = jnp.where(
            upper, jnp.concatenate([other, spectrum], axis=0), jnp.concatenate([spectrum, other], axis=0)
        )
    eta = BROAD * (jnp.max(spectrum) - jnp.min(spectrum)) / (count - 1)
    eta = jnp.broadcast_to(eta, (8, HALF))
    table = jnp.pad(spectrum.reshape(count // HALF, HALF), ((1, 1), (0, 0)), constant_values=1.0)
    ends = band.reshape(2 * modes // HALF, HALF)
    capacity = (freq * freq * jnp.exp(freq) / jnp.expm1(freq) ** 2).reshape(1, modes)

    both = rounded_sum(keep, swap(send, "atom", 1))
    main, side = both[:, :HALF], both[:, HALF:]
    steps = bits_of("atom")[1:]
    for step, (one, two) in enumerate(zip(steps, reversed(steps))):
        main_other, side_other = swap(main, "atom", one), swap(side, "atom", two)
        if step < len(steps) - 1:
            main, side = rounded_sum(main, main_other), rounded_sum(side, side_other)
    diff_own = weigh(table, eta, ends, main, main_other, side, side_other, modes, count)

    diff, running, total = running_sum(diff_own, swap(diff_own, "atom", 1), capacity)
    earlier = jnp.zeros_like(total)
    for bit in bits_of("mode"):
        other = swap(total, "mode", bit)
        earlier = earlier + jnp.where((block & bit) != 0, other, 0.0)
        total = total + other
    conductivity = (earlier[0, 0] + running) / modes
    return diff.reshape(modes), conductivity.reshape(modes)


def solution(mesh):
    in_specs = (
        P(None, "atom", "mode"),
        P(None, None, None, "atom"),
        P(None, None, "atom"),
        P(None, "atom"),
        P(None, "mode"),
        P("mode"),
    )
    out_specs = (P("mode"), P("mode"))
    return jax.shard_map(body, mesh=mesh, in_specs=in_specs, out_specs=out_specs, check_vma=False)
```

time: 158 us -> 52.2 us (0.33)
  waiting for transfers between devices: 52.9 us -> 13.8 us
  local copies, waits for them, and re-layouts: 40 us -> 7 us
  blocking collectives: 21.2 us -> 0 us
  between operations: 15.5 us -> 2.13 us
  matrix products: 12.2 us -> 0 us
  Pallas kernels: 0 us -> 9.77 us
  starting transfers between devices: 9.95 us -> 16 us
  other arithmetic: 6.14 us -> 3.16 us
    psum x1 -> x0, waiting for transfers between devices: 52.9 us -> none  [body(): summed_pair = lax.psum(pair_terms, 'atom')]
    gather x1 -> x0, local copies, waits for them, and re-layouts: 32.8 us -> none  [body(): gathered = jnp.take(row_major, local_ids, axis=0)]
    ppermute x4 -> x14, waiting for transfers between devices: 0.01 us -> 13.8 us  [the longest x10 13.8 us: swap(): lax.ppermute(x, axis, [(i, i ^ bit) for i in range(lax.axis_size(axis))])]
    dot_general x2 -> x0, matrix products: 12.2 us -> none  [the longest x1 9.23 us: body(): jnp.einsum('kcdna,nadi->kcai', coupling, gathered, preferred_element_type...]
    unnamed x1 -> x0, blocking collectives: 11.8 us -> none
    pallas_call x0 -> x4, Pallas kernels: none -> 9.77 us  [the longest x1 4.31 us: coupling_matrix(): pl.pallas_call(functools.partial(coupling_kernel, atoms), out_shape=jax.S...]
    all_gather x1 -> x0, blocking collectives: 9.39 us -> none  [body(): spectrum = lax.all_gather(freq, 'mode', axis=0, tiled=True)]
    ppermute x4 -> x14, starting transfers between devices: 9.91 us -> 16 us  [the longest x10 9.51 us: swap(): lax.ppermute(x, axis, [(i, i ^ bit) for i in range(lax.axis_size(axis))])]
  transfers between devices with their start and end apart: 5 -> 14, of which waited for: 1 -> 7; matrix products, arithmetic and copies ran while one was open for 31% -> 7% of each run, Pallas kernels for 0% -> 8%
where the time goes in v1:
time: 52.2 us; the launch traced here: 51.8 us
  starting transfers between devices  16 us (31%)
  waiting for transfers between devices  13.8 us (26%)
  Pallas kernels  9.77 us (19%)
  local copies, waits for them, and re-layouts  7 us (13%)
  other arithmetic  3.16 us (6%)
  between operations  2.13 us (4%)
    ppermute x10, waiting for transfers between devices, swap(): lax.ppermute(x, axis, [(i, i ^ bit) for i in range(lax.axis_size(axis))])  13.8 us
    ppermute x10, starting transfers between devices, swap(): lax.ppermute(x, axis, [(i, i ^ bit) for i in range(lax.axis_size(axis))])  9.51 us
    pallas_call x1, Pallas kernels, coupling_matrix(): pl.pallas_call(functools.partial(coupling_kernel, atoms), out_shape=jax.S...  4.31 us
    ppermute x1, starting transfers between devices, body(): lax.ppermute(lax.dynamic_slice_in_dim(eigvec, (own - RIM) * odd, RIM, 1),...  3.56 us
    unnamed x22, local copies, waits for them, and re-layouts  3.06 us
    pallas_call x1, Pallas kernels, pair_parts(): pl.pallas_call(pair_kernel, out_shape=(jax.ShapeDtypeStruct(shape, F32),...  2.21 us
    pallas_call x1, Pallas kernels, weigh(): pl.pallas_call(functools.partial(weigh_kernel, modes, count), out_shape=j...  1.77 us
    ppermute x1, starting transfers between devices, body(): lax.ppermute(lax.dynamic_slice_in_dim(eigvec, (modes - HALF) * (1 - high)...  1.64 us
  transfers between devices with their start and end apart: 14, of which 7 were waited for; matrix products, arithmetic and copies ran while one was open for 7% of the time, Pallas kernels for 8%

profile of v1, /device:TPU:0, one launch (start us, length us, event | category | flops | bytes accessed | tf_op | source)
XLA Modules:
  0.0 51.8 jit_solution(92403798436562492)
XLA Ops:
  0.6 1.1 %constant_dynamic-slice_fusion.2 = (bf16[3,128,256]{2,1,0:T(8,128)(2,1)S(1)}, bf16[3,128,256]{2,1,0:T(8,128)(2,1)S(1)}) fusion(bf16[3,256,256]{2,1,0:T(8,128)(2,1)} %own_ref.1, s32[]{:T(128)S(6)} %select_n.52, s32[]{:T(128)S(6)} %select_n.51), kind=kLoop, calls=%fused_computation.9 | loop fusion | bytes 786440 | tf_op jit(solution)/shard_map/dynamic_slice | solution.py:254
  1.7 0.5 collective-permute-start.2
  2.2 3.6 %collective-permute-start.3 = (bf16[3,128,256]{2,1,0:T(8,128)(2,1)S(1)}, bf16[3,128,256]{2,1,0:T(8,128)(2,1)S(1)}, u32[]{:S(2)}, u32[]{:S(2)}) collective-permute-start(bf16[3,128,256]{2,1,0:T(8,128)(2,1)S(1)} %get-tuple-element.17), channel_id=1, source_target_pairs={{0,28},{4,8},{8,4},{12,16},{16,12},{20,24},{24,20},{28,0},{1,29},{... | collective-permute-start | bytes 589832 | tf_op jit(solution)/shard_map/ppermute | solution.py:254
  5.8 1.0 %constant_dynamic-slice_fusion = (bf16[3,256,128]{2,1,0:T(8,128)(2,1)S(1)}, bf16[3,256,128]{2,1,0:T(8,128)(2,1)S(1)}) fusion(bf16[3,256,256]{2,1,0:T(8,128)(2,1)} %own_ref.1, s32[]{:T(128)S(6)} %select_n.54, s32[]{:T(128)S(6)} %select_n.53), kind=kLoop, calls=%fused_computation.7 | loop fusion | bytes 786440 | tf_op jit(solution)/shard_map/dynamic_slice | solution.py:259
  6.8 1.6 %collective-permute-start.4 = (bf16[3,256,128]{2,1,0:T(8,128)(2,1)S(1)}, bf16[3,256,128]{2,1,0:T(8,128)(2,1)S(1)}, u32[]{:S(2)}, u32[]{:S(2)}) collective-permute-start(bf16[3,256,128]{2,1,0:T(8,128)(2,1)S(1)} %get-tuple-element.16), channel_id=1, source_target_pairs={{0,1},{1,0},{2,3},{3,2},{4,5},{5,4},{6,7},{7,6},{8,9},{9,8},{10,11... | collective-permute-start | bytes 589832 | tf_op jit(solution)/shard_map/ppermute | solution.py:258
  8.5 0.8 %collective-permute-start.5 = (bf16[3,256,128]{2,1,0:T(8,128)(2,1)S(1)}, bf16[3,256,128]{2,1,0:T(8,128)(2,1)S(1)}, u32[]{:S(2)}, u32[]{:S(2)}) collective-permute-start(bf16[3,256,128]{2,1,0:T(8,128)(2,1)S(1)} %get-tuple-element.15), channel_id=1, source_target_pairs={{1,2},{2,1},{5,6},{6,5},{9,10},{10,9},{13,14},{14,13},{17,18},{18,... | collective-permute-start | bytes 589832 | tf_op jit(solution)/shard_map/ppermute | solution.py:259
  9.3 0.0 copy-start.1
  9.3 0.9 %copy-done.1 = f32[3,3,16,256]{3,2,1,0:T(8,128)S(1)} copy-done((f32[3,3,16,256]{3,2,1,0:T(8,128)S(1)}, f32[3,3,16,256]{3,2,1,0:T(8,128)}, u32[]{:S(2)}) %copy-start.1) | copy-done | bytes 147480
  10.2 0.8 %copy-done.2 = f32[3,16,256]{2,1,0:T(8,128)S(1)} copy-done((f32[3,16,256]{2,1,0:T(8,128)S(1)}, f32[3,16,256]{2,1,0:T(8,128)}, u32[]{:S(2)}) %copy-start.2) | copy-done | bytes 49176
  11.0 0.7 %copy-done.3 = s32[16,256]{1,0:T(8,128)S(1)} copy-done((s32[16,256]{1,0:T(8,128)S(1)}, s32[16,256]{1,0:T(8,128)}, u32[]{:S(2)}) %copy-start.3) | copy-done | bytes 16408
  11.7 4.3 %shard_map.77.cpl_ref = bf16[2,1152,1152]{2,1,0:T(8,128)(2,1)S(1)} custom-call(f32[3,3,16,256]{3,2,1,0:T(8,128)S(1)} %copy-done.1, f32[3,16,256]{2,1,0:T(8,128)S(1)} %copy-done.2, s32[16,256]{1,0:T(8,128)S(1)} %copy-done.3), custom_call_target="tpu_custom_call" | custom-call | flops 4000000000 | bytes 6000000 | tf_op jit(solution)/shard_map/pallas_call | solution.py:70
  16.0 0.0 copy-start.8
  16.0 0.0 copy-start.9
  16.0 0.0 collective-permute-done.2.rim_one
  16.1 0.0 collective-permute-done.3.rim_two
  16.1 0.0 collective-permute-done.4.halo_one
  16.1 0.0 collective-permute-done.5.halo_two
  16.1 2.2 %shard_map.78 = (f32[3,272,128]{2,1,0:T(8,128)S(1)}, bf16[3,272,128]{2,1,0:T(8,128)(2,1)S(1)}) custom-call(bf16[2,1152,1152]{2,1,0:T(8,128)(2,1)S(1)} %shard_map.77.cpl_ref, bf16[3,256,256]{2,1,0:T(8,128)(2,1)S(1)} %copy-done, bf16[3,128,256]{2,1,0:T(8,128)(2,1)S(1)} %collective-permute-done.2.rim_one, ...), custom_call_target="tpu_custom_call" | custom-call | flops 2000000000 | bytes 6000000 | tf_op jit(solution)/shard_map/pallas_call | solution.py:135
  18.3 0.1 collective-permute-start.6
  18.4 4.4 %collective-permute-start = (f32[1,256]{1,0:T(1,128)S(1)}, f32[1,256]{1,0:T(1,128)S(1)}, u32[]{:S(2)}, u32[]{:S(2)}) collective-permute-start(f32[1,256]{1,0:T(1,128)S(1)} %bitcast.7), channel_id=1, source_target_pairs={{0,1},{1,0},{2,3},{3,2},{4,5},{5,4},{6,7},{7,6},{8,9},{9,8},{10,11... | collective-permute-start | bytes 3080 | tf_op jit(solution)/shard_map/ppermute | solution.py:233
  22.8 0.6 %reshape.25.band_ref = s32[4,128]{1,0:T(4,128)} reshape(s32[2,256]{1,0:T(2,128)S(1)} %copy-done.9) | data formatting | bytes 4096 | tf_op jit(solution)/shard_map/reshape | solution.py:274
  23.4 0.0 collective-permute-done.6
  23.5 0.1 collective-permute-start.7
  23.6 0.8 %collective-permute-done = f32[1,256]{1,0:T(1,128)S(1)} collective-permute-done((f32[1,256]{1,0:T(1,128)S(1)}, f32[1,256]{1,0:T(1,128)S(1)}, u32[]{:S(2)}, u32[]{:S(2)}) %collective-permute-start) | collective-permute-done | bytes 1056 | tf_op jit(solution)/shard_map/ppermute | solution.py:233
  24.4 1.5 %collective-permute-start.1 = (f32[2,256]{1,0:T(2,128)S(1)}, f32[2,256]{1,0:T(2,128)S(1)}, u32[]{:S(2)}, u32[]{:S(2)}) collective-permute-start(f32[2,256]{1,0:T(2,128)S(1)} %maximum_select_fusion.1), channel_id=1, source_target_pairs={{0,2},{1,3},{2,0},{3,1},{4,6},{5,7},{6,4},{7,5},{8,10},{9,11},{10,... | collective-permute-start | bytes 6152 | tf_op jit(solution)/shard_map/ppermute | solution.py:233
  26.0 0.6 %collective-permute-start.9 = (bf16[3,144,128]{2,1,0:T(8,128)(2,1)S(1)}, bf16[3,144,128]{2,1,0:T(8,128)(2,1)S(1)}, u32[]{:S(2)}, u32[]{:S(2)}) collective-permute-start(bf16[3,144,128]{2,1,0:T(8,128)(2,1)S(1)} %slice.13), channel_id=1, source_target_pairs={{0,16},{4,20},{8,24},{12,28},{16,0},{20,4},{24,8},{28,12},{1,17},{... | collective-permute-start | bytes 331784 | tf_op jit(solution)/shard_map/ppermute | solution.py:233
  26.5 1.9 %collective-permute-done.7 = bf16[3,128,128]{2,1,0:T(8,128)(2,1)S(1)} collective-permute-done((bf16[3,128,128]{2,1,0:T(8,128)(2,1)S(1)}, bf16[3,128,128]{2,1,0:T(8,128)(2,1)S(1)}, u32[]{:S(2)}, u32[]{:S(2)}) %collective-permute-start.7) | collective-permute-done | bytes 98336 | tf_op jit(solution)/shard_map/ppermute | solution.py:233
  28.5 0.6 %collective-permute-start.8 = (bf16[3,128,128]{2,1,0:T(8,128)(2,1)S(1)}, bf16[3,128,128]{2,1,0:T(8,128)(2,1)S(1)}, u32[]{:S(2)}, u32[]{:S(2)}) collective-permute-start(bf16[3,128,128]{2,1,0:T(8,128)(2,1)S(1)} %reduce-precision_convert_fusion.2.main_one), channel_id=1, source_target_pairs={{0,16},{4,20},{8,24},{12,28},{16,0},{20,4},{24,8},{28,12},{1,17},{... | collective-permute-start | bytes 294920 | tf_op jit(solution)/shard_map/ppermute | solution.py:233
  29.1 2.0 %collective-permute-done.9 = bf16[3,144,128]{2,1,0:T(8,128)(2,1)S(1)} collective-permute-done((bf16[3,144,128]{2,1,0:T(8,128)(2,1)S(1)}, bf16[3,144,128]{2,1,0:T(8,128)(2,1)S(1)}, u32[]{:S(2)}, u32[]{:S(2)}) %collective-permute-start.9) | collective-permute-done | bytes 110624 | tf_op jit(solution)/shard_map/ppermute | solution.py:233
  31.2 0.1 collective-permute-start.10
  31.2 0.0 collective-permute-done.1
  31.2 0.6 %fusion.1 = (f32[]{:T(128)}, f32[]{:T(128)}, f32[4,256]{1,0:T(4,128)S(1)}) fusion(f32[2,256]{1,0:T(2,128)S(1)} %collective-permute-done.1, f32[2,256]{1,0:T(2,128)S(1)} %maximum_select_fusion.1, pred[]{:T(512)S(6)} %ne.8), kind=kLoop, calls=%fused_computation.14 | loop fusion | flops 5118 | bytes 8201 | tf_op jit(solution)/shard_map/reduce_min | solution.py:271
  33.2 0.6 %pad.4.table_ref = f32[10,128]{1,0:T(8,128)} pad(f32[8,128]{1,0:T(8,128)S(1)} %select_n.50, f32[]{:T(128)} %constant.13.clone.1), padding=1_1x0_0 | pad | bytes 9220 | tf_op jit(solution)/shard_map/jit(_pad)/pad | solution.py:273
  33.8 2.2 %collective-permute-done.10.side_two = bf16[3,144,128]{2,1,0:T(8,128)(2,1)S(1)} collective-permute-done((bf16[3,144,128]{2,1,0:T(8,128)(2,1)S(1)}, bf16[3,144,128]{2,1,0:T(8,128)(2,1)S(1)}, u32[]{:S(2)}, u32[]{:S(2)}) %collective-permute-start.10) | collective-permute-done | bytes 110624 | tf_op jit(solution)/shard_map/ppermute | solution.py:233
  36.0 0.6 %broadcast_in_dim.8.eta_ref = f32[8,128]{1,0:T(8,128)} broadcast(f32[]{:T(128)S(6)} %div.12), dimensions={} | broadcast | bytes 4100 | tf_op jit(solution)/shard_map/broadcast_in_dim | solution.py:272
  36.6 0.0 copy-done.6
  36.6 1.8 %shard_map.79.own_ref = f32[1,128]{1,0:T(1,128)} custom-call(f32[10,128]{1,0:T(8,128)} %pad.4.table_ref, f32[8,128]{1,0:T(8,128)} %broadcast_in_dim.8.eta_ref, s32[4,128]{1,0:T(4,128)} %reshape.25.band_ref, bf16[3,128,128]{2,1,0:T(8,128)(2,1)} %copy-done.5, bf16[3,128,128]{2,1,0:T(8,128)(2,1)} %copy-done.7, bf16[3,144,128]{2,1,0:T(8,128)(2,1)} %copy-done.4, ...), custom_call_target="tpu_custom_call" | custom-call | flops 1000000 | bytes 1000000 | tf_op jit(solution)/shard_map/pallas_call | solution.py:197
  38.4 0.0 collective-permute-start.11
  38.4 0.6 %multiply_divide_fusion = f32[256]{0:T(256)} fusion(f32[256]{0:T(256)S(1)} %copy-done.8), kind=kLoop, calls=%fused_computation.6 | loop fusion | flops 1024 | bytes 2048 | tf_op jit(solution)/shard_map/div | solution.py:275
  39.0 0.7 %collective-permute-done.11.other_ref = f32[1,128]{1,0:T(1,128)S(1)} collective-permute-done((f32[1,128]{1,0:T(1,128)}, f32[1,128]{1,0:T(1,128)S(1)}, u32[]{:S(2)}, u32[]{:S(2)}) %collective-permute-start.11) | collective-permute-done | bytes 544 | tf_op jit(solution)/shard_map/ppermute | solution.py:233
  39.7 0.6 %copy-done.10 = f32[1,128]{1,0:T(1,128)} copy-done((f32[1,128]{1,0:T(1,128)}, f32[1,128]{1,0:T(1,128)S(1)}, u32[]{:S(2)}) %copy-start.10) | copy-done | bytes 536
  40.3 1.5 %shard_map.80 = (f32[1,256]{1,0:T(1,128)}, f32[1,256]{1,0:T(1,128)}, f32[1,128]{1,0:T(1,128)}) custom-call(f32[1,128]{1,0:T(1,128)} %shard_map.79.own_ref, f32[1,128]{1,0:T(1,128)} %copy-done.10, f32[1,256]{1,0:T(1,128)} %bitcast.6), custom_call_target="tpu_custom_call" | custom-call | tf_op jit(solution)/shard_map/pallas_call | solution.py:224
  41.8 0.3 collective-permute-start.12
  42.1 3.4 %collective-permute-done.12 = f32[1,128]{1,0:T(1,128)S(1)} collective-permute-done((f32[1,128]{1,0:T(1,128)}, f32[1,128]{1,0:T(1,128)S(1)}, u32[]{:S(2)}, u32[]{:S(2)}) %collective-permute-start.12) | collective-permute-done | bytes 544 | tf_op jit(solution)/shard_map/ppermute | solution.py:233
  45.5 0.6 %add.42 = f32[1,128]{1,0:T(1,128)S(1)} add(f32[1,128]{1,0:T(1,128)} %get-tuple-element.10, f32[1,128]{1,0:T(1,128)S(1)} %collective-permute-done.12) | non-fusion elementwise | flops 128 | bytes 1536 | tf_op jit(solution)/shard_map/add | solution.py:291
  46.2 1.8 %collective-permute-start.13 = (f32[1,128]{1,0:T(1,128)S(1)}, f32[1,128]{1,0:T(1,128)S(1)}, u32[]{:S(2)}, u32[]{:S(2)}) collective-permute-start(f32[1,128]{1,0:T(1,128)S(1)} %add.42), channel_id=1, source_target_pairs={{0,2},{1,3},{2,0},{3,1},{4,6},{5,7},{6,4},{7,5},{8,10},{9,11},{10,... | collective-permute-start | bytes 1544 | tf_op jit(solution)/shard_map/ppermute | solution.py:233
  48.0 2.6 %collective-permute-done.13 = f32[1,128]{1,0:T(1,128)S(1)} collective-permute-done((f32[1,128]{1,0:T(1,128)S(1)}, f32[1,128]{1,0:T(1,128)S(1)}, u32[]{:S(2)}, u32[]{:S(2)}) %collective-permute-start.13) | collective-permute-done | bytes 544 | tf_op jit(solution)/shard_map/ppermute | solution.py:233
  50.6 1.2 %add_multiply_fusion = f32[1,256]{1,0:T(1,128)} fusion(f32[1,256]{1,0:T(1,128)} %get-tuple-element.11, f32[]{:T(128)S(1)} %bitcast.9), kind=kLoop, calls=%fused_computation.5 | loop fusion | flops 512 | bytes 2052 | tf_op jit(solution)/shard_map/div | solution.py:292
  (23 shorter events, 0.2 us)
Async XLA Ops:
  1.7 14.3 %collective-permute-start.2 = (bf16[3,128,256]{2,1,0:T(8,128)(2,1)S(1)}, bf16[3,128,256]{2,1,0:T(8,128)(2,1)S(1)}, u32[]{:S(2)}, u32[]{:S(2)}) collective-permute-start(bf16[3,128,256]{2,1,0:T(8,128)(2,1)S(1)} %get-tuple-element.18), channel_id=1, source_target_pairs={{0,4},{4,0},{8,12},{12,8},{16,20},{20,16},{24,28},{28,24},{1,5},{5... | collective-permute-start | bytes 589832 | tf_op jit(solution)/shard_map/ppermute | solution.py:255
  2.2 13.8 %collective-permute-start.3 = (bf16[3,128,256]{2,1,0:T(8,128)(2,1)S(1)}, bf16[3,128,256]{2,1,0:T(8,128)(2,1)S(1)}, u32[]{:S(2)}, u32[]{:S(2)}) collective-permute-start(bf16[3,128,256]{2,1,0:T(8,128)(2,1)S(1)} %get-tuple-element.17), channel_id=1, source_target_pairs={{0,28},{4,8},{8,4},{12,16},{16,12},{20,24},{24,20},{28,0},{1,29},{... | collective-permute-start | bytes 589832 | tf_op jit(solution)/shard_map/ppermute | solution.py:254
  6.8 9.2 %collective-permute-start.4 = (bf16[3,256,128]{2,1,0:T(8,128)(2,1)S(1)}, bf16[3,256,128]{2,1,0:T(8,128)(2,1)S(1)}, u32[]{:S(2)}, u32[]{:S(2)}) collective-permute-start(bf16[3,256,128]{2,1,0:T(8,128)(2,1)S(1)} %get-tuple-element.16), channel_id=1, source_target_pairs={{0,1},{1,0},{2,3},{3,2},{4,5},{5,4},{6,7},{7,6},{8,9},{9,8},{10,11... | collective-permute-start | bytes 589832 | tf_op jit(solution)/shard_map/ppermute | solution.py:258
  8.5 7.6 %copy-start = (bf16[3,256,256]{2,1,0:T(8,128)(2,1)S(1)}, bf16[3,256,256]{2,1,0:T(8,128)(2,1)}, u32[]{:S(2)}) copy-start(bf16[3,256,256]{2,1,0:T(8,128)(2,1)} %own_ref.1) | copy-start | bytes 1179652
  8.5 7.6 %collective-permute-start.5 = (bf16[3,256,128]{2,1,0:T(8,128)(2,1)S(1)}, bf16[3,256,128]{2,1,0:T(8,128)(2,1)S(1)}, u32[]{:S(2)}, u32[]{:S(2)}) collective-permute-start(bf16[3,256,128]{2,1,0:T(8,128)(2,1)S(1)} %get-tuple-element.15), channel_id=1, source_target_pairs={{1,2},{2,1},{5,6},{6,5},{9,10},{10,9},{13,14},{14,13},{17,18},{18,... | collective-permute-start | bytes 589832 | tf_op jit(solution)/shard_map/ppermute | solution.py:259
  9.3 0.9 %copy-start.1 = (f32[3,3,16,256]{3,2,1,0:T(8,128)S(1)}, f32[3,3,16,256]{3,2,1,0:T(8,128)}, u32[]{:S(2)}) copy-start(f32[3,3,16,256]{3,2,1,0:T(8,128)} %force_ref.1) | copy-start | bytes 442372
  10.2 0.8 %copy-start.2 = (f32[3,16,256]{2,1,0:T(8,128)S(1)}, f32[3,16,256]{2,1,0:T(8,128)}, u32[]{:S(2)}) copy-start(f32[3,16,256]{2,1,0:T(8,128)} %bond_ref.1) | copy-start | bytes 147460
  11.0 0.7 %copy-start.3 = (s32[16,256]{1,0:T(8,128)S(1)}, s32[16,256]{1,0:T(8,128)}, u32[]{:S(2)}) copy-start(s32[16,256]{1,0:T(8,128)} %nbr_ref.1) | copy-start | bytes 49156
  16.0 2.4 %copy-start.8 = (f32[256]{0:T(256)S(1)}, f32[256]{0:T(256)}, u32[]{:S(2)}) copy-start(f32[256]{0:T(256)} %param.11) | copy-start | bytes 3076
  16.0 6.8 %copy-start.9 = (s32[2,256]{1,0:T(2,128)S(1)}, s32[2,256]{1,0:T(2,128)}, u32[]{:S(2)}) copy-start(s32[2,256]{1,0:T(2,128)} %param.10) | copy-start | bytes 6148
  18.3 5.1 %collective-permute-start.6 = (bf16[3,272,128]{2,1,0:T(8,128)(2,1)S(1)}, bf16[3,272,128]{2,1,0:T(8,128)(2,1)S(1)}, u32[]{:S(2)}, u32[]{:S(2)}) collective-permute-start(bf16[3,272,128]{2,1,0:T(8,128)(2,1)S(1)} %get-tuple-element.8), channel_id=1, source_target_pairs={{0,4},{4,0},{8,12},{12,8},{16,20},{20,16},{24,28},{28,24},{1,5},{5... | collective-permute-start | bytes 626696 | tf_op jit(solution)/shard_map/ppermute | solution.py:233
  18.4 6.0 %collective-permute-start = (f32[1,256]{1,0:T(1,128)S(1)}, f32[1,256]{1,0:T(1,128)S(1)}, u32[]{:S(2)}, u32[]{:S(2)}) collective-permute-start(f32[1,256]{1,0:T(1,128)S(1)} %bitcast.7), channel_id=1, source_target_pairs={{0,1},{1,0},{2,3},{3,2},{4,5},{5,4},{6,7},{7,6},{8,9},{9,8},{10,11... | collective-permute-start | bytes 3080 | tf_op jit(solution)/shard_map/ppermute | solution.py:233
  23.5 4.9 %collective-permute-start.7 = (bf16[3,128,128]{2,1,0:T(8,128)(2,1)S(1)}, bf16[3,128,128]{2,1,0:T(8,128)(2,1)S(1)}, u32[]{:S(2)}, u32[]{:S(2)}) collective-permute-start(bf16[3,128,128]{2,1,0:T(8,128)(2,1)S(1)} %slice.12), channel_id=1, source_target_pairs={{0,8},{4,12},{8,0},{12,4},{16,24},{20,28},{24,16},{28,20},{1,9},{5... | collective-permute-start | bytes 294920 | tf_op jit(solution)/shard_map/ppermute | solution.py:233
  24.4 6.8 %collective-permute-start.1 = (f32[2,256]{1,0:T(2,128)S(1)}, f32[2,256]{1,0:T(2,128)S(1)}, u32[]{:S(2)}, u32[]{:S(2)}) collective-permute-start(f32[2,256]{1,0:T(2,128)S(1)} %maximum_select_fusion.1), channel_id=1, source_target_pairs={{0,2},{1,3},{2,0},{3,1},{4,6},{5,7},{6,4},{7,5},{8,10},{9,11},{10,... | collective-permute-start | bytes 6152 | tf_op jit(solution)/shard_map/ppermute | solution.py:233
  26.0 5.1 %collective-permute-start.9 = (bf16[3,144,128]{2,1,0:T(8,128)(2,1)S(1)}, bf16[3,144,128]{2,1,0:T(8,128)(2,1)S(1)}, u32[]{:S(2)}, u32[]{:S(2)}) collective-permute-start(bf16[3,144,128]{2,1,0:T(8,128)(2,1)S(1)} %slice.13), channel_id=1, source_target_pairs={{0,16},{4,20},{8,24},{12,28},{16,0},{20,4},{24,8},{28,12},{1,17},{... | collective-permute-start | bytes 331784 | tf_op jit(solution)/shard_map/ppermute | solution.py:233
  28.5 8.1 %copy-start.5 = (bf16[3,128,128]{2,1,0:T(8,128)(2,1)}, bf16[3,128,128]{2,1,0:T(8,128)(2,1)S(1)}, u32[]{:S(2)}) copy-start(bf16[3,128,128]{2,1,0:T(8,128)(2,1)S(1)} %reduce-precision_convert_fusion.2.main_one) | copy-start | bytes 294916
  28.5 5.3 %collective-permute-start.8 = (bf16[3,128,128]{2,1,0:T(8,128)(2,1)S(1)}, bf16[3,128,128]{2,1,0:T(8,128)(2,1)S(1)}, u32[]{:S(2)}, u32[]{:S(2)}) collective-permute-start(bf16[3,128,128]{2,1,0:T(8,128)(2,1)S(1)} %reduce-precision_convert_fusion.2.main_one), channel_id=1, source_target_pairs={{0,16},{4,20},{8,24},{12,28},{16,0},{20,4},{24,8},{28,12},{1,17},{... | collective-permute-start | bytes 294920 | tf_op jit(solution)/shard_map/ppermute | solution.py:233
  31.1 5.5 %copy-start.4 = (bf16[3,144,128]{2,1,0:T(8,128)(2,1)}, bf16[3,144,128]{2,1,0:T(8,128)(2,1)S(1)}, u32[]{:S(2)}) copy-start(bf16[3,144,128]{2,1,0:T(8,128)(2,1)S(1)} %reduce-precision_convert_fusion.1.side_one) | copy-start | bytes 331780
  31.2 4.8 %collective-permute-start.10 = (bf16[3,144,128]{2,1,0:T(8,128)(2,1)S(1)}, bf16[3,144,128]{2,1,0:T(8,128)(2,1)S(1)}, u32[]{:S(2)}, u32[]{:S(2)}) collective-permute-start(bf16[3,144,128]{2,1,0:T(8,128)(2,1)S(1)} %reduce-precision_convert_fusion.1.side_one), channel_id=1, source_target_pairs={{0,8},{4,12},{8,0},{12,4},{16,24},{20,28},{24,16},{28,20},{1,9},{5... | collective-permute-start | bytes 331784 | tf_op jit(solution)/shard_map/ppermute | solution.py:233
  33.8 2.8 %copy-start.7 = (bf16[3,128,128]{2,1,0:T(8,128)(2,1)}, bf16[3,128,128]{2,1,0:T(8,128)(2,1)S(1)}, u32[]{:S(2)}) copy-start(bf16[3,128,128]{2,1,0:T(8,128)(2,1)S(1)} %collective-permute-done.8.main_two) | copy-start | bytes 294916
  36.0 0.6 %copy-start.6 = (bf16[3,144,128]{2,1,0:T(8,128)(2,1)}, bf16[3,144,128]{2,1,0:T(8,128)(2,1)S(1)}, u32[]{:S(2)}) copy-start(bf16[3,144,128]{2,1,0:T(8,128)(2,1)S(1)} %collective-permute-done.10.side_two) | copy-start | bytes 331780
  38.4 1.3 %collective-permute-start.11 = (f32[1,128]{1,0:T(1,128)}, f32[1,128]{1,0:T(1,128)S(1)}, u32[]{:S(2)}, u32[]{:S(2)}) collective-permute-start(f32[1,128]{1,0:T(1,128)} %shard_map.79.own_ref), channel_id=1, source_target_pairs={{0,4},{4,0},{8,12},{12,8},{16,20},{20,16},{24,28},{28,24},{1,5},{5... | collective-permute-start | bytes 1544 | tf_op jit(solution)/shard_map/ppermute | solution.py:233
  39.7 0.6 %copy-start.10 = (f32[1,128]{1,0:T(1,128)}, f32[1,128]{1,0:T(1,128)S(1)}, u32[]{:S(2)}) copy-start(f32[1,128]{1,0:T(1,128)S(1)} %collective-permute-done.11.other_ref) | copy-start | bytes 1540
  41.8 3.8 %collective-permute-start.12 = (f32[1,128]{1,0:T(1,128)}, f32[1,128]{1,0:T(1,128)S(1)}, u32[]{:S(2)}, u32[]{:S(2)}) collective-permute-start(f32[1,128]{1,0:T(1,128)} %get-tuple-element.10), channel_id=1, source_target_pairs={{0,1},{1,0},{2,3},{3,2},{4,5},{5,4},{6,7},{7,6},{8,9},{9,8},{10,11... | collective-permute-start | bytes 1544 | tf_op jit(solution)/shard_map/ppermute | solution.py:233
  46.2 4.4 %collective-permute-start.13 = (f32[1,128]{1,0:T(1,128)S(1)}, f32[1,128]{1,0:T(1,128)S(1)}, u32[]{:S(2)}, u32[]{:S(2)}) collective-permute-start(f32[1,128]{1,0:T(1,128)S(1)} %add.42), channel_id=1, source_target_pairs={{0,2},{1,3},{2,0},{3,1},{4,6},{5,7},{6,4},{7,5},{8,10},{9,11},{10,... | collective-permute-start | bytes 1544 | tf_op jit(solution)/shard_map/ppermute | solution.py:233

commit v2 on v1

--- a/solution.py
+++ b/solution.py
@@ -16,13 +16,70 @@
 F32 = jnp.float32
 BF16 = jnp.bfloat16
 VMEM = pl.BlockSpec(memory_space=pltpu.VMEM)
+ANY = pl.BlockSpec(memory_space=pl.ANY)
+SMALL = 8 * 2**20
+LARGE = 24 * 2**20
 
 
 def iota(shape, dim):
     return lax.broadcasted_iota(jnp.int32, shape, dim)
 
 
-def coupling_kernel(atoms, force_ref, bond_ref, nbr_ref, out_ref, cpl_ref):
+def edge_kernel(eig_ref, freq_ref, inner_ref, outer_ref, near_ref, far_ref, sems):
+    comps, own, modes = eig_ref.shape
+    odd = lax.rem(lax.axis_index("atom"), 2)
+    high = lax.rem(lax.axis_index("mode"), 2)
+
+    def rows(flag):
+        return pl.ds(pl.multiple_of(flag * (own - RIM), RIM), RIM)
+
+    def columns(flag):
+        return pl.ds(pl.multiple_of(flag * (modes - HALF), HALF), HALF)
+
+    copies = [
+        pltpu.make_async_copy(eig_ref.at[:, rows(odd), :], outer_ref, sems.at[0]),
+        pltpu.make_async_copy(eig_ref.at[:, rows(1 - odd), :], inner_ref, sems.at[1]),
+        pltpu.make_async_copy(eig_ref.at[:, :, columns(1 - high)], near_ref.at[:, pl.ds(0, own), :], sems.at[2]),
+        pltpu.make_async_copy(eig_ref.at[:, :, columns(high)], far_ref.at[:, pl.ds(0, own), :], sems.at[3]),
+    ]
+    for copy in copies:
+        copy.start()
+    freq = freq_ref[...]
+    rest = jnp.where(iota((EXTRA, HALF), 0) < EXTRA // 2, freq[:, 0:HALF], freq[:, modes - HALF : modes])
+    for part in range(comps):
+        piece = rest.astype(BF16)
+        rest = rest - piece.astype(F32)
+        near_ref[part, own : own + EXTRA, :] = piece
+        far_ref[part, own : own + EXTRA, :] = piece
+    for copy in copies:
+        copy.wait()
+
+
+def edges(eigvec, freq):
+    comps, own, modes = eigvec.shape
+    rim = jax.ShapeDtypeStruct((comps, RIM, modes), BF16)
+    halo = jax.ShapeDtypeStruct((comps, own + EXTRA, HALF), BF16)
+    return pl.pallas_call(
+        edge_kernel,
+        out_shape=(rim, rim, halo, halo),
+        in_specs=[ANY, VMEM],
+        out_specs=(VMEM,) * 4,
+        scratch_shapes=[pltpu.SemaphoreType.DMA((4,))],
+        compiler_params=pltpu.CompilerParams(vmem_limit_bytes=SMALL),
+        cost_estimate=pl.CostEstimate(flops=10**4, bytes_accessed=10**6, transcendentals=0),
+    )(eigvec, freq)
+
+
+def coupling_kernel(atoms, force_hbm, bond_hbm, nbr_hbm, out_ref, force_ref, bond_ref, nbr_ref, cpl_ref, sems):
+    copies = [
+        pltpu.make_async_copy(nbr_hbm, nbr_ref, sems.at[0]),
+        pltpu.make_async_copy(bond_hbm, bond_ref, sems.at[1]),
+        pltpu.make_async_copy(force_hbm, force_ref, sems.at[2]),
+    ]
+    for copy in copies:
+        copy.start()
+    for copy in copies:
+        copy.wait()
     comps, _, slots, own = force_ref.shape
     wide = slots * GROUP
     span = own + RIM
@@ -70,10 +127,16 @@
     return pl.pallas_call(
         functools.partial(coupling_kernel, atoms),
         out_shape=jax.ShapeDtypeStruct((own // RIM, comps * comps * RIM, size), BF16),
-        in_specs=[VMEM] * 3,
+        in_specs=[ANY] * 3,
         out_specs=VMEM,
-        scratch_shapes=[pltpu.VMEM((comps**3, own, slots), BF16)],
-        compiler_params=pltpu.CompilerParams(vmem_limit_bytes=40 * 2**20),
+        scratch_shapes=[
+            pltpu.VMEM(force.shape, force.dtype),
+            pltpu.VMEM(bond.shape, bond.dtype),
+            pltpu.VMEM(nbr.shape, nbr.dtype),
+            pltpu.VMEM((comps**3, own, slots), BF16),
+            pltpu.SemaphoreType.DMA((3,)),
+        ],
+        compiler_params=pltpu.CompilerParams(vmem_limit_bytes=LARGE),
         cost_estimate=pl.CostEstimate(flops=4 * 10**9, bytes_accessed=6 * 10**6, transcendentals=0),
     )(force, bond, nbr)
 
@@ -99,8 +162,8 @@
     flux = flux_ref[...].reshape(depth, comps * modes)
     contract = (((0,), (0,)), ((), ()))
     pairs = lax.dot_general(own_ref[...].reshape(depth, modes), flux, contract, preferred_element_type=F32)
-    first = halo_one[...].reshape(depth, HALF)
-    second = halo_two[...].reshape(depth, HALF)
+    first = halo_one[:, 0:own, :].reshape(depth, HALF)
+    second = halo_two[:, 0:own, :].reshape(depth, HALF)
     before = jnp.where(high, first, second)
     after = jnp.where(high, second, first)
     low_flux = jnp.concatenate([flux[:, k * modes : k * modes + HALF] for k in range(comps)], axis=1)
@@ -141,33 +204,56 @@
             pltpu.VMEM((own // RIM, comps * (own + RIM), modes), BF16),
             pltpu.VMEM((comps, own, comps * modes), BF16),
         ],
-        compiler_params=pltpu.CompilerParams(vmem_limit_bytes=40 * 2**20),
+        compiler_params=pltpu.CompilerParams(vmem_limit_bytes=LARGE),
         cost_estimate=pl.CostEstimate(flops=2 * 10**9, bytes_accessed=6 * 10**6, transcendentals=0),
     )(matrix, eigvec, rim_one, rim_two, halo_one, halo_two)
 
 
-def weigh_kernel(modes, count, table_ref, eta_ref, band_ref, main_one, main_two, side_one, side_two, out_ref):
-    part = lax.rem(lax.axis_index("atom"), 2)
-    block = lax.axis_index("mode")
-    base = block * (modes // HALF) + part
-    start = block * modes + part * HALF
-    prev = table_ref[pl.ds(base, 1), :]
-    freq = table_ref[pl.ds(base + 1, 1), :]
-    following = table_ref[pl.ds(base + 2, 1), :]
-    low_end = band_ref[pl.ds(part, 1), :]
-    high_end = band_ref[pl.ds(part + 2, 1), :]
-    eta = eta_ref[0:1, :]
+def halo_freq(halo_ref, own):
+    total = jnp.zeros((EXTRA, HALF), F32)
+    for part in reversed(range(halo_ref.shape[0])):
+        total = halo_ref[part, own : own + EXTRA, :].astype(F32) + total
+    return total[0:1], total[EXTRA // 2 : EXTRA // 2 + 1]
+
+
+def ends_kernel(own, freq_ref, halo_ref, out_ref):
+    modes = freq_ref.shape[1]
+    rows = (freq_ref[:, 0:HALF], freq_ref[:, modes - HALF : modes], *halo_freq(halo_ref, own))
+    least = jnp.min(functools.reduce(jnp.minimum, rows), axis=1, keepdims=True)
+    most = jnp.max(functools.reduce(jnp.maximum, rows), axis=1, keepdims=True)
+    out_ref[...] = jnp.where(iota(out_ref.shape, 0) < 4, least, most)
+
+
+def weigh_kernel(count, own, freq_ref, ends_ref, band_ref, halo_one, halo_two, main_one, main_two, side_one, side_two, out_ref):
+    comps = main_one.shape[0]
+    modes = freq_ref.shape[1]
+    second = lax.rem(lax.axis_index("atom"), 2) == 1
+    high = lax.rem(lax.axis_index("mode"), 2) == 1
+    shift = jnp.where(second, HALF, 0)
+    start = lax.axis_index("mode") * modes + shift
+    (one_first, one_last), (two_first, two_last) = halo_freq(halo_one, own), halo_freq(halo_two, own)
+    one, two = jnp.where(high, one_last, one_first), jnp.where(high, two_first, two_last)
+    outside = jnp.where(high == second, two, one)
+    inside = jnp.where(second, freq_ref[:, 0:HALF], freq_ref[:, HALF:modes])
+    freq = jnp.where(second, freq_ref[:, HALF:modes], freq_ref[:, 0:HALF])
+    prev = jnp.where(second, inside, outside)
+    following = jnp.where(second, outside, inside)
+    prev = jnp.where(start == 0, 1.0, prev)
+    following = jnp.where(start == count - HALF, 1.0, following)
+    band = jnp.where(second, band_ref[:, HALF:modes], band_ref[:, 0:HALF])
+    low_end, high_end = band[0:1], band[1:2]
+    eta = BROAD * (ends_ref[7:8, :] - ends_ref[0:1, :]) / (count - 1)
 
     def column(row):
         return jnp.transpose(jnp.broadcast_to(row, (HALF, HALF)))
 
     def weight(partner_freq, partner_ids, own_ids):
-        inside = (partner_ids >= low_end) & (partner_ids < high_end) & (partner_ids != own_ids)
+        within = (partner_ids >= low_end) & (partner_ids < high_end) & (partner_ids != own_ids)
         detune = freq - partner_freq
-        lorentz = (eta / math.pi) / (detune * detune + eta * eta)
         total = freq + partner_freq
-        factor = total * total / (4.0 * freq * partner_freq)
-        return jnp.where(inside, lorentz * factor, 0.0)
+        scale = (eta / math.pi) * (total * total)
+        value = scale / ((detune * detune + eta * eta) * (4.0 * freq * partner_freq))
+        return jnp.where(within, value, 0.0)
 
     rows = iota((HALF, HALF), 0)
     own_ids = start + iota((HALF, HALF), 1)
@@ -177,7 +263,6 @@
     side_weight = weight(side_freq, start + rows + jnp.where(lower, -HALF, HALF), own_ids)
     edge_own = start + iota((1, HALF), 1)
     edge_weight = weight(prev, edge_own - HALF, edge_own)
-    comps = main_one.shape[0]
     main_strength = jnp.zeros((HALF, HALF), F32)
     side_strength = jnp.zeros((HALF, HALF), F32)
     edge_strength = jnp.zeros((1, HALF), F32)
@@ -190,43 +275,38 @@
         edge_strength += edge * edge
     total = jnp.sum(main_weight * main_strength + side_weight * side_strength, axis=0, keepdims=True)
     total += edge_weight * edge_strength
-    out_ref[...] = math.pi / (3.0 * freq * freq) * total
-
-
-def weigh(table, eta, band, main_one, main_two, side_one, side_two, modes, count):
+    diff = math.pi / (3.0 * freq * freq) * total
+    grown = jnp.exp(freq)
+    carried = freq * freq * grown / ((grown - 1.0) * (grown - 1.0)) * diff
+    out_ref[0:1] = diff
+    out_ref[1:2] = carried
+    out_ref[2:8] = jnp.broadcast_to(jnp.sum(carried, axis=1, keepdims=True), (6, HALF))
+
+
+def local_call(kernel, out_shape, *operands):
     return pl.pallas_call(
-        functools.partial(weigh_kernel, modes, count),
-        out_shape=jax.ShapeDtypeStruct((1, HALF), F32),
-        in_specs=[VMEM] * 7,
-        out_specs=VMEM,
+        kernel,
+        out_shape=out_shape,
+        in_specs=[VMEM] * len(operands),
+        out_specs=jax.tree.map(lambda _: VMEM, out_shape),
+        compiler_params=pltpu.CompilerParams(vmem_limit_bytes=SMALL),
         cost_estimate=pl.CostEstimate(flops=10**6, bytes_accessed=10**6, transcendentals=0),
-    )(table, eta, band, main_one, main_two, side_one, side_two)
-
-
-def running_kernel(own_ref, other_ref, capacity_ref, diff_ref, run_ref, total_ref):
-    modes = capacity_ref.shape[1]
+    )(*operands)
+
+
+def running_kernel(modes, own_ref, other_ref, diff_ref, run_ref):
     odd = lax.rem(lax.axis_index("atom"), 2) == 1
     own, other = own_ref[...], other_ref[...]
-    diff = jnp.concatenate([jnp.where(odd, other, own), jnp.where(odd, own, other)], axis=1)
-    diff_ref[...] = diff
-    carried = capacity_ref[...] * diff
+    whole = jnp.concatenate([jnp.where(odd, other, own), jnp.where(odd, own, other)], axis=1)
+    diff_ref[...] = whole[0:1]
     until = jnp.where(iota((modes, modes), 0) <= iota((modes, modes), 1), 1.0, 0.0)
-    running = jnp.dot(
-        jnp.broadcast_to(carried, (8, modes)), until, precision=lax.Precision.HIGHEST, preferred_element_type=F32
-    )
-    run_ref[...] = running[0:1]
-    total_ref[...] = jnp.broadcast_to(running[0:1, modes - 1 : modes], total_ref.shape)
-
-
-def running_sum(own, other, capacity):
-    modes = capacity.shape[1]
-    row = jax.ShapeDtypeStruct((1, modes), F32)
-    return pl.pallas_call(
-        running_kernel,
-        out_shape=(row, row, jax.ShapeDtypeStruct((1, HALF), F32)),
-        in_specs=[VMEM] * 3,
-        out_specs=(VMEM,) * 3,
-    )(own, other, capacity)
+    running = jnp.dot(whole, until, precision=lax.Precision.HIGHEST, preferred_element_type=F32)
+    run_ref[...] = running[1:2]
+
+
+def last_kernel(run_ref, earlier_ref, out_ref):
+    modes = run_ref.shape[1]
+    out_ref[...] = (run_ref[...] + earlier_ref[0:1, 0:1]) / modes
 
 
 def swap(x, axis, bit):
@@ -246,33 +326,25 @@
     domains, blocks = lax.axis_size("atom"), lax.axis_size("mode")
     comps, own, modes = eigvec.shape
     atoms, count = own * domains, modes * blocks
-    place, block = lax.axis_index("atom"), lax.axis_index("mode")
-    odd, high = lax.rem(place, 2), lax.rem(block, 2)
+    block = lax.axis_index("mode")
+    freq_row = freq.reshape(1, modes)
 
     inner = [(i, i ^ 1) for i in range(domains)]
     outer = [(i, (i + 1) % domains if i % 2 else (i - 1) % domains) for i in range(domains)]
-    rim_two = lax.ppermute(lax.dynamic_slice_in_dim(eigvec, (own - RIM) * odd, RIM, 1), "atom", outer)
-    rim_one = lax.ppermute(lax.dynamic_slice_in_dim(eigvec, (own - RIM) * (1 - odd), RIM, 1), "atom", inner)
     near = [(i, i ^ 1) for i in range(blocks)]
     far = [(i, i + 1 if i % 2 else i - 1) for i in range(1, blocks - 1)]
-    halo_one = lax.ppermute(lax.dynamic_slice_in_dim(eigvec, (modes - HALF) * (1 - high), HALF, 2), "mode", near)
-    halo_two = lax.ppermute(lax.dynamic_slice_in_dim(eigvec, (modes - HALF) * high, HALF, 2), "mode", far)
+    inner_edge, outer_edge, near_edge, far_edge = edges(eigvec, freq_row)
+    rim_two = lax.ppermute(outer_edge, "atom", outer)
+    rim_one = lax.ppermute(inner_edge, "atom", inner)
+    halo_one = lax.ppermute(near_edge, "mode", near)
+    halo_two = lax.ppermute(far_edge, "mode", far)
 
     matrix = coupling_matrix(force, bond, nbr, atoms)
     keep, send = pair_parts(matrix, eigvec, rim_one, rim_two, halo_one, halo_two)
 
-    spectrum = freq.reshape(1, modes)
-    for bit in bits_of("mode"):
-        other = swap(spectrum, "mode", bit)
-        upper = (block & bit) != 0
-        spectrum = jnp.where(
-            upper, jnp.concatenate([other, spectrum], axis=0), jnp.concatenate([spectrum, other], axis=0)
-        )
-    eta = BROAD * (jnp.max(spectrum) - jnp.min(spectrum)) / (count - 1)
-    eta = jnp.broadcast_to(eta, (8, HALF))
-    table = jnp.pad(spectrum.reshape(count // HALF, HALF), ((1, 1), (0, 0)), constant_values=1.0)
-    ends = band.reshape(2 * modes // HALF, HALF)
-    capacity = (freq * freq * jnp.exp(freq) / jnp.expm1(freq) ** 2).reshape(1, modes)
+    tile = jax.ShapeDtypeStruct((8, HALF), F32)
+    row = jax.ShapeDtypeStruct((1, modes), F32)
+    ends = local_call(functools.partial(ends_kernel, own), tile, freq_row, halo_one)
 
     both = rounded_sum(keep, swap(send, "atom", 1))
     main, side = both[:, :HALF], both[:, HALF:]
@@ -280,16 +352,27 @@
     for step, (one, two) in enumerate(zip(steps, reversed(steps))):
         main_other, side_other = swap(main, "atom", one), swap(side, "atom", two)
         if step < len(steps) - 1:
-            main, side = rounded_sum(main, main_other), rounded_sum(side, side_other)
-    diff_own = weigh(table, eta, ends, main, main_other, side, side_other, modes, count)
-
-    diff, running, total = running_sum(diff_own, swap(diff_own, "atom", 1), capacity)
+            main = rounded_sum(main, main_other)
+            if step == 0:
+                ends, main = lax.optimization_barrier((ends, main))
+            side = rounded_sum(side, side_other)
+    for bit in bits_of("mode")[1:]:
+        other = swap(ends, "mode", bit)
+        ends = jnp.where(iota((8, HALF), 0) < 4, jnp.minimum(ends, other), jnp.maximum(ends, other))
+    summary = local_call(
+        functools.partial(weigh_kernel, count, own),
+        tile, freq_row, ends, band, halo_one, halo_two, main, main_other, side, side_other,
+    )
+
+    other = swap(summary, "atom", 1)
+    diff, running = local_call(functools.partial(running_kernel, modes), (row, row), summary, other)
+    total = summary + other
     earlier = jnp.zeros_like(total)
     for bit in bits_of("mode"):
         other = swap(total, "mode", bit)
         earlier = earlier + jnp.where((block & bit) != 0, other, 0.0)
         total = total + other
-    conductivity = (earlier[0, 0] + running) / modes
+    conductivity = local_call(last_kernel, row, running, earlier[2:3])
     return diff.reshape(modes), conductivity.reshape(modes)
 
 

time: 52.2 us -> 44.7 us (0.86)
  other arithmetic: 3.16 us -> 0.19 us
  local copies, waits for them, and re-layouts: 7 us -> 4.14 us
  waiting for transfers between devices: 13.8 us -> 15.7 us
  between operations: 2.13 us -> 0.8 us
  starting transfers between devices: 16 us -> 14.8 us
  Pallas kernels: 9.77 us -> 8.78 us
    dynamic_slice x2 -> x0, local copies, waits for them, and re-layouts: 2.11 us -> none  [the longest x1 1.06 us: body(): lax.dynamic_slice_in_dim(eigvec, (own - RIM) * odd, RIM, 1)]
    ppermute x10 -> x9, waiting for transfers between devices: 13.8 us -> 15.7 us  [swap(): lax.ppermute(x, axis, [(i, i ^ bit) for i in range(lax.axis_size(axis))])]
    div x2 -> x0, other arithmetic: 1.81 us -> none  [the longest x1 1.23 us: body(): conductivity = (earlier[0, 0] + running) / modes]
    pallas_call x2 -> x5, Pallas kernels: 3.25 us -> 1.93 us  [the longest x4 1.66 us: local_call(): pl.pallas_call(kernel, out_shape=out_shape, in_specs=[VMEM] * len(operand...]
    ppermute x10 -> x9, starting transfers between devices: 9.51 us -> 8.4 us  [swap(): lax.ppermute(x, axis, [(i, i ^ bit) for i in range(lax.axis_size(axis))])]
    unnamed x22 -> x16, local copies, waits for them, and re-layouts: 3.06 us -> 4.11 us
    broadcast_in_dim x1 -> x0, local copies, waits for them, and re-layouts: 0.62 us -> none  [body(): eta = jnp.broadcast_to(eta, (8, HALF))]
    reduce_min x1 -> x0, other arithmetic: 0.61 us -> none  [body(): eta = BROAD * (jnp.max(spectrum) - jnp.min(spectrum)) / (count - 1)]
  transfers between devices with their start and end apart: 14 -> 13, of which waited for: 7 -> 7; matrix products, arithmetic and copies ran while one was open for 7% -> 0% of each run, Pallas kernels for 8% -> 12%
where the time goes in v2:
time: 44.7 us; the launch traced here: 44.4 us
  waiting for transfers between devices  15.7 us (35%)
  starting transfers between devices  14.8 us (33%)
  Pallas kernels  8.78 us (20%)
  local copies, waits for them, and re-layouts  4.14 us (9%)
  between operations  0.8 us (2%)
    ppermute x9, waiting for transfers between devices, swap(): lax.ppermute(x, axis, [(i, i ^ bit) for i in range(lax.axis_size(axis))])  15.7 us
    ppermute x9, starting transfers between devices, swap(): lax.ppermute(x, axis, [(i, i ^ bit) for i in range(lax.axis_size(axis))])  8.4 us
    pallas_call x1, Pallas kernels, coupling_matrix(): pl.pallas_call(functools.partial(coupling_kernel, atoms), out_shape=jax.S...  4.59 us
    unnamed x16, local copies, waits for them, and re-layouts  4.11 us
    ppermute x1, starting transfers between devices, body(): halo_one = lax.ppermute(near_edge, 'mode', near)  3.09 us
    ppermute x1, starting transfers between devices, body(): rim_two = lax.ppermute(outer_edge, 'atom', outer)  2.54 us
    pallas_call x1, Pallas kernels, pair_parts(): pl.pallas_call(pair_kernel, out_shape=(jax.ShapeDtypeStruct(shape, F32),...  2.26 us
    pallas_call x4, Pallas kernels, local_call(): pl.pallas_call(kernel, out_shape=out_shape, in_specs=[VMEM] * len(operand...  1.66 us
  transfers between devices with their start and end apart: 13, of which 7 were waited for; matrix products, arithmetic and copies ran while one was open for 0% of the time, Pallas kernels for 12%

profile of v2, /device:TPU:0, one launch (start us, length us, event | category | flops | bytes accessed | tf_op | source)
XLA Modules:
  0.0 44.4 jit_solution(11030248940378930848)
XLA Ops:
  0.6 0.0 copy-start
  0.6 1.0 %copy-done = bf16[3,256,256]{2,1,0:T(8,128)(2,1)S(1)} copy-done((bf16[3,256,256]{2,1,0:T(8,128)(2,1)S(1)}, bf16[3,256,256]{2,1,0:T(8,128)(2,1)}, u32[]{:S(2)}) %copy-start) | copy-done | bytes 393240
  1.6 0.0 copy-start.2
  1.6 0.7 %copy-done.2 = f32[256]{0:T(256)S(1)} copy-done((f32[256]{0:T(256)S(1)}, f32[256]{0:T(256)}, u32[]{:S(2)}) %copy-start.2) | copy-done | bytes 1048
  2.3 0.3 shard_map.77
  2.6 3.1 %collective-permute-start = (bf16[3,272,128]{2,1,0:T(8,128)(2,1)S(1)}, bf16[3,272,128]{2,1,0:T(8,128)(2,1)S(1)}, u32[]{:S(2)}, u32[]{:S(2)}) collective-permute-start(bf16[3,272,128]{2,1,0:T(8,128)(2,1)S(1)} %get-tuple-element.12), channel_id=1, source_target_pairs={{0,1},{1,0},{2,3},{3,2},{4,5},{5,4},{6,7},{7,6},{8,9},{9,8},{10,11... | collective-permute-start | bytes 626696 | tf_op jit(solution)/shard_map/ppermute | solution.py:339
  5.7 0.7 %collective-permute-start.3 = (bf16[3,272,128]{2,1,0:T(8,128)(2,1)S(1)}, bf16[3,272,128]{2,1,0:T(8,128)(2,1)S(1)}, u32[]{:S(2)}, u32[]{:S(2)}) collective-permute-start(bf16[3,272,128]{2,1,0:T(8,128)(2,1)S(1)} %get-tuple-element.15), channel_id=1, source_target_pairs={{1,2},{2,1},{5,6},{6,5},{9,10},{10,9},{13,14},{14,13},{17,18},{18,... | collective-permute-start | bytes 626696 | tf_op jit(solution)/shard_map/ppermute | solution.py:340
  6.3 0.1 collective-permute-start.1
  6.4 0.0 copy-start.1
  6.4 2.5 %collective-permute-start.2 = (bf16[3,128,256]{2,1,0:T(8,128)(2,1)S(1)}, bf16[3,128,256]{2,1,0:T(8,128)(2,1)S(1)}, u32[]{:S(2)}, u32[]{:S(2)}) collective-permute-start(bf16[3,128,256]{2,1,0:T(8,128)(2,1)S(1)} %get-tuple-element.14), channel_id=1, source_target_pairs={{0,28},{4,8},{8,4},{12,16},{16,12},{20,24},{24,20},{28,0},{1,29},{... | collective-permute-start | bytes 589832 | tf_op jit(solution)/shard_map/ppermute | solution.py:337
  9.0 0.0 copy-start.5
  9.0 0.9 %copy-done.5 = f32[3,3,16,256]{3,2,1,0:T(8,128)S(1)} copy-done((f32[3,3,16,256]{3,2,1,0:T(8,128)S(1)}, f32[3,3,16,256]{3,2,1,0:T(8,128)}, u32[]{:S(2)}) %copy-start.5) | copy-done | bytes 147480
  9.9 0.8 %copy-done.6 = f32[3,16,256]{2,1,0:T(8,128)S(1)} copy-done((f32[3,16,256]{2,1,0:T(8,128)S(1)}, f32[3,16,256]{2,1,0:T(8,128)}, u32[]{:S(2)}) %copy-start.6) | copy-done | bytes 49176
  10.7 0.7 %copy-done.7 = s32[16,256]{1,0:T(8,128)S(1)} copy-done((s32[16,256]{1,0:T(8,128)S(1)}, s32[16,256]{1,0:T(8,128)}, u32[]{:S(2)}) %copy-start.7) | copy-done | bytes 16408
  11.4 4.6 %shard_map.79.cpl_ref = bf16[2,1152,1152]{2,1,0:T(8,128)(2,1)S(1)} custom-call(f32[3,3,16,256]{3,2,1,0:T(8,128)S(1)} %copy-done.5, f32[3,16,256]{2,1,0:T(8,128)S(1)} %copy-done.6, s32[16,256]{1,0:T(8,128)S(1)} %copy-done.7), custom_call_target="tpu_custom_call" | custom-call | flops 4000000000 | bytes 6000000 | tf_op jit(solution)/shard_map/pallas_call | solution.py:127
  16.0 0.0 copy-start.3
  16.0 0.0 copy-start.4
  16.0 0.0 collective-permute-done.1.rim_one
  16.0 0.0 collective-permute-done.2.rim_two
  16.1 0.0 collective-permute-done.halo_ref.halo_one
  16.1 0.0 collective-permute-done.3.halo_two
  16.1 0.0 copy-done.1
  16.1 2.3 %shard_map.80 = (f32[3,272,128]{2,1,0:T(8,128)S(1)}, bf16[3,272,128]{2,1,0:T(8,128)(2,1)S(1)}) custom-call(bf16[2,1152,1152]{2,1,0:T(8,128)(2,1)S(1)} %shard_map.79.cpl_ref, bf16[3,256,256]{2,1,0:T(8,128)(2,1)S(1)} %copy-done.1, bf16[3,128,256]{2,1,0:T(8,128)(2,1)S(1)} %collective-permute-done.1.rim_one, ...), custom_call_target="tpu_custom_call" | custom-call | flops 2000000000 | bytes 6000000 | tf_op jit(solution)/shard_map/pallas_call | solution.py:198
  18.3 0.1 collective-permute-start.4
  18.4 1.4 %collective-permute-done.4 = bf16[3,272,128]{2,1,0:T(8,128)(2,1)S(1)} collective-permute-done((bf16[3,272,128]{2,1,0:T(8,128)(2,1)S(1)}, bf16[3,272,128]{2,1,0:T(8,128)(2,1)S(1)}, u32[]{:S(2)}, u32[]{:S(2)}) %collective-permute-start.4) | collective-permute-done | bytes 208928 | tf_op jit(solution)/shard_map/ppermute | solution.py:313
  19.9 0.3 collective-permute-start.5
  20.3 0.0 copy-done.3
  20.3 0.1 shard_map.78
  20.4 0.9 %collective-permute-start.8 = (bf16[3,144,128]{2,1,0:T(8,128)(2,1)S(1)}, bf16[3,144,128]{2,1,0:T(8,128)(2,1)S(1)}, u32[]{:S(2)}, u32[]{:S(2)}) collective-permute-start(bf16[3,144,128]{2,1,0:T(8,128)(2,1)S(1)} %slice.13), channel_id=1, source_target_pairs={{0,16},{4,20},{8,24},{12,28},{16,0},{20,4},{24,8},{28,12},{1,17},{... | collective-permute-start | bytes 331784 | tf_op jit(solution)/shard_map/ppermute | solution.py:313
  21.3 3.6 %collective-permute-done.5 = bf16[3,128,128]{2,1,0:T(8,128)(2,1)S(1)} collective-permute-done((bf16[3,128,128]{2,1,0:T(8,128)(2,1)S(1)}, bf16[3,128,128]{2,1,0:T(8,128)(2,1)S(1)}, u32[]{:S(2)}, u32[]{:S(2)}) %collective-permute-start.5) | collective-permute-done | bytes 98336 | tf_op jit(solution)/shard_map/ppermute | solution.py:313
  24.9 0.6 %collective-permute-start.7 = (bf16[3,128,128]{2,1,0:T(8,128)(2,1)S(1)}, bf16[3,128,128]{2,1,0:T(8,128)(2,1)S(1)}, u32[]{:S(2)}, u32[]{:S(2)}) collective-permute-start(bf16[3,128,128]{2,1,0:T(8,128)(2,1)S(1)} %reduce-precision_convert_fusion.2.main_one), channel_id=1, source_target_pairs={{0,16},{4,20},{8,24},{12,28},{16,0},{20,4},{24,8},{28,12},{1,17},{... | collective-permute-start | bytes 294920 | tf_op jit(solution)/shard_map/ppermute | solution.py:313
  25.4 3.9 %collective-permute-start.6 = (f32[8,128]{1,0:T(8,128)S(1)}, f32[8,128]{1,0:T(8,128)S(1)}, u32[]{:S(2)}, u32[]{:S(2)}) collective-permute-start(f32[8,128]{1,0:T(8,128)S(1)} %shard_map.78), channel_id=1, source_target_pairs={{0,2},{1,3},{2,0},{3,1},{4,6},{5,7},{6,4},{7,5},{8,10},{9,11},{10,... | collective-permute-start | bytes 12296 | tf_op jit(solution)/shard_map/ppermute | solution.py:313
  29.3 0.0 collective-permute-done.8
  29.3 0.6 %collective-permute-start.9 = (bf16[3,144,128]{2,1,0:T(8,128)(2,1)S(1)}, bf16[3,144,128]{2,1,0:T(8,128)(2,1)S(1)}, u32[]{:S(2)}, u32[]{:S(2)}) collective-permute-start(bf16[3,144,128]{2,1,0:T(8,128)(2,1)S(1)} %reduce-precision_convert_fusion.1.side_one), channel_id=1, source_target_pairs={{0,8},{4,12},{8,0},{12,4},{16,24},{20,28},{24,16},{28,20},{1,9},{5... | collective-permute-start | bytes 331784 | tf_op jit(solution)/shard_map/ppermute | solution.py:313
  30.0 0.9 %collective-permute-done.6 = f32[8,128]{1,0:T(8,128)S(1)} collective-permute-done((f32[8,128]{1,0:T(8,128)S(1)}, f32[8,128]{1,0:T(8,128)S(1)}, u32[]{:S(2)}, u32[]{:S(2)}) %collective-permute-start.6) | collective-permute-done | bytes 4128 | tf_op jit(solution)/shard_map/ppermute | solution.py:313
  30.9 0.1 maximum_select_fusion.ends_ref
  31.0 0.0 collective-permute-done.7.main_two
  31.0 3.2 %collective-permute-done.9.side_two = bf16[3,144,128]{2,1,0:T(8,128)(2,1)S(1)} collective-permute-done((bf16[3,144,128]{2,1,0:T(8,128)(2,1)S(1)}, bf16[3,144,128]{2,1,0:T(8,128)(2,1)S(1)}, u32[]{:S(2)}, u32[]{:S(2)}) %collective-permute-start.9) | collective-permute-done | bytes 110624 | tf_op jit(solution)/shard_map/ppermute | solution.py:313
  34.2 0.0 copy-done.4
  34.2 0.3 shard_map.81.own_ref
  34.4 0.0 collective-permute-start.10
  34.4 1.2 %collective-permute-done.10.other_ref = f32[8,128]{1,0:T(8,128)S(1)} collective-permute-done((f32[8,128]{1,0:T(8,128)S(1)}, f32[8,128]{1,0:T(8,128)S(1)}, u32[]{:S(2)}, u32[]{:S(2)}) %collective-permute-start.10) | collective-permute-done | bytes 4128 | tf_op jit(solution)/shard_map/ppermute | solution.py:313
  35.6 0.6 %collective-permute-start.11 = (f32[8,128]{1,0:T(8,128)S(1)}, f32[8,128]{1,0:T(8,128)S(1)}, u32[]{:S(2)}, u32[]{:S(2)}) collective-permute-start(f32[8,128]{1,0:T(8,128)S(1)} %add.21), channel_id=1, source_target_pairs={{0,1},{1,0},{2,3},{3,2},{4,5},{5,4},{6,7},{7,6},{8,9},{9,8},{10,11... | collective-permute-start | bytes 12296 | tf_op jit(solution)/shard_map/ppermute | solution.py:313
  36.2 3.0 %collective-permute-done.11 = f32[8,128]{1,0:T(8,128)S(1)} collective-permute-done((f32[8,128]{1,0:T(8,128)S(1)}, f32[8,128]{1,0:T(8,128)S(1)}, u32[]{:S(2)}, u32[]{:S(2)}) %collective-permute-start.11) | collective-permute-done | bytes 4128 | tf_op jit(solution)/shard_map/ppermute | solution.py:313
  39.2 1.5 %collective-permute-start.12 = (f32[8,128]{1,0:T(8,128)S(1)}, f32[8,128]{1,0:T(8,128)S(1)}, u32[]{:S(2)}, u32[]{:S(2)}) collective-permute-start(f32[8,128]{1,0:T(8,128)S(1)} %add.22), channel_id=1, source_target_pairs={{0,2},{1,3},{2,0},{3,1},{4,6},{5,7},{6,4},{7,5},{8,10},{9,11},{10,... | collective-permute-start | bytes 12296 | tf_op jit(solution)/shard_map/ppermute | solution.py:313
  40.7 0.7 %shard_map.82 = (f32[1,256]{1,0:T(1,128)}, f32[1,256]{1,0:T(1,128)S(1)}) custom-call(f32[8,128]{1,0:T(8,128)S(1)} %shard_map.81.own_ref, f32[8,128]{1,0:T(8,128)S(1)} %collective-permute-done.10.other_ref), custom_call_target="tpu_custom_call" | custom-call | flops 1000000 | bytes 1000000 | tf_op jit(solution)/shard_map/pallas_call | solution.py:287
  41.3 2.4 %collective-permute-done.12 = f32[8,128]{1,0:T(8,128)S(1)} collective-permute-done((f32[8,128]{1,0:T(8,128)S(1)}, f32[8,128]{1,0:T(8,128)S(1)}, u32[]{:S(2)}, u32[]{:S(2)}) %collective-permute-start.12) | collective-permute-done | bytes 4128 | tf_op jit(solution)/shard_map/ppermute | solution.py:313
  43.8 0.6 %shard_map.83 = f32[1,256]{1,0:T(1,128)} custom-call(f32[1,256]{1,0:T(1,128)S(1)} %get-tuple-element.21.run_ref, f32[1,128]{1,0:T(1,128)S(1)} %slice.11.earlier_ref), custom_call_target="tpu_custom_call" | custom-call | flops 1000000 | bytes 1000000 | tf_op jit(solution)/shard_map/pallas_call | solution.py:287
  (12 shorter events, 0.1 us)
Async XLA Ops:
  0.6 1.0 %copy-start = (bf16[3,256,256]{2,1,0:T(8,128)(2,1)S(1)}, bf16[3,256,256]{2,1,0:T(8,128)(2,1)}, u32[]{:S(2)}) copy-start(bf16[3,256,256]{2,1,0:T(8,128)(2,1)} %own_ref.1) | copy-start | bytes 1179652
  1.6 0.7 %copy-start.2 = (f32[256]{0:T(256)S(1)}, f32[256]{0:T(256)}, u32[]{:S(2)}) copy-start(f32[256]{0:T(256)} %param.11) | copy-start | bytes 3076
  2.6 13.5 %collective-permute-start = (bf16[3,272,128]{2,1,0:T(8,128)(2,1)S(1)}, bf16[3,272,128]{2,1,0:T(8,128)(2,1)S(1)}, u32[]{:S(2)}, u32[]{:S(2)}) collective-permute-start(bf16[3,272,128]{2,1,0:T(8,128)(2,1)S(1)} %get-tuple-element.12), channel_id=1, source_target_pairs={{0,1},{1,0},{2,3},{3,2},{4,5},{5,4},{6,7},{7,6},{8,9},{9,8},{10,11... | collective-permute-start | bytes 626696 | tf_op jit(solution)/shard_map/ppermute | solution.py:339
  5.7 10.4 %collective-permute-start.3 = (bf16[3,272,128]{2,1,0:T(8,128)(2,1)S(1)}, bf16[3,272,128]{2,1,0:T(8,128)(2,1)S(1)}, u32[]{:S(2)}, u32[]{:S(2)}) collective-permute-start(bf16[3,272,128]{2,1,0:T(8,128)(2,1)S(1)} %get-tuple-element.15), channel_id=1, source_target_pairs={{1,2},{2,1},{5,6},{6,5},{9,10},{10,9},{13,14},{14,13},{17,18},{18,... | collective-permute-start | bytes 626696 | tf_op jit(solution)/shard_map/ppermute | solution.py:340
  6.3 9.7 %collective-permute-start.1 = (bf16[3,128,256]{2,1,0:T(8,128)(2,1)S(1)}, bf16[3,128,256]{2,1,0:T(8,128)(2,1)S(1)}, u32[]{:S(2)}, u32[]{:S(2)}) collective-permute-start(bf16[3,128,256]{2,1,0:T(8,128)(2,1)S(1)} %get-tuple-element.13), channel_id=1, source_target_pairs={{0,4},{4,0},{8,12},{12,8},{16,20},{20,16},{24,28},{28,24},{1,5},{5... | collective-permute-start | bytes 589832 | tf_op jit(solution)/shard_map/ppermute | solution.py:338
  6.4 9.6 %copy-start.1 = (bf16[3,256,256]{2,1,0:T(8,128)(2,1)S(1)}, bf16[3,256,256]{2,1,0:T(8,128)(2,1)}, u32[]{:S(2)}) copy-start(bf16[3,256,256]{2,1,0:T(8,128)(2,1)} %own_ref.1) | copy-start | bytes 1179652
  6.4 9.6 %collective-permute-start.2 = (bf16[3,128,256]{2,1,0:T(8,128)(2,1)S(1)}, bf16[3,128,256]{2,1,0:T(8,128)(2,1)S(1)}, u32[]{:S(2)}, u32[]{:S(2)}) collective-permute-start(bf16[3,128,256]{2,1,0:T(8,128)(2,1)S(1)} %get-tuple-element.14), channel_id=1, source_target_pairs={{0,28},{4,8},{8,4},{12,16},{16,12},{20,24},{24,20},{28,0},{1,29},{... | collective-permute-start | bytes 589832 | tf_op jit(solution)/shard_map/ppermute | solution.py:337
  9.0 0.9 %copy-start.5 = (f32[3,3,16,256]{3,2,1,0:T(8,128)S(1)}, f32[3,3,16,256]{3,2,1,0:T(8,128)}, u32[]{:S(2)}) copy-start(f32[3,3,16,256]{3,2,1,0:T(8,128)} %force_hbm.1) | copy-start | bytes 442372
  9.9 0.8 %copy-start.6 = (f32[3,16,256]{2,1,0:T(8,128)S(1)}, f32[3,16,256]{2,1,0:T(8,128)}, u32[]{:S(2)}) copy-start(f32[3,16,256]{2,1,0:T(8,128)} %bond_hbm.1) | copy-start | bytes 147460
  10.7 0.7 %copy-start.7 = (s32[16,256]{1,0:T(8,128)S(1)}, s32[16,256]{1,0:T(8,128)}, u32[]{:S(2)}) copy-start(s32[16,256]{1,0:T(8,128)} %nbr_hbm.1) | copy-start | bytes 49156
  16.0 4.3 %copy-start.3 = (f32[256]{0:T(256)S(1)}, f32[256]{0:T(256)}, u32[]{:S(2)}) copy-start(f32[256]{0:T(256)} %param.11) | copy-start | bytes 3076
  16.0 18.1 %copy-start.4 = (s32[2,256]{1,0:T(2,128)S(1)}, s32[2,256]{1,0:T(2,128)}, u32[]{:S(2)}) copy-start(s32[2,256]{1,0:T(2,128)} %band_ref.1) | copy-start | bytes 6148
  18.3 1.5 %collective-permute-start.4 = (bf16[3,272,128]{2,1,0:T(8,128)(2,1)S(1)}, bf16[3,272,128]{2,1,0:T(8,128)(2,1)S(1)}, u32[]{:S(2)}, u32[]{:S(2)}) collective-permute-start(bf16[3,272,128]{2,1,0:T(8,128)(2,1)S(1)} %get-tuple-element.17), channel_id=1, source_target_pairs={{0,4},{4,0},{8,12},{12,8},{16,20},{20,16},{24,28},{28,24},{1,5},{5... | collective-permute-start | bytes 626696 | tf_op jit(solution)/shard_map/ppermute | solution.py:313
  19.9 4.9 %collective-permute-start.5 = (bf16[3,128,128]{2,1,0:T(8,128)(2,1)S(1)}, bf16[3,128,128]{2,1,0:T(8,128)(2,1)S(1)}, u32[]{:S(2)}, u32[]{:S(2)}) collective-permute-start(bf16[3,128,128]{2,1,0:T(8,128)(2,1)S(1)} %slice.12), channel_id=1, source_target_pairs={{0,8},{4,12},{8,0},{12,4},{16,24},{20,28},{24,16},{28,20},{1,9},{5... | collective-permute-start | bytes 294920 | tf_op jit(solution)/shard_map/ppermute | solution.py:313
  20.4 8.9 %collective-permute-start.8 = (bf16[3,144,128]{2,1,0:T(8,128)(2,1)S(1)}, bf16[3,144,128]{2,1,0:T(8,128)(2,1)S(1)}, u32[]{:S(2)}, u32[]{:S(2)}) collective-permute-start(bf16[3,144,128]{2,1,0:T(8,128)(2,1)S(1)} %slice.13), channel_id=1, source_target_pairs={{0,16},{4,20},{8,24},{12,28},{16,0},{20,4},{24,8},{28,12},{1,17},{... | collective-permute-start | bytes 331784 | tf_op jit(solution)/shard_map/ppermute | solution.py:313
  24.9 6.1 %collective-permute-start.7 = (bf16[3,128,128]{2,1,0:T(8,128)(2,1)S(1)}, bf16[3,128,128]{2,1,0:T(8,128)(2,1)S(1)}, u32[]{:S(2)}, u32[]{:S(2)}) collective-permute-start(bf16[3,128,128]{2,1,0:T(8,128)(2,1)S(1)} %reduce-precision_convert_fusion.2.main_one), channel_id=1, source_target_pairs={{0,16},{4,20},{8,24},{12,28},{16,0},{20,4},{24,8},{28,12},{1,17},{... | collective-permute-start | bytes 294920 | tf_op jit(solution)/shard_map/ppermute | solution.py:313
  25.4 5.4 %collective-permute-start.6 = (f32[8,128]{1,0:T(8,128)S(1)}, f32[8,128]{1,0:T(8,128)S(1)}, u32[]{:S(2)}, u32[]{:S(2)}) collective-permute-start(f32[8,128]{1,0:T(8,128)S(1)} %shard_map.78), channel_id=1, source_target_pairs={{0,2},{1,3},{2,0},{3,1},{4,6},{5,7},{6,4},{7,5},{8,10},{9,11},{10,... | collective-permute-start | bytes 12296 | tf_op jit(solution)/shard_map/ppermute | solution.py:313
  29.3 4.8 %collective-permute-start.9 = (bf16[3,144,128]{2,1,0:T(8,128)(2,1)S(1)}, bf16[3,144,128]{2,1,0:T(8,128)(2,1)S(1)}, u32[]{:S(2)}, u32[]{:S(2)}) collective-permute-start(bf16[3,144,128]{2,1,0:T(8,128)(2,1)S(1)} %reduce-precision_convert_fusion.1.side_one), channel_id=1, source_target_pairs={{0,8},{4,12},{8,0},{12,4},{16,24},{20,28},{24,16},{28,20},{1,9},{5... | collective-permute-start | bytes 331784 | tf_op jit(solution)/shard_map/ppermute | solution.py:313
  34.4 1.2 %collective-permute-start.10 = (f32[8,128]{1,0:T(8,128)S(1)}, f32[8,128]{1,0:T(8,128)S(1)}, u32[]{:S(2)}, u32[]{:S(2)}) collective-permute-start(f32[8,128]{1,0:T(8,128)S(1)} %shard_map.81.own_ref), channel_id=1, source_target_pairs={{0,4},{4,0},{8,12},{12,8},{16,20},{20,16},{24,28},{28,24},{1,5},{5... | collective-permute-start | bytes 12296 | tf_op jit(solution)/shard_map/ppermute | solution.py:313
  35.6 3.6 %collective-permute-start.11 = (f32[8,128]{1,0:T(8,128)S(1)}, f32[8,128]{1,0:T(8,128)S(1)}, u32[]{:S(2)}, u32[]{:S(2)}) collective-permute-start(f32[8,128]{1,0:T(8,128)S(1)} %add.21), channel_id=1, source_target_pairs={{0,1},{1,0},{2,3},{3,2},{4,5},{5,4},{6,7},{7,6},{8,9},{9,8},{10,11... | collective-permute-start | bytes 12296 | tf_op jit(solution)/shard_map/ppermute | solution.py:313
  39.2 4.5 %collective-permute-start.12 = (f32[8,128]{1,0:T(8,128)S(1)}, f32[8,128]{1,0:T(8,128)S(1)}, u32[]{:S(2)}, u32[]{:S(2)}) collective-permute-start(f32[8,128]{1,0:T(8,128)S(1)} %add.22), channel_id=1, source_target_pairs={{0,2},{1,3},{2,0},{3,1},{4,6},{5,7},{6,4},{7,5},{8,10},{9,11},{10,... | collective-permute-start | bytes 12296 | tf_op jit(solution)/shard_map/ppermute | solution.py:313

commit v3 on v2

--- a/solution.py
+++ b/solution.py
@@ -16,7 +16,7 @@
 F32 = jnp.float32
 BF16 = jnp.bfloat16
 VMEM = pl.BlockSpec(memory_space=pltpu.VMEM)
-ANY = pl.BlockSpec(memory_space=pl.ANY)
+HBM = pl.BlockSpec(memory_space=pltpu.HBM)
 SMALL = 8 * 2**20
 LARGE = 24 * 2**20
 
@@ -25,8 +25,9 @@
     return lax.broadcasted_iota(jnp.int32, shape, dim)
 
 
-def edge_kernel(eig_ref, freq_ref, inner_ref, outer_ref, near_ref, far_ref, sems):
-    comps, own, modes = eig_ref.shape
+def stage_kernel(eig_hbm, freq_hbm, force_hbm, bond_hbm, nbr_hbm, *refs):
+    inner_ref, outer_ref, near_ref, far_ref, freq_ref, force_ref, bond_ref, nbr_ref, sems = refs
+    comps, own, modes = eig_hbm.shape
     odd = lax.rem(lax.axis_index("atom"), 2)
     high = lax.rem(lax.axis_index("mode"), 2)
 
@@ -36,14 +37,20 @@
     def columns(flag):
         return pl.ds(pl.multiple_of(flag * (modes - HALF), HALF), HALF)
 
-    copies = [
-        pltpu.make_async_copy(eig_ref.at[:, rows(odd), :], outer_ref, sems.at[0]),
-        pltpu.make_async_copy(eig_ref.at[:, rows(1 - odd), :], inner_ref, sems.at[1]),
-        pltpu.make_async_copy(eig_ref.at[:, :, columns(1 - high)], near_ref.at[:, pl.ds(0, own), :], sems.at[2]),
-        pltpu.make_async_copy(eig_ref.at[:, :, columns(high)], far_ref.at[:, pl.ds(0, own), :], sems.at[3]),
-    ]
+    moves = (
+        (freq_hbm, freq_ref),
+        (eig_hbm.at[:, rows(odd), :], outer_ref),
+        (eig_hbm.at[:, rows(1 - odd), :], inner_ref),
+        (eig_hbm.at[:, :, columns(1 - high)], near_ref.at[:, pl.ds(0, own), :]),
+        (eig_hbm.at[:, :, columns(high)], far_ref.at[:, pl.ds(0, own), :]),
+        (nbr_hbm, nbr_ref),
+        (bond_hbm, bond_ref),
+        (force_hbm, force_ref),
+    )
+    copies = [pltpu.make_async_copy(*move, sems.at[i]) for i, move in enumerate(moves)]
     for copy in copies:
         copy.start()
+    copies[0].wait()
     freq = freq_ref[...]
     rest = jnp.where(iota((EXTRA, HALF), 0) < EXTRA // 2, freq[:, 0:HALF], freq[:, modes - HALF : modes])
     for part in range(comps):
@@ -51,35 +58,27 @@
         rest = rest - piece.astype(F32)
         near_ref[part, own : own + EXTRA, :] = piece
         far_ref[part, own : own + EXTRA, :] = piece
-    for copy in copies:
+    for copy in copies[1:]:
         copy.wait()
 
 
-def edges(eigvec, freq):
+def stage(eigvec, freq, force, bond, nbr):
     comps, own, modes = eigvec.shape
     rim = jax.ShapeDtypeStruct((comps, RIM, modes), BF16)
     halo = jax.ShapeDtypeStruct((comps, own + EXTRA, HALF), BF16)
+    same = [jax.ShapeDtypeStruct(x.shape, x.dtype) for x in (freq, force, bond, nbr)]
     return pl.pallas_call(
-        edge_kernel,
-        out_shape=(rim, rim, halo, halo),
-        in_specs=[ANY, VMEM],
-        out_specs=(VMEM,) * 4,
-        scratch_shapes=[pltpu.SemaphoreType.DMA((4,))],
+        stage_kernel,
+        out_shape=(rim, rim, halo, halo, *same),
+        in_specs=[HBM] * 5,
+        out_specs=(VMEM,) * 8,
+        scratch_shapes=[pltpu.SemaphoreType.DMA((8,))],
         compiler_params=pltpu.CompilerParams(vmem_limit_bytes=SMALL),
         cost_estimate=pl.CostEstimate(flops=10**4, bytes_accessed=10**6, transcendentals=0),
-    )(eigvec, freq)
-
-
-def coupling_kernel(atoms, force_hbm, bond_hbm, nbr_hbm, out_ref, force_ref, bond_ref, nbr_ref, cpl_ref, sems):
-    copies = [
-        pltpu.make_async_copy(nbr_hbm, nbr_ref, sems.at[0]),
-        pltpu.make_async_copy(bond_hbm, bond_ref, sems.at[1]),
-        pltpu.make_async_copy(force_hbm, force_ref, sems.at[2]),
-    ]
-    for copy in copies:
-        copy.start()
-    for copy in copies:
-        copy.wait()
+    )(eigvec, freq, force, bond, nbr)
+
+
+def coupling_kernel(atoms, force_ref, bond_ref, nbr_ref, out_ref, cpl_ref):
     comps, _, slots, own = force_ref.shape
     wide = slots * GROUP
     span = own + RIM
@@ -127,15 +126,9 @@
     return pl.pallas_call(
         functools.partial(coupling_kernel, atoms),
         out_shape=jax.ShapeDtypeStruct((own // RIM, comps * comps * RIM, size), BF16),
-        in_specs=[ANY] * 3,
+        in_specs=[VMEM] * 3,
         out_specs=VMEM,
-        scratch_shapes=[
-            pltpu.VMEM(force.shape, force.dtype),
-            pltpu.VMEM(bond.shape, bond.dtype),
-            pltpu.VMEM(nbr.shape, nbr.dtype),
-            pltpu.VMEM((comps**3, own, slots), BF16),
-            pltpu.SemaphoreType.DMA((3,)),
-        ],
+        scratch_shapes=[pltpu.VMEM((comps**3, own, slots), BF16)],
         compiler_params=pltpu.CompilerParams(vmem_limit_bytes=LARGE),
         cost_estimate=pl.CostEstimate(flops=4 * 10**9, bytes_accessed=6 * 10**6, transcendentals=0),
     )(force, bond, nbr)
@@ -224,8 +217,8 @@
     out_ref[...] = jnp.where(iota(out_ref.shape, 0) < 4, least, most)
 
 
-def weigh_kernel(count, own, freq_ref, ends_ref, band_ref, halo_one, halo_two, main_one, main_two, side_one, side_two, out_ref):
-    comps = main_one.shape[0]
+def weigh_kernel(count, own, freq_ref, ends_ref, band_ref, halo_one, halo_two, pair_one, pair_two, out_ref):
+    comps = pair_one.shape[0]
     modes = freq_ref.shape[1]
     second = lax.rem(lax.axis_index("atom"), 2) == 1
     high = lax.rem(lax.axis_index("mode"), 2) == 1
@@ -267,11 +260,10 @@
     side_strength = jnp.zeros((HALF, HALF), F32)
     edge_strength = jnp.zeros((1, HALF), F32)
     for k in range(comps):
-        main = main_one[k].astype(F32) + main_two[k].astype(F32)
-        side = side_one[k].astype(F32) + side_two[k].astype(F32)
+        pair = pair_one[k].astype(F32) + pair_two[k].astype(F32)
+        main, side, edge = pair[:HALF], pair[HALF : 2 * HALF], pair[2 * HALF : 2 * HALF + 1]
         main_strength += main * main
-        side_strength += side[:HALF] * side[:HALF]
-        edge = side[HALF : HALF + 1]
+        side_strength += side * side
         edge_strength += edge * edge
     total = jnp.sum(main_weight * main_strength + side_weight * side_strength, axis=0, keepdims=True)
     total += edge_weight * edge_strength
@@ -327,13 +319,13 @@
     comps, own, modes = eigvec.shape
     atoms, count = own * domains, modes * blocks
     block = lax.axis_index("mode")
-    freq_row = freq.reshape(1, modes)
+    staged = stage(eigvec, freq.reshape(1, modes), force, bond, nbr)
+    inner_edge, outer_edge, near_edge, far_edge, freq_row, force, bond, nbr = staged
 
     inner = [(i, i ^ 1) for i in range(domains)]
     outer = [(i, (i + 1) % domains if i % 2 else (i - 1) % domains) for i in range(domains)]
     near = [(i, i ^ 1) for i in range(blocks)]
     far = [(i, i + 1 if i % 2 else i - 1) for i in range(1, blocks - 1)]
-    inner_edge, outer_edge, near_edge, far_edge = edges(eigvec, freq_row)
     rim_two = lax.ppermute(outer_edge, "atom", outer)
     rim_one = lax.ppermute(inner_edge, "atom", inner)
     halo_one = lax.ppermute(near_edge, "mode", near)
@@ -346,22 +338,20 @@
     row = jax.ShapeDtypeStruct((1, modes), F32)
     ends = local_call(functools.partial(ends_kernel, own), tile, freq_row, halo_one)
 
-    both = rounded_sum(keep, swap(send, "atom", 1))
-    main, side = both[:, :HALF], both[:, HALF:]
+    total = rounded_sum(keep, swap(send, "atom", 1))
     steps = bits_of("atom")[1:]
     for step, (one, two) in enumerate(zip(steps, reversed(steps))):
-        main_other, side_other = swap(main, "atom", one), swap(side, "atom", two)
+        total_other = lax.ppermute(total, "atom", [(i, i ^ (two if i % 2 else one)) for i in range(domains)])
         if step < len(steps) - 1:
-            main = rounded_sum(main, main_other)
+            total = rounded_sum(total, total_other)
             if step == 0:
-                ends, main = lax.optimization_barrier((ends, main))
-            side = rounded_sum(side, side_other)
+                ends, total = lax.optimization_barrier((ends, total))
     for bit in bits_of("mode")[1:]:
         other = swap(ends, "mode", bit)
         ends = jnp.where(iota((8, HALF), 0) < 4, jnp.minimum(ends, other), jnp.maximum(ends, other))
     summary = local_call(
         functools.partial(weigh_kernel, count, own),
-        tile, freq_row, ends, band, halo_one, halo_two, main, main_other, side, side_other,
+        tile, freq_row, ends, band, halo_one, halo_two, total, total_other,
     )
 
     other = swap(summary, "atom", 1)

time: 44.7 us -> 46.7 us (1.045)
  starting transfers between devices: 14.8 us -> 16 us
  waiting for transfers between devices: 15.7 us -> 16.5 us
    ppermute x0 -> x2, waiting for transfers between devices: none -> 8.02 us  [body(): lax.ppermute(total, 'atom', [(i, i ^ (two if i % 2 else one)) for i in ra...]
    ppermute x9 -> x5, waiting for transfers between devices: 15.7 us -> 7.86 us  [swap(): lax.ppermute(x, axis, [(i, i ^ bit) for i in range(lax.axis_size(axis))])]
    ppermute x0 -> x2, starting transfers between devices: none -> 3.49 us  [body(): lax.ppermute(total, 'atom', [(i, i ^ (two if i % 2 else one)) for i in ra...]
    ppermute x9 -> x5, starting transfers between devices: 8.4 us -> 6.18 us  [swap(): lax.ppermute(x, axis, [(i, i ^ bit) for i in range(lax.axis_size(axis))])]
    ppermute x1, waiting for transfers between devices: 0.01 us -> 0.66 us  [body(): rim_two = lax.ppermute(outer_edge, 'atom', outer)]
    unnamed x16 -> x14, local copies, waits for them, and re-layouts: 4.11 us -> 4.1 us
  transfers between devices with their start and end apart: 13 -> 11, of which waited for: 7 -> 7; matrix products, arithmetic and copies ran while one was open for 0% -> 0% of each run, Pallas kernels for 12% -> 11%
where the time goes in v3:
time: 46.7 us; the launch traced here: 46.4 us
  waiting for transfers between devices  16.5 us (35%)
  starting transfers between devices  16 us (34%)
  Pallas kernels  8.82 us (19%)
  local copies, waits for them, and re-layouts  4.11 us (9%)
  between operations  0.73 us (2%)
    ppermute x2, waiting for transfers between devices, body(): lax.ppermute(total, 'atom', [(i, i ^ (two if i % 2 else one)) for i in ra...  8.02 us
    ppermute x5, waiting for transfers between devices, swap(): lax.ppermute(x, axis, [(i, i ^ bit) for i in range(lax.axis_size(axis))])  7.86 us
    ppermute x5, starting transfers between devices, swap(): lax.ppermute(x, axis, [(i, i ^ bit) for i in range(lax.axis_size(axis))])  6.18 us
    pallas_call x1, Pallas kernels, coupling_matrix(): pl.pallas_call(functools.partial(coupling_kernel, atoms), out_shape=jax.S...  4.31 us
    unnamed x14, local copies, waits for them, and re-layouts  4.1 us
    ppermute x2, starting transfers between devices, body(): lax.ppermute(total, 'atom', [(i, i ^ (two if i % 2 else one)) for i in ra...  3.49 us
    ppermute x1, starting transfers between devices, body(): halo_one = lax.ppermute(near_edge, 'mode', near)  3.09 us
    ppermute x1, starting transfers between devices, body(): rim_two = lax.ppermute(outer_edge, 'atom', outer)  2.55 us
  transfers between devices with their start and end apart: 11, of which 7 were waited for; matrix products, arithmetic and copies ran while one was open for 0% of the time, Pallas kernels for 11%

profile of v3, /device:TPU:0, one launch (start us, length us, event | category | flops | bytes accessed | tf_op | source)
XLA Modules:
  0.0 46.4 jit_solution(786583004363744892)
XLA Ops:
  0.6 0.0 copy-start
  0.6 1.0 %copy-done = bf16[3,256,256]{2,1,0:T(8,128)(2,1)S(1)} copy-done((bf16[3,256,256]{2,1,0:T(8,128)(2,1)S(1)}, bf16[3,256,256]{2,1,0:T(8,128)(2,1)}, u32[]{:S(2)}) %copy-start) | copy-done | bytes 393240
  1.6 0.0 copy-start.2
  1.6 0.9 %copy-done.2 = f32[3,3,16,256]{3,2,1,0:T(8,128)S(1)} copy-done((f32[3,3,16,256]{3,2,1,0:T(8,128)S(1)}, f32[3,3,16,256]{3,2,1,0:T(8,128)}, u32[]{:S(2)}) %copy-start.2) | copy-done | bytes 147480
  2.5 0.0 copy-start.3
  2.5 0.8 %copy-done.3 = f32[3,16,256]{2,1,0:T(8,128)S(1)} copy-done((f32[3,16,256]{2,1,0:T(8,128)S(1)}, f32[3,16,256]{2,1,0:T(8,128)}, u32[]{:S(2)}) %copy-start.3) | copy-done | bytes 49176
  3.3 0.0 copy-start.4
  3.3 0.7 %copy-done.4 = s32[16,256]{1,0:T(8,128)S(1)} copy-done((s32[16,256]{1,0:T(8,128)S(1)}, s32[16,256]{1,0:T(8,128)}, u32[]{:S(2)}) %copy-start.4) | copy-done | bytes 16408
  4.1 0.0 copy-start.6
  4.1 0.7 %copy-done.6 = f32[256]{0:T(256)S(1)} copy-done((f32[256]{0:T(256)S(1)}, f32[256]{0:T(256)}, u32[]{:S(2)}) %copy-start.6) | copy-done | bytes 1048
  4.7 0.6 %shard_map.77 = (bf16[3,128,256]{2,1,0:T(8,128)(2,1)S(1)}, bf16[3,128,256]{2,1,0:T(8,128)(2,1)S(1)}, bf16[3,272,128]{2,1,0:T(8,128)(2,1)S(1)}, bf16[3,272,128]{2...) custom-call(bf16[3,256,256]{2,1,0:T(8,128)(2,1)S(1)} %copy-done, ...), custom_call_target="tpu_custom_call" | custom-call | flops 10000 | bytes 1000000 | tf_op jit(solution)/shard_map/pallas_call | solution.py:70
  5.3 3.1 %collective-permute-start = (bf16[3,272,128]{2,1,0:T(8,128)(2,1)S(1)}, bf16[3,272,128]{2,1,0:T(8,128)(2,1)S(1)}, u32[]{:S(2)}, u32[]{:S(2)}) collective-permute-start(bf16[3,272,128]{2,1,0:T(8,128)(2,1)S(1)} %get-tuple-element.17), channel_id=1, source_target_pairs={{0,1},{1,0},{2,3},{3,2},{4,5},{5,4},{6,7},{7,6},{8,9},{9,8},{10,11... | collective-permute-start | bytes 626696 | tf_op jit(solution)/shard_map/ppermute | solution.py:331
  8.4 0.7 %collective-permute-start.3 = (bf16[3,272,128]{2,1,0:T(8,128)(2,1)S(1)}, bf16[3,272,128]{2,1,0:T(8,128)(2,1)S(1)}, u32[]{:S(2)}, u32[]{:S(2)}) collective-permute-start(bf16[3,272,128]{2,1,0:T(8,128)(2,1)S(1)} %get-tuple-element.23), channel_id=1, source_target_pairs={{1,2},{2,1},{5,6},{6,5},{9,10},{10,9},{13,14},{14,13},{17,18},{18,... | collective-permute-start | bytes 626696 | tf_op jit(solution)/shard_map/ppermute | solution.py:332
  9.1 0.1 collective-permute-start.1
  9.2 2.5 %collective-permute-start.2 = (bf16[3,128,256]{2,1,0:T(8,128)(2,1)S(1)}, bf16[3,128,256]{2,1,0:T(8,128)(2,1)S(1)}, u32[]{:S(2)}, u32[]{:S(2)}) collective-permute-start(bf16[3,128,256]{2,1,0:T(8,128)(2,1)S(1)} %get-tuple-element.22), channel_id=1, source_target_pairs={{0,28},{4,8},{8,4},{12,16},{16,12},{20,24},{24,20},{28,0},{1,29},{... | collective-permute-start | bytes 589832 | tf_op jit(solution)/shard_map/ppermute | solution.py:329
  11.7 0.0 copy-start.1
  11.7 4.3 %shard_map.79.cpl_ref = bf16[2,1152,1152]{2,1,0:T(8,128)(2,1)S(1)} custom-call(f32[3,3,16,256]{3,2,1,0:T(8,128)S(1)} %get-tuple-element.18.force_ref, f32[3,16,256]{2,1,0:T(8,128)S(1)} %get-tuple-element.19.bond_ref, s32[16,256]{1,0:T(8,128)S(1)} %get-tuple-element.20.nbr_ref), custom_call_target="tpu_custom_call" | custom-call | flops 4000000000 | bytes 6000000 | tf_op jit(solution)/shard_map/pallas_call | solution.py:126
  16.0 0.0 copy-start.5
  16.1 0.0 collective-permute-done.1.rim_one
  16.1 0.7 %collective-permute-done.2.rim_two = bf16[3,128,256]{2,1,0:T(8,128)(2,1)S(1)} collective-permute-done((bf16[3,128,256]{2,1,0:T(8,128)(2,1)S(1)}, bf16[3,128,256]{2,1,0:T(8,128)(2,1)S(1)}, u32[]{:S(2)}, u32[]{:S(2)}) %collective-permute-start.2) | collective-permute-done | bytes 196640 | tf_op jit(solution)/shard_map/ppermute | solution.py:329
  16.7 0.0 collective-permute-done.halo_ref.halo_one
  16.7 0.0 collective-permute-done.3.halo_two
  16.7 0.0 copy-done.1
  16.7 2.3 %shard_map.80 = (f32[3,272,128]{2,1,0:T(8,128)S(1)}, bf16[3,272,128]{2,1,0:T(8,128)(2,1)S(1)}) custom-call(bf16[2,1152,1152]{2,1,0:T(8,128)(2,1)S(1)} %shard_map.79.cpl_ref, bf16[3,256,256]{2,1,0:T(8,128)(2,1)S(1)} %copy-done.1, bf16[3,128,256]{2,1,0:T(8,128)(2,1)S(1)} %collective-permute-done.1.rim_one, ...), custom_call_target="tpu_custom_call" | custom-call | flops 2000000000 | bytes 6000000 | tf_op jit(solution)/shard_map/pallas_call | solution.py:191
  19.0 0.2 collective-permute-start.4
  19.2 1.3 %collective-permute-done.4 = bf16[3,272,128]{2,1,0:T(8,128)(2,1)S(1)} collective-permute-done((bf16[3,272,128]{2,1,0:T(8,128)(2,1)S(1)}, bf16[3,272,128]{2,1,0:T(8,128)(2,1)S(1)}, u32[]{:S(2)}, u32[]{:S(2)}) %collective-permute-start.4) | collective-permute-done | bytes 208928 | tf_op jit(solution)/shard_map/ppermute | solution.py:305
  20.6 1.7 %collective-permute-start.5 = (bf16[3,272,128]{2,1,0:T(8,128)(2,1)S(1)}, bf16[3,272,128]{2,1,0:T(8,128)(2,1)S(1)}, u32[]{:S(2)}, u32[]{:S(2)}) collective-permute-start(bf16[3,272,128]{2,1,0:T(8,128)(2,1)S(1)} %reduce-precision_convert_fusion.1), channel_id=1, source_target_pairs={{0,8},{4,20},{8,0},{12,28},{16,24},{20,4},{24,16},{28,12},{1,9},{5... | collective-permute-start | bytes 626696 | tf_op jit(solution)/shard_map/ppermute | solution.py:344
  22.3 0.1 shard_map.78
  22.3 4.1 %collective-permute-done.5 = bf16[3,272,128]{2,1,0:T(8,128)(2,1)S(1)} collective-permute-done((bf16[3,272,128]{2,1,0:T(8,128)(2,1)S(1)}, bf16[3,272,128]{2,1,0:T(8,128)(2,1)S(1)}, u32[]{:S(2)}, u32[]{:S(2)}) %collective-permute-start.5) | collective-permute-done | bytes 208928 | tf_op jit(solution)/shard_map/ppermute | solution.py:344
  26.4 0.1 reduce-precision_convert_fusion.pair_one
  26.5 3.9 %collective-permute-start.6 = (f32[8,128]{1,0:T(8,128)S(1)}, f32[8,128]{1,0:T(8,128)S(1)}, u32[]{:S(2)}, u32[]{:S(2)}) collective-permute-start(f32[8,128]{1,0:T(8,128)S(1)} %shard_map.78), channel_id=1, source_target_pairs={{0,2},{1,3},{2,0},{3,1},{4,6},{5,7},{6,4},{7,5},{8,10},{9,11},{10,... | collective-permute-start | bytes 12296 | tf_op jit(solution)/shard_map/ppermute | solution.py:305
  30.4 1.8 %collective-permute-start.7 = (bf16[3,272,128]{2,1,0:T(8,128)(2,1)S(1)}, bf16[3,272,128]{2,1,0:T(8,128)(2,1)S(1)}, u32[]{:S(2)}, u32[]{:S(2)}) collective-permute-start(bf16[3,272,128]{2,1,0:T(8,128)(2,1)S(1)} %reduce-precision_convert_fusion.pair_one), channel_id=1, source_target_pairs={{0,16},{4,12},{8,24},{12,4},{16,0},{20,28},{24,8},{28,20},{1,17},{... | collective-permute-start | bytes 626696 | tf_op jit(solution)/shard_map/ppermute | solution.py:344
  32.2 0.0 collective-permute-done.6
  32.2 0.1 maximum_select_fusion.ends_ref
  32.3 3.9 %collective-permute-done.7.pair_two = bf16[3,272,128]{2,1,0:T(8,128)(2,1)S(1)} collective-permute-done((bf16[3,272,128]{2,1,0:T(8,128)(2,1)S(1)}, bf16[3,272,128]{2,1,0:T(8,128)(2,1)S(1)}, u32[]{:S(2)}, u32[]{:S(2)}) %collective-permute-start.7) | collective-permute-done | bytes 208928 | tf_op jit(solution)/shard_map/ppermute | solution.py:344
  36.2 0.0 copy-done.5
  36.2 0.3 shard_map.81.own_ref
  36.5 0.0 collective-permute-start.8
  36.5 1.2 %collective-permute-done.8.other_ref = f32[8,128]{1,0:T(8,128)S(1)} collective-permute-done((f32[8,128]{1,0:T(8,128)S(1)}, f32[8,128]{1,0:T(8,128)S(1)}, u32[]{:S(2)}, u32[]{:S(2)}) %collective-permute-start.8) | collective-permute-done | bytes 4128 | tf_op jit(solution)/shard_map/ppermute | solution.py:305
  37.7 0.6 %collective-permute-start.9 = (f32[8,128]{1,0:T(8,128)S(1)}, f32[8,128]{1,0:T(8,128)S(1)}, u32[]{:S(2)}, u32[]{:S(2)}) collective-permute-start(f32[8,128]{1,0:T(8,128)S(1)} %add.17), channel_id=1, source_target_pairs={{0,1},{1,0},{2,3},{3,2},{4,5},{5,4},{6,7},{7,6},{8,9},{9,8},{10,11... | collective-permute-start | bytes 12296 | tf_op jit(solution)/shard_map/ppermute | solution.py:305
  38.3 3.0 %collective-permute-done.9 = f32[8,128]{1,0:T(8,128)S(1)} collective-permute-done((f32[8,128]{1,0:T(8,128)S(1)}, f32[8,128]{1,0:T(8,128)S(1)}, u32[]{:S(2)}, u32[]{:S(2)}) %collective-permute-start.9) | collective-permute-done | bytes 4128 | tf_op jit(solution)/shard_map/ppermute | solution.py:305
  41.3 1.5 %collective-permute-start.10 = (f32[8,128]{1,0:T(8,128)S(1)}, f32[8,128]{1,0:T(8,128)S(1)}, u32[]{:S(2)}, u32[]{:S(2)}) collective-permute-start(f32[8,128]{1,0:T(8,128)S(1)} %add.18), channel_id=1, source_target_pairs={{0,2},{1,3},{2,0},{3,1},{4,6},{5,7},{6,4},{7,5},{8,10},{9,11},{10,... | collective-permute-start | bytes 12296 | tf_op jit(solution)/shard_map/ppermute | solution.py:305
  42.7 0.7 %shard_map.82 = (f32[1,256]{1,0:T(1,128)}, f32[1,256]{1,0:T(1,128)S(1)}) custom-call(f32[8,128]{1,0:T(8,128)S(1)} %shard_map.81.own_ref, f32[8,128]{1,0:T(8,128)S(1)} %collective-permute-done.8.other_ref), custom_call_target="tpu_custom_call" | custom-call | flops 1000000 | bytes 1000000 | tf_op jit(solution)/shard_map/pallas_call | solution.py:279
  43.4 2.4 %collective-permute-done.10 = f32[8,128]{1,0:T(8,128)S(1)} collective-permute-done((f32[8,128]{1,0:T(8,128)S(1)}, f32[8,128]{1,0:T(8,128)S(1)}, u32[]{:S(2)}, u32[]{:S(2)}) %collective-permute-start.10) | collective-permute-done | bytes 4128 | tf_op jit(solution)/shard_map/ppermute | solution.py:305
  45.8 0.6 %shard_map.83 = f32[1,256]{1,0:T(1,128)} custom-call(f32[1,256]{1,0:T(1,128)S(1)} %get-tuple-element.29.run_ref, f32[1,128]{1,0:T(1,128)S(1)} %slice.3.earlier_ref), custom_call_target="tpu_custom_call" | custom-call | flops 1000000 | bytes 1000000 | tf_op jit(solution)/shard_map/pallas_call | solution.py:279
  (6 shorter events, 0.1 us)
Async XLA Ops:
  0.6 1.0 %copy-start = (bf16[3,256,256]{2,1,0:T(8,128)(2,1)S(1)}, bf16[3,256,256]{2,1,0:T(8,128)(2,1)}, u32[]{:S(2)}) copy-start(bf16[3,256,256]{2,1,0:T(8,128)(2,1)} %own_ref.1) | copy-start | bytes 1179652
  1.6 0.9 %copy-start.2 = (f32[3,3,16,256]{3,2,1,0:T(8,128)S(1)}, f32[3,3,16,256]{3,2,1,0:T(8,128)}, u32[]{:S(2)}) copy-start(f32[3,3,16,256]{3,2,1,0:T(8,128)} %force_hbm.1) | copy-start | bytes 442372
  2.5 0.8 %copy-start.3 = (f32[3,16,256]{2,1,0:T(8,128)S(1)}, f32[3,16,256]{2,1,0:T(8,128)}, u32[]{:S(2)}) copy-start(f32[3,16,256]{2,1,0:T(8,128)} %bond_hbm.1) | copy-start | bytes 147460
  3.3 0.7 %copy-start.4 = (s32[16,256]{1,0:T(8,128)S(1)}, s32[16,256]{1,0:T(8,128)}, u32[]{:S(2)}) copy-start(s32[16,256]{1,0:T(8,128)} %nbr_hbm.1) | copy-start | bytes 49156
  4.1 0.7 %copy-start.6 = (f32[256]{0:T(256)S(1)}, f32[256]{0:T(256)}, u32[]{:S(2)}) copy-start(f32[256]{0:T(256)} %param.11) | copy-start | bytes 3076
  5.3 11.4 %collective-permute-start = (bf16[3,272,128]{2,1,0:T(8,128)(2,1)S(1)}, bf16[3,272,128]{2,1,0:T(8,128)(2,1)S(1)}, u32[]{:S(2)}, u32[]{:S(2)}) collective-permute-start(bf16[3,272,128]{2,1,0:T(8,128)(2,1)S(1)} %get-tuple-element.17), channel_id=1, source_target_pairs={{0,1},{1,0},{2,3},{3,2},{4,5},{5,4},{6,7},{7,6},{8,9},{9,8},{10,11... | collective-permute-start | bytes 626696 | tf_op jit(solution)/shard_map/ppermute | solution.py:331
  8.4 8.3 %collective-permute-start.3 = (bf16[3,272,128]{2,1,0:T(8,128)(2,1)S(1)}, bf16[3,272,128]{2,1,0:T(8,128)(2,1)S(1)}, u32[]{:S(2)}, u32[]{:S(2)}) collective-permute-start(bf16[3,272,128]{2,1,0:T(8,128)(2,1)S(1)} %get-tuple-element.23), channel_id=1, source_target_pairs={{1,2},{2,1},{5,6},{6,5},{9,10},{10,9},{13,14},{14,13},{17,18},{18,... | collective-permute-start | bytes 626696 | tf_op jit(solution)/shard_map/ppermute | solution.py:332
  9.1 7.0 %collective-permute-start.1 = (bf16[3,128,256]{2,1,0:T(8,128)(2,1)S(1)}, bf16[3,128,256]{2,1,0:T(8,128)(2,1)S(1)}, u32[]{:S(2)}, u32[]{:S(2)}) collective-permute-start(bf16[3,128,256]{2,1,0:T(8,128)(2,1)S(1)} %get-tuple-element.21), channel_id=1, source_target_pairs={{0,4},{4,0},{8,12},{12,8},{16,20},{20,16},{24,28},{28,24},{1,5},{5... | collective-permute-start | bytes 589832 | tf_op jit(solution)/shard_map/ppermute | solution.py:330
  9.2 7.5 %collective-permute-start.2 = (bf16[3,128,256]{2,1,0:T(8,128)(2,1)S(1)}, bf16[3,128,256]{2,1,0:T(8,128)(2,1)S(1)}, u32[]{:S(2)}, u32[]{:S(2)}) collective-permute-start(bf16[3,128,256]{2,1,0:T(8,128)(2,1)S(1)} %get-tuple-element.22), channel_id=1, source_target_pairs={{0,28},{4,8},{8,4},{12,16},{16,12},{20,24},{24,20},{28,0},{1,29},{... | collective-permute-start | bytes 589832 | tf_op jit(solution)/shard_map/ppermute | solution.py:329
  11.7 5.0 %copy-start.1 = (bf16[3,256,256]{2,1,0:T(8,128)(2,1)S(1)}, bf16[3,256,256]{2,1,0:T(8,128)(2,1)}, u32[]{:S(2)}) copy-start(bf16[3,256,256]{2,1,0:T(8,128)(2,1)} %own_ref.1) | copy-start | bytes 1179652
  16.0 20.2 %copy-start.5 = (s32[2,256]{1,0:T(2,128)S(1)}, s32[2,256]{1,0:T(2,128)}, u32[]{:S(2)}) copy-start(s32[2,256]{1,0:T(2,128)} %band_ref.1) | copy-start | bytes 6148
  19.0 1.5 %collective-permute-start.4 = (bf16[3,272,128]{2,1,0:T(8,128)(2,1)S(1)}, bf16[3,272,128]{2,1,0:T(8,128)(2,1)S(1)}, u32[]{:S(2)}, u32[]{:S(2)}) collective-permute-start(bf16[3,272,128]{2,1,0:T(8,128)(2,1)S(1)} %get-tuple-element.25), channel_id=1, source_target_pairs={{0,4},{4,0},{8,12},{12,8},{16,20},{20,16},{24,28},{28,24},{1,5},{5... | collective-permute-start | bytes 626696 | tf_op jit(solution)/shard_map/ppermute | solution.py:305
  20.6 5.9 %collective-permute-start.5 = (bf16[3,272,128]{2,1,0:T(8,128)(2,1)S(1)}, bf16[3,272,128]{2,1,0:T(8,128)(2,1)S(1)}, u32[]{:S(2)}, u32[]{:S(2)}) collective-permute-start(bf16[3,272,128]{2,1,0:T(8,128)(2,1)S(1)} %reduce-precision_convert_fusion.1), channel_id=1, source_target_pairs={{0,8},{4,20},{8,0},{12,28},{16,24},{20,4},{24,16},{28,12},{1,9},{5... | collective-permute-start | bytes 626696 | tf_op jit(solution)/shard_map/ppermute | solution.py:344
  26.5 5.7 %collective-permute-start.6 = (f32[8,128]{1,0:T(8,128)S(1)}, f32[8,128]{1,0:T(8,128)S(1)}, u32[]{:S(2)}, u32[]{:S(2)}) collective-permute-start(f32[8,128]{1,0:T(8,128)S(1)} %shard_map.78), channel_id=1, source_target_pairs={{0,2},{1,3},{2,0},{3,1},{4,6},{5,7},{6,4},{7,5},{8,10},{9,11},{10,... | collective-permute-start | bytes 12296 | tf_op jit(solution)/shard_map/ppermute | solution.py:305
  30.4 5.8 %collective-permute-start.7 = (bf16[3,272,128]{2,1,0:T(8,128)(2,1)S(1)}, bf16[3,272,128]{2,1,0:T(8,128)(2,1)S(1)}, u32[]{:S(2)}, u32[]{:S(2)}) collective-permute-start(bf16[3,272,128]{2,1,0:T(8,128)(2,1)S(1)} %reduce-precision_convert_fusion.pair_one), channel_id=1, source_target_pairs={{0,16},{4,12},{8,24},{12,4},{16,0},{20,28},{24,8},{28,20},{1,17},{... | collective-permute-start | bytes 626696 | tf_op jit(solution)/shard_map/ppermute | solution.py:344
  36.5 1.2 %collective-permute-start.8 = (f32[8,128]{1,0:T(8,128)S(1)}, f32[8,128]{1,0:T(8,128)S(1)}, u32[]{:S(2)}, u32[]{:S(2)}) collective-permute-start(f32[8,128]{1,0:T(8,128)S(1)} %shard_map.81.own_ref), channel_id=1, source_target_pairs={{0,4},{4,0},{8,12},{12,8},{16,20},{20,16},{24,28},{28,24},{1,5},{5... | collective-permute-start | bytes 12296 | tf_op jit(solution)/shard_map/ppermute | solution.py:305
  37.7 3.6 %collective-permute-start.9 = (f32[8,128]{1,0:T(8,128)S(1)}, f32[8,128]{1,0:T(8,128)S(1)}, u32[]{:S(2)}, u32[]{:S(2)}) collective-permute-start(f32[8,128]{1,0:T(8,128)S(1)} %add.17), channel_id=1, source_target_pairs={{0,1},{1,0},{2,3},{3,2},{4,5},{5,4},{6,7},{7,6},{8,9},{9,8},{10,11... | collective-permute-start | bytes 12296 | tf_op jit(solution)/shard_map/ppermute | solution.py:305
  41.3 4.5 %collective-permute-start.10 = (f32[8,128]{1,0:T(8,128)S(1)}, f32[8,128]{1,0:T(8,128)S(1)}, u32[]{:S(2)}, u32[]{:S(2)}) collective-permute-start(f32[8,128]{1,0:T(8,128)S(1)} %add.18), channel_id=1, source_target_pairs={{0,2},{1,3},{2,0},{3,1},{4,6},{5,7},{6,4},{7,5},{8,10},{9,11},{10,... | collective-permute-start | bytes 12296 | tf_op jit(solution)/shard_map/ppermute | solution.py:305

commit v4 on v3

--- a/solution.py
+++ b/solution.py
@@ -18,6 +18,7 @@
 VMEM = pl.BlockSpec(memory_space=pltpu.VMEM)
 HBM = pl.BlockSpec(memory_space=pltpu.HBM)
 SMALL = 8 * 2**20
+COST = 10**10
 LARGE = 24 * 2**20
 
 
@@ -25,32 +26,29 @@
     return lax.broadcasted_iota(jnp.int32, shape, dim)
 
 
-def stage_kernel(eig_hbm, freq_hbm, force_hbm, bond_hbm, nbr_hbm, *refs):
-    inner_ref, outer_ref, near_ref, far_ref, freq_ref, force_ref, bond_ref, nbr_ref, sems = refs
-    comps, own, modes = eig_hbm.shape
+def rim_kernel(eig_ref, inner_ref, outer_ref, sems):
+    own = eig_ref.shape[1]
     odd = lax.rem(lax.axis_index("atom"), 2)
-    high = lax.rem(lax.axis_index("mode"), 2)
-
-    def rows(flag):
-        return pl.ds(pl.multiple_of(flag * (own - RIM), RIM), RIM)
-
-    def columns(flag):
-        return pl.ds(pl.multiple_of(flag * (modes - HALF), HALF), HALF)
-
-    moves = (
-        (freq_hbm, freq_ref),
-        (eig_hbm.at[:, rows(odd), :], outer_ref),
-        (eig_hbm.at[:, rows(1 - odd), :], inner_ref),
-        (eig_hbm.at[:, :, columns(1 - high)], near_ref.at[:, pl.ds(0, own), :]),
-        (eig_hbm.at[:, :, columns(high)], far_ref.at[:, pl.ds(0, own), :]),
-        (nbr_hbm, nbr_ref),
-        (bond_hbm, bond_ref),
-        (force_hbm, force_ref),
-    )
-    copies = [pltpu.make_async_copy(*move, sems.at[i]) for i, move in enumerate(moves)]
+    copies = []
+    for place, (flag, ref) in enumerate(((odd, outer_ref), (1 - odd, inner_ref))):
+        rows = pl.ds(pl.multiple_of(flag * (own - RIM), RIM), RIM)
+        copies.append(pltpu.make_async_copy(eig_ref.at[:, rows, :], ref, sems.at[place]))
     for copy in copies:
         copy.start()
-    copies[0].wait()
+    for copy in copies:
+        copy.wait()
+
+
+def halo_kernel(eig_ref, freq_ref, near_ref, far_ref, sems):
+    comps, own, modes = eig_ref.shape
+    high = lax.rem(lax.axis_index("mode"), 2)
+    copies = []
+    for place, (flag, ref) in enumerate(((1 - high, near_ref), (high, far_ref))):
+        columns = pl.ds(pl.multiple_of(flag * (modes - HALF), HALF), HALF)
+        target = ref.at[:, pl.ds(0, own), :]
+        copies.append(pltpu.make_async_copy(eig_ref.at[:, :, columns], target, sems.at[place]))
+    for copy in copies:
+        copy.start()
     freq = freq_ref[...]
     rest = jnp.where(iota((EXTRA, HALF), 0) < EXTRA // 2, freq[:, 0:HALF], freq[:, modes - HALF : modes])
     for part in range(comps):
@@ -58,27 +56,23 @@
         rest = rest - piece.astype(F32)
         near_ref[part, own : own + EXTRA, :] = piece
         far_ref[part, own : own + EXTRA, :] = piece
-    for copy in copies[1:]:
+    for copy in copies:
         copy.wait()
 
 
-def stage(eigvec, freq, force, bond, nbr):
-    comps, own, modes = eigvec.shape
-    rim = jax.ShapeDtypeStruct((comps, RIM, modes), BF16)
-    halo = jax.ShapeDtypeStruct((comps, own + EXTRA, HALF), BF16)
-    same = [jax.ShapeDtypeStruct(x.shape, x.dtype) for x in (freq, force, bond, nbr)]
+def edge_call(kernel, shape, cost, *operands):
     return pl.pallas_call(
-        stage_kernel,
-        out_shape=(rim, rim, halo, halo, *same),
-        in_specs=[HBM] * 5,
-        out_specs=(VMEM,) * 8,
-        scratch_shapes=[pltpu.SemaphoreType.DMA((8,))],
+        kernel,
+        out_shape=(jax.ShapeDtypeStruct(shape, BF16),) * 2,
+        in_specs=[VMEM] * len(operands),
+        out_specs=(VMEM,) * 2,
+        scratch_shapes=[pltpu.SemaphoreType.DMA((2,))],
         compiler_params=pltpu.CompilerParams(vmem_limit_bytes=SMALL),
-        cost_estimate=pl.CostEstimate(flops=10**4, bytes_accessed=10**6, transcendentals=0),
-    )(eigvec, freq, force, bond, nbr)
-
-
-def coupling_kernel(atoms, force_ref, bond_ref, nbr_ref, out_ref, cpl_ref):
+        cost_estimate=pl.CostEstimate(flops=cost, bytes_accessed=10**6, transcendentals=0),
+    )(*operands)
+
+
+def coupling_kernel(atoms, force_ref, bond_ref, nbr_ref, eig_ref, image_ref, rim_ref, cpl_ref, own_ref):
     comps, _, slots, own = force_ref.shape
     wide = slots * GROUP
     span = own + RIM
@@ -115,39 +109,42 @@
                 for d in range(comps):
                     top = (kc * comps + d) * GROUP
                     piece = block[top : top + GROUP]
-                    out_ref[h, rows, d * own : (d + 1) * own] = piece[:, :own]
-                    left = comps * own + d * RIM
-                    out_ref[h, rows, left : left + RIM] = piece[:, own:span]
-
-
-def coupling_matrix(force, bond, nbr, atoms):
+                    own_ref[h, rows, d * own : (d + 1) * own] = piece[:, :own]
+                    rim_ref[h, rows, d * RIM : (d + 1) * RIM] = piece[:, own:span]
+        eig = eig_ref[...].reshape(comps * own, eig_ref.shape[2])
+        image_ref[h] = jnp.dot(own_ref[h], eig, preferred_element_type=F32)
+
+
+def own_image(force, bond, nbr, eigvec, atoms):
     comps, _, slots, own = force.shape
-    size = comps * (own + RIM)
+    halves, rows = own // RIM, comps * comps * RIM
     return pl.pallas_call(
         functools.partial(coupling_kernel, atoms),
-        out_shape=jax.ShapeDtypeStruct((own // RIM, comps * comps * RIM, size), BF16),
-        in_specs=[VMEM] * 3,
-        out_specs=VMEM,
-        scratch_shapes=[pltpu.VMEM((comps**3, own, slots), BF16)],
+        out_shape=(
+            jax.ShapeDtypeStruct((halves, rows, eigvec.shape[2]), F32),
+            jax.ShapeDtypeStruct((halves, rows, comps * RIM), BF16),
+        ),
+        in_specs=[VMEM] * 4,
+        out_specs=(VMEM,) * 2,
+        scratch_shapes=[
+            pltpu.VMEM((comps**3, own, slots), BF16),
+            pltpu.VMEM((halves, rows, comps * own), BF16),
+        ],
         compiler_params=pltpu.CompilerParams(vmem_limit_bytes=LARGE),
         cost_estimate=pl.CostEstimate(flops=4 * 10**9, bytes_accessed=6 * 10**6, transcendentals=0),
-    )(force, bond, nbr)
-
-
-def pair_kernel(cpl_ref, own_ref, rim_one, rim_two, halo_one, halo_two, keep_ref, send_ref, rows_ref, flux_ref):
+    )(force, bond, nbr, eigvec)
+
+
+def pair_kernel(image_ref, cpl_ref, own_ref, rim_one, rim_two, halo_one, halo_two, keep_ref, send_ref, flux_ref):
     comps, own, modes = own_ref.shape
     depth = comps * own
     place = lax.axis_index("atom")
     odd = lax.rem(place, 2) == 1
     high = lax.rem(lax.axis_index("mode"), 2) == 1
-    for h in range(2):
-        rows_ref[h, 0:depth] = own_ref[...].reshape(depth, modes)
     one = rim_one[...].reshape(comps * RIM, modes)
     two = rim_two[...].reshape(comps * RIM, modes)
-    rows_ref[0, depth:] = jnp.where(odd, one, two)
-    rows_ref[1, depth:] = jnp.where(odd, two, one)
-    for h in range(2):
-        image = jnp.dot(cpl_ref[h], rows_ref[h], preferred_element_type=F32).astype(BF16)
+    for h, rim in enumerate((jnp.where(odd, one, two), jnp.where(odd, two, one))):
+        image = (image_ref[h] + jnp.dot(cpl_ref[h], rim, preferred_element_type=F32)).astype(BF16)
         for k in range(comps):
             for c in range(comps):
                 top = (k * comps + c) * RIM
@@ -185,21 +182,20 @@
         send_ref[k] = jnp.where(second_core, sets[0], sets[1]).astype(BF16)
 
 
-def pair_parts(matrix, eigvec, rim_one, rim_two, halo_one, halo_two):
+def pair_parts(image, matrix, eigvec, rim_one, rim_two, halo_one, halo_two):
     comps, own, modes = eigvec.shape
     shape = (comps, 2 * HALF + EXTRA, HALF)
     return pl.pallas_call(
         pair_kernel,
         out_shape=(jax.ShapeDtypeStruct(shape, F32), jax.ShapeDtypeStruct(shape, BF16)),
-        in_specs=[VMEM] * 6,
+        in_specs=[VMEM] * 7,
         out_specs=(VMEM, VMEM),
         scratch_shapes=[
-            pltpu.VMEM((own // RIM, comps * (own + RIM), modes), BF16),
             pltpu.VMEM((comps, own, comps * modes), BF16),
         ],
         compiler_params=pltpu.CompilerParams(vmem_limit_bytes=LARGE),
         cost_estimate=pl.CostEstimate(flops=2 * 10**9, bytes_accessed=6 * 10**6, transcendentals=0),
-    )(matrix, eigvec, rim_one, rim_two, halo_one, halo_two)
+    )(image, matrix, eigvec, rim_one, rim_two, halo_one, halo_two)
 
 
 def halo_freq(halo_ref, own):
@@ -319,33 +315,32 @@
     comps, own, modes = eigvec.shape
     atoms, count = own * domains, modes * blocks
     block = lax.axis_index("mode")
-    staged = stage(eigvec, freq.reshape(1, modes), force, bond, nbr)
-    inner_edge, outer_edge, near_edge, far_edge, freq_row, force, bond, nbr = staged
-
+    freq_row = freq.reshape(1, modes)
     inner = [(i, i ^ 1) for i in range(domains)]
     outer = [(i, (i + 1) % domains if i % 2 else (i - 1) % domains) for i in range(domains)]
     near = [(i, i ^ 1) for i in range(blocks)]
     far = [(i, i + 1 if i % 2 else i - 1) for i in range(1, blocks - 1)]
+    inner_edge, outer_edge = edge_call(rim_kernel, (comps, RIM, modes), COST, eigvec)
+    outer_edge, later = lax.optimization_barrier((outer_edge, freq_row))
+    near_edge, far_edge = edge_call(halo_kernel, (comps, own + EXTRA, HALF), COST, eigvec, later)
     rim_two = lax.ppermute(outer_edge, "atom", outer)
     rim_one = lax.ppermute(inner_edge, "atom", inner)
     halo_one = lax.ppermute(near_edge, "mode", near)
     halo_two = lax.ppermute(far_edge, "mode", far)
 
-    matrix = coupling_matrix(force, bond, nbr, atoms)
-    keep, send = pair_parts(matrix, eigvec, rim_one, rim_two, halo_one, halo_two)
+    image, matrix = own_image(force, bond, nbr, eigvec, atoms)
+    keep, send = pair_parts(image, matrix, eigvec, rim_one, rim_two, halo_one, halo_two)
 
     tile = jax.ShapeDtypeStruct((8, HALF), F32)
     row = jax.ShapeDtypeStruct((1, modes), F32)
-    ends = local_call(functools.partial(ends_kernel, own), tile, freq_row, halo_one)
-
     total = rounded_sum(keep, swap(send, "atom", 1))
+    total, own_freq = lax.optimization_barrier((total, freq_row))
+    ends = local_call(functools.partial(ends_kernel, own), tile, own_freq, halo_one)
     steps = bits_of("atom")[1:]
     for step, (one, two) in enumerate(zip(steps, reversed(steps))):
         total_other = lax.ppermute(total, "atom", [(i, i ^ (two if i % 2 else one)) for i in range(domains)])
         if step < len(steps) - 1:
             total = rounded_sum(total, total_other)
-            if step == 0:
-                ends, total = lax.optimization_barrier((ends, total))
     for bit in bits_of("mode")[1:]:
         other = swap(ends, "mode", bit)
         ends = jnp.where(iota((8, HALF), 0) < 4, jnp.minimum(ends, other), jnp.maximum(ends, other))
@@ -357,11 +352,8 @@
     other = swap(summary, "atom", 1)
     diff, running = local_call(functools.partial(running_kernel, modes), (row, row), summary, other)
     total = summary + other
-    earlier = jnp.zeros_like(total)
-    for bit in bits_of("mode"):
-        other = swap(total, "mode", bit)
-        earlier = earlier + jnp.where((block & bit) != 0, other, 0.0)
-        total = total + other
+    parts = [(bit, swap(total, "mode", bit)) for bit in reversed(range(1, blocks))]
+    earlier = sum(jnp.where((block ^ bit) < block, part, 0.0) for bit, part in parts)
     conductivity = local_call(last_kernel, row, running, earlier[2:3])
     return diff.reshape(modes), conductivity.reshape(modes)
 

time: 46.7 us -> 40.7 us (0.87)
  waiting for transfers between devices: 16.5 us -> 11.1 us
  local copies, waits for them, and re-layouts: 4.11 us -> 1.04 us
  starting transfers between devices: 16 us -> 18.2 us
    ppermute x5 -> x6, starting transfers between devices: 6.18 us -> 10.7 us  [swap(): lax.ppermute(x, axis, [(i, i ^ bit) for i in range(lax.axis_size(axis))])]
    unnamed x14, local copies, waits for them, and re-layouts: 4.1 us -> 1.03 us
    ppermute x5 -> x6, waiting for transfers between devices: 7.86 us -> 4.99 us  [swap(): lax.ppermute(x, axis, [(i, i ^ bit) for i in range(lax.axis_size(axis))])]
    ppermute x2, waiting for transfers between devices: 8.02 us -> 5.58 us  [body(): lax.ppermute(total, 'atom', [(i, i ^ (two if i % 2 else one)) for i in ra...]
    ppermute x2, starting transfers between devices: 3.49 us -> 2.16 us  [body(): lax.ppermute(total, 'atom', [(i, i ^ (two if i % 2 else one)) for i in ra...]
    pallas_call x2 -> x3, Pallas kernels: 4.91 us -> 6.14 us  [the longest x1 5.85 us: own_image(): pl.pallas_call(functools.partial(coupling_kernel, atoms), out_shape=(jax....]
    ppermute x1, starting transfers between devices: 2.55 us -> 1.67 us  [body(): rim_two = lax.ppermute(outer_edge, 'atom', outer)]
    pallas_call x1, Pallas kernels: 2.25 us -> 1.39 us  [pair_parts(): pl.pallas_call(pair_kernel, out_shape=(jax.ShapeDtypeStruct(shape, F32),...]
  transfers between devices with their start and end apart: 11 -> 12, of which waited for: 7 -> 6; matrix products, arithmetic and copies ran while one was open for 0% -> 0% of each run, Pallas kernels for 11% -> 16%
where the time goes in v4:
time: 40.7 us; the launch traced here: 40.5 us
  starting transfers between devices  18.2 us (45%)
  waiting for transfers between devices  11.1 us (27%)
  Pallas kernels  9.19 us (23%)
  local copies, waits for them, and re-layouts  1.04 us (3%)
  between operations  0.78 us (2%)
    ppermute x6, starting transfers between devices, swap(): lax.ppermute(x, axis, [(i, i ^ bit) for i in range(lax.axis_size(axis))])  10.7 us
    pallas_call x1, Pallas kernels, own_image(): pl.pallas_call(functools.partial(coupling_kernel, atoms), out_shape=(jax....  5.85 us
    ppermute x2, waiting for transfers between devices, body(): lax.ppermute(total, 'atom', [(i, i ^ (two if i % 2 else one)) for i in ra...  5.58 us
    ppermute x6, waiting for transfers between devices, swap(): lax.ppermute(x, axis, [(i, i ^ bit) for i in range(lax.axis_size(axis))])  4.99 us
    ppermute x1, starting transfers between devices, body(): halo_one = lax.ppermute(near_edge, 'mode', near)  3.09 us
    ppermute x2, starting transfers between devices, body(): lax.ppermute(total, 'atom', [(i, i ^ (two if i % 2 else one)) for i in ra...  2.16 us
    ppermute x1, starting transfers between devices, body(): rim_two = lax.ppermute(outer_edge, 'atom', outer)  1.67 us
    pallas_call x4, Pallas kernels, local_call(): pl.pallas_call(kernel, out_shape=out_shape, in_specs=[VMEM] * len(operand...  1.66 us
  transfers between devices with their start and end apart: 12, of which 6 were waited for; matrix products, arithmetic and copies ran while one was open for 0% of the time, Pallas kernels for 16%

profile of v4, /device:TPU:0, one launch (start us, length us, event | category | flops | bytes accessed | tf_op | source)
XLA Modules:
  0.0 40.5 jit_solution(10402490421471135016)
XLA Ops:
  0.6 0.0 copy-start
  0.6 0.0 copy-start.2
  0.7 1.0 %copy-done.2 = bf16[3,256,256]{2,1,0:T(8,128)(2,1)S(1)} copy-done((bf16[3,256,256]{2,1,0:T(8,128)(2,1)S(1)}, bf16[3,256,256]{2,1,0:T(8,128)(2,1)}, u32[]{:S(2)}) %copy-start.2) | copy-done | bytes 393240
  1.6 0.2 shard_map.78
  1.8 0.0 copy-done
  1.8 0.0 copy-start.3
  1.8 0.0 copy-start.4
  1.9 0.0 copy-start.5
  1.9 0.0 copy-start.6
  1.9 0.1 shard_map.79
  2.0 3.1 %collective-permute-start.2 = (bf16[3,272,128]{2,1,0:T(8,128)(2,1)S(1)}, bf16[3,272,128]{2,1,0:T(8,128)(2,1)S(1)}, u32[]{:S(2)}, u32[]{:S(2)}) collective-permute-start(bf16[3,272,128]{2,1,0:T(8,128)(2,1)S(1)} %get-tuple-element.22), channel_id=1, source_target_pairs={{0,1},{1,0},{2,3},{3,2},{4,5},{5,4},{6,7},{7,6},{8,9},{9,8},{10,11... | collective-permute-start | bytes 626696 | tf_op jit(solution)/shard_map/ppermute | solution.py:328
  5.1 0.7 %collective-permute-start.3 = (bf16[3,272,128]{2,1,0:T(8,128)(2,1)S(1)}, bf16[3,272,128]{2,1,0:T(8,128)(2,1)S(1)}, u32[]{:S(2)}, u32[]{:S(2)}) collective-permute-start(bf16[3,272,128]{2,1,0:T(8,128)(2,1)S(1)} %get-tuple-element.23), channel_id=1, source_target_pairs={{1,2},{2,1},{5,6},{6,5},{9,10},{10,9},{13,14},{14,13},{17,18},{18,... | collective-permute-start | bytes 626696 | tf_op jit(solution)/shard_map/ppermute | solution.py:329
  5.8 1.7 %collective-permute-start.1 = (bf16[3,128,256]{2,1,0:T(8,128)(2,1)S(1)}, bf16[3,128,256]{2,1,0:T(8,128)(2,1)S(1)}, u32[]{:S(2)}, u32[]{:S(2)}) collective-permute-start(bf16[3,128,256]{2,1,0:T(8,128)(2,1)S(1)} %get-tuple-element.20), channel_id=1, source_target_pairs={{0,28},{4,8},{8,4},{12,16},{16,12},{20,24},{24,20},{28,0},{1,29},{... | collective-permute-start | bytes 589832 | tf_op jit(solution)/shard_map/ppermute | solution.py:326
  7.4 0.0 collective-permute-start
  7.4 0.0 copy-done.3
  7.4 0.0 copy-done.4
  7.4 0.0 copy-done.5
  7.5 0.0 copy-done.6
  7.5 5.9 %shard_map.77 = (f32[2,1152,256]{2,1,0:T(8,128)S(1)}, bf16[2,1152,384]{2,1,0:T(8,128)(2,1)S(1)}) custom-call(f32[3,3,16,256]{3,2,1,0:T(8,128)S(1)} %copy-done.4, f32[3,16,256]{2,1,0:T(8,128)S(1)} %copy-done.5, s32[16,256]{1,0:T(8,128)S(1)} %copy-done.6, bf16[3,256,256]{2,1,0:T(8,128)(2,1)S(1)} %copy-done.3), custom_call_target="tpu_custom_call" | custom-call | flops 4000000000 | bytes 6000000 | tf_op jit(solution)/shard_map/pallas_call | solution.py:121
  13.3 0.5 %collective-permute-done.1.rim_two = bf16[3,128,256]{2,1,0:T(8,128)(2,1)S(1)} collective-permute-done((bf16[3,128,256]{2,1,0:T(8,128)(2,1)S(1)}, bf16[3,128,256]{2,1,0:T(8,128)(2,1)S(1)}, u32[]{:S(2)}, u32[]{:S(2)}) %collective-permute-start.1) | collective-permute-done | bytes 196640 | tf_op jit(solution)/shard_map/ppermute | solution.py:326
  13.8 0.0 collective-permute-done.rim_one
  13.8 0.0 collective-permute-done.2.halo_one.halo_ref
  13.8 0.0 collective-permute-done.3.halo_two
  13.8 0.0 copy-start.1
  13.9 1.4 %shard_map.80 = (f32[3,272,128]{2,1,0:T(8,128)S(1)}, bf16[3,272,128]{2,1,0:T(8,128)(2,1)S(1)}) custom-call(f32[2,1152,256]{2,1,0:T(8,128)S(1)} %get-tuple-element.16.image_ref, bf16[2,1152,384]{2,1,0:T(8,128)(2,1)S(1)} %get-tuple-element.17.cpl_ref, bf16[3,256,256]{2,1,0:T(8,128)(2,1)S(1)} %copy-done.3, ...), custom_call_target="tpu_custom_call" | custom-call | flops 2000000000 | bytes 6000000 | tf_op jit(solution)/shard_map/pallas_call | solution.py:188
  15.2 0.1 collective-permute-start.4
  15.3 1.4 %collective-permute-done.4 = bf16[3,272,128]{2,1,0:T(8,128)(2,1)S(1)} collective-permute-done((bf16[3,272,128]{2,1,0:T(8,128)(2,1)S(1)}, bf16[3,272,128]{2,1,0:T(8,128)(2,1)S(1)}, u32[]{:S(2)}, u32[]{:S(2)}) %collective-permute-start.4) | collective-permute-done | bytes 208928 | tf_op jit(solution)/shard_map/ppermute | solution.py:301
  16.8 0.1 reduce-precision_convert_fusion.1
  16.8 1.1 %collective-permute-start.6 = (bf16[3,272,128]{2,1,0:T(8,128)(2,1)S(1)}, bf16[3,272,128]{2,1,0:T(8,128)(2,1)S(1)}, u32[]{:S(2)}, u32[]{:S(2)}) collective-permute-start(bf16[3,272,128]{2,1,0:T(8,128)(2,1)S(1)} %reduce-precision_convert_fusion.1), channel_id=1, source_target_pairs={{0,8},{4,20},{8,0},{12,28},{16,24},{20,4},{24,16},{28,12},{1,9},{5... | collective-permute-start | bytes 626696 | tf_op jit(solution)/shard_map/ppermute | solution.py:341
  17.9 0.1 shard_map.81
  18.0 3.8 %collective-permute-start.5 = (f32[8,128]{1,0:T(8,128)S(1)}, f32[8,128]{1,0:T(8,128)S(1)}, u32[]{:S(2)}, u32[]{:S(2)}) collective-permute-start(f32[8,128]{1,0:T(8,128)S(1)} %shard_map.81), channel_id=1, source_target_pairs={{0,2},{1,3},{2,0},{3,1},{4,6},{5,7},{6,4},{7,5},{8,10},{9,11},{10,... | collective-permute-start | bytes 12296 | tf_op jit(solution)/shard_map/ppermute | solution.py:301
  21.8 0.9 %collective-permute-done.6 = bf16[3,272,128]{2,1,0:T(8,128)(2,1)S(1)} collective-permute-done((bf16[3,272,128]{2,1,0:T(8,128)(2,1)S(1)}, bf16[3,272,128]{2,1,0:T(8,128)(2,1)S(1)}, u32[]{:S(2)}, u32[]{:S(2)}) %collective-permute-start.6) | collective-permute-done | bytes 208928 | tf_op jit(solution)/shard_map/ppermute | solution.py:341
  22.7 0.1 reduce-precision_convert_fusion.pair_one
  22.8 1.1 %collective-permute-start.7 = (bf16[3,272,128]{2,1,0:T(8,128)(2,1)S(1)}, bf16[3,272,128]{2,1,0:T(8,128)(2,1)S(1)}, u32[]{:S(2)}, u32[]{:S(2)}) collective-permute-start(bf16[3,272,128]{2,1,0:T(8,128)(2,1)S(1)} %reduce-precision_convert_fusion.pair_one), channel_id=1, source_target_pairs={{0,16},{4,12},{8,24},{12,4},{16,0},{20,28},{24,8},{28,20},{1,17},{... | collective-permute-start | bytes 626696 | tf_op jit(solution)/shard_map/ppermute | solution.py:341
  23.9 0.0 collective-permute-done.5
  23.9 0.1 maximum_select_fusion.ends_ref
  23.9 4.7 %collective-permute-done.7.pair_two = bf16[3,272,128]{2,1,0:T(8,128)(2,1)S(1)} collective-permute-done((bf16[3,272,128]{2,1,0:T(8,128)(2,1)S(1)}, bf16[3,272,128]{2,1,0:T(8,128)(2,1)S(1)}, u32[]{:S(2)}, u32[]{:S(2)}) %collective-permute-start.7) | collective-permute-done | bytes 208928 | tf_op jit(solution)/shard_map/ppermute | solution.py:341
  28.6 0.3 shard_map.82.own_ref
  28.9 0.0 collective-permute-start.8
  28.9 1.2 %collective-permute-done.8.other_ref = f32[8,128]{1,0:T(8,128)S(1)} collective-permute-done((f32[8,128]{1,0:T(8,128)S(1)}, f32[8,128]{1,0:T(8,128)S(1)}, u32[]{:S(2)}, u32[]{:S(2)}) %collective-permute-start.8) | collective-permute-done | bytes 4128 | tf_op jit(solution)/shard_map/ppermute | solution.py:301
  30.1 3.8 %collective-permute-start.10 = (f32[8,128]{1,0:T(8,128)S(1)}, f32[8,128]{1,0:T(8,128)S(1)}, u32[]{:S(2)}, u32[]{:S(2)}) collective-permute-start(f32[8,128]{1,0:T(8,128)S(1)} %add.17), channel_id=1, source_target_pairs={{0,2},{1,3},{2,0},{3,1},{4,6},{5,7},{6,4},{7,5},{8,10},{9,11},{10,... | collective-permute-start | bytes 12296 | tf_op jit(solution)/shard_map/ppermute | solution.py:301
  33.9 0.6 %collective-permute-start.11 = (f32[8,128]{1,0:T(8,128)S(1)}, f32[8,128]{1,0:T(8,128)S(1)}, u32[]{:S(2)}, u32[]{:S(2)}) collective-permute-start(f32[8,128]{1,0:T(8,128)S(1)} %add.17), channel_id=1, source_target_pairs={{0,1},{1,0},{2,3},{3,2},{4,5},{5,4},{6,7},{7,6},{8,9},{9,8},{10,11... | collective-permute-start | bytes 12296 | tf_op jit(solution)/shard_map/ppermute | solution.py:301
  34.5 2.4 %collective-permute-start.9 = (f32[8,128]{1,0:T(8,128)S(1)}, f32[8,128]{1,0:T(8,128)S(1)}, u32[]{:S(2)}, u32[]{:S(2)}) collective-permute-start(f32[8,128]{1,0:T(8,128)S(1)} %add.17), channel_id=1, source_target_pairs={{0,3},{1,2},{2,1},{3,0},{4,7},{5,6},{6,5},{7,4},{8,11},{9,10},{10,... | collective-permute-start | bytes 12296 | tf_op jit(solution)/shard_map/ppermute | solution.py:301
  36.8 0.7 %shard_map.83 = (f32[1,256]{1,0:T(1,128)}, f32[1,256]{1,0:T(1,128)S(1)}) custom-call(f32[8,128]{1,0:T(8,128)S(1)} %shard_map.82.own_ref, f32[8,128]{1,0:T(8,128)S(1)} %collective-permute-done.8.other_ref), custom_call_target="tpu_custom_call" | custom-call | flops 1000000 | bytes 1000000 | tf_op jit(solution)/shard_map/pallas_call | solution.py:275
  37.5 0.0 collective-permute-done.10
  37.5 0.0 collective-permute-done.11
  37.5 2.4 %collective-permute-done.9 = f32[8,128]{1,0:T(8,128)S(1)} collective-permute-done((f32[8,128]{1,0:T(8,128)S(1)}, f32[8,128]{1,0:T(8,128)S(1)}, u32[]{:S(2)}, u32[]{:S(2)}) %collective-permute-start.9) | collective-permute-done | bytes 4128 | tf_op jit(solution)/shard_map/ppermute | solution.py:301
  39.9 0.6 %shard_map.84 = f32[1,256]{1,0:T(1,128)} custom-call(f32[1,256]{1,0:T(1,128)S(1)} %get-tuple-element.29.run_ref, f32[1,128]{1,0:T(1,128)S(1)} %slice.3.earlier_ref), custom_call_target="tpu_custom_call" | custom-call | flops 1000000 | bytes 1000000 | tf_op jit(solution)/shard_map/pallas_call | solution.py:275
  (5 shorter events, 0.0 us)
Async XLA Ops:
  0.6 1.2 %copy-start = (f32[256]{0:T(256)S(1)}, f32[256]{0:T(256)}, u32[]{:S(2)}) copy-start(f32[256]{0:T(256)} %param.11) | copy-start | bytes 3076
  0.6 1.0 %copy-start.2 = (bf16[3,256,256]{2,1,0:T(8,128)(2,1)S(1)}, bf16[3,256,256]{2,1,0:T(8,128)(2,1)}, u32[]{:S(2)}) copy-start(bf16[3,256,256]{2,1,0:T(8,128)(2,1)} %own_ref.1) | copy-start | bytes 1179652
  1.8 5.6 %copy-start.3 = (bf16[3,256,256]{2,1,0:T(8,128)(2,1)S(1)}, bf16[3,256,256]{2,1,0:T(8,128)(2,1)}, u32[]{:S(2)}) copy-start(bf16[3,256,256]{2,1,0:T(8,128)(2,1)} %own_ref.1) | copy-start | bytes 1179652
  1.8 5.6 %copy-start.4 = (f32[3,3,16,256]{3,2,1,0:T(8,128)S(1)}, f32[3,3,16,256]{3,2,1,0:T(8,128)}, u32[]{:S(2)}) copy-start(f32[3,3,16,256]{3,2,1,0:T(8,128)} %force_ref.1) | copy-start | bytes 442372
  1.9 5.6 %copy-start.5 = (f32[3,16,256]{2,1,0:T(8,128)S(1)}, f32[3,16,256]{2,1,0:T(8,128)}, u32[]{:S(2)}) copy-start(f32[3,16,256]{2,1,0:T(8,128)} %bond_ref.1) | copy-start | bytes 147460
  1.9 5.6 %copy-start.6 = (s32[16,256]{1,0:T(8,128)S(1)}, s32[16,256]{1,0:T(8,128)}, u32[]{:S(2)}) copy-start(s32[16,256]{1,0:T(8,128)} %nbr_ref.1) | copy-start | bytes 49156
  2.0 11.8 %collective-permute-start.2 = (bf16[3,272,128]{2,1,0:T(8,128)(2,1)S(1)}, bf16[3,272,128]{2,1,0:T(8,128)(2,1)S(1)}, u32[]{:S(2)}, u32[]{:S(2)}) collective-permute-start(bf16[3,272,128]{2,1,0:T(8,128)(2,1)S(1)} %get-tuple-element.22), channel_id=1, source_target_pairs={{0,1},{1,0},{2,3},{3,2},{4,5},{5,4},{6,7},{7,6},{8,9},{9,8},{10,11... | collective-permute-start | bytes 626696 | tf_op jit(solution)/shard_map/ppermute | solution.py:328
  5.1 8.7 %collective-permute-start.3 = (bf16[3,272,128]{2,1,0:T(8,128)(2,1)S(1)}, bf16[3,272,128]{2,1,0:T(8,128)(2,1)S(1)}, u32[]{:S(2)}, u32[]{:S(2)}) collective-permute-start(bf16[3,272,128]{2,1,0:T(8,128)(2,1)S(1)} %get-tuple-element.23), channel_id=1, source_target_pairs={{1,2},{2,1},{5,6},{6,5},{9,10},{10,9},{13,14},{14,13},{17,18},{18,... | collective-permute-start | bytes 626696 | tf_op jit(solution)/shard_map/ppermute | solution.py:329
  5.8 8.1 %collective-permute-start.1 = (bf16[3,128,256]{2,1,0:T(8,128)(2,1)S(1)}, bf16[3,128,256]{2,1,0:T(8,128)(2,1)S(1)}, u32[]{:S(2)}, u32[]{:S(2)}) collective-permute-start(bf16[3,128,256]{2,1,0:T(8,128)(2,1)S(1)} %get-tuple-element.20), channel_id=1, source_target_pairs={{0,28},{4,8},{8,4},{12,16},{16,12},{20,24},{24,20},{28,0},{1,29},{... | collective-permute-start | bytes 589832 | tf_op jit(solution)/shard_map/ppermute | solution.py:326
  7.4 6.4 %collective-permute-start = (bf16[3,128,256]{2,1,0:T(8,128)(2,1)S(1)}, bf16[3,128,256]{2,1,0:T(8,128)(2,1)S(1)}, u32[]{:S(2)}, u32[]{:S(2)}) collective-permute-start(bf16[3,128,256]{2,1,0:T(8,128)(2,1)S(1)} %get-tuple-element.18), channel_id=1, source_target_pairs={{0,4},{4,0},{8,12},{12,8},{16,20},{20,16},{24,28},{28,24},{1,5},{5... | collective-permute-start | bytes 589832 | tf_op jit(solution)/shard_map/ppermute | solution.py:327
  13.8 14.8 %copy-start.1 = (s32[2,256]{1,0:T(2,128)S(1)}, s32[2,256]{1,0:T(2,128)}, u32[]{:S(2)}) copy-start(s32[2,256]{1,0:T(2,128)} %band_ref.1) | copy-start | bytes 6148
  15.2 1.5 %collective-permute-start.4 = (bf16[3,272,128]{2,1,0:T(8,128)(2,1)S(1)}, bf16[3,272,128]{2,1,0:T(8,128)(2,1)S(1)}, u32[]{:S(2)}, u32[]{:S(2)}) collective-permute-start(bf16[3,272,128]{2,1,0:T(8,128)(2,1)S(1)} %get-tuple-element.25), channel_id=1, source_target_pairs={{0,4},{4,0},{8,12},{12,8},{16,20},{20,16},{24,28},{28,24},{1,5},{5... | collective-permute-start | bytes 626696 | tf_op jit(solution)/shard_map/ppermute | solution.py:301
  16.8 5.9 %collective-permute-start.6 = (bf16[3,272,128]{2,1,0:T(8,128)(2,1)S(1)}, bf16[3,272,128]{2,1,0:T(8,128)(2,1)S(1)}, u32[]{:S(2)}, u32[]{:S(2)}) collective-permute-start(bf16[3,272,128]{2,1,0:T(8,128)(2,1)S(1)} %reduce-precision_convert_fusion.1), channel_id=1, source_target_pairs={{0,8},{4,20},{8,0},{12,28},{16,24},{20,4},{24,16},{28,12},{1,9},{5... | collective-permute-start | bytes 626696 | tf_op jit(solution)/shard_map/ppermute | solution.py:341
  18.0 5.9 %collective-permute-start.5 = (f32[8,128]{1,0:T(8,128)S(1)}, f32[8,128]{1,0:T(8,128)S(1)}, u32[]{:S(2)}, u32[]{:S(2)}) collective-permute-start(f32[8,128]{1,0:T(8,128)S(1)} %shard_map.81), channel_id=1, source_target_pairs={{0,2},{1,3},{2,0},{3,1},{4,6},{5,7},{6,4},{7,5},{8,10},{9,11},{10,... | collective-permute-start | bytes 12296 | tf_op jit(solution)/shard_map/ppermute | solution.py:301
  22.8 5.9 %collective-permute-start.7 = (bf16[3,272,128]{2,1,0:T(8,128)(2,1)S(1)}, bf16[3,272,128]{2,1,0:T(8,128)(2,1)S(1)}, u32[]{:S(2)}, u32[]{:S(2)}) collective-permute-start(bf16[3,272,128]{2,1,0:T(8,128)(2,1)S(1)} %reduce-precision_convert_fusion.pair_one), channel_id=1, source_target_pairs={{0,16},{4,12},{8,24},{12,4},{16,0},{20,28},{24,8},{28,20},{1,17},{... | collective-permute-start | bytes 626696 | tf_op jit(solution)/shard_map/ppermute | solution.py:341
  28.9 1.2 %collective-permute-start.8 = (f32[8,128]{1,0:T(8,128)S(1)}, f32[8,128]{1,0:T(8,128)S(1)}, u32[]{:S(2)}, u32[]{:S(2)}) collective-permute-start(f32[8,128]{1,0:T(8,128)S(1)} %shard_map.82.own_ref), channel_id=1, source_target_pairs={{0,4},{4,0},{8,12},{12,8},{16,20},{20,16},{24,28},{28,24},{1,5},{5... | collective-permute-start | bytes 12296 | tf_op jit(solution)/shard_map/ppermute | solution.py:301
  30.1 7.4 %collective-permute-start.10 = (f32[8,128]{1,0:T(8,128)S(1)}, f32[8,128]{1,0:T(8,128)S(1)}, u32[]{:S(2)}, u32[]{:S(2)}) collective-permute-start(f32[8,128]{1,0:T(8,128)S(1)} %add.17), channel_id=1, source_target_pairs={{0,2},{1,3},{2,0},{3,1},{4,6},{5,7},{6,4},{7,5},{8,10},{9,11},{10,... | collective-permute-start | bytes 12296 | tf_op jit(solution)/shard_map/ppermute | solution.py:301
  33.9 3.6 %collective-permute-start.11 = (f32[8,128]{1,0:T(8,128)S(1)}, f32[8,128]{1,0:T(8,128)S(1)}, u32[]{:S(2)}, u32[]{:S(2)}) collective-permute-start(f32[8,128]{1,0:T(8,128)S(1)} %add.17), channel_id=1, source_target_pairs={{0,1},{1,0},{2,3},{3,2},{4,5},{5,4},{6,7},{7,6},{8,9},{9,8},{10,11... | collective-permute-start | bytes 12296 | tf_op jit(solution)/shard_map/ppermute | solution.py:301
  34.5 5.4 %collective-permute-start.9 = (f32[8,128]{1,0:T(8,128)S(1)}, f32[8,128]{1,0:T(8,128)S(1)}, u32[]{:S(2)}, u32[]{:S(2)}) collective-permute-start(f32[8,128]{1,0:T(8,128)S(1)} %add.17), channel_id=1, source_target_pairs={{0,3},{1,2},{2,1},{3,0},{4,7},{5,6},{6,5},{7,4},{8,11},{9,10},{10,... | collective-permute-start | bytes 12296 | tf_op jit(solution)/shard_map/ppermute | solution.py:301

commit v5 on v4

--- a/solution.py
+++ b/solution.py
@@ -326,7 +326,12 @@
     rim_two = lax.ppermute(outer_edge, "atom", outer)
     rim_one = lax.ppermute(inner_edge, "atom", inner)
     halo_one = lax.ppermute(near_edge, "mode", near)
-    halo_two = lax.ppermute(far_edge, "mode", far)
+    hops = []
+    for a in range(domains):
+        for i in range(blocks):
+            inside = 0 < i < blocks - 1
+            hops.append((a * blocks + i, a * blocks + (i + 1 if i % 2 else i - 1) if inside else (a ^ 1) * blocks + i))
+    halo_two = lax.ppermute(far_edge, ("atom", "mode"), hops)
 
     image, matrix = own_image(force, bond, nbr, eigvec, atoms)
     keep, send = pair_parts(image, matrix, eigvec, rim_one, rim_two, halo_one, halo_two)

time: 40.7 us -> 39.2 us (0.963)
  starting transfers between devices: 18.2 us -> 15 us
  waiting for transfers between devices: 11.1 us -> 12.8 us
    ppermute x6, starting transfers between devices: 10.7 us -> 7.96 us  [swap(): lax.ppermute(x, axis, [(i, i ^ bit) for i in range(lax.axis_size(axis))])]
    ppermute x2, waiting for transfers between devices: 5.58 us -> 7.69 us  [body(): lax.ppermute(total, 'atom', [(i, i ^ (two if i % 2 else one)) for i in ra...]
    ppermute x1, starting transfers between devices: 1.67 us -> 2.56 us  [body(): rim_two = lax.ppermute(outer_edge, 'atom', outer)]
    ppermute x2, starting transfers between devices: 2.16 us -> 1.38 us  [body(): lax.ppermute(total, 'atom', [(i, i ^ (two if i % 2 else one)) for i in ra...]
    ppermute x1, starting transfers between devices: 0.66 us -> 0.01 us  [body(): halo_two = lax.ppermute(far_edge, ('atom', 'mode'), hops)]
    ppermute x1, waiting for transfers between devices: 0.5 us -> 0.01 us  [body(): rim_two = lax.ppermute(outer_edge, 'atom', outer)]
  transfers between devices with their start and end apart: 12 -> 12, of which waited for: 6 -> 5; matrix products, arithmetic and copies ran while one was open for 0% -> 0% of each run, Pallas kernels for 16% -> 17%
where the time goes in v5:
time: 39.2 us; the launch traced here: 39.1 us
  starting transfers between devices  15 us (38%)
  waiting for transfers between devices  12.8 us (33%)
  Pallas kernels  9.2 us (23%)
  local copies, waits for them, and re-layouts  1.04 us (3%)
  between operations  0.8 us (2%)
    ppermute x6, starting transfers between devices, swap(): lax.ppermute(x, axis, [(i, i ^ bit) for i in range(lax.axis_size(axis))])  7.96 us
    ppermute x2, waiting for transfers between devices, body(): lax.ppermute(total, 'atom', [(i, i ^ (two if i % 2 else one)) for i in ra...  7.69 us
    pallas_call x1, Pallas kernels, own_image(): pl.pallas_call(functools.partial(coupling_kernel, atoms), out_shape=(jax....  5.86 us
    ppermute x6, waiting for transfers between devices, swap(): lax.ppermute(x, axis, [(i, i ^ bit) for i in range(lax.axis_size(axis))])  5.12 us
    ppermute x1, starting transfers between devices, body(): halo_one = lax.ppermute(near_edge, 'mode', near)  3.09 us
    ppermute x1, starting transfers between devices, body(): rim_two = lax.ppermute(outer_edge, 'atom', outer)  2.56 us
    pallas_call x4, Pallas kernels, local_call(): pl.pallas_call(kernel, out_shape=out_shape, in_specs=[VMEM] * len(operand...  1.66 us
    pallas_call x1, Pallas kernels, pair_parts(): pl.pallas_call(pair_kernel, out_shape=(jax.ShapeDtypeStruct(shape, F32),...  1.39 us
  transfers between devices with their start and end apart: 12, of which 5 were waited for; matrix products, arithmetic and copies ran while one was open for 0% of the time, Pallas kernels for 17%

profile of v5, /device:TPU:0, one launch (start us, length us, event | category | flops | bytes accessed | tf_op | source)
XLA Modules:
  0.0 39.1 jit_solution(1871417187697650500)
XLA Ops:
  0.6 0.0 copy-start
  0.6 0.0 copy-start.2
  0.7 1.0 %copy-done.2 = bf16[3,256,256]{2,1,0:T(8,128)(2,1)S(1)} copy-done((bf16[3,256,256]{2,1,0:T(8,128)(2,1)S(1)}, bf16[3,256,256]{2,1,0:T(8,128)(2,1)}, u32[]{:S(2)}) %copy-start.2) | copy-done | bytes 393240
  1.6 0.2 shard_map.78
  1.8 0.0 copy-done
  1.8 0.0 copy-start.3
  1.8 0.0 copy-start.4
  1.9 0.0 copy-start.5
  1.9 0.0 copy-start.6
  1.9 0.1 shard_map.79
  2.0 3.1 %collective-permute-start.2 = (bf16[3,272,128]{2,1,0:T(8,128)(2,1)S(1)}, bf16[3,272,128]{2,1,0:T(8,128)(2,1)S(1)}, u32[]{:S(2)}, u32[]{:S(2)}) collective-permute-start(bf16[3,272,128]{2,1,0:T(8,128)(2,1)S(1)} %get-tuple-element.22), channel_id=1, source_target_pairs={{0,1},{1,0},{2,3},{3,2},{4,5},{5,4},{6,7},{7,6},{8,9},{9,8},{10,11... | collective-permute-start | bytes 626696 | tf_op jit(solution)/shard_map/ppermute | solution.py:328
  5.1 0.0 collective-permute-start.3
  5.1 2.6 %collective-permute-start.1 = (bf16[3,128,256]{2,1,0:T(8,128)(2,1)S(1)}, bf16[3,128,256]{2,1,0:T(8,128)(2,1)S(1)}, u32[]{:S(2)}, u32[]{:S(2)}) collective-permute-start(bf16[3,128,256]{2,1,0:T(8,128)(2,1)S(1)} %get-tuple-element.20), channel_id=1, source_target_pairs={{0,28},{4,8},{8,4},{12,16},{16,12},{20,24},{24,20},{28,0},{1,29},{... | collective-permute-start | bytes 589832 | tf_op jit(solution)/shard_map/ppermute | solution.py:326
  7.7 0.0 collective-permute-start
  7.7 0.0 copy-done.3
  7.7 0.0 copy-done.4
  7.7 0.0 copy-done.5
  7.7 0.0 copy-done.6
  7.7 5.9 %shard_map.77 = (f32[2,1152,256]{2,1,0:T(8,128)S(1)}, bf16[2,1152,384]{2,1,0:T(8,128)(2,1)S(1)}) custom-call(f32[3,3,16,256]{3,2,1,0:T(8,128)S(1)} %copy-done.4, f32[3,16,256]{2,1,0:T(8,128)S(1)} %copy-done.5, s32[16,256]{1,0:T(8,128)S(1)} %copy-done.6, bf16[3,256,256]{2,1,0:T(8,128)(2,1)S(1)} %copy-done.3), custom_call_target="tpu_custom_call" | custom-call | flops 4000000000 | bytes 6000000 | tf_op jit(solution)/shard_map/pallas_call | solution.py:121
  13.6 0.0 collective-permute-done.1.rim_two
  13.6 0.0 collective-permute-done.rim_one
  13.6 0.0 collective-permute-done.2.halo_one.halo_ref
  13.6 0.0 collective-permute-done.3.halo_two
  13.6 0.0 copy-start.1
  13.6 1.4 %shard_map.80 = (f32[3,272,128]{2,1,0:T(8,128)S(1)}, bf16[3,272,128]{2,1,0:T(8,128)(2,1)S(1)}) custom-call(f32[2,1152,256]{2,1,0:T(8,128)S(1)} %get-tuple-element.16.image_ref, bf16[2,1152,384]{2,1,0:T(8,128)(2,1)S(1)} %get-tuple-element.17.cpl_ref, bf16[3,256,256]{2,1,0:T(8,128)(2,1)S(1)} %copy-done.3, ...), custom_call_target="tpu_custom_call" | custom-call | flops 2000000000 | bytes 6000000 | tf_op jit(solution)/shard_map/pallas_call | solution.py:188
  15.0 0.5 %collective-permute-start.4 = (bf16[3,272,128]{2,1,0:T(8,128)(2,1)S(1)}, bf16[3,272,128]{2,1,0:T(8,128)(2,1)S(1)}, u32[]{:S(2)}, u32[]{:S(2)}) collective-permute-start(bf16[3,272,128]{2,1,0:T(8,128)(2,1)S(1)} %get-tuple-element.25), channel_id=1, source_target_pairs={{0,4},{4,0},{8,12},{12,8},{16,20},{20,16},{24,28},{28,24},{1,5},{5... | collective-permute-start | bytes 626696 | tf_op jit(solution)/shard_map/ppermute | solution.py:301
  15.5 1.1 %collective-permute-done.4 = bf16[3,272,128]{2,1,0:T(8,128)(2,1)S(1)} collective-permute-done((bf16[3,272,128]{2,1,0:T(8,128)(2,1)S(1)}, bf16[3,272,128]{2,1,0:T(8,128)(2,1)S(1)}, u32[]{:S(2)}, u32[]{:S(2)}) %collective-permute-start.4) | collective-permute-done | bytes 208928 | tf_op jit(solution)/shard_map/ppermute | solution.py:301
  16.6 0.1 reduce-precision_convert_fusion.1
  16.7 0.6 %collective-permute-start.6 = (bf16[3,272,128]{2,1,0:T(8,128)(2,1)S(1)}, bf16[3,272,128]{2,1,0:T(8,128)(2,1)S(1)}, u32[]{:S(2)}, u32[]{:S(2)}) collective-permute-start(bf16[3,272,128]{2,1,0:T(8,128)(2,1)S(1)} %reduce-precision_convert_fusion.1), channel_id=1, source_target_pairs={{0,8},{4,20},{8,0},{12,28},{16,24},{20,4},{24,16},{28,12},{1,9},{5... | collective-permute-start | bytes 626696 | tf_op jit(solution)/shard_map/ppermute | solution.py:346
  17.3 0.1 shard_map.81
  17.3 2.5 %collective-permute-start.5 = (f32[8,128]{1,0:T(8,128)S(1)}, f32[8,128]{1,0:T(8,128)S(1)}, u32[]{:S(2)}, u32[]{:S(2)}) collective-permute-start(f32[8,128]{1,0:T(8,128)S(1)} %shard_map.81), channel_id=1, source_target_pairs={{0,2},{1,3},{2,0},{3,1},{4,6},{5,7},{6,4},{7,5},{8,10},{9,11},{10,... | collective-permute-start | bytes 12296 | tf_op jit(solution)/shard_map/ppermute | solution.py:301
  19.8 2.7 %collective-permute-done.6 = bf16[3,272,128]{2,1,0:T(8,128)(2,1)S(1)} collective-permute-done((bf16[3,272,128]{2,1,0:T(8,128)(2,1)S(1)}, bf16[3,272,128]{2,1,0:T(8,128)(2,1)S(1)}, u32[]{:S(2)}, u32[]{:S(2)}) %collective-permute-start.6) | collective-permute-done | bytes 208928 | tf_op jit(solution)/shard_map/ppermute | solution.py:346
  22.6 0.1 reduce-precision_convert_fusion.pair_one
  22.6 0.8 %collective-permute-start.7 = (bf16[3,272,128]{2,1,0:T(8,128)(2,1)S(1)}, bf16[3,272,128]{2,1,0:T(8,128)(2,1)S(1)}, u32[]{:S(2)}, u32[]{:S(2)}) collective-permute-start(bf16[3,272,128]{2,1,0:T(8,128)(2,1)S(1)} %reduce-precision_convert_fusion.pair_one), channel_id=1, source_target_pairs={{0,16},{4,12},{8,24},{12,4},{16,0},{20,28},{24,8},{28,20},{1,17},{... | collective-permute-start | bytes 626696 | tf_op jit(solution)/shard_map/ppermute | solution.py:346
  23.5 0.0 collective-permute-done.5
  23.5 0.1 maximum_select_fusion.ends_ref
  23.5 5.0 %collective-permute-done.7.pair_two = bf16[3,272,128]{2,1,0:T(8,128)(2,1)S(1)} collective-permute-done((bf16[3,272,128]{2,1,0:T(8,128)(2,1)S(1)}, bf16[3,272,128]{2,1,0:T(8,128)(2,1)S(1)}, u32[]{:S(2)}, u32[]{:S(2)}) %collective-permute-start.7) | collective-permute-done | bytes 208928 | tf_op jit(solution)/shard_map/ppermute | solution.py:346
  28.5 0.3 shard_map.82.own_ref
  28.8 0.0 collective-permute-start.8
  28.8 1.2 %collective-permute-done.8.other_ref = f32[8,128]{1,0:T(8,128)S(1)} collective-permute-done((f32[8,128]{1,0:T(8,128)S(1)}, f32[8,128]{1,0:T(8,128)S(1)}, u32[]{:S(2)}, u32[]{:S(2)}) %collective-permute-start.8) | collective-permute-done | bytes 4128 | tf_op jit(solution)/shard_map/ppermute | solution.py:301
  30.0 2.0 %collective-permute-start.10 = (f32[8,128]{1,0:T(8,128)S(1)}, f32[8,128]{1,0:T(8,128)S(1)}, u32[]{:S(2)}, u32[]{:S(2)}) collective-permute-start(f32[8,128]{1,0:T(8,128)S(1)} %add.17), channel_id=1, source_target_pairs={{0,2},{1,3},{2,0},{3,1},{4,6},{5,7},{6,4},{7,5},{8,10},{9,11},{10,... | collective-permute-start | bytes 12296 | tf_op jit(solution)/shard_map/ppermute | solution.py:301
  32.0 1.0 %collective-permute-start.11 = (f32[8,128]{1,0:T(8,128)S(1)}, f32[8,128]{1,0:T(8,128)S(1)}, u32[]{:S(2)}, u32[]{:S(2)}) collective-permute-start(f32[8,128]{1,0:T(8,128)S(1)} %add.17), channel_id=1, source_target_pairs={{0,1},{1,0},{2,3},{3,2},{4,5},{5,4},{6,7},{7,6},{8,9},{9,8},{10,11... | collective-permute-start | bytes 12296 | tf_op jit(solution)/shard_map/ppermute | solution.py:301
  33.0 1.9 %collective-permute-start.9 = (f32[8,128]{1,0:T(8,128)S(1)}, f32[8,128]{1,0:T(8,128)S(1)}, u32[]{:S(2)}, u32[]{:S(2)}) collective-permute-start(f32[8,128]{1,0:T(8,128)S(1)} %add.17), channel_id=1, source_target_pairs={{0,3},{1,2},{2,1},{3,0},{4,7},{5,6},{6,5},{7,4},{8,11},{9,10},{10,... | collective-permute-start | bytes 12296 | tf_op jit(solution)/shard_map/ppermute | solution.py:301
  34.9 0.7 %shard_map.83 = (f32[1,256]{1,0:T(1,128)}, f32[1,256]{1,0:T(1,128)S(1)}) custom-call(f32[8,128]{1,0:T(8,128)S(1)} %shard_map.82.own_ref, f32[8,128]{1,0:T(8,128)S(1)} %collective-permute-done.8.other_ref), custom_call_target="tpu_custom_call" | custom-call | flops 1000000 | bytes 1000000 | tf_op jit(solution)/shard_map/pallas_call | solution.py:275
  35.5 0.0 collective-permute-done.10
  35.5 0.0 collective-permute-done.11
  35.6 2.8 %collective-permute-done.9 = f32[8,128]{1,0:T(8,128)S(1)} collective-permute-done((f32[8,128]{1,0:T(8,128)S(1)}, f32[8,128]{1,0:T(8,128)S(1)}, u32[]{:S(2)}, u32[]{:S(2)}) %collective-permute-start.9) | collective-permute-done | bytes 4128 | tf_op jit(solution)/shard_map/ppermute | solution.py:301
  38.4 0.6 %shard_map.84 = f32[1,256]{1,0:T(1,128)} custom-call(f32[1,256]{1,0:T(1,128)S(1)} %get-tuple-element.29.run_ref, f32[1,128]{1,0:T(1,128)S(1)} %slice.3.earlier_ref), custom_call_target="tpu_custom_call" | custom-call | flops 1000000 | bytes 1000000 | tf_op jit(solution)/shard_map/pallas_call | solution.py:275
  (5 shorter events, 0.0 us)
Async XLA Ops:
  0.6 1.2 %copy-start = (f32[256]{0:T(256)S(1)}, f32[256]{0:T(256)}, u32[]{:S(2)}) copy-start(f32[256]{0:T(256)} %param.11) | copy-start | bytes 3076
  0.6 1.0 %copy-start.2 = (bf16[3,256,256]{2,1,0:T(8,128)(2,1)S(1)}, bf16[3,256,256]{2,1,0:T(8,128)(2,1)}, u32[]{:S(2)}) copy-start(bf16[3,256,256]{2,1,0:T(8,128)(2,1)} %own_ref.1) | copy-start | bytes 1179652
  1.8 5.8 %copy-start.3 = (bf16[3,256,256]{2,1,0:T(8,128)(2,1)S(1)}, bf16[3,256,256]{2,1,0:T(8,128)(2,1)}, u32[]{:S(2)}) copy-start(bf16[3,256,256]{2,1,0:T(8,128)(2,1)} %own_ref.1) | copy-start | bytes 1179652
  1.8 5.8 %copy-start.4 = (f32[3,3,16,256]{3,2,1,0:T(8,128)S(1)}, f32[3,3,16,256]{3,2,1,0:T(8,128)}, u32[]{:S(2)}) copy-start(f32[3,3,16,256]{3,2,1,0:T(8,128)} %force_ref.1) | copy-start | bytes 442372
  1.9 5.8 %copy-start.5 = (f32[3,16,256]{2,1,0:T(8,128)S(1)}, f32[3,16,256]{2,1,0:T(8,128)}, u32[]{:S(2)}) copy-start(f32[3,16,256]{2,1,0:T(8,128)} %bond_ref.1) | copy-start | bytes 147460
  1.9 5.8 %copy-start.6 = (s32[16,256]{1,0:T(8,128)S(1)}, s32[16,256]{1,0:T(8,128)}, u32[]{:S(2)}) copy-start(s32[16,256]{1,0:T(8,128)} %nbr_ref.1) | copy-start | bytes 49156
  2.0 11.6 %collective-permute-start.2 = (bf16[3,272,128]{2,1,0:T(8,128)(2,1)S(1)}, bf16[3,272,128]{2,1,0:T(8,128)(2,1)S(1)}, u32[]{:S(2)}, u32[]{:S(2)}) collective-permute-start(bf16[3,272,128]{2,1,0:T(8,128)(2,1)S(1)} %get-tuple-element.22), channel_id=1, source_target_pairs={{0,1},{1,0},{2,3},{3,2},{4,5},{5,4},{6,7},{7,6},{8,9},{9,8},{10,11... | collective-permute-start | bytes 626696 | tf_op jit(solution)/shard_map/ppermute | solution.py:328
  5.1 8.5 %collective-permute-start.3 = (bf16[3,272,128]{2,1,0:T(8,128)(2,1)S(1)}, bf16[3,272,128]{2,1,0:T(8,128)(2,1)S(1)}, u32[]{:S(2)}, u32[]{:S(2)}) collective-permute-start(bf16[3,272,128]{2,1,0:T(8,128)(2,1)S(1)} %get-tuple-element.23), channel_id=1, source_target_pairs={{0,4},{1,2},{2,1},{3,7},{4,0},{5,6},{6,5},{7,3},{8,12},{9,10},{10,... | collective-permute-start | bytes 626696 | tf_op jit(solution)/shard_map/ppermute | solution.py:334
  5.1 8.5 %collective-permute-start.1 = (bf16[3,128,256]{2,1,0:T(8,128)(2,1)S(1)}, bf16[3,128,256]{2,1,0:T(8,128)(2,1)S(1)}, u32[]{:S(2)}, u32[]{:S(2)}) collective-permute-start(bf16[3,128,256]{2,1,0:T(8,128)(2,1)S(1)} %get-tuple-element.20), channel_id=1, source_target_pairs={{0,28},{4,8},{8,4},{12,16},{16,12},{20,24},{24,20},{28,0},{1,29},{... | collective-permute-start | bytes 589832 | tf_op jit(solution)/shard_map/ppermute | solution.py:326
  7.7 5.9 %collective-permute-start = (bf16[3,128,256]{2,1,0:T(8,128)(2,1)S(1)}, bf16[3,128,256]{2,1,0:T(8,128)(2,1)S(1)}, u32[]{:S(2)}, u32[]{:S(2)}) collective-permute-start(bf16[3,128,256]{2,1,0:T(8,128)(2,1)S(1)} %get-tuple-element.18), channel_id=1, source_target_pairs={{0,4},{4,0},{8,12},{12,8},{16,20},{20,16},{24,28},{28,24},{1,5},{5... | collective-permute-start | bytes 589832 | tf_op jit(solution)/shard_map/ppermute | solution.py:327
  13.6 14.9 %copy-start.1 = (s32[2,256]{1,0:T(2,128)S(1)}, s32[2,256]{1,0:T(2,128)}, u32[]{:S(2)}) copy-start(s32[2,256]{1,0:T(2,128)} %band_ref.1) | copy-start | bytes 6148
  15.0 1.6 %collective-permute-start.4 = (bf16[3,272,128]{2,1,0:T(8,128)(2,1)S(1)}, bf16[3,272,128]{2,1,0:T(8,128)(2,1)S(1)}, u32[]{:S(2)}, u32[]{:S(2)}) collective-permute-start(bf16[3,272,128]{2,1,0:T(8,128)(2,1)S(1)} %get-tuple-element.25), channel_id=1, source_target_pairs={{0,4},{4,0},{8,12},{12,8},{16,20},{20,16},{24,28},{28,24},{1,5},{5... | collective-permute-start | bytes 626696 | tf_op jit(solution)/shard_map/ppermute | solution.py:301
  16.7 5.9 %collective-permute-start.6 = (bf16[3,272,128]{2,1,0:T(8,128)(2,1)S(1)}, bf16[3,272,128]{2,1,0:T(8,128)(2,1)S(1)}, u32[]{:S(2)}, u32[]{:S(2)}) collective-permute-start(bf16[3,272,128]{2,1,0:T(8,128)(2,1)S(1)} %reduce-precision_convert_fusion.1), channel_id=1, source_target_pairs={{0,8},{4,20},{8,0},{12,28},{16,24},{20,4},{24,16},{28,12},{1,9},{5... | collective-permute-start | bytes 626696 | tf_op jit(solution)/shard_map/ppermute | solution.py:346
  17.3 6.1 %collective-permute-start.5 = (f32[8,128]{1,0:T(8,128)S(1)}, f32[8,128]{1,0:T(8,128)S(1)}, u32[]{:S(2)}, u32[]{:S(2)}) collective-permute-start(f32[8,128]{1,0:T(8,128)S(1)} %shard_map.81), channel_id=1, source_target_pairs={{0,2},{1,3},{2,0},{3,1},{4,6},{5,7},{6,4},{7,5},{8,10},{9,11},{10,... | collective-permute-start | bytes 12296 | tf_op jit(solution)/shard_map/ppermute | solution.py:301
  22.6 5.9 %collective-permute-start.7 = (bf16[3,272,128]{2,1,0:T(8,128)(2,1)S(1)}, bf16[3,272,128]{2,1,0:T(8,128)(2,1)S(1)}, u32[]{:S(2)}, u32[]{:S(2)}) collective-permute-start(bf16[3,272,128]{2,1,0:T(8,128)(2,1)S(1)} %reduce-precision_convert_fusion.pair_one), channel_id=1, source_target_pairs={{0,16},{4,12},{8,24},{12,4},{16,0},{20,28},{24,8},{28,20},{1,17},{... | collective-permute-start | bytes 626696 | tf_op jit(solution)/shard_map/ppermute | solution.py:346
  28.8 1.2 %collective-permute-start.8 = (f32[8,128]{1,0:T(8,128)S(1)}, f32[8,128]{1,0:T(8,128)S(1)}, u32[]{:S(2)}, u32[]{:S(2)}) collective-permute-start(f32[8,128]{1,0:T(8,128)S(1)} %shard_map.82.own_ref), channel_id=1, source_target_pairs={{0,4},{4,0},{8,12},{12,8},{16,20},{20,16},{24,28},{28,24},{1,5},{5... | collective-permute-start | bytes 12296 | tf_op jit(solution)/shard_map/ppermute | solution.py:301
  30.0 5.6 %collective-permute-start.10 = (f32[8,128]{1,0:T(8,128)S(1)}, f32[8,128]{1,0:T(8,128)S(1)}, u32[]{:S(2)}, u32[]{:S(2)}) collective-permute-start(f32[8,128]{1,0:T(8,128)S(1)} %add.17), channel_id=1, source_target_pairs={{0,2},{1,3},{2,0},{3,1},{4,6},{5,7},{6,4},{7,5},{8,10},{9,11},{10,... | collective-permute-start | bytes 12296 | tf_op jit(solution)/shard_map/ppermute | solution.py:301
  32.0 3.6 %collective-permute-start.11 = (f32[8,128]{1,0:T(8,128)S(1)}, f32[8,128]{1,0:T(8,128)S(1)}, u32[]{:S(2)}, u32[]{:S(2)}) collective-permute-start(f32[8,128]{1,0:T(8,128)S(1)} %add.17), channel_id=1, source_target_pairs={{0,1},{1,0},{2,3},{3,2},{4,5},{5,4},{6,7},{7,6},{8,9},{9,8},{10,11... | collective-permute-start | bytes 12296 | tf_op jit(solution)/shard_map/ppermute | solution.py:301
  33.0 5.4 %collective-permute-start.9 = (f32[8,128]{1,0:T(8,128)S(1)}, f32[8,128]{1,0:T(8,128)S(1)}, u32[]{:S(2)}, u32[]{:S(2)}) collective-permute-start(f32[8,128]{1,0:T(8,128)S(1)} %add.17), channel_id=1, source_target_pairs={{0,3},{1,2},{2,1},{3,0},{4,7},{5,6},{6,5},{7,4},{8,11},{9,10},{10,... | collective-permute-start | bytes 12296 | tf_op jit(solution)/shard_map/ppermute | solution.py:301

commit v6 on v5

--- a/solution.py
+++ b/solution.py
@@ -72,7 +72,8 @@
     )(*operands)
 
 
-def coupling_kernel(atoms, force_ref, bond_ref, nbr_ref, eig_ref, image_ref, rim_ref, cpl_ref, own_ref):
+def coupling_kernel(atoms, force_ref, bond_ref, nbr_ref, eig_ref, image_ref, rim_ref, *scratch):
+    cpl_ref, diag_ref, hot_ref, own_ref = scratch
     comps, _, slots, own = force_ref.shape
     wide = slots * GROUP
     span = own + RIM
@@ -91,17 +92,21 @@
             for k in range(comps):
                 cpl_ref[(k * comps + c) * comps + d] = (bonds[k] * column).astype(BF16)
     own_ids = iota((own, wide), 0) - RIM
-    halves = own // RIM
+    halves, groups, tall = own // RIM, RIM // GROUP, comps**3 * GROUP
     for h in range(halves):
         rim_ids = iota((RIM, wide), 0) + (-2 * RIM if h == 0 else own - RIM)
         ids = jnp.concatenate([own_ids, rim_ids], axis=0)
-        for g in range(RIM // GROUP):
+        for g in range(groups):
             base = h * RIM + g * GROUP
             row = jnp.sum(jnp.where(same, placed[base : base + GROUP], 0.0), axis=0, keepdims=True)
-            hot = jnp.where(ids == row.astype(jnp.int32), 1.0, 0.0).astype(BF16)
-            part = cpl_ref[:, base : base + GROUP, :].reshape(comps**3 * GROUP, slots)
+            hot_ref[h * groups + g] = jnp.where(ids == row.astype(jnp.int32), 1.0, 0.0).astype(BF16)
+            part = cpl_ref[:, base : base + GROUP, :].reshape(tall, slots)
             diag = jnp.dot(part, spread, preferred_element_type=F32).reshape(comps**3, GROUP, wide)
-            diag = jnp.where(same[None], diag, 0.0).astype(BF16).reshape(comps**3 * GROUP, wide)
+            diag_ref[h * groups + g] = jnp.where(same[None], diag, 0.0).astype(BF16).reshape(tall, wide)
+    eig = eig_ref[...].reshape(comps * own, eig_ref.shape[2])
+    for h in range(halves):
+        for g in range(groups):
+            diag, hot = diag_ref[h * groups + g], hot_ref[h * groups + g]
             block = lax.dot_general(diag, hot, (((1,), (1,)), ((), ())), preferred_element_type=F32)
             block = block.astype(BF16)
             for kc in range(comps * comps):
@@ -111,7 +116,6 @@
                     piece = block[top : top + GROUP]
                     own_ref[h, rows, d * own : (d + 1) * own] = piece[:, :own]
                     rim_ref[h, rows, d * RIM : (d + 1) * RIM] = piece[:, own:span]
-        eig = eig_ref[...].reshape(comps * own, eig_ref.shape[2])
         image_ref[h] = jnp.dot(own_ref[h], eig, preferred_element_type=F32)
 
 
@@ -128,6 +132,8 @@
         out_specs=(VMEM,) * 2,
         scratch_shapes=[
             pltpu.VMEM((comps**3, own, slots), BF16),
+            pltpu.VMEM((own // GROUP, comps**3 * GROUP, slots * GROUP), BF16),
+            pltpu.VMEM((own // GROUP, own + RIM, slots * GROUP), BF16),
             pltpu.VMEM((halves, rows, comps * own), BF16),
         ],
         compiler_params=pltpu.CompilerParams(vmem_limit_bytes=LARGE),
@@ -213,8 +219,8 @@
     out_ref[...] = jnp.where(iota(out_ref.shape, 0) < 4, least, most)
 
 
-def weigh_kernel(count, own, freq_ref, ends_ref, band_ref, halo_one, halo_two, pair_one, pair_two, out_ref):
-    comps = pair_one.shape[0]
+def weigh_kernel(count, own, freq_ref, ends_ref, band_ref, halo_one, halo_two, main_one, main_two, side_one, side_two, out_ref):
+    comps = main_one.shape[0]
     modes = freq_ref.shape[1]
     second = lax.rem(lax.axis_index("atom"), 2) == 1
     high = lax.rem(lax.axis_index("mode"), 2) == 1
@@ -256,10 +262,11 @@
     side_strength = jnp.zeros((HALF, HALF), F32)
     edge_strength = jnp.zeros((1, HALF), F32)
     for k in range(comps):
-        pair = pair_one[k].astype(F32) + pair_two[k].astype(F32)
-        main, side, edge = pair[:HALF], pair[HALF : 2 * HALF], pair[2 * HALF : 2 * HALF + 1]
+        main = main_one[k].astype(F32) + main_two[k].astype(F32)
+        side = side_one[k].astype(F32) + side_two[k].astype(F32)
         main_strength += main * main
-        side_strength += side * side
+        side_strength += side[:HALF] * side[:HALF]
+        edge = side[HALF : HALF + 1]
         edge_strength += edge * edge
     total = jnp.sum(main_weight * main_strength + side_weight * side_strength, axis=0, keepdims=True)
     total += edge_weight * edge_strength
@@ -341,17 +348,18 @@
     total = rounded_sum(keep, swap(send, "atom", 1))
     total, own_freq = lax.optimization_barrier((total, freq_row))
     ends = local_call(functools.partial(ends_kernel, own), tile, own_freq, halo_one)
+    main, side = total[:, :HALF], total[:, HALF:]
     steps = bits_of("atom")[1:]
     for step, (one, two) in enumerate(zip(steps, reversed(steps))):
-        total_other = lax.ppermute(total, "atom", [(i, i ^ (two if i % 2 else one)) for i in range(domains)])
+        main_other, side_other = swap(main, "atom", one), swap(side, "atom", two)
         if step < len(steps) - 1:
-            total = rounded_sum(total, total_other)
+            main, side = rounded_sum(main, main_other), rounded_sum(side, side_other)
     for bit in bits_of("mode")[1:]:
         other = swap(ends, "mode", bit)
         ends = jnp.where(iota((8, HALF), 0) < 4, jnp.minimum(ends, other), jnp.maximum(ends, other))
     summary = local_call(
         functools.partial(weigh_kernel, count, own),
-        tile, freq_row, ends, band, halo_one, halo_two, total, total_other,
+        tile, freq_row, ends, band, halo_one, halo_two, main, main_other, side, side_other,
     )
 
     other = swap(summary, "atom", 1)

time: 39.2 us -> 37.2 us (0.949)
  waiting for transfers between devices: 12.8 us -> 9.25 us
  starting transfers between devices: 15 us -> 17.9 us
  Pallas kernels: 9.2 us -> 7.84 us
    ppermute x2 -> x0, waiting for transfers between devices: 7.69 us -> none  [body(): lax.ppermute(total, 'atom', [(i, i ^ (two if i % 2 else one)) for i in ra...]
    ppermute x6 -> x10, starting transfers between devices: 7.96 us -> 12.2 us  [swap(): lax.ppermute(x, axis, [(i, i ^ bit) for i in range(lax.axis_size(axis))])]
    ppermute x6 -> x10, waiting for transfers between devices: 5.12 us -> 8.96 us  [swap(): lax.ppermute(x, axis, [(i, i ^ bit) for i in range(lax.axis_size(axis))])]
    ppermute x2 -> x0, starting transfers between devices: 1.38 us -> none  [body(): lax.ppermute(total, 'atom', [(i, i ^ (two if i % 2 else one)) for i in ra...]
    pallas_call x1, Pallas kernels: 5.86 us -> 4.52 us  [own_image(): pl.pallas_call(functools.partial(coupling_kernel, atoms), out_shape=(jax....]
  transfers between devices with their start and end apart: 12 -> 14, of which waited for: 5 -> 8; matrix products, arithmetic and copies ran while one was open for 0% -> 0% of each run, Pallas kernels for 17% -> 14%
where the time goes in v6:
time: 37.2 us; the launch traced here: 37 us
  starting transfers between devices  17.9 us (48%)
  waiting for transfers between devices  9.25 us (25%)
  Pallas kernels  7.84 us (21%)
  local copies, waits for them, and re-layouts  1.05 us (3%)
  between operations  0.79 us (2%)
    ppermute x10, starting transfers between devices, swap(): lax.ppermute(x, axis, [(i, i ^ bit) for i in range(lax.axis_size(axis))])  12.2 us
    ppermute x10, waiting for transfers between devices, swap(): lax.ppermute(x, axis, [(i, i ^ bit) for i in range(lax.axis_size(axis))])  8.96 us
    pallas_call x1, Pallas kernels, own_image(): pl.pallas_call(functools.partial(coupling_kernel, atoms), out_shape=(jax....  4.52 us
    ppermute x1, starting transfers between devices, body(): halo_one = lax.ppermute(near_edge, 'mode', near)  3.09 us
    ppermute x1, starting transfers between devices, body(): rim_two = lax.ppermute(outer_edge, 'atom', outer)  2.56 us
    pallas_call x4, Pallas kernels, local_call(): pl.pallas_call(kernel, out_shape=out_shape, in_specs=[VMEM] * len(operand...  1.66 us
    pallas_call x1, Pallas kernels, pair_parts(): pl.pallas_call(pair_kernel, out_shape=(jax.ShapeDtypeStruct(shape, F32),...  1.38 us
    unnamed x14, local copies, waits for them, and re-layouts  1.03 us
  transfers between devices with their start and end apart: 14, of which 8 were waited for; matrix products, arithmetic and copies ran while one was open for 0% of the time, Pallas kernels for 14%

profile of v6, /device:TPU:0, one launch (start us, length us, event | category | flops | bytes accessed | tf_op | source)
XLA Modules:
  0.0 37.0 jit_solution(6942574145552136885)
XLA Ops:
  0.6 0.0 copy-start
  0.6 0.0 copy-start.2
  0.7 1.0 %copy-done.2 = bf16[3,256,256]{2,1,0:T(8,128)(2,1)S(1)} copy-done((bf16[3,256,256]{2,1,0:T(8,128)(2,1)S(1)}, bf16[3,256,256]{2,1,0:T(8,128)(2,1)}, u32[]{:S(2)}) %copy-start.2) | copy-done | bytes 393240
  1.6 0.2 shard_map.78
  1.8 0.0 copy-done
  1.8 0.0 copy-start.3
  1.8 0.0 copy-start.4
  1.9 0.0 copy-start.5
  1.9 0.0 copy-start.6
  1.9 0.1 shard_map.79
  2.0 3.1 %collective-permute-start.2 = (bf16[3,272,128]{2,1,0:T(8,128)(2,1)S(1)}, bf16[3,272,128]{2,1,0:T(8,128)(2,1)S(1)}, u32[]{:S(2)}, u32[]{:S(2)}) collective-permute-start(bf16[3,272,128]{2,1,0:T(8,128)(2,1)S(1)} %get-tuple-element.22), channel_id=1, source_target_pairs={{0,1},{1,0},{2,3},{3,2},{4,5},{5,4},{6,7},{7,6},{8,9},{9,8},{10,11... | collective-permute-start | bytes 626696 | tf_op jit(solution)/shard_map/ppermute | solution.py:335
  5.1 0.0 collective-permute-start.3
  5.1 2.6 %collective-permute-start.1 = (bf16[3,128,256]{2,1,0:T(8,128)(2,1)S(1)}, bf16[3,128,256]{2,1,0:T(8,128)(2,1)S(1)}, u32[]{:S(2)}, u32[]{:S(2)}) collective-permute-start(bf16[3,128,256]{2,1,0:T(8,128)(2,1)S(1)} %get-tuple-element.20), channel_id=1, source_target_pairs={{0,28},{4,8},{8,4},{12,16},{16,12},{20,24},{24,20},{28,0},{1,29},{... | collective-permute-start | bytes 589832 | tf_op jit(solution)/shard_map/ppermute | solution.py:333
  7.7 0.0 collective-permute-start
  7.7 0.0 copy-done.3
  7.7 4.5 %shard_map.77 = (f32[2,1152,256]{2,1,0:T(8,128)S(1)}, bf16[2,1152,384]{2,1,0:T(8,128)(2,1)S(1)}) custom-call(f32[3,3,16,256]{3,2,1,0:T(8,128)S(1)} %copy-done.4, f32[3,16,256]{2,1,0:T(8,128)S(1)} %copy-done.5, s32[16,256]{1,0:T(8,128)S(1)} %copy-done.6, bf16[3,256,256]{2,1,0:T(8,128)(2,1)S(1)} %copy-done.3), custom_call_target="tpu_custom_call" | custom-call | flops 4000000000 | bytes 6000000 | tf_op jit(solution)/shard_map/pallas_call | solution.py:125
  12.2 0.3 collective-permute-done.1.rim_two
  12.5 0.0 collective-permute-done.rim_one
  12.5 0.0 collective-permute-done.2.halo_one.halo_ref
  12.5 0.0 collective-permute-done.3.halo_two
  12.5 0.0 copy-start.1
  12.5 1.4 %shard_map.80 = (f32[3,272,128]{2,1,0:T(8,128)S(1)}, bf16[3,272,128]{2,1,0:T(8,128)(2,1)S(1)}) custom-call(f32[2,1152,256]{2,1,0:T(8,128)S(1)} %get-tuple-element.16.image_ref, bf16[2,1152,384]{2,1,0:T(8,128)(2,1)S(1)} %get-tuple-element.17.cpl_ref, bf16[3,256,256]{2,1,0:T(8,128)(2,1)S(1)} %copy-done.3, ...), custom_call_target="tpu_custom_call" | custom-call | flops 2000000000 | bytes 6000000 | tf_op jit(solution)/shard_map/pallas_call | solution.py:194
  13.9 0.3 collective-permute-start.4
  14.2 1.2 %collective-permute-done.4 = bf16[3,272,128]{2,1,0:T(8,128)(2,1)S(1)} collective-permute-done((bf16[3,272,128]{2,1,0:T(8,128)(2,1)S(1)}, bf16[3,272,128]{2,1,0:T(8,128)(2,1)S(1)}, u32[]{:S(2)}, u32[]{:S(2)}) %collective-permute-start.4) | collective-permute-done | bytes 208928 | tf_op jit(solution)/shard_map/ppermute | solution.py:308
  15.4 0.1 reduce-precision_convert_fusion
  15.5 1.8 %collective-permute-start.6 = (bf16[3,128,128]{2,1,0:T(8,128)(2,1)S(1)}, bf16[3,128,128]{2,1,0:T(8,128)(2,1)S(1)}, u32[]{:S(2)}, u32[]{:S(2)}) collective-permute-start(bf16[3,128,128]{2,1,0:T(8,128)(2,1)S(1)} %slice.9), channel_id=1, source_target_pairs={{0,8},{4,12},{8,0},{12,4},{16,24},{20,28},{24,16},{28,20},{1,9},{5... | collective-permute-start | bytes 294920 | tf_op jit(solution)/shard_map/ppermute | solution.py:308
  17.3 0.6 %collective-permute-start.8 = (bf16[3,144,128]{2,1,0:T(8,128)(2,1)S(1)}, bf16[3,144,128]{2,1,0:T(8,128)(2,1)S(1)}, u32[]{:S(2)}, u32[]{:S(2)}) collective-permute-start(bf16[3,144,128]{2,1,0:T(8,128)(2,1)S(1)} %slice.10), channel_id=1, source_target_pairs={{0,16},{4,20},{8,24},{12,28},{16,0},{20,4},{24,8},{28,12},{1,17},{... | collective-permute-start | bytes 331784 | tf_op jit(solution)/shard_map/ppermute | solution.py:308
  17.9 0.1 shard_map.81
  18.0 2.8 %collective-permute-start.5 = (f32[8,128]{1,0:T(8,128)S(1)}, f32[8,128]{1,0:T(8,128)S(1)}, u32[]{:S(2)}, u32[]{:S(2)}) collective-permute-start(f32[8,128]{1,0:T(8,128)S(1)} %shard_map.81), channel_id=1, source_target_pairs={{0,2},{1,3},{2,0},{3,1},{4,6},{5,7},{6,4},{7,5},{8,10},{9,11},{10,... | collective-permute-start | bytes 12296 | tf_op jit(solution)/shard_map/ppermute | solution.py:308
  20.8 0.0 collective-permute-done.6
  20.9 1.6 %collective-permute-start.7 = (bf16[3,128,128]{2,1,0:T(8,128)(2,1)S(1)}, bf16[3,128,128]{2,1,0:T(8,128)(2,1)S(1)}, u32[]{:S(2)}, u32[]{:S(2)}) collective-permute-start(bf16[3,128,128]{2,1,0:T(8,128)(2,1)S(1)} %reduce-precision_convert_fusion.2.main_one), channel_id=1, source_target_pairs={{0,16},{4,20},{8,24},{12,28},{16,0},{20,4},{24,8},{28,12},{1,17},{... | collective-permute-start | bytes 294920 | tf_op jit(solution)/shard_map/ppermute | solution.py:308
  22.5 0.0 collective-permute-done.8
  22.5 0.7 %collective-permute-start.9 = (bf16[3,144,128]{2,1,0:T(8,128)(2,1)S(1)}, bf16[3,144,128]{2,1,0:T(8,128)(2,1)S(1)}, u32[]{:S(2)}, u32[]{:S(2)}) collective-permute-start(bf16[3,144,128]{2,1,0:T(8,128)(2,1)S(1)} %reduce-precision_convert_fusion.1.side_one), channel_id=1, source_target_pairs={{0,8},{4,12},{8,0},{12,4},{16,24},{20,28},{24,16},{28,20},{1,9},{5... | collective-permute-start | bytes 331784 | tf_op jit(solution)/shard_map/ppermute | solution.py:308
  23.2 0.0 collective-permute-done.5
  23.2 0.1 maximum_select_fusion.ends_ref
  23.3 2.3 %collective-permute-done.7.main_two = bf16[3,128,128]{2,1,0:T(8,128)(2,1)S(1)} collective-permute-done((bf16[3,128,128]{2,1,0:T(8,128)(2,1)S(1)}, bf16[3,128,128]{2,1,0:T(8,128)(2,1)S(1)}, u32[]{:S(2)}, u32[]{:S(2)}) %collective-permute-start.7) | collective-permute-done | bytes 98336 | tf_op jit(solution)/shard_map/ppermute | solution.py:308
  25.5 1.8 %collective-permute-done.9.side_two = bf16[3,144,128]{2,1,0:T(8,128)(2,1)S(1)} collective-permute-done((bf16[3,144,128]{2,1,0:T(8,128)(2,1)S(1)}, bf16[3,144,128]{2,1,0:T(8,128)(2,1)S(1)}, u32[]{:S(2)}, u32[]{:S(2)}) %collective-permute-start.9) | collective-permute-done | bytes 110624 | tf_op jit(solution)/shard_map/ppermute | solution.py:308
  27.3 0.3 shard_map.82.own_ref
  27.6 0.0 collective-permute-start.10
  27.6 1.2 %collective-permute-done.10.other_ref = f32[8,128]{1,0:T(8,128)S(1)} collective-permute-done((f32[8,128]{1,0:T(8,128)S(1)}, f32[8,128]{1,0:T(8,128)S(1)}, u32[]{:S(2)}, u32[]{:S(2)}) %collective-permute-start.10) | collective-permute-done | bytes 4128 | tf_op jit(solution)/shard_map/ppermute | solution.py:308
  28.8 2.5 %collective-permute-start.11 = (f32[8,128]{1,0:T(8,128)S(1)}, f32[8,128]{1,0:T(8,128)S(1)}, u32[]{:S(2)}, u32[]{:S(2)}) collective-permute-start(f32[8,128]{1,0:T(8,128)S(1)} %add.21), channel_id=1, source_target_pairs={{0,3},{1,2},{2,1},{3,0},{4,7},{5,6},{6,5},{7,4},{8,11},{9,10},{10,... | collective-permute-start | bytes 12296 | tf_op jit(solution)/shard_map/ppermute | solution.py:308
  31.2 1.5 %collective-permute-start.12 = (f32[8,128]{1,0:T(8,128)S(1)}, f32[8,128]{1,0:T(8,128)S(1)}, u32[]{:S(2)}, u32[]{:S(2)}) collective-permute-start(f32[8,128]{1,0:T(8,128)S(1)} %add.21), channel_id=1, source_target_pairs={{0,2},{1,3},{2,0},{3,1},{4,6},{5,7},{6,4},{7,5},{8,10},{9,11},{10,... | collective-permute-start | bytes 12296 | tf_op jit(solution)/shard_map/ppermute | solution.py:308
  32.7 0.4 %collective-permute-start.13 = (f32[8,128]{1,0:T(8,128)S(1)}, f32[8,128]{1,0:T(8,128)S(1)}, u32[]{:S(2)}, u32[]{:S(2)}) collective-permute-start(f32[8,128]{1,0:T(8,128)S(1)} %add.21), channel_id=1, source_target_pairs={{0,1},{1,0},{2,3},{3,2},{4,5},{5,4},{6,7},{7,6},{8,9},{9,8},{10,11... | collective-permute-start | bytes 12296 | tf_op jit(solution)/shard_map/ppermute | solution.py:308
  33.2 0.7 %shard_map.83 = (f32[1,256]{1,0:T(1,128)}, f32[1,256]{1,0:T(1,128)S(1)}) custom-call(f32[8,128]{1,0:T(8,128)S(1)} %shard_map.82.own_ref, f32[8,128]{1,0:T(8,128)S(1)} %collective-permute-done.10.other_ref), custom_call_target="tpu_custom_call" | custom-call | flops 1000000 | bytes 1000000 | tf_op jit(solution)/shard_map/pallas_call | solution.py:282
  33.8 0.4 collective-permute-done.11
  34.2 1.6 %collective-permute-done.12 = f32[8,128]{1,0:T(8,128)S(1)} collective-permute-done((f32[8,128]{1,0:T(8,128)S(1)}, f32[8,128]{1,0:T(8,128)S(1)}, u32[]{:S(2)}, u32[]{:S(2)}) %collective-permute-start.12) | collective-permute-done | bytes 4128 | tf_op jit(solution)/shard_map/ppermute | solution.py:308
  35.7 0.6 %collective-permute-done.13 = f32[8,128]{1,0:T(8,128)S(1)} collective-permute-done((f32[8,128]{1,0:T(8,128)S(1)}, f32[8,128]{1,0:T(8,128)S(1)}, u32[]{:S(2)}, u32[]{:S(2)}) %collective-permute-start.13) | collective-permute-done | bytes 4128 | tf_op jit(solution)/shard_map/ppermute | solution.py:308
  36.4 0.6 %shard_map.84 = f32[1,256]{1,0:T(1,128)} custom-call(f32[1,256]{1,0:T(1,128)S(1)} %get-tuple-element.29.run_ref, f32[1,128]{1,0:T(1,128)S(1)} %slice.11.earlier_ref), custom_call_target="tpu_custom_call" | custom-call | flops 1000000 | bytes 1000000 | tf_op jit(solution)/shard_map/pallas_call | solution.py:282
  (12 shorter events, 0.1 us)
Async XLA Ops:
  0.6 1.2 %copy-start = (f32[256]{0:T(256)S(1)}, f32[256]{0:T(256)}, u32[]{:S(2)}) copy-start(f32[256]{0:T(256)} %param.11) | copy-start | bytes 3076
  0.6 1.0 %copy-start.2 = (bf16[3,256,256]{2,1,0:T(8,128)(2,1)S(1)}, bf16[3,256,256]{2,1,0:T(8,128)(2,1)}, u32[]{:S(2)}) copy-start(bf16[3,256,256]{2,1,0:T(8,128)(2,1)} %own_ref.1) | copy-start | bytes 1179652
  1.8 5.8 %copy-start.3 = (bf16[3,256,256]{2,1,0:T(8,128)(2,1)S(1)}, bf16[3,256,256]{2,1,0:T(8,128)(2,1)}, u32[]{:S(2)}) copy-start(bf16[3,256,256]{2,1,0:T(8,128)(2,1)} %own_ref.1) | copy-start | bytes 1179652
  1.8 5.8 %copy-start.4 = (f32[3,3,16,256]{3,2,1,0:T(8,128)S(1)}, f32[3,3,16,256]{3,2,1,0:T(8,128)}, u32[]{:S(2)}) copy-start(f32[3,3,16,256]{3,2,1,0:T(8,128)} %force_ref.1) | copy-start | bytes 442372
  1.9 5.8 %copy-start.5 = (f32[3,16,256]{2,1,0:T(8,128)S(1)}, f32[3,16,256]{2,1,0:T(8,128)}, u32[]{:S(2)}) copy-start(f32[3,16,256]{2,1,0:T(8,128)} %bond_ref.1) | copy-start | bytes 147460
  1.9 5.8 %copy-start.6 = (s32[16,256]{1,0:T(8,128)S(1)}, s32[16,256]{1,0:T(8,128)}, u32[]{:S(2)}) copy-start(s32[16,256]{1,0:T(8,128)} %nbr_ref.1) | copy-start | bytes 49156
  2.0 10.5 %collective-permute-start.2 = (bf16[3,272,128]{2,1,0:T(8,128)(2,1)S(1)}, bf16[3,272,128]{2,1,0:T(8,128)(2,1)S(1)}, u32[]{:S(2)}, u32[]{:S(2)}) collective-permute-start(bf16[3,272,128]{2,1,0:T(8,128)(2,1)S(1)} %get-tuple-element.22), channel_id=1, source_target_pairs={{0,1},{1,0},{2,3},{3,2},{4,5},{5,4},{6,7},{7,6},{8,9},{9,8},{10,11... | collective-permute-start | bytes 626696 | tf_op jit(solution)/shard_map/ppermute | solution.py:335
  5.1 7.4 %collective-permute-start.3 = (bf16[3,272,128]{2,1,0:T(8,128)(2,1)S(1)}, bf16[3,272,128]{2,1,0:T(8,128)(2,1)S(1)}, u32[]{:S(2)}, u32[]{:S(2)}) collective-permute-start(bf16[3,272,128]{2,1,0:T(8,128)(2,1)S(1)} %get-tuple-element.23), channel_id=1, source_target_pairs={{0,4},{1,2},{2,1},{3,7},{4,0},{5,6},{6,5},{7,3},{8,12},{9,10},{10,... | collective-permute-start | bytes 626696 | tf_op jit(solution)/shard_map/ppermute | solution.py:341
  5.1 7.4 %collective-permute-start.1 = (bf16[3,128,256]{2,1,0:T(8,128)(2,1)S(1)}, bf16[3,128,256]{2,1,0:T(8,128)(2,1)S(1)}, u32[]{:S(2)}, u32[]{:S(2)}) collective-permute-start(bf16[3,128,256]{2,1,0:T(8,128)(2,1)S(1)} %get-tuple-element.20), channel_id=1, source_target_pairs={{0,28},{4,8},{8,4},{12,16},{16,12},{20,24},{24,20},{28,0},{1,29},{... | collective-permute-start | bytes 589832 | tf_op jit(solution)/shard_map/ppermute | solution.py:333
  7.7 4.8 %collective-permute-start = (bf16[3,128,256]{2,1,0:T(8,128)(2,1)S(1)}, bf16[3,128,256]{2,1,0:T(8,128)(2,1)S(1)}, u32[]{:S(2)}, u32[]{:S(2)}) collective-permute-start(bf16[3,128,256]{2,1,0:T(8,128)(2,1)S(1)} %get-tuple-element.18), channel_id=1, source_target_pairs={{0,4},{4,0},{8,12},{12,8},{16,20},{20,16},{24,28},{28,24},{1,5},{5... | collective-permute-start | bytes 589832 | tf_op jit(solution)/shard_map/ppermute | solution.py:334
  12.5 14.8 %copy-start.1 = (s32[2,256]{1,0:T(2,128)S(1)}, s32[2,256]{1,0:T(2,128)}, u32[]{:S(2)}) copy-start(s32[2,256]{1,0:T(2,128)} %band_ref.1) | copy-start | bytes 6148
  13.9 1.5 %collective-permute-start.4 = (bf16[3,272,128]{2,1,0:T(8,128)(2,1)S(1)}, bf16[3,272,128]{2,1,0:T(8,128)(2,1)S(1)}, u32[]{:S(2)}, u32[]{:S(2)}) collective-permute-start(bf16[3,272,128]{2,1,0:T(8,128)(2,1)S(1)} %get-tuple-element.25), channel_id=1, source_target_pairs={{0,4},{4,0},{8,12},{12,8},{16,20},{20,16},{24,28},{28,24},{1,5},{5... | collective-permute-start | bytes 626696 | tf_op jit(solution)/shard_map/ppermute | solution.py:308
  15.5 5.3 %collective-permute-start.6 = (bf16[3,128,128]{2,1,0:T(8,128)(2,1)S(1)}, bf16[3,128,128]{2,1,0:T(8,128)(2,1)S(1)}, u32[]{:S(2)}, u32[]{:S(2)}) collective-permute-start(bf16[3,128,128]{2,1,0:T(8,128)(2,1)S(1)} %slice.9), channel_id=1, source_target_pairs={{0,8},{4,12},{8,0},{12,4},{16,24},{20,28},{24,16},{28,20},{1,9},{5... | collective-permute-start | bytes 294920 | tf_op jit(solution)/shard_map/ppermute | solution.py:308
  17.3 5.2 %collective-permute-start.8 = (bf16[3,144,128]{2,1,0:T(8,128)(2,1)S(1)}, bf16[3,144,128]{2,1,0:T(8,128)(2,1)S(1)}, u32[]{:S(2)}, u32[]{:S(2)}) collective-permute-start(bf16[3,144,128]{2,1,0:T(8,128)(2,1)S(1)} %slice.10), channel_id=1, source_target_pairs={{0,16},{4,20},{8,24},{12,28},{16,0},{20,4},{24,8},{28,12},{1,17},{... | collective-permute-start | bytes 331784 | tf_op jit(solution)/shard_map/ppermute | solution.py:308
  18.0 5.2 %collective-permute-start.5 = (f32[8,128]{1,0:T(8,128)S(1)}, f32[8,128]{1,0:T(8,128)S(1)}, u32[]{:S(2)}, u32[]{:S(2)}) collective-permute-start(f32[8,128]{1,0:T(8,128)S(1)} %shard_map.81), channel_id=1, source_target_pairs={{0,2},{1,3},{2,0},{3,1},{4,6},{5,7},{6,4},{7,5},{8,10},{9,11},{10,... | collective-permute-start | bytes 12296 | tf_op jit(solution)/shard_map/ppermute | solution.py:308
  20.9 4.7 %collective-permute-start.7 = (bf16[3,128,128]{2,1,0:T(8,128)(2,1)S(1)}, bf16[3,128,128]{2,1,0:T(8,128)(2,1)S(1)}, u32[]{:S(2)}, u32[]{:S(2)}) collective-permute-start(bf16[3,128,128]{2,1,0:T(8,128)(2,1)S(1)} %reduce-precision_convert_fusion.2.main_one), channel_id=1, source_target_pairs={{0,16},{4,20},{8,24},{12,28},{16,0},{20,4},{24,8},{28,12},{1,17},{... | collective-permute-start | bytes 294920 | tf_op jit(solution)/shard_map/ppermute | solution.py:308
  22.5 4.8 %collective-permute-start.9 = (bf16[3,144,128]{2,1,0:T(8,128)(2,1)S(1)}, bf16[3,144,128]{2,1,0:T(8,128)(2,1)S(1)}, u32[]{:S(2)}, u32[]{:S(2)}) collective-permute-start(bf16[3,144,128]{2,1,0:T(8,128)(2,1)S(1)} %reduce-precision_convert_fusion.1.side_one), channel_id=1, source_target_pairs={{0,8},{4,12},{8,0},{12,4},{16,24},{20,28},{24,16},{28,20},{1,9},{5... | collective-permute-start | bytes 331784 | tf_op jit(solution)/shard_map/ppermute | solution.py:308
  27.6 1.2 %collective-permute-start.10 = (f32[8,128]{1,0:T(8,128)S(1)}, f32[8,128]{1,0:T(8,128)S(1)}, u32[]{:S(2)}, u32[]{:S(2)}) collective-permute-start(f32[8,128]{1,0:T(8,128)S(1)} %shard_map.82.own_ref), channel_id=1, source_target_pairs={{0,4},{4,0},{8,12},{12,8},{16,20},{20,16},{24,28},{28,24},{1,5},{5... | collective-permute-start | bytes 12296 | tf_op jit(solution)/shard_map/ppermute | solution.py:308
  28.8 5.4 %collective-permute-start.11 = (f32[8,128]{1,0:T(8,128)S(1)}, f32[8,128]{1,0:T(8,128)S(1)}, u32[]{:S(2)}, u32[]{:S(2)}) collective-permute-start(f32[8,128]{1,0:T(8,128)S(1)} %add.21), channel_id=1, source_target_pairs={{0,3},{1,2},{2,1},{3,0},{4,7},{5,6},{6,5},{7,4},{8,11},{9,10},{10,... | collective-permute-start | bytes 12296 | tf_op jit(solution)/shard_map/ppermute | solution.py:308
  31.2 4.5 %collective-permute-start.12 = (f32[8,128]{1,0:T(8,128)S(1)}, f32[8,128]{1,0:T(8,128)S(1)}, u32[]{:S(2)}, u32[]{:S(2)}) collective-permute-start(f32[8,128]{1,0:T(8,128)S(1)} %add.21), channel_id=1, source_target_pairs={{0,2},{1,3},{2,0},{3,1},{4,6},{5,7},{6,4},{7,5},{8,10},{9,11},{10,... | collective-permute-start | bytes 12296 | tf_op jit(solution)/shard_map/ppermute | solution.py:308
  32.7 3.6 %collective-permute-start.13 = (f32[8,128]{1,0:T(8,128)S(1)}, f32[8,128]{1,0:T(8,128)S(1)}, u32[]{:S(2)}, u32[]{:S(2)}) collective-permute-start(f32[8,128]{1,0:T(8,128)S(1)} %add.21), channel_id=1, source_target_pairs={{0,1},{1,0},{2,3},{3,2},{4,5},{5,4},{6,7},{7,6},{8,9},{9,8},{10,11... | collective-permute-start | bytes 12296 | tf_op jit(solution)/shard_map/ppermute | solution.py:308

commit v7 on v6

--- a/solution.py
+++ b/solution.py
@@ -330,6 +330,7 @@
     inner_edge, outer_edge = edge_call(rim_kernel, (comps, RIM, modes), COST, eigvec)
     outer_edge, later = lax.optimization_barrier((outer_edge, freq_row))
     near_edge, far_edge = edge_call(halo_kernel, (comps, own + EXTRA, HALF), COST, eigvec, later)
+    far_edge, held = lax.optimization_barrier((far_edge, eigvec))
     rim_two = lax.ppermute(outer_edge, "atom", outer)
     rim_one = lax.ppermute(inner_edge, "atom", inner)
     halo_one = lax.ppermute(near_edge, "mode", near)
@@ -340,7 +341,7 @@
             hops.append((a * blocks + i, a * blocks + (i + 1 if i % 2 else i - 1) if inside else (a ^ 1) * blocks + i))
     halo_two = lax.ppermute(far_edge, ("atom", "mode"), hops)
 
-    image, matrix = own_image(force, bond, nbr, eigvec, atoms)
+    image, matrix = own_image(force, bond, nbr, held, atoms)
     keep, send = pair_parts(image, matrix, eigvec, rim_one, rim_two, halo_one, halo_two)
 
     tile = jax.ShapeDtypeStruct((8, HALF), F32)

time: 37.2 us -> 36.5 us (0.981)
  starting transfers between devices: 17.9 us -> 16 us
  waiting for transfers between devices: 9.25 us -> 10.5 us
    ppermute x10, starting transfers between devices: 12.2 us -> 9.72 us  [swap(): lax.ppermute(x, axis, [(i, i ^ bit) for i in range(lax.axis_size(axis))])]
    ppermute x1, waiting for transfers between devices: 0.28 us -> 1.86 us  [body(): rim_two = lax.ppermute(outer_edge, 'atom', outer)]
    ppermute x1, starting transfers between devices: 2.56 us -> 1.33 us  [body(): rim_two = lax.ppermute(outer_edge, 'atom', outer)]
    ppermute x1, starting transfers between devices: 3.09 us -> 4.15 us  [body(): halo_one = lax.ppermute(near_edge, 'mode', near)]
    ppermute x1, starting transfers between devices: 0.01 us -> 0.52 us  [body(): halo_two = lax.ppermute(far_edge, ('atom', 'mode'), hops)]
    ppermute x10, waiting for transfers between devices: 8.96 us -> 8.59 us  [swap(): lax.ppermute(x, axis, [(i, i ^ bit) for i in range(lax.axis_size(axis))])]
  transfers between devices with their start and end apart: 14 -> 14, of which waited for: 8 -> 9; matrix products, arithmetic and copies ran while one was open for 0% -> 0% of each run, Pallas kernels for 14% -> 14%
where the time goes in v7:
time: 36.5 us; the launch traced here: 36.3 us
  starting transfers between devices  16 us (44%)
  waiting for transfers between devices  10.5 us (29%)
  Pallas kernels  7.85 us (22%)
  local copies, waits for them, and re-layouts  1.05 us (3%)
  between operations  0.78 us (2%)
    ppermute x10, starting transfers between devices, swap(): lax.ppermute(x, axis, [(i, i ^ bit) for i in range(lax.axis_size(axis))])  9.72 us
    ppermute x10, waiting for transfers between devices, swap(): lax.ppermute(x, axis, [(i, i ^ bit) for i in range(lax.axis_size(axis))])  8.59 us
    pallas_call x1, Pallas kernels, own_image(): pl.pallas_call(functools.partial(coupling_kernel, atoms), out_shape=(jax....  4.51 us
    ppermute x1, starting transfers between devices, body(): halo_one = lax.ppermute(near_edge, 'mode', near)  4.15 us
    ppermute x1, waiting for transfers between devices, body(): rim_two = lax.ppermute(outer_edge, 'atom', outer)  1.86 us
    pallas_call x4, Pallas kernels, local_call(): pl.pallas_call(kernel, out_shape=out_shape, in_specs=[VMEM] * len(operand...  1.66 us
    pallas_call x1, Pallas kernels, pair_parts(): pl.pallas_call(pair_kernel, out_shape=(jax.ShapeDtypeStruct(shape, F32),...  1.39 us
    ppermute x1, starting transfers between devices, body(): rim_two = lax.ppermute(outer_edge, 'atom', outer)  1.33 us
  transfers between devices with their start and end apart: 14, of which 9 were waited for; matrix products, arithmetic and copies ran while one was open for 0% of the time, Pallas kernels for 14%

profile of v7, /device:TPU:0, one launch (start us, length us, event | category | flops | bytes accessed | tf_op | source)
XLA Modules:
  0.0 36.3 jit_solution(6291014442164106718)
XLA Ops:
  0.6 0.0 copy-start
  0.6 0.0 copy-start.2
  0.7 1.0 %copy-done.2 = bf16[3,256,256]{2,1,0:T(8,128)(2,1)S(1)} copy-done((bf16[3,256,256]{2,1,0:T(8,128)(2,1)S(1)}, bf16[3,256,256]{2,1,0:T(8,128)(2,1)}, u32[]{:S(2)}) %copy-start.2) | copy-done | bytes 393240
  1.6 0.2 shard_map.77
  1.8 0.0 copy-start.3
  1.8 0.0 copy-start.4
  1.9 0.0 copy-start.5
  1.9 0.0 copy-start.6
  1.9 0.1 shard_map.78
  2.0 0.5 %collective-permute-start.3 = (bf16[3,272,128]{2,1,0:T(8,128)(2,1)S(1)}, bf16[3,272,128]{2,1,0:T(8,128)(2,1)S(1)}, u32[]{:S(2)}, u32[]{:S(2)}) collective-permute-start(bf16[3,272,128]{2,1,0:T(8,128)(2,1)S(1)} %get-tuple-element.27), channel_id=1, source_target_pairs={{0,4},{1,2},{2,1},{3,7},{4,0},{5,6},{6,5},{7,3},{8,12},{9,10},{10,... | collective-permute-start | bytes 626696 | tf_op jit(solution)/shard_map/ppermute | solution.py:342
  2.5 4.1 %collective-permute-start.2 = (bf16[3,272,128]{2,1,0:T(8,128)(2,1)S(1)}, bf16[3,272,128]{2,1,0:T(8,128)(2,1)S(1)}, u32[]{:S(2)}, u32[]{:S(2)}) collective-permute-start(bf16[3,272,128]{2,1,0:T(8,128)(2,1)S(1)} %get-tuple-element.26), channel_id=1, source_target_pairs={{0,1},{1,0},{2,3},{3,2},{4,5},{5,4},{6,7},{7,6},{8,9},{9,8},{10,11... | collective-permute-start | bytes 626696 | tf_op jit(solution)/shard_map/ppermute | solution.py:336
  6.7 1.3 %collective-permute-start.1 = (bf16[3,128,256]{2,1,0:T(8,128)(2,1)S(1)}, bf16[3,128,256]{2,1,0:T(8,128)(2,1)S(1)}, u32[]{:S(2)}, u32[]{:S(2)}) collective-permute-start(bf16[3,128,256]{2,1,0:T(8,128)(2,1)S(1)} %get-tuple-element.25), channel_id=1, source_target_pairs={{0,28},{4,8},{8,4},{12,16},{16,12},{20,24},{24,20},{28,0},{1,29},{... | collective-permute-start | bytes 589832 | tf_op jit(solution)/shard_map/ppermute | solution.py:334
  8.0 0.3 collective-permute-start
  8.3 0.0 copy-done.6
  8.3 4.5 %shard_map.79 = (f32[2,1152,256]{2,1,0:T(8,128)S(1)}, bf16[2,1152,384]{2,1,0:T(8,128)(2,1)S(1)}) custom-call(f32[3,3,16,256]{3,2,1,0:T(8,128)S(1)} %copy-done.4, f32[3,16,256]{2,1,0:T(8,128)S(1)} %copy-done.5, s32[16,256]{1,0:T(8,128)S(1)} %copy-done.6, bf16[3,256,256]{2,1,0:T(8,128)(2,1)S(1)} %copy-done.3), custom_call_target="tpu_custom_call" | custom-call | flops 4000000000 | bytes 6000000 | tf_op jit(solution)/shard_map/pallas_call | solution.py:125
  12.8 1.9 %collective-permute-done.1.rim_two = bf16[3,128,256]{2,1,0:T(8,128)(2,1)S(1)} collective-permute-done((bf16[3,128,256]{2,1,0:T(8,128)(2,1)S(1)}, bf16[3,128,256]{2,1,0:T(8,128)(2,1)S(1)}, u32[]{:S(2)}, u32[]{:S(2)}) %collective-permute-start.1) | collective-permute-done | bytes 196640 | tf_op jit(solution)/shard_map/ppermute | solution.py:334
  14.7 0.0 collective-permute-done.rim_one
  14.7 0.0 collective-permute-done.3.halo_two
  14.7 0.0 collective-permute-done.2.halo_one.halo_ref
  14.7 0.0 copy-start.1
  14.7 1.4 %shard_map.80 = (f32[3,272,128]{2,1,0:T(8,128)S(1)}, bf16[3,272,128]{2,1,0:T(8,128)(2,1)S(1)}) custom-call(f32[2,1152,256]{2,1,0:T(8,128)S(1)} %get-tuple-element.22.image_ref, bf16[2,1152,384]{2,1,0:T(8,128)(2,1)S(1)} %get-tuple-element.23.cpl_ref, bf16[3,256,256]{2,1,0:T(8,128)(2,1)S(1)} %copy-done.3, ...), custom_call_target="tpu_custom_call" | custom-call | flops 2000000000 | bytes 6000000 | tf_op jit(solution)/shard_map/pallas_call | solution.py:194
  16.1 0.1 collective-permute-start.4
  16.2 1.4 %collective-permute-done.4 = bf16[3,272,128]{2,1,0:T(8,128)(2,1)S(1)} collective-permute-done((bf16[3,272,128]{2,1,0:T(8,128)(2,1)S(1)}, bf16[3,272,128]{2,1,0:T(8,128)(2,1)S(1)}, u32[]{:S(2)}, u32[]{:S(2)}) %collective-permute-start.4) | collective-permute-done | bytes 208928 | tf_op jit(solution)/shard_map/ppermute | solution.py:308
  17.6 0.1 reduce-precision_convert_fusion
  17.7 0.4 %collective-permute-start.6 = (bf16[3,128,128]{2,1,0:T(8,128)(2,1)S(1)}, bf16[3,128,128]{2,1,0:T(8,128)(2,1)S(1)}, u32[]{:S(2)}, u32[]{:S(2)}) collective-permute-start(bf16[3,128,128]{2,1,0:T(8,128)(2,1)S(1)} %slice.9), channel_id=1, source_target_pairs={{0,8},{4,12},{8,0},{12,4},{16,24},{20,28},{24,16},{28,20},{1,9},{5... | collective-permute-start | bytes 294920 | tf_op jit(solution)/shard_map/ppermute | solution.py:308
  18.1 1.3 %collective-permute-start.8 = (bf16[3,144,128]{2,1,0:T(8,128)(2,1)S(1)}, bf16[3,144,128]{2,1,0:T(8,128)(2,1)S(1)}, u32[]{:S(2)}, u32[]{:S(2)}) collective-permute-start(bf16[3,144,128]{2,1,0:T(8,128)(2,1)S(1)} %slice.10), channel_id=1, source_target_pairs={{0,16},{4,20},{8,24},{12,28},{16,0},{20,4},{24,8},{28,12},{1,17},{... | collective-permute-start | bytes 331784 | tf_op jit(solution)/shard_map/ppermute | solution.py:308
  19.5 0.1 shard_map.81
  19.5 1.4 %collective-permute-start.5 = (f32[8,128]{1,0:T(8,128)S(1)}, f32[8,128]{1,0:T(8,128)S(1)}, u32[]{:S(2)}, u32[]{:S(2)}) collective-permute-start(f32[8,128]{1,0:T(8,128)S(1)} %shard_map.81), channel_id=1, source_target_pairs={{0,2},{1,3},{2,0},{3,1},{4,6},{5,7},{6,4},{7,5},{8,10},{9,11},{10,... | collective-permute-start | bytes 12296 | tf_op jit(solution)/shard_map/ppermute | solution.py:308
  20.9 1.7 %collective-permute-done.6 = bf16[3,128,128]{2,1,0:T(8,128)(2,1)S(1)} collective-permute-done((bf16[3,128,128]{2,1,0:T(8,128)(2,1)S(1)}, bf16[3,128,128]{2,1,0:T(8,128)(2,1)S(1)}, u32[]{:S(2)}, u32[]{:S(2)}) %collective-permute-start.6) | collective-permute-done | bytes 98336 | tf_op jit(solution)/shard_map/ppermute | solution.py:308
  22.6 0.8 %collective-permute-start.7 = (bf16[3,128,128]{2,1,0:T(8,128)(2,1)S(1)}, bf16[3,128,128]{2,1,0:T(8,128)(2,1)S(1)}, u32[]{:S(2)}, u32[]{:S(2)}) collective-permute-start(bf16[3,128,128]{2,1,0:T(8,128)(2,1)S(1)} %reduce-precision_convert_fusion.2.main_one), channel_id=1, source_target_pairs={{0,16},{4,20},{8,24},{12,28},{16,0},{20,4},{24,8},{28,12},{1,17},{... | collective-permute-start | bytes 294920 | tf_op jit(solution)/shard_map/ppermute | solution.py:308
  23.4 0.0 collective-permute-done.8
  23.4 1.3 %collective-permute-start.9 = (bf16[3,144,128]{2,1,0:T(8,128)(2,1)S(1)}, bf16[3,144,128]{2,1,0:T(8,128)(2,1)S(1)}, u32[]{:S(2)}, u32[]{:S(2)}) collective-permute-start(bf16[3,144,128]{2,1,0:T(8,128)(2,1)S(1)} %reduce-precision_convert_fusion.1.side_one), channel_id=1, source_target_pairs={{0,8},{4,12},{8,0},{12,4},{16,24},{20,28},{24,16},{28,20},{1,9},{5... | collective-permute-start | bytes 331784 | tf_op jit(solution)/shard_map/ppermute | solution.py:308
  24.8 0.0 collective-permute-done.5
  24.8 0.1 maximum_select_fusion.ends_ref
  24.9 2.4 %collective-permute-done.7.main_two = bf16[3,128,128]{2,1,0:T(8,128)(2,1)S(1)} collective-permute-done((bf16[3,128,128]{2,1,0:T(8,128)(2,1)S(1)}, bf16[3,128,128]{2,1,0:T(8,128)(2,1)S(1)}, u32[]{:S(2)}, u32[]{:S(2)}) %collective-permute-start.7) | collective-permute-done | bytes 98336 | tf_op jit(solution)/shard_map/ppermute | solution.py:308
  27.3 0.9 %collective-permute-done.9.side_two = bf16[3,144,128]{2,1,0:T(8,128)(2,1)S(1)} collective-permute-done((bf16[3,144,128]{2,1,0:T(8,128)(2,1)S(1)}, bf16[3,144,128]{2,1,0:T(8,128)(2,1)S(1)}, u32[]{:S(2)}, u32[]{:S(2)}) %collective-permute-start.9) | collective-permute-done | bytes 110624 | tf_op jit(solution)/shard_map/ppermute | solution.py:308
  28.3 0.0 copy-done.1
  28.3 0.3 shard_map.82.own_ref
  28.5 0.0 collective-permute-start.10
  28.5 1.2 %collective-permute-done.10.other_ref = f32[8,128]{1,0:T(8,128)S(1)} collective-permute-done((f32[8,128]{1,0:T(8,128)S(1)}, f32[8,128]{1,0:T(8,128)S(1)}, u32[]{:S(2)}, u32[]{:S(2)}) %collective-permute-start.10) | collective-permute-done | bytes 4128 | tf_op jit(solution)/shard_map/ppermute | solution.py:308
  29.7 1.4 %collective-permute-start.11 = (f32[8,128]{1,0:T(8,128)S(1)}, f32[8,128]{1,0:T(8,128)S(1)}, u32[]{:S(2)}, u32[]{:S(2)}) collective-permute-start(f32[8,128]{1,0:T(8,128)S(1)} %add.21), channel_id=1, source_target_pairs={{0,3},{1,2},{2,1},{3,0},{4,7},{5,6},{6,5},{7,4},{8,11},{9,10},{10,... | collective-permute-start | bytes 12296 | tf_op jit(solution)/shard_map/ppermute | solution.py:308
  31.1 0.3 collective-permute-start.12
  31.4 2.7 %collective-permute-start.13 = (f32[8,128]{1,0:T(8,128)S(1)}, f32[8,128]{1,0:T(8,128)S(1)}, u32[]{:S(2)}, u32[]{:S(2)}) collective-permute-start(f32[8,128]{1,0:T(8,128)S(1)} %add.21), channel_id=1, source_target_pairs={{0,1},{1,0},{2,3},{3,2},{4,5},{5,4},{6,7},{7,6},{8,9},{9,8},{10,11... | collective-permute-start | bytes 12296 | tf_op jit(solution)/shard_map/ppermute | solution.py:308
  34.1 0.7 %shard_map.83 = (f32[1,256]{1,0:T(1,128)}, f32[1,256]{1,0:T(1,128)S(1)}) custom-call(f32[8,128]{1,0:T(8,128)S(1)} %shard_map.82.own_ref, f32[8,128]{1,0:T(8,128)S(1)} %collective-permute-done.10.other_ref), custom_call_target="tpu_custom_call" | custom-call | flops 1000000 | bytes 1000000 | tf_op jit(solution)/shard_map/pallas_call | solution.py:282
  34.8 0.4 collective-permute-done.11
  35.1 0.5 %collective-permute-done.12 = f32[8,128]{1,0:T(8,128)S(1)} collective-permute-done((f32[8,128]{1,0:T(8,128)S(1)}, f32[8,128]{1,0:T(8,128)S(1)}, u32[]{:S(2)}, u32[]{:S(2)}) %collective-permute-start.12) | collective-permute-done | bytes 4128 | tf_op jit(solution)/shard_map/ppermute | solution.py:308
  35.6 0.1 collective-permute-done.13
  35.7 0.6 %shard_map.84 = f32[1,256]{1,0:T(1,128)} custom-call(f32[1,256]{1,0:T(1,128)S(1)} %get-tuple-element.33.run_ref, f32[1,128]{1,0:T(1,128)S(1)} %slice.11.earlier_ref), custom_call_target="tpu_custom_call" | custom-call | flops 1000000 | bytes 1000000 | tf_op jit(solution)/shard_map/pallas_call | solution.py:282
  (12 shorter events, 0.1 us)
Async XLA Ops:
  0.6 1.2 %copy-start = (f32[256]{0:T(256)S(1)}, f32[256]{0:T(256)}, u32[]{:S(2)}) copy-start(f32[256]{0:T(256)} %param.11) | copy-start | bytes 3076
  0.6 1.0 %copy-start.2 = (bf16[3,256,256]{2,1,0:T(8,128)(2,1)S(1)}, bf16[3,256,256]{2,1,0:T(8,128)(2,1)}, u32[]{:S(2)}) copy-start(bf16[3,256,256]{2,1,0:T(8,128)(2,1)} %own_ref.1) | copy-start | bytes 1179652
  1.8 6.4 %copy-start.3 = (bf16[3,256,256]{2,1,0:T(8,128)(2,1)S(1)}, bf16[3,256,256]{2,1,0:T(8,128)(2,1)}, u32[]{:S(2)}) copy-start(bf16[3,256,256]{2,1,0:T(8,128)(2,1)} %own_ref.1) | copy-start | bytes 1179652
  1.8 6.4 %copy-start.4 = (f32[3,3,16,256]{3,2,1,0:T(8,128)S(1)}, f32[3,3,16,256]{3,2,1,0:T(8,128)}, u32[]{:S(2)}) copy-start(f32[3,3,16,256]{3,2,1,0:T(8,128)} %force_ref.1) | copy-start | bytes 442372
  1.9 6.4 %copy-start.5 = (f32[3,16,256]{2,1,0:T(8,128)S(1)}, f32[3,16,256]{2,1,0:T(8,128)}, u32[]{:S(2)}) copy-start(f32[3,16,256]{2,1,0:T(8,128)} %bond_ref.1) | copy-start | bytes 147460
  1.9 6.4 %copy-start.6 = (s32[16,256]{1,0:T(8,128)S(1)}, s32[16,256]{1,0:T(8,128)}, u32[]{:S(2)}) copy-start(s32[16,256]{1,0:T(8,128)} %nbr_ref.1) | copy-start | bytes 49156
  2.0 12.7 %collective-permute-start.3 = (bf16[3,272,128]{2,1,0:T(8,128)(2,1)S(1)}, bf16[3,272,128]{2,1,0:T(8,128)(2,1)S(1)}, u32[]{:S(2)}, u32[]{:S(2)}) collective-permute-start(bf16[3,272,128]{2,1,0:T(8,128)(2,1)S(1)} %get-tuple-element.27), channel_id=1, source_target_pairs={{0,4},{1,2},{2,1},{3,7},{4,0},{5,6},{6,5},{7,3},{8,12},{9,10},{10,... | collective-permute-start | bytes 626696 | tf_op jit(solution)/shard_map/ppermute | solution.py:342
  2.5 12.2 %collective-permute-start.2 = (bf16[3,272,128]{2,1,0:T(8,128)(2,1)S(1)}, bf16[3,272,128]{2,1,0:T(8,128)(2,1)S(1)}, u32[]{:S(2)}, u32[]{:S(2)}) collective-permute-start(bf16[3,272,128]{2,1,0:T(8,128)(2,1)S(1)} %get-tuple-element.26), channel_id=1, source_target_pairs={{0,1},{1,0},{2,3},{3,2},{4,5},{5,4},{6,7},{7,6},{8,9},{9,8},{10,11... | collective-permute-start | bytes 626696 | tf_op jit(solution)/shard_map/ppermute | solution.py:336
  6.7 8.0 %collective-permute-start.1 = (bf16[3,128,256]{2,1,0:T(8,128)(2,1)S(1)}, bf16[3,128,256]{2,1,0:T(8,128)(2,1)S(1)}, u32[]{:S(2)}, u32[]{:S(2)}) collective-permute-start(bf16[3,128,256]{2,1,0:T(8,128)(2,1)S(1)} %get-tuple-element.25), channel_id=1, source_target_pairs={{0,28},{4,8},{8,4},{12,16},{16,12},{20,24},{24,20},{28,0},{1,29},{... | collective-permute-start | bytes 589832 | tf_op jit(solution)/shard_map/ppermute | solution.py:334
  8.0 6.7 %collective-permute-start = (bf16[3,128,256]{2,1,0:T(8,128)(2,1)S(1)}, bf16[3,128,256]{2,1,0:T(8,128)(2,1)S(1)}, u32[]{:S(2)}, u32[]{:S(2)}) collective-permute-start(bf16[3,128,256]{2,1,0:T(8,128)(2,1)S(1)} %get-tuple-element.24), channel_id=1, source_target_pairs={{0,4},{4,0},{8,12},{12,8},{16,20},{20,16},{24,28},{28,24},{1,5},{5... | collective-permute-start | bytes 589832 | tf_op jit(solution)/shard_map/ppermute | solution.py:335
  14.7 13.6 %copy-start.1 = (s32[2,256]{1,0:T(2,128)S(1)}, s32[2,256]{1,0:T(2,128)}, u32[]{:S(2)}) copy-start(s32[2,256]{1,0:T(2,128)} %band_ref.1) | copy-start | bytes 6148
  16.1 1.5 %collective-permute-start.4 = (bf16[3,272,128]{2,1,0:T(8,128)(2,1)S(1)}, bf16[3,272,128]{2,1,0:T(8,128)(2,1)S(1)}, u32[]{:S(2)}, u32[]{:S(2)}) collective-permute-start(bf16[3,272,128]{2,1,0:T(8,128)(2,1)S(1)} %get-tuple-element.29), channel_id=1, source_target_pairs={{0,4},{4,0},{8,12},{12,8},{16,20},{20,16},{24,28},{28,24},{1,5},{5... | collective-permute-start | bytes 626696 | tf_op jit(solution)/shard_map/ppermute | solution.py:308
  17.7 4.9 %collective-permute-start.6 = (bf16[3,128,128]{2,1,0:T(8,128)(2,1)S(1)}, bf16[3,128,128]{2,1,0:T(8,128)(2,1)S(1)}, u32[]{:S(2)}, u32[]{:S(2)}) collective-permute-start(bf16[3,128,128]{2,1,0:T(8,128)(2,1)S(1)} %slice.9), channel_id=1, source_target_pairs={{0,8},{4,12},{8,0},{12,4},{16,24},{20,28},{24,16},{28,20},{1,9},{5... | collective-permute-start | bytes 294920 | tf_op jit(solution)/shard_map/ppermute | solution.py:308
  18.1 5.3 %collective-permute-start.8 = (bf16[3,144,128]{2,1,0:T(8,128)(2,1)S(1)}, bf16[3,144,128]{2,1,0:T(8,128)(2,1)S(1)}, u32[]{:S(2)}, u32[]{:S(2)}) collective-permute-start(bf16[3,144,128]{2,1,0:T(8,128)(2,1)S(1)} %slice.10), channel_id=1, source_target_pairs={{0,16},{4,20},{8,24},{12,28},{16,0},{20,4},{24,8},{28,12},{1,17},{... | collective-permute-start | bytes 331784 | tf_op jit(solution)/shard_map/ppermute | solution.py:308
  19.5 5.2 %collective-permute-start.5 = (f32[8,128]{1,0:T(8,128)S(1)}, f32[8,128]{1,0:T(8,128)S(1)}, u32[]{:S(2)}, u32[]{:S(2)}) collective-permute-start(f32[8,128]{1,0:T(8,128)S(1)} %shard_map.81), channel_id=1, source_target_pairs={{0,2},{1,3},{2,0},{3,1},{4,6},{5,7},{6,4},{7,5},{8,10},{9,11},{10,... | collective-permute-start | bytes 12296 | tf_op jit(solution)/shard_map/ppermute | solution.py:308
  22.6 4.7 %collective-permute-start.7 = (bf16[3,128,128]{2,1,0:T(8,128)(2,1)S(1)}, bf16[3,128,128]{2,1,0:T(8,128)(2,1)S(1)}, u32[]{:S(2)}, u32[]{:S(2)}) collective-permute-start(bf16[3,128,128]{2,1,0:T(8,128)(2,1)S(1)} %reduce-precision_convert_fusion.2.main_one), channel_id=1, source_target_pairs={{0,16},{4,20},{8,24},{12,28},{16,0},{20,4},{24,8},{28,12},{1,17},{... | collective-permute-start | bytes 294920 | tf_op jit(solution)/shard_map/ppermute | solution.py:308
  23.4 4.8 %collective-permute-start.9 = (bf16[3,144,128]{2,1,0:T(8,128)(2,1)S(1)}, bf16[3,144,128]{2,1,0:T(8,128)(2,1)S(1)}, u32[]{:S(2)}, u32[]{:S(2)}) collective-permute-start(bf16[3,144,128]{2,1,0:T(8,128)(2,1)S(1)} %reduce-precision_convert_fusion.1.side_one), channel_id=1, source_target_pairs={{0,8},{4,12},{8,0},{12,4},{16,24},{20,28},{24,16},{28,20},{1,9},{5... | collective-permute-start | bytes 331784 | tf_op jit(solution)/shard_map/ppermute | solution.py:308
  28.5 1.2 %collective-permute-start.10 = (f32[8,128]{1,0:T(8,128)S(1)}, f32[8,128]{1,0:T(8,128)S(1)}, u32[]{:S(2)}, u32[]{:S(2)}) collective-permute-start(f32[8,128]{1,0:T(8,128)S(1)} %shard_map.82.own_ref), channel_id=1, source_target_pairs={{0,4},{4,0},{8,12},{12,8},{16,20},{20,16},{24,28},{28,24},{1,5},{5... | collective-permute-start | bytes 12296 | tf_op jit(solution)/shard_map/ppermute | solution.py:308
  29.7 5.4 %collective-permute-start.11 = (f32[8,128]{1,0:T(8,128)S(1)}, f32[8,128]{1,0:T(8,128)S(1)}, u32[]{:S(2)}, u32[]{:S(2)}) collective-permute-start(f32[8,128]{1,0:T(8,128)S(1)} %add.21), channel_id=1, source_target_pairs={{0,3},{1,2},{2,1},{3,0},{4,7},{5,6},{6,5},{7,4},{8,11},{9,10},{10,... | collective-permute-start | bytes 12296 | tf_op jit(solution)/shard_map/ppermute | solution.py:308
  31.1 4.5 %collective-permute-start.12 = (f32[8,128]{1,0:T(8,128)S(1)}, f32[8,128]{1,0:T(8,128)S(1)}, u32[]{:S(2)}, u32[]{:S(2)}) collective-permute-start(f32[8,128]{1,0:T(8,128)S(1)} %add.21), channel_id=1, source_target_pairs={{0,2},{1,3},{2,0},{3,1},{4,6},{5,7},{6,4},{7,5},{8,10},{9,11},{10,... | collective-permute-start | bytes 12296 | tf_op jit(solution)/shard_map/ppermute | solution.py:308
  31.4 4.3 %collective-permute-start.13 = (f32[8,128]{1,0:T(8,128)S(1)}, f32[8,128]{1,0:T(8,128)S(1)}, u32[]{:S(2)}, u32[]{:S(2)}) collective-permute-start(f32[8,128]{1,0:T(8,128)S(1)} %add.21), channel_id=1, source_target_pairs={{0,1},{1,0},{2,3},{3,2},{4,5},{5,4},{6,7},{7,6},{8,9},{9,8},{10,11... | collective-permute-start | bytes 12296 | tf_op jit(solution)/shard_map/ppermute | solution.py:308

commit v8 on v7

--- a/solution.py
+++ b/solution.py
@@ -141,12 +141,10 @@
     )(force, bond, nbr, eigvec)
 
 
-def pair_kernel(image_ref, cpl_ref, own_ref, rim_one, rim_two, halo_one, halo_two, keep_ref, send_ref, flux_ref):
+def main_kernel(image_ref, cpl_ref, own_ref, rim_one, rim_two, keep_ref, send_ref, cross_ref, flux_ref):
     comps, own, modes = own_ref.shape
     depth = comps * own
-    place = lax.axis_index("atom")
-    odd = lax.rem(place, 2) == 1
-    high = lax.rem(lax.axis_index("mode"), 2) == 1
+    odd = lax.rem(lax.axis_index("atom"), 2) == 1
     one = rim_one[...].reshape(comps * RIM, modes)
     two = rim_two[...].reshape(comps * RIM, modes)
     for h, rim in enumerate((jnp.where(odd, one, two), jnp.where(odd, two, one))):
@@ -156,52 +154,54 @@
                 top = (k * comps + c) * RIM
                 flux_ref[c, h * RIM : (h + 1) * RIM, k * modes : (k + 1) * modes] = image[top : top + RIM]
     flux = flux_ref[...].reshape(depth, comps * modes)
-    contract = (((0,), (0,)), ((), ()))
-    pairs = lax.dot_general(own_ref[...].reshape(depth, modes), flux, contract, preferred_element_type=F32)
+    eig = own_ref[...].reshape(depth, modes)
+    pairs = lax.dot_general(eig, flux, (((0,), (0,)), ((), ())), preferred_element_type=F32)
+    for k in range(comps):
+        left, middle, right = k * modes, k * modes + HALF, (k + 1) * modes
+        first, second = pairs[0:HALF, left:middle], pairs[HALF : 2 * HALF, middle:right]
+        keep_ref[k] = jnp.where(odd, second, first)
+        send_ref[k] = jnp.where(odd, first, second).astype(BF16)
+        cross_ref[0, k] = pairs[HALF : 2 * HALF, left:middle]
+        cross_ref[1, k] = pairs[0:HALF, middle:right]
+
+
+def side_kernel(flux_ref, cross_ref, halo_one, halo_two, keep_ref, send_ref):
+    comps, own, wide = flux_ref.shape
+    modes, depth = wide // comps, comps * own
+    odd = lax.rem(lax.axis_index("atom"), 2) == 1
+    high = lax.rem(lax.axis_index("mode"), 2) == 1
+    flux = flux_ref[...].reshape(depth, wide)
     first = halo_one[:, 0:own, :].reshape(depth, HALF)
     second = halo_two[:, 0:own, :].reshape(depth, HALF)
     before = jnp.where(high, first, second)
     after = jnp.where(high, second, first)
     low_flux = jnp.concatenate([flux[:, k * modes : k * modes + HALF] for k in range(comps)], axis=1)
     high_flux = jnp.concatenate([flux[:, k * modes + HALF : (k + 1) * modes] for k in range(comps)], axis=1)
+    contract = (((0,), (0,)), ((), ()))
     below = lax.dot_general(before, low_flux, contract, preferred_element_type=F32)
     above = lax.dot_general(after, high_flux, contract, preferred_element_type=F32)
     lower = iota((HALF, HALF), 0) > iota((HALF, HALF), 1)
     equal = iota((HALF, HALF), 0) == iota((HALF, HALF), 1)
-    second_core = odd
     for k in range(comps):
-        left, middle, right = k * modes, k * modes + HALF, (k + 1) * modes
         sets = []
         for part in range(2):
-            if part == 0:
-                main = pairs[0:HALF, left:middle]
-                low = below[:, k * HALF : (k + 1) * HALF]
-                up = pairs[HALF : 2 * HALF, left:middle]
-            else:
-                main = pairs[HALF : 2 * HALF, middle:right]
-                low = pairs[0:HALF, middle:right]
-                up = above[:, k * HALF : (k + 1) * HALF]
+            outside = (below, above)[part][:, k * HALF : (k + 1) * HALF]
+            low, up = (outside, cross_ref[0, k]) if part == 0 else (cross_ref[1, k], outside)
             edge = jnp.sum(jnp.where(equal, low, 0.0), axis=0, keepdims=True)
-            edge = jnp.broadcast_to(edge, (EXTRA, HALF))
-            sets.append(jnp.concatenate([main, jnp.where(lower, low, up), edge], axis=0))
-        keep_ref[k] = jnp.where(second_core, sets[1], sets[0])
-        send_ref[k] = jnp.where(second_core, sets[0], sets[1]).astype(BF16)
-
-
-def pair_parts(image, matrix, eigvec, rim_one, rim_two, halo_one, halo_two):
-    comps, own, modes = eigvec.shape
-    shape = (comps, 2 * HALF + EXTRA, HALF)
+            sets.append(jnp.concatenate([jnp.where(lower, low, up), jnp.broadcast_to(edge, (EXTRA, HALF))], axis=0))
+        keep_ref[k] = jnp.where(odd, sets[1], sets[0])
+        send_ref[k] = jnp.where(odd, sets[0], sets[1]).astype(BF16)
+
+
+def pair_call(kernel, out_shape, flops, *operands):
     return pl.pallas_call(
-        pair_kernel,
-        out_shape=(jax.ShapeDtypeStruct(shape, F32), jax.ShapeDtypeStruct(shape, BF16)),
-        in_specs=[VMEM] * 7,
-        out_specs=(VMEM, VMEM),
-        scratch_shapes=[
-            pltpu.VMEM((comps, own, comps * modes), BF16),
-        ],
+        kernel,
+        out_shape=tuple(jax.ShapeDtypeStruct(shape, kind) for shape, kind in out_shape),
+        in_specs=[VMEM] * len(operands),
+        out_specs=(VMEM,) * len(out_shape),
         compiler_params=pltpu.CompilerParams(vmem_limit_bytes=LARGE),
-        cost_estimate=pl.CostEstimate(flops=2 * 10**9, bytes_accessed=6 * 10**6, transcendentals=0),
-    )(image, matrix, eigvec, rim_one, rim_two, halo_one, halo_two)
+        cost_estimate=pl.CostEstimate(flops=flops, bytes_accessed=10**6, transcendentals=0),
+    )(*operands)
 
 
 def halo_freq(halo_ref, own):
@@ -342,14 +342,22 @@
     halo_two = lax.ppermute(far_edge, ("atom", "mode"), hops)
 
     image, matrix = own_image(force, bond, nbr, held, atoms)
-    keep, send = pair_parts(image, matrix, eigvec, rim_one, rim_two, halo_one, halo_two)
+    square, tall = (comps, HALF, HALF), (comps, HALF + EXTRA, HALF)
+    keep_main, send_main, cross, flux = pair_call(
+        main_kernel,
+        ((square, F32), (square, BF16), ((2, *square), F32), ((comps, own, comps * modes), BF16)),
+        10**9, image, matrix, eigvec, rim_one, rim_two,
+    )
+    keep_side, send_side = pair_call(
+        side_kernel, ((tall, F32), (tall, BF16)), 10**9, flux, cross, halo_one, halo_two
+    )
 
     tile = jax.ShapeDtypeStruct((8, HALF), F32)
     row = jax.ShapeDtypeStruct((1, modes), F32)
-    total = rounded_sum(keep, swap(send, "atom", 1))
-    total, own_freq = lax.optimization_barrier((total, freq_row))
+    main = rounded_sum(keep_main, swap(send_main, "atom", 1))
+    side = rounded_sum(keep_side, swap(send_side, "atom", 1))
+    side, own_freq = lax.optimization_barrier((side, freq_row))
     ends = local_call(functools.partial(ends_kernel, own), tile, own_freq, halo_one)
-    main, side = total[:, :HALF], total[:, HALF:]
     steps = bits_of("atom")[1:]
     for step, (one, two) in enumerate(zip(steps, reversed(steps))):
         main_other, side_other = swap(main, "atom", one), swap(side, "atom", two)

time: 36.5 us -> 35.4 us (0.970)
  waiting for transfers between devices: 10.5 us -> 8.11 us
  starting transfers between devices: 16 us -> 17.1 us
    ppermute x1, starting transfers between devices: 1.33 us -> 3.4 us  [body(): rim_two = lax.ppermute(outer_edge, 'atom', outer)]
    ppermute x1, waiting for transfers between devices: 1.86 us -> 0.01 us  [body(): rim_two = lax.ppermute(outer_edge, 'atom', outer)]
    ppermute x1, starting transfers between devices: 4.15 us -> 2.68 us  [body(): halo_one = lax.ppermute(near_edge, 'mode', near)]
    ppermute x10 -> x11, starting transfers between devices: 9.72 us -> 10.4 us  [swap(): lax.ppermute(x, axis, [(i, i ^ bit) for i in range(lax.axis_size(axis))])]
    ppermute x10 -> x11, waiting for transfers between devices: 8.59 us -> 8.1 us  [swap(): lax.ppermute(x, axis, [(i, i ^ bit) for i in range(lax.axis_size(axis))])]
    pallas_call x1 -> x2, Pallas kernels: 1.39 us -> 1.59 us  [pair_call(): pl.pallas_call(kernel, out_shape=tuple((jax.ShapeDtypeStruct(shape, kind)...]
  transfers between devices with their start and end apart: 14 -> 15, of which waited for: 9 -> 7; matrix products, arithmetic and copies ran while one was open for 0% -> 1% of each run, Pallas kernels for 14% -> 20%
where the time goes in v8:
time: 35.4 us; the launch traced here: 35.3 us
  starting transfers between devices  17.1 us (48%)
  waiting for transfers between devices  8.11 us (23%)
  Pallas kernels  8.05 us (23%)
  local copies, waits for them, and re-layouts  1.02 us (3%)
  between operations  0.79 us (2%)
    ppermute x11, starting transfers between devices, swap(): lax.ppermute(x, axis, [(i, i ^ bit) for i in range(lax.axis_size(axis))])  10.4 us
    ppermute x11, waiting for transfers between devices, swap(): lax.ppermute(x, axis, [(i, i ^ bit) for i in range(lax.axis_size(axis))])  8.1 us
    pallas_call x1, Pallas kernels, own_image(): pl.pallas_call(functools.partial(coupling_kernel, atoms), out_shape=(jax....  4.52 us
    ppermute x1, starting transfers between devices, body(): rim_two = lax.ppermute(outer_edge, 'atom', outer)  3.4 us
    ppermute x1, starting transfers between devices, body(): halo_one = lax.ppermute(near_edge, 'mode', near)  2.68 us
    pallas_call x4, Pallas kernels, local_call(): pl.pallas_call(kernel, out_shape=out_shape, in_specs=[VMEM] * len(operand...  1.65 us
    pallas_call x2, Pallas kernels, pair_call(): pl.pallas_call(kernel, out_shape=tuple((jax.ShapeDtypeStruct(shape, kind)...  1.59 us
    unnamed x14, local copies, waits for them, and re-layouts  1.02 us
  transfers between devices with their start and end apart: 15, of which 7 were waited for; matrix products, arithmetic and copies ran while one was open for 1% of the time, Pallas kernels for 20%

profile of v8, /device:TPU:0, one launch (start us, length us, event | category | flops | bytes accessed | tf_op | source)
XLA Modules:
  0.0 35.3 jit_solution(14047332016635990480)
XLA Ops:
  0.6 0.0 copy-start
  0.6 1.0 %copy-done = bf16[3,256,256]{2,1,0:T(8,128)(2,1)S(1)} copy-done((bf16[3,256,256]{2,1,0:T(8,128)(2,1)S(1)}, bf16[3,256,256]{2,1,0:T(8,128)(2,1)}, u32[]{:S(2)}) %copy-start) | copy-done | bytes 393240
  1.6 0.2 shard_map.77
  1.8 3.4 %collective-permute-start.1 = (bf16[3,128,256]{2,1,0:T(8,128)(2,1)S(1)}, bf16[3,128,256]{2,1,0:T(8,128)(2,1)S(1)}, u32[]{:S(2)}, u32[]{:S(2)}) collective-permute-start(bf16[3,128,256]{2,1,0:T(8,128)(2,1)S(1)} %get-tuple-element.29), channel_id=1, source_target_pairs={{0,28},{4,8},{8,4},{12,16},{16,12},{20,24},{24,20},{28,0},{1,29},{... | collective-permute-start | bytes 589832 | tf_op jit(solution)/shard_map/ppermute | solution.py:334
  5.2 0.1 collective-permute-start
  5.3 0.0 copy-done.2
  5.3 0.1 shard_map.78
  5.4 0.5 %collective-permute-start.3 = (bf16[3,272,128]{2,1,0:T(8,128)(2,1)S(1)}, bf16[3,272,128]{2,1,0:T(8,128)(2,1)S(1)}, u32[]{:S(2)}, u32[]{:S(2)}) collective-permute-start(bf16[3,272,128]{2,1,0:T(8,128)(2,1)S(1)} %get-tuple-element.33), channel_id=1, source_target_pairs={{0,4},{1,2},{2,1},{3,7},{4,0},{5,6},{6,5},{7,3},{8,12},{9,10},{10,... | collective-permute-start | bytes 626696 | tf_op jit(solution)/shard_map/ppermute | solution.py:342
  6.0 2.7 %collective-permute-start.2 = (bf16[3,272,128]{2,1,0:T(8,128)(2,1)S(1)}, bf16[3,272,128]{2,1,0:T(8,128)(2,1)S(1)}, u32[]{:S(2)}, u32[]{:S(2)}) collective-permute-start(bf16[3,272,128]{2,1,0:T(8,128)(2,1)S(1)} %get-tuple-element.32), channel_id=1, source_target_pairs={{0,1},{1,0},{2,3},{3,2},{4,5},{5,4},{6,7},{7,6},{8,9},{9,8},{10,11... | collective-permute-start | bytes 626696 | tf_op jit(solution)/shard_map/ppermute | solution.py:336
  8.7 0.0 copy-done.1
  8.7 0.0 copy-done.4
  8.7 0.0 copy-done.5
  8.7 0.0 copy-done.6
  8.7 4.5 %shard_map.79 = (f32[2,1152,256]{2,1,0:T(8,128)S(1)}, bf16[2,1152,384]{2,1,0:T(8,128)(2,1)S(1)}) custom-call(f32[3,3,16,256]{3,2,1,0:T(8,128)S(1)} %copy-done.4, f32[3,16,256]{2,1,0:T(8,128)S(1)} %copy-done.5, s32[16,256]{1,0:T(8,128)S(1)} %copy-done.6, bf16[3,256,256]{2,1,0:T(8,128)(2,1)S(1)} %copy-done.1), custom_call_target="tpu_custom_call" | custom-call | flops 4000000000 | bytes 6000000 | tf_op jit(solution)/shard_map/pallas_call | solution.py:125
  13.2 0.0 collective-permute-done.1.rim_two
  13.2 0.0 collective-permute-done.rim_one
  13.2 1.1 %shard_map.80 = (f32[3,128,128]{2,1,0:T(8,128)S(1)}, bf16[3,128,128]{2,1,0:T(8,128)(2,1)S(1)}, f32[2,3,128,128]{3,2,1,0:T(8,128)S(1)}, bf16[3,256,768]{2,1,0:T(8,128)(2,1)S(1)}) custom-call(f32[2,1152,256]{2,1,0:T(8,128)S(1)} %get-tuple-element.26.image_ref, bf16[2,1152,384]{2,1,0:T(8,128)(2,1)S(1)} %get-tuple-element.27.cpl_ref, ...), custom_call_target="tpu_custom_call" | custom-call | flops 1000000000 | bytes 1000000 | tf_op jit(solution)/shard_map/pallas_call | solution.py:197
  14.4 0.1 collective-permute-start.6
  14.5 0.0 collective-permute-done.3.halo_two
  14.5 0.0 collective-permute-done.2.halo_one.halo_ref
  14.5 0.0 copy-start.3
  14.5 0.4 %shard_map.81 = (f32[3,144,128]{2,1,0:T(8,128)S(1)}, bf16[3,144,128]{2,1,0:T(8,128)(2,1)S(1)}) custom-call(bf16[3,256,768]{2,1,0:T(8,128)(2,1)S(1)} %get-tuple-element.30.flux_ref, f32[2,3,128,128]{3,2,1,0:T(8,128)S(1)} %get-tuple-element.31.cross_ref, bf16[3,272,128]{2,1,0:T(8,128)(2,1)S(1)} %collective-permute-done.2.halo_one.halo_ref, ...), custom_call_target="tpu_custom_call" | custom-call | flops 1000000000 | bytes 1000000 | tf_op jit(solution)/shard_map/pallas_call | solution.py:197
  14.9 0.5 %collective-permute-start.4 = (bf16[3,144,128]{2,1,0:T(8,128)(2,1)S(1)}, bf16[3,144,128]{2,1,0:T(8,128)(2,1)S(1)}, u32[]{:S(2)}, u32[]{:S(2)}) collective-permute-start(bf16[3,144,128]{2,1,0:T(8,128)(2,1)S(1)} %get-tuple-element.35), channel_id=1, source_target_pairs={{0,4},{4,0},{8,12},{12,8},{16,20},{20,16},{24,28},{28,24},{1,5},{5... | collective-permute-start | bytes 331784 | tf_op jit(solution)/shard_map/ppermute | solution.py:308
  15.5 0.3 collective-permute-done.6
  15.8 1.2 %collective-permute-start.7 = (bf16[3,128,128]{2,1,0:T(8,128)(2,1)S(1)}, bf16[3,128,128]{2,1,0:T(8,128)(2,1)S(1)}, u32[]{:S(2)}, u32[]{:S(2)}) collective-permute-start(bf16[3,128,128]{2,1,0:T(8,128)(2,1)S(1)} %reduce-precision_convert_fusion.3), channel_id=1, source_target_pairs={{0,8},{4,12},{8,0},{12,4},{16,24},{20,28},{24,16},{28,20},{1,9},{5... | collective-permute-start | bytes 294920 | tf_op jit(solution)/shard_map/ppermute | solution.py:308
  17.0 0.0 collective-permute-done.4
  17.0 0.7 %collective-permute-start.9 = (bf16[3,144,128]{2,1,0:T(8,128)(2,1)S(1)}, bf16[3,144,128]{2,1,0:T(8,128)(2,1)S(1)}, u32[]{:S(2)}, u32[]{:S(2)}) collective-permute-start(bf16[3,144,128]{2,1,0:T(8,128)(2,1)S(1)} %reduce-precision_convert_fusion.1), channel_id=1, source_target_pairs={{0,16},{4,20},{8,24},{12,28},{16,0},{20,4},{24,8},{28,12},{1,17},{... | collective-permute-start | bytes 331784 | tf_op jit(solution)/shard_map/ppermute | solution.py:308
  17.8 0.1 shard_map.82
  17.8 1.1 %collective-permute-start.5 = (f32[8,128]{1,0:T(8,128)S(1)}, f32[8,128]{1,0:T(8,128)S(1)}, u32[]{:S(2)}, u32[]{:S(2)}) collective-permute-start(f32[8,128]{1,0:T(8,128)S(1)} %shard_map.82), channel_id=1, source_target_pairs={{0,2},{1,3},{2,0},{3,1},{4,6},{5,7},{6,4},{7,5},{8,10},{9,11},{10,... | collective-permute-start | bytes 12296 | tf_op jit(solution)/shard_map/ppermute | solution.py:308
  18.9 1.8 %collective-permute-done.7 = bf16[3,128,128]{2,1,0:T(8,128)(2,1)S(1)} collective-permute-done((bf16[3,128,128]{2,1,0:T(8,128)(2,1)S(1)}, bf16[3,128,128]{2,1,0:T(8,128)(2,1)S(1)}, u32[]{:S(2)}, u32[]{:S(2)}) %collective-permute-start.7) | collective-permute-done | bytes 98336 | tf_op jit(solution)/shard_map/ppermute | solution.py:308
  20.7 1.3 %collective-permute-start.8 = (bf16[3,128,128]{2,1,0:T(8,128)(2,1)S(1)}, bf16[3,128,128]{2,1,0:T(8,128)(2,1)S(1)}, u32[]{:S(2)}, u32[]{:S(2)}) collective-permute-start(bf16[3,128,128]{2,1,0:T(8,128)(2,1)S(1)} %reduce-precision_convert_fusion.2.main_one), channel_id=1, source_target_pairs={{0,16},{4,20},{8,24},{12,28},{16,0},{20,4},{24,8},{28,12},{1,17},{... | collective-permute-start | bytes 294920 | tf_op jit(solution)/shard_map/ppermute | solution.py:308
  22.0 0.0 collective-permute-done.9
  22.0 1.1 %collective-permute-start.10 = (bf16[3,144,128]{2,1,0:T(8,128)(2,1)S(1)}, bf16[3,144,128]{2,1,0:T(8,128)(2,1)S(1)}, u32[]{:S(2)}, u32[]{:S(2)}) collective-permute-start(bf16[3,144,128]{2,1,0:T(8,128)(2,1)S(1)} %reduce-precision_convert_fusion.side_one), channel_id=1, source_target_pairs={{0,8},{4,12},{8,0},{12,4},{16,24},{20,28},{24,16},{28,20},{1,9},{5... | collective-permute-start | bytes 331784 | tf_op jit(solution)/shard_map/ppermute | solution.py:308
  23.1 0.0 collective-permute-done.5
  23.1 0.1 maximum_select_fusion.ends_ref
  23.2 2.2 %collective-permute-done.8.main_two = bf16[3,128,128]{2,1,0:T(8,128)(2,1)S(1)} collective-permute-done((bf16[3,128,128]{2,1,0:T(8,128)(2,1)S(1)}, bf16[3,128,128]{2,1,0:T(8,128)(2,1)S(1)}, u32[]{:S(2)}, u32[]{:S(2)}) %collective-permute-start.8) | collective-permute-done | bytes 98336 | tf_op jit(solution)/shard_map/ppermute | solution.py:308
  25.4 1.4 %collective-permute-done.10.side_two = bf16[3,144,128]{2,1,0:T(8,128)(2,1)S(1)} collective-permute-done((bf16[3,144,128]{2,1,0:T(8,128)(2,1)S(1)}, bf16[3,144,128]{2,1,0:T(8,128)(2,1)S(1)}, u32[]{:S(2)}, u32[]{:S(2)}) %collective-permute-start.10) | collective-permute-done | bytes 110624 | tf_op jit(solution)/shard_map/ppermute | solution.py:308
  26.8 0.3 shard_map.83.own_ref
  27.1 0.0 collective-permute-start.11
  27.1 1.2 %collective-permute-done.11.other_ref = f32[8,128]{1,0:T(8,128)S(1)} collective-permute-done((f32[8,128]{1,0:T(8,128)S(1)}, f32[8,128]{1,0:T(8,128)S(1)}, u32[]{:S(2)}, u32[]{:S(2)}) %collective-permute-start.11) | collective-permute-done | bytes 4128 | tf_op jit(solution)/shard_map/ppermute | solution.py:308
  28.3 1.8 %collective-permute-start.12 = (f32[8,128]{1,0:T(8,128)S(1)}, f32[8,128]{1,0:T(8,128)S(1)}, u32[]{:S(2)}, u32[]{:S(2)}) collective-permute-start(f32[8,128]{1,0:T(8,128)S(1)} %add.25), channel_id=1, source_target_pairs={{0,3},{1,2},{2,1},{3,0},{4,7},{5,6},{6,5},{7,4},{8,11},{9,10},{10,... | collective-permute-start | bytes 12296 | tf_op jit(solution)/shard_map/ppermute | solution.py:308
  30.1 0.6 %collective-permute-start.13 = (f32[8,128]{1,0:T(8,128)S(1)}, f32[8,128]{1,0:T(8,128)S(1)}, u32[]{:S(2)}, u32[]{:S(2)}) collective-permute-start(f32[8,128]{1,0:T(8,128)S(1)} %add.25), channel_id=1, source_target_pairs={{0,2},{1,3},{2,0},{3,1},{4,6},{5,7},{6,4},{7,5},{8,10},{9,11},{10,... | collective-permute-start | bytes 12296 | tf_op jit(solution)/shard_map/ppermute | solution.py:308
  30.7 2.0 %collective-permute-start.14 = (f32[8,128]{1,0:T(8,128)S(1)}, f32[8,128]{1,0:T(8,128)S(1)}, u32[]{:S(2)}, u32[]{:S(2)}) collective-permute-start(f32[8,128]{1,0:T(8,128)S(1)} %add.25), channel_id=1, source_target_pairs={{0,1},{1,0},{2,3},{3,2},{4,5},{5,4},{6,7},{7,6},{8,9},{9,8},{10,11... | collective-permute-start | bytes 12296 | tf_op jit(solution)/shard_map/ppermute | solution.py:308
  32.7 0.7 %shard_map.84 = (f32[1,256]{1,0:T(1,128)}, f32[1,256]{1,0:T(1,128)S(1)}) custom-call(f32[8,128]{1,0:T(8,128)S(1)} %shard_map.83.own_ref, f32[8,128]{1,0:T(8,128)S(1)} %collective-permute-done.11.other_ref), custom_call_target="tpu_custom_call" | custom-call | flops 1000000 | bytes 1000000 | tf_op jit(solution)/shard_map/pallas_call | solution.py:282
  33.3 0.4 %collective-permute-done.12 = f32[8,128]{1,0:T(8,128)S(1)} collective-permute-done((f32[8,128]{1,0:T(8,128)S(1)}, f32[8,128]{1,0:T(8,128)S(1)}, u32[]{:S(2)}, u32[]{:S(2)}) %collective-permute-start.12) | collective-permute-done | bytes 4128 | tf_op jit(solution)/shard_map/ppermute | solution.py:308
  33.7 0.9 %collective-permute-done.13 = f32[8,128]{1,0:T(8,128)S(1)} collective-permute-done((f32[8,128]{1,0:T(8,128)S(1)}, f32[8,128]{1,0:T(8,128)S(1)}, u32[]{:S(2)}, u32[]{:S(2)}) %collective-permute-start.13) | collective-permute-done | bytes 4128 | tf_op jit(solution)/shard_map/ppermute | solution.py:308
  34.6 0.0 collective-permute-done.14
  34.7 0.6 %shard_map.85 = f32[1,256]{1,0:T(1,128)} custom-call(f32[1,256]{1,0:T(1,128)S(1)} %get-tuple-element.41.run_ref, f32[1,128]{1,0:T(1,128)S(1)} %slice.3.earlier_ref), custom_call_target="tpu_custom_call" | custom-call | flops 1000000 | bytes 1000000 | tf_op jit(solution)/shard_map/pallas_call | solution.py:282
  (14 shorter events, 0.2 us)
Async XLA Ops:
  0.6 1.0 %copy-start = (bf16[3,256,256]{2,1,0:T(8,128)(2,1)S(1)}, bf16[3,256,256]{2,1,0:T(8,128)(2,1)}, u32[]{:S(2)}) copy-start(bf16[3,256,256]{2,1,0:T(8,128)(2,1)} %own_ref.1) | copy-start | bytes 1179652
  1.6 3.7 %copy-start.2 = (f32[256]{0:T(256)S(1)}, f32[256]{0:T(256)}, u32[]{:S(2)}) copy-start(f32[256]{0:T(256)} %param.11) | copy-start | bytes 3076
  1.8 11.4 %collective-permute-start.1 = (bf16[3,128,256]{2,1,0:T(8,128)(2,1)S(1)}, bf16[3,128,256]{2,1,0:T(8,128)(2,1)S(1)}, u32[]{:S(2)}, u32[]{:S(2)}) collective-permute-start(bf16[3,128,256]{2,1,0:T(8,128)(2,1)S(1)} %get-tuple-element.29), channel_id=1, source_target_pairs={{0,28},{4,8},{8,4},{12,16},{16,12},{20,24},{24,20},{28,0},{1,29},{... | collective-permute-start | bytes 589832 | tf_op jit(solution)/shard_map/ppermute | solution.py:334
  5.2 3.4 %copy-start.1 = (bf16[3,256,256]{2,1,0:T(8,128)(2,1)S(1)}, bf16[3,256,256]{2,1,0:T(8,128)(2,1)}, u32[]{:S(2)}) copy-start(bf16[3,256,256]{2,1,0:T(8,128)(2,1)} %own_ref.1) | copy-start | bytes 1179652
  5.2 3.4 %copy-start.4 = (f32[3,3,16,256]{3,2,1,0:T(8,128)S(1)}, f32[3,3,16,256]{3,2,1,0:T(8,128)}, u32[]{:S(2)}) copy-start(f32[3,3,16,256]{3,2,1,0:T(8,128)} %force_ref.1) | copy-start | bytes 442372
  5.2 3.4 %copy-start.5 = (f32[3,16,256]{2,1,0:T(8,128)S(1)}, f32[3,16,256]{2,1,0:T(8,128)}, u32[]{:S(2)}) copy-start(f32[3,16,256]{2,1,0:T(8,128)} %bond_ref.1) | copy-start | bytes 147460
  5.2 3.4 %copy-start.6 = (s32[16,256]{1,0:T(8,128)S(1)}, s32[16,256]{1,0:T(8,128)}, u32[]{:S(2)}) copy-start(s32[16,256]{1,0:T(8,128)} %nbr_ref.1) | copy-start | bytes 49156
  5.2 8.0 %collective-permute-start = (bf16[3,128,256]{2,1,0:T(8,128)(2,1)S(1)}, bf16[3,128,256]{2,1,0:T(8,128)(2,1)S(1)}, u32[]{:S(2)}, u32[]{:S(2)}) collective-permute-start(bf16[3,128,256]{2,1,0:T(8,128)(2,1)S(1)} %get-tuple-element.28), channel_id=1, source_target_pairs={{0,4},{4,0},{8,12},{12,8},{16,20},{20,16},{24,28},{28,24},{1,5},{5... | collective-permute-start | bytes 589832 | tf_op jit(solution)/shard_map/ppermute | solution.py:335
  5.4 9.0 %collective-permute-start.3 = (bf16[3,272,128]{2,1,0:T(8,128)(2,1)S(1)}, bf16[3,272,128]{2,1,0:T(8,128)(2,1)S(1)}, u32[]{:S(2)}, u32[]{:S(2)}) collective-permute-start(bf16[3,272,128]{2,1,0:T(8,128)(2,1)S(1)} %get-tuple-element.33), channel_id=1, source_target_pairs={{0,4},{1,2},{2,1},{3,7},{4,0},{5,6},{6,5},{7,3},{8,12},{9,10},{10,... | collective-permute-start | bytes 626696 | tf_op jit(solution)/shard_map/ppermute | solution.py:342
  6.0 8.5 %collective-permute-start.2 = (bf16[3,272,128]{2,1,0:T(8,128)(2,1)S(1)}, bf16[3,272,128]{2,1,0:T(8,128)(2,1)S(1)}, u32[]{:S(2)}, u32[]{:S(2)}) collective-permute-start(bf16[3,272,128]{2,1,0:T(8,128)(2,1)S(1)} %get-tuple-element.32), channel_id=1, source_target_pairs={{0,1},{1,0},{2,3},{3,2},{4,5},{5,4},{6,7},{7,6},{8,9},{9,8},{10,11... | collective-permute-start | bytes 626696 | tf_op jit(solution)/shard_map/ppermute | solution.py:336
  14.4 1.4 %collective-permute-start.6 = (bf16[3,128,128]{2,1,0:T(8,128)(2,1)S(1)}, bf16[3,128,128]{2,1,0:T(8,128)(2,1)S(1)}, u32[]{:S(2)}, u32[]{:S(2)}) collective-permute-start(bf16[3,128,128]{2,1,0:T(8,128)(2,1)S(1)} %get-tuple-element.38), channel_id=1, source_target_pairs={{0,4},{4,0},{8,12},{12,8},{16,20},{20,16},{24,28},{28,24},{1,5},{5... | collective-permute-start | bytes 294920 | tf_op jit(solution)/shard_map/ppermute | solution.py:308
  14.5 12.4 %copy-start.3 = (s32[2,256]{1,0:T(2,128)S(1)}, s32[2,256]{1,0:T(2,128)}, u32[]{:S(2)}) copy-start(s32[2,256]{1,0:T(2,128)} %band_ref.1) | copy-start | bytes 6148
  14.9 2.1 %collective-permute-start.4 = (bf16[3,144,128]{2,1,0:T(8,128)(2,1)S(1)}, bf16[3,144,128]{2,1,0:T(8,128)(2,1)S(1)}, u32[]{:S(2)}, u32[]{:S(2)}) collective-permute-start(bf16[3,144,128]{2,1,0:T(8,128)(2,1)S(1)} %get-tuple-element.35), channel_id=1, source_target_pairs={{0,4},{4,0},{8,12},{12,8},{16,20},{20,16},{24,28},{28,24},{1,5},{5... | collective-permute-start | bytes 331784 | tf_op jit(solution)/shard_map/ppermute | solution.py:308
  15.8 4.9 %collective-permute-start.7 = (bf16[3,128,128]{2,1,0:T(8,128)(2,1)S(1)}, bf16[3,128,128]{2,1,0:T(8,128)(2,1)S(1)}, u32[]{:S(2)}, u32[]{:S(2)}) collective-permute-start(bf16[3,128,128]{2,1,0:T(8,128)(2,1)S(1)} %reduce-precision_convert_fusion.3), channel_id=1, source_target_pairs={{0,8},{4,12},{8,0},{12,4},{16,24},{20,28},{24,16},{28,20},{1,9},{5... | collective-permute-start | bytes 294920 | tf_op jit(solution)/shard_map/ppermute | solution.py:308
  17.0 4.9 %collective-permute-start.9 = (bf16[3,144,128]{2,1,0:T(8,128)(2,1)S(1)}, bf16[3,144,128]{2,1,0:T(8,128)(2,1)S(1)}, u32[]{:S(2)}, u32[]{:S(2)}) collective-permute-start(bf16[3,144,128]{2,1,0:T(8,128)(2,1)S(1)} %reduce-precision_convert_fusion.1), channel_id=1, source_target_pairs={{0,16},{4,20},{8,24},{12,28},{16,0},{20,4},{24,8},{28,12},{1,17},{... | collective-permute-start | bytes 331784 | tf_op jit(solution)/shard_map/ppermute | solution.py:308
  17.8 5.3 %collective-permute-start.5 = (f32[8,128]{1,0:T(8,128)S(1)}, f32[8,128]{1,0:T(8,128)S(1)}, u32[]{:S(2)}, u32[]{:S(2)}) collective-permute-start(f32[8,128]{1,0:T(8,128)S(1)} %shard_map.82), channel_id=1, source_target_pairs={{0,2},{1,3},{2,0},{3,1},{4,6},{5,7},{6,4},{7,5},{8,10},{9,11},{10,... | collective-permute-start | bytes 12296 | tf_op jit(solution)/shard_map/ppermute | solution.py:308
  20.7 4.7 %collective-permute-start.8 = (bf16[3,128,128]{2,1,0:T(8,128)(2,1)S(1)}, bf16[3,128,128]{2,1,0:T(8,128)(2,1)S(1)}, u32[]{:S(2)}, u32[]{:S(2)}) collective-permute-start(bf16[3,128,128]{2,1,0:T(8,128)(2,1)S(1)} %reduce-precision_convert_fusion.2.main_one), channel_id=1, source_target_pairs={{0,16},{4,20},{8,24},{12,28},{16,0},{20,4},{24,8},{28,12},{1,17},{... | collective-permute-start | bytes 294920 | tf_op jit(solution)/shard_map/ppermute | solution.py:308
  22.0 4.8 %collective-permute-start.10 = (bf16[3,144,128]{2,1,0:T(8,128)(2,1)S(1)}, bf16[3,144,128]{2,1,0:T(8,128)(2,1)S(1)}, u32[]{:S(2)}, u32[]{:S(2)}) collective-permute-start(bf16[3,144,128]{2,1,0:T(8,128)(2,1)S(1)} %reduce-precision_convert_fusion.side_one), channel_id=1, source_target_pairs={{0,8},{4,12},{8,0},{12,4},{16,24},{20,28},{24,16},{28,20},{1,9},{5... | collective-permute-start | bytes 331784 | tf_op jit(solution)/shard_map/ppermute | solution.py:308
  27.1 1.2 %collective-permute-start.11 = (f32[8,128]{1,0:T(8,128)S(1)}, f32[8,128]{1,0:T(8,128)S(1)}, u32[]{:S(2)}, u32[]{:S(2)}) collective-permute-start(f32[8,128]{1,0:T(8,128)S(1)} %shard_map.83.own_ref), channel_id=1, source_target_pairs={{0,4},{4,0},{8,12},{12,8},{16,20},{20,16},{24,28},{28,24},{1,5},{5... | collective-permute-start | bytes 12296 | tf_op jit(solution)/shard_map/ppermute | solution.py:308
  28.3 5.4 %collective-permute-start.12 = (f32[8,128]{1,0:T(8,128)S(1)}, f32[8,128]{1,0:T(8,128)S(1)}, u32[]{:S(2)}, u32[]{:S(2)}) collective-permute-start(f32[8,128]{1,0:T(8,128)S(1)} %add.25), channel_id=1, source_target_pairs={{0,3},{1,2},{2,1},{3,0},{4,7},{5,6},{6,5},{7,4},{8,11},{9,10},{10,... | collective-permute-start | bytes 12296 | tf_op jit(solution)/shard_map/ppermute | solution.py:308
  30.1 4.5 %collective-permute-start.13 = (f32[8,128]{1,0:T(8,128)S(1)}, f32[8,128]{1,0:T(8,128)S(1)}, u32[]{:S(2)}, u32[]{:S(2)}) collective-permute-start(f32[8,128]{1,0:T(8,128)S(1)} %add.25), channel_id=1, source_target_pairs={{0,2},{1,3},{2,0},{3,1},{4,6},{5,7},{6,4},{7,5},{8,10},{9,11},{10,... | collective-permute-start | bytes 12296 | tf_op jit(solution)/shard_map/ppermute | solution.py:308
  30.7 3.9 %collective-permute-start.14 = (f32[8,128]{1,0:T(8,128)S(1)}, f32[8,128]{1,0:T(8,128)S(1)}, u32[]{:S(2)}, u32[]{:S(2)}) collective-permute-start(f32[8,128]{1,0:T(8,128)S(1)} %add.25), channel_id=1, source_target_pairs={{0,1},{1,0},{2,3},{3,2},{4,5},{5,4},{6,7},{7,6},{8,9},{9,8},{10,11... | collective-permute-start | bytes 12296 | tf_op jit(solution)/shard_map/ppermute | solution.py:308

commit v9 on v8

--- a/solution.py
+++ b/solution.py
@@ -156,13 +156,16 @@
     flux = flux_ref[...].reshape(depth, comps * modes)
     eig = own_ref[...].reshape(depth, modes)
     pairs = lax.dot_general(eig, flux, (((0,), (0,)), ((), ())), preferred_element_type=F32)
+    equal = iota((HALF, HALF), 0) == iota((HALF, HALF), 1)
     for k in range(comps):
         left, middle, right = k * modes, k * modes + HALF, (k + 1) * modes
-        first, second = pairs[0:HALF, left:middle], pairs[HALF : 2 * HALF, middle:right]
+        above, below = pairs[HALF : 2 * HALF, left:middle], pairs[0:HALF, middle:right]
+        first = jnp.where(equal, above, pairs[0:HALF, left:middle])
+        second = jnp.where(equal, below, pairs[HALF : 2 * HALF, middle:right])
         keep_ref[k] = jnp.where(odd, second, first)
         send_ref[k] = jnp.where(odd, first, second).astype(BF16)
-        cross_ref[0, k] = pairs[HALF : 2 * HALF, left:middle]
-        cross_ref[1, k] = pairs[0:HALF, middle:right]
+        cross_ref[0, k] = above
+        cross_ref[1, k] = below
 
 
 def side_kernel(flux_ref, cross_ref, halo_one, halo_two, keep_ref, send_ref):
@@ -180,17 +183,13 @@
     contract = (((0,), (0,)), ((), ()))
     below = lax.dot_general(before, low_flux, contract, preferred_element_type=F32)
     above = lax.dot_general(after, high_flux, contract, preferred_element_type=F32)
-    lower = iota((HALF, HALF), 0) > iota((HALF, HALF), 1)
-    equal = iota((HALF, HALF), 0) == iota((HALF, HALF), 1)
+    rows, columns = iota((HALF, HALF), 0), iota((HALF, HALF), 1)
     for k in range(comps):
-        sets = []
-        for part in range(2):
-            outside = (below, above)[part][:, k * HALF : (k + 1) * HALF]
-            low, up = (outside, cross_ref[0, k]) if part == 0 else (cross_ref[1, k], outside)
-            edge = jnp.sum(jnp.where(equal, low, 0.0), axis=0, keepdims=True)
-            sets.append(jnp.concatenate([jnp.where(lower, low, up), jnp.broadcast_to(edge, (EXTRA, HALF))], axis=0))
-        keep_ref[k] = jnp.where(odd, sets[1], sets[0])
-        send_ref[k] = jnp.where(odd, sets[0], sets[1]).astype(BF16)
+        here = slice(k * HALF, (k + 1) * HALF)
+        first = jnp.where(rows >= columns, below[:, here], cross_ref[0, k])
+        second = jnp.where(rows > columns, cross_ref[1, k], above[:, here])
+        keep_ref[k] = jnp.where(odd, second, first)
+        send_ref[k] = jnp.where(odd, first, second).astype(BF16)
 
 
 def pair_call(kernel, out_shape, flops, *operands):
@@ -250,26 +249,23 @@
         value = scale / ((detune * detune + eta * eta) * (4.0 * freq * partner_freq))
         return jnp.where(within, value, 0.0)
 
-    rows = iota((HALF, HALF), 0)
-    own_ids = start + iota((HALF, HALF), 1)
-    lower = rows > iota((HALF, HALF), 1)
-    main_weight = weight(column(freq), start + rows, own_ids)
+    rows, columns = iota((HALF, HALF), 0), iota((HALF, HALF), 1)
+    own_ids = start + columns
+    corner = rows == columns
+    corner_freq, corner_shift = jnp.where(second, prev, following), jnp.where(second, -HALF, HALF)
+    main_freq = jnp.where(corner, corner_freq, column(freq))
+    main_weight = weight(main_freq, start + rows + jnp.where(corner, corner_shift, 0), own_ids)
+    lower = rows + jnp.where(second, 0, 1) > columns
     side_freq = jnp.where(lower, column(prev), column(following))
     side_weight = weight(side_freq, start + rows + jnp.where(lower, -HALF, HALF), own_ids)
-    edge_own = start + iota((1, HALF), 1)
-    edge_weight = weight(prev, edge_own - HALF, edge_own)
     main_strength = jnp.zeros((HALF, HALF), F32)
     side_strength = jnp.zeros((HALF, HALF), F32)
-    edge_strength = jnp.zeros((1, HALF), F32)
     for k in range(comps):
         main = main_one[k].astype(F32) + main_two[k].astype(F32)
         side = side_one[k].astype(F32) + side_two[k].astype(F32)
         main_strength += main * main
-        side_strength += side[:HALF] * side[:HALF]
-        edge = side[HALF : HALF + 1]
-        edge_strength += edge * edge
+        side_strength += side * side
     total = jnp.sum(main_weight * main_strength + side_weight * side_strength, axis=0, keepdims=True)
-    total += edge_weight * edge_strength
     diff = math.pi / (3.0 * freq * freq) * total
     grown = jnp.exp(freq)
     carried = freq * freq * grown / ((grown - 1.0) * (grown - 1.0)) * diff
@@ -342,14 +338,14 @@
     halo_two = lax.ppermute(far_edge, ("atom", "mode"), hops)
 
     image, matrix = own_image(force, bond, nbr, held, atoms)
-    square, tall = (comps, HALF, HALF), (comps, HALF + EXTRA, HALF)
+    square = (comps, HALF, HALF)
     keep_main, send_main, cross, flux = pair_call(
         main_kernel,
         ((square, F32), (square, BF16), ((2, *square), F32), ((comps, own, comps * modes), BF16)),
         10**9, image, matrix, eigvec, rim_one, rim_two,
     )
     keep_side, send_side = pair_call(
-        side_kernel, ((tall, F32), (tall, BF16)), 10**9, flux, cross, halo_one, halo_two
+        side_kernel, ((square, F32), (square, BF16)), 10**9, flux, cross, halo_one, halo_two
     )
 
     tile = jax.ShapeDtypeStruct((8, HALF), F32)

time: 35.4 us -> 35.3 us (level)
  no operation moved by 1% of the time
where the time goes in v9:
time: 35.3 us; the launch traced here: 35.2 us
  starting transfers between devices  16.8 us (48%)
  waiting for transfers between devices  8.29 us (23%)
  Pallas kernels  8.06 us (23%)
  local copies, waits for them, and re-layouts  1.02 us (3%)
  between operations  0.79 us (2%)
    ppermute x11, starting transfers between devices, swap(): lax.ppermute(x, axis, [(i, i ^ bit) for i in range(lax.axis_size(axis))])  10.1 us
    ppermute x11, waiting for transfers between devices, swap(): lax.ppermute(x, axis, [(i, i ^ bit) for i in range(lax.axis_size(axis))])  8.28 us
    pallas_call x1, Pallas kernels, own_image(): pl.pallas_call(functools.partial(coupling_kernel, atoms), out_shape=(jax....  4.52 us
    ppermute x1, starting transfers between devices, body(): rim_two = lax.ppermute(outer_edge, 'atom', outer)  3.4 us
    ppermute x1, starting transfers between devices, body(): halo_one = lax.ppermute(near_edge, 'mode', near)  2.68 us
    pallas_call x4, Pallas kernels, local_call(): pl.pallas_call(kernel, out_shape=out_shape, in_specs=[VMEM] * len(operand...  1.66 us
    pallas_call x2, Pallas kernels, pair_call(): pl.pallas_call(kernel, out_shape=tuple((jax.ShapeDtypeStruct(shape, kind)...  1.58 us
    unnamed x14, local copies, waits for them, and re-layouts  1.02 us
  transfers between devices with their start and end apart: 15, of which 7 were waited for; matrix products, arithmetic and copies ran while one was open for 1% of the time, Pallas kernels for 20%

profile of v9, /device:TPU:0, one launch (start us, length us, event | category | flops | bytes accessed | tf_op | source)
XLA Modules:
  0.0 35.2 jit_solution(6896787223254130783)
XLA Ops:
  0.6 0.0 copy-start
  0.6 1.0 %copy-done = bf16[3,256,256]{2,1,0:T(8,128)(2,1)S(1)} copy-done((bf16[3,256,256]{2,1,0:T(8,128)(2,1)S(1)}, bf16[3,256,256]{2,1,0:T(8,128)(2,1)}, u32[]{:S(2)}) %copy-start) | copy-done | bytes 393240
  1.6 0.2 shard_map.77
  1.8 3.4 %collective-permute-start.1 = (bf16[3,128,256]{2,1,0:T(8,128)(2,1)S(1)}, bf16[3,128,256]{2,1,0:T(8,128)(2,1)S(1)}, u32[]{:S(2)}, u32[]{:S(2)}) collective-permute-start(bf16[3,128,256]{2,1,0:T(8,128)(2,1)S(1)} %get-tuple-element.29), channel_id=1, source_target_pairs={{0,28},{4,8},{8,4},{12,16},{16,12},{20,24},{24,20},{28,0},{1,29},{... | collective-permute-start | bytes 589832 | tf_op jit(solution)/shard_map/ppermute | solution.py:330
  5.2 0.1 collective-permute-start
  5.3 0.0 copy-done.2
  5.3 0.1 shard_map.78
  5.4 0.5 %collective-permute-start.3 = (bf16[3,272,128]{2,1,0:T(8,128)(2,1)S(1)}, bf16[3,272,128]{2,1,0:T(8,128)(2,1)S(1)}, u32[]{:S(2)}, u32[]{:S(2)}) collective-permute-start(bf16[3,272,128]{2,1,0:T(8,128)(2,1)S(1)} %get-tuple-element.33), channel_id=1, source_target_pairs={{0,4},{1,2},{2,1},{3,7},{4,0},{5,6},{6,5},{7,3},{8,12},{9,10},{10,... | collective-permute-start | bytes 626696 | tf_op jit(solution)/shard_map/ppermute | solution.py:338
  6.0 2.7 %collective-permute-start.2 = (bf16[3,272,128]{2,1,0:T(8,128)(2,1)S(1)}, bf16[3,272,128]{2,1,0:T(8,128)(2,1)S(1)}, u32[]{:S(2)}, u32[]{:S(2)}) collective-permute-start(bf16[3,272,128]{2,1,0:T(8,128)(2,1)S(1)} %get-tuple-element.32), channel_id=1, source_target_pairs={{0,1},{1,0},{2,3},{3,2},{4,5},{5,4},{6,7},{7,6},{8,9},{9,8},{10,11... | collective-permute-start | bytes 626696 | tf_op jit(solution)/shard_map/ppermute | solution.py:332
  8.7 0.0 copy-done.1
  8.7 0.0 copy-done.4
  8.7 0.0 copy-done.5
  8.7 4.5 %shard_map.79 = (f32[2,1152,256]{2,1,0:T(8,128)S(1)}, bf16[2,1152,384]{2,1,0:T(8,128)(2,1)S(1)}) custom-call(f32[3,3,16,256]{3,2,1,0:T(8,128)S(1)} %copy-done.4, f32[3,16,256]{2,1,0:T(8,128)S(1)} %copy-done.5, s32[16,256]{1,0:T(8,128)S(1)} %copy-done.6, bf16[3,256,256]{2,1,0:T(8,128)(2,1)S(1)} %copy-done.1), custom_call_target="tpu_custom_call" | custom-call | flops 4000000000 | bytes 6000000 | tf_op jit(solution)/shard_map/pallas_call | solution.py:125
  13.2 0.0 collective-permute-done.1.rim_two
  13.2 0.0 collective-permute-done.rim_one
  13.2 1.1 %shard_map.80 = (f32[3,128,128]{2,1,0:T(8,128)S(1)}, bf16[3,128,128]{2,1,0:T(8,128)(2,1)S(1)}, f32[2,3,128,128]{3,2,1,0:T(8,128)S(1)}, bf16[3,256,768]{2,1,0:T(8,128)(2,1)S(1)}) custom-call(f32[2,1152,256]{2,1,0:T(8,128)S(1)} %get-tuple-element.26.image_ref, bf16[2,1152,384]{2,1,0:T(8,128)(2,1)S(1)} %get-tuple-element.27.cpl_ref, ...), custom_call_target="tpu_custom_call" | custom-call | flops 1000000000 | bytes 1000000 | tf_op jit(solution)/shard_map/pallas_call | solution.py:196
  14.4 0.1 collective-permute-start.6
  14.5 0.0 collective-permute-done.3.halo_two
  14.5 0.0 collective-permute-done.2.halo_one.halo_ref
  14.5 0.0 copy-start.3
  14.5 0.4 %shard_map.81 = (f32[3,128,128]{2,1,0:T(8,128)S(1)}, bf16[3,128,128]{2,1,0:T(8,128)(2,1)S(1)}) custom-call(bf16[3,256,768]{2,1,0:T(8,128)(2,1)S(1)} %get-tuple-element.30.flux_ref, f32[2,3,128,128]{3,2,1,0:T(8,128)S(1)} %get-tuple-element.31.cross_ref, bf16[3,272,128]{2,1,0:T(8,128)(2,1)S(1)} %collective-permute-done.2.halo_one.halo_ref, ...), custom_call_target="tpu_custom_call" | custom-call | flops 1000000000 | bytes 1000000 | tf_op jit(solution)/shard_map/pallas_call | solution.py:196
  14.9 0.5 %collective-permute-start.4 = (bf16[3,128,128]{2,1,0:T(8,128)(2,1)S(1)}, bf16[3,128,128]{2,1,0:T(8,128)(2,1)S(1)}, u32[]{:S(2)}, u32[]{:S(2)}) collective-permute-start(bf16[3,128,128]{2,1,0:T(8,128)(2,1)S(1)} %get-tuple-element.35), channel_id=1, source_target_pairs={{0,4},{4,0},{8,12},{12,8},{16,20},{20,16},{24,28},{28,24},{1,5},{5... | collective-permute-start | bytes 294920 | tf_op jit(solution)/shard_map/ppermute | solution.py:304
  15.5 0.3 collective-permute-done.6
  15.8 1.2 %collective-permute-start.7 = (bf16[3,128,128]{2,1,0:T(8,128)(2,1)S(1)}, bf16[3,128,128]{2,1,0:T(8,128)(2,1)S(1)}, u32[]{:S(2)}, u32[]{:S(2)}) collective-permute-start(bf16[3,128,128]{2,1,0:T(8,128)(2,1)S(1)} %reduce-precision_convert_fusion.2), channel_id=1, source_target_pairs={{0,8},{4,12},{8,0},{12,4},{16,24},{20,28},{24,16},{28,20},{1,9},{5... | collective-permute-start | bytes 294920 | tf_op jit(solution)/shard_map/ppermute | solution.py:304
  17.0 0.0 collective-permute-done.4
  17.0 0.7 %collective-permute-start.9 = (bf16[3,128,128]{2,1,0:T(8,128)(2,1)S(1)}, bf16[3,128,128]{2,1,0:T(8,128)(2,1)S(1)}, u32[]{:S(2)}, u32[]{:S(2)}) collective-permute-start(bf16[3,128,128]{2,1,0:T(8,128)(2,1)S(1)} %reduce-precision_convert_fusion.3), channel_id=1, source_target_pairs={{0,16},{4,20},{8,24},{12,28},{16,0},{20,4},{24,8},{28,12},{1,17},{... | collective-permute-start | bytes 294920 | tf_op jit(solution)/shard_map/ppermute | solution.py:304
  17.7 0.1 shard_map.82
  17.8 1.1 %collective-permute-start.5 = (f32[8,128]{1,0:T(8,128)S(1)}, f32[8,128]{1,0:T(8,128)S(1)}, u32[]{:S(2)}, u32[]{:S(2)}) collective-permute-start(f32[8,128]{1,0:T(8,128)S(1)} %shard_map.82), channel_id=1, source_target_pairs={{0,2},{1,3},{2,0},{3,1},{4,6},{5,7},{6,4},{7,5},{8,10},{9,11},{10,... | collective-permute-start | bytes 12296 | tf_op jit(solution)/shard_map/ppermute | solution.py:304
  18.9 1.8 %collective-permute-done.7 = bf16[3,128,128]{2,1,0:T(8,128)(2,1)S(1)} collective-permute-done((bf16[3,128,128]{2,1,0:T(8,128)(2,1)S(1)}, bf16[3,128,128]{2,1,0:T(8,128)(2,1)S(1)}, u32[]{:S(2)}, u32[]{:S(2)}) %collective-permute-start.7) | collective-permute-done | bytes 98336 | tf_op jit(solution)/shard_map/ppermute | solution.py:304
  20.7 1.3 %collective-permute-start.8 = (bf16[3,128,128]{2,1,0:T(8,128)(2,1)S(1)}, bf16[3,128,128]{2,1,0:T(8,128)(2,1)S(1)}, u32[]{:S(2)}, u32[]{:S(2)}) collective-permute-start(bf16[3,128,128]{2,1,0:T(8,128)(2,1)S(1)} %reduce-precision_convert_fusion.1.main_one), channel_id=1, source_target_pairs={{0,16},{4,20},{8,24},{12,28},{16,0},{20,4},{24,8},{28,12},{1,17},{... | collective-permute-start | bytes 294920 | tf_op jit(solution)/shard_map/ppermute | solution.py:304
  22.0 0.0 collective-permute-done.9
  22.0 0.8 %collective-permute-start.10 = (bf16[3,128,128]{2,1,0:T(8,128)(2,1)S(1)}, bf16[3,128,128]{2,1,0:T(8,128)(2,1)S(1)}, u32[]{:S(2)}, u32[]{:S(2)}) collective-permute-start(bf16[3,128,128]{2,1,0:T(8,128)(2,1)S(1)} %reduce-precision_convert_fusion.side_one), channel_id=1, source_target_pairs={{0,8},{4,12},{8,0},{12,4},{16,24},{20,28},{24,16},{28,20},{1,9},{5... | collective-permute-start | bytes 294920 | tf_op jit(solution)/shard_map/ppermute | solution.py:304
  22.8 0.0 collective-permute-done.5
  22.8 0.1 maximum_select_fusion.ends_ref
  22.9 2.5 %collective-permute-done.8.main_two = bf16[3,128,128]{2,1,0:T(8,128)(2,1)S(1)} collective-permute-done((bf16[3,128,128]{2,1,0:T(8,128)(2,1)S(1)}, bf16[3,128,128]{2,1,0:T(8,128)(2,1)S(1)}, u32[]{:S(2)}, u32[]{:S(2)}) %collective-permute-start.8) | collective-permute-done | bytes 98336 | tf_op jit(solution)/shard_map/ppermute | solution.py:304
  25.4 1.3 %collective-permute-done.10.side_two = bf16[3,128,128]{2,1,0:T(8,128)(2,1)S(1)} collective-permute-done((bf16[3,128,128]{2,1,0:T(8,128)(2,1)S(1)}, bf16[3,128,128]{2,1,0:T(8,128)(2,1)S(1)}, u32[]{:S(2)}, u32[]{:S(2)}) %collective-permute-start.10) | collective-permute-done | bytes 98336 | tf_op jit(solution)/shard_map/ppermute | solution.py:304
  26.7 0.0 copy-done.3
  26.7 0.3 shard_map.83.own_ref
  27.0 0.0 collective-permute-start.11
  27.0 1.2 %collective-permute-done.11.other_ref = f32[8,128]{1,0:T(8,128)S(1)} collective-permute-done((f32[8,128]{1,0:T(8,128)S(1)}, f32[8,128]{1,0:T(8,128)S(1)}, u32[]{:S(2)}, u32[]{:S(2)}) %collective-permute-start.11) | collective-permute-done | bytes 4128 | tf_op jit(solution)/shard_map/ppermute | solution.py:304
  28.2 1.8 %collective-permute-start.12 = (f32[8,128]{1,0:T(8,128)S(1)}, f32[8,128]{1,0:T(8,128)S(1)}, u32[]{:S(2)}, u32[]{:S(2)}) collective-permute-start(f32[8,128]{1,0:T(8,128)S(1)} %add.25), channel_id=1, source_target_pairs={{0,3},{1,2},{2,1},{3,0},{4,7},{5,6},{6,5},{7,4},{8,11},{9,10},{10,... | collective-permute-start | bytes 12296 | tf_op jit(solution)/shard_map/ppermute | solution.py:304
  30.0 0.3 collective-permute-start.13
  30.3 2.3 %collective-permute-start.14 = (f32[8,128]{1,0:T(8,128)S(1)}, f32[8,128]{1,0:T(8,128)S(1)}, u32[]{:S(2)}, u32[]{:S(2)}) collective-permute-start(f32[8,128]{1,0:T(8,128)S(1)} %add.25), channel_id=1, source_target_pairs={{0,1},{1,0},{2,3},{3,2},{4,5},{5,4},{6,7},{7,6},{8,9},{9,8},{10,11... | collective-permute-start | bytes 12296 | tf_op jit(solution)/shard_map/ppermute | solution.py:304
  32.6 0.7 %shard_map.84 = (f32[1,256]{1,0:T(1,128)}, f32[1,256]{1,0:T(1,128)S(1)}) custom-call(f32[8,128]{1,0:T(8,128)S(1)} %shard_map.83.own_ref, f32[8,128]{1,0:T(8,128)S(1)} %collective-permute-done.11.other_ref), custom_call_target="tpu_custom_call" | custom-call | flops 1000000 | bytes 1000000 | tf_op jit(solution)/shard_map/pallas_call | solution.py:278
  33.2 0.4 %collective-permute-done.12 = f32[8,128]{1,0:T(8,128)S(1)} collective-permute-done((f32[8,128]{1,0:T(8,128)S(1)}, f32[8,128]{1,0:T(8,128)S(1)}, u32[]{:S(2)}, u32[]{:S(2)}) %collective-permute-start.12) | collective-permute-done | bytes 4128 | tf_op jit(solution)/shard_map/ppermute | solution.py:304
  33.6 0.9 %collective-permute-done.13 = f32[8,128]{1,0:T(8,128)S(1)} collective-permute-done((f32[8,128]{1,0:T(8,128)S(1)}, f32[8,128]{1,0:T(8,128)S(1)}, u32[]{:S(2)}, u32[]{:S(2)}) %collective-permute-start.13) | collective-permute-done | bytes 4128 | tf_op jit(solution)/shard_map/ppermute | solution.py:304
  34.5 0.0 collective-permute-done.14
  34.5 0.6 %shard_map.85 = f32[1,256]{1,0:T(1,128)} custom-call(f32[1,256]{1,0:T(1,128)S(1)} %get-tuple-element.41.run_ref, f32[1,128]{1,0:T(1,128)S(1)} %slice.3.earlier_ref), custom_call_target="tpu_custom_call" | custom-call | flops 1000000 | bytes 1000000 | tf_op jit(solution)/shard_map/pallas_call | solution.py:278
  (14 shorter events, 0.1 us)
Async XLA Ops:
  0.6 1.0 %copy-start = (bf16[3,256,256]{2,1,0:T(8,128)(2,1)S(1)}, bf16[3,256,256]{2,1,0:T(8,128)(2,1)}, u32[]{:S(2)}) copy-start(bf16[3,256,256]{2,1,0:T(8,128)(2,1)} %own_ref.1) | copy-start | bytes 1179652
  1.6 3.7 %copy-start.2 = (f32[256]{0:T(256)S(1)}, f32[256]{0:T(256)}, u32[]{:S(2)}) copy-start(f32[256]{0:T(256)} %param.11) | copy-start | bytes 3076
  1.8 11.4 %collective-permute-start.1 = (bf16[3,128,256]{2,1,0:T(8,128)(2,1)S(1)}, bf16[3,128,256]{2,1,0:T(8,128)(2,1)S(1)}, u32[]{:S(2)}, u32[]{:S(2)}) collective-permute-start(bf16[3,128,256]{2,1,0:T(8,128)(2,1)S(1)} %get-tuple-element.29), channel_id=1, source_target_pairs={{0,28},{4,8},{8,4},{12,16},{16,12},{20,24},{24,20},{28,0},{1,29},{... | collective-permute-start | bytes 589832 | tf_op jit(solution)/shard_map/ppermute | solution.py:330
  5.2 3.4 %copy-start.1 = (bf16[3,256,256]{2,1,0:T(8,128)(2,1)S(1)}, bf16[3,256,256]{2,1,0:T(8,128)(2,1)}, u32[]{:S(2)}) copy-start(bf16[3,256,256]{2,1,0:T(8,128)(2,1)} %own_ref.1) | copy-start | bytes 1179652
  5.2 3.4 %copy-start.4 = (f32[3,3,16,256]{3,2,1,0:T(8,128)S(1)}, f32[3,3,16,256]{3,2,1,0:T(8,128)}, u32[]{:S(2)}) copy-start(f32[3,3,16,256]{3,2,1,0:T(8,128)} %force_ref.1) | copy-start | bytes 442372
  5.2 3.4 %copy-start.5 = (f32[3,16,256]{2,1,0:T(8,128)S(1)}, f32[3,16,256]{2,1,0:T(8,128)}, u32[]{:S(2)}) copy-start(f32[3,16,256]{2,1,0:T(8,128)} %bond_ref.1) | copy-start | bytes 147460
  5.2 3.4 %copy-start.6 = (s32[16,256]{1,0:T(8,128)S(1)}, s32[16,256]{1,0:T(8,128)}, u32[]{:S(2)}) copy-start(s32[16,256]{1,0:T(8,128)} %nbr_ref.1) | copy-start | bytes 49156
  5.2 8.0 %collective-permute-start = (bf16[3,128,256]{2,1,0:T(8,128)(2,1)S(1)}, bf16[3,128,256]{2,1,0:T(8,128)(2,1)S(1)}, u32[]{:S(2)}, u32[]{:S(2)}) collective-permute-start(bf16[3,128,256]{2,1,0:T(8,128)(2,1)S(1)} %get-tuple-element.28), channel_id=1, source_target_pairs={{0,4},{4,0},{8,12},{12,8},{16,20},{20,16},{24,28},{28,24},{1,5},{5... | collective-permute-start | bytes 589832 | tf_op jit(solution)/shard_map/ppermute | solution.py:331
  5.4 9.0 %collective-permute-start.3 = (bf16[3,272,128]{2,1,0:T(8,128)(2,1)S(1)}, bf16[3,272,128]{2,1,0:T(8,128)(2,1)S(1)}, u32[]{:S(2)}, u32[]{:S(2)}) collective-permute-start(bf16[3,272,128]{2,1,0:T(8,128)(2,1)S(1)} %get-tuple-element.33), channel_id=1, source_target_pairs={{0,4},{1,2},{2,1},{3,7},{4,0},{5,6},{6,5},{7,3},{8,12},{9,10},{10,... | collective-permute-start | bytes 626696 | tf_op jit(solution)/shard_map/ppermute | solution.py:338
  6.0 8.5 %collective-permute-start.2 = (bf16[3,272,128]{2,1,0:T(8,128)(2,1)S(1)}, bf16[3,272,128]{2,1,0:T(8,128)(2,1)S(1)}, u32[]{:S(2)}, u32[]{:S(2)}) collective-permute-start(bf16[3,272,128]{2,1,0:T(8,128)(2,1)S(1)} %get-tuple-element.32), channel_id=1, source_target_pairs={{0,1},{1,0},{2,3},{3,2},{4,5},{5,4},{6,7},{7,6},{8,9},{9,8},{10,11... | collective-permute-start | bytes 626696 | tf_op jit(solution)/shard_map/ppermute | solution.py:332
  14.4 1.4 %collective-permute-start.6 = (bf16[3,128,128]{2,1,0:T(8,128)(2,1)S(1)}, bf16[3,128,128]{2,1,0:T(8,128)(2,1)S(1)}, u32[]{:S(2)}, u32[]{:S(2)}) collective-permute-start(bf16[3,128,128]{2,1,0:T(8,128)(2,1)S(1)} %get-tuple-element.38), channel_id=1, source_target_pairs={{0,4},{4,0},{8,12},{12,8},{16,20},{20,16},{24,28},{28,24},{1,5},{5... | collective-permute-start | bytes 294920 | tf_op jit(solution)/shard_map/ppermute | solution.py:304
  14.5 12.2 %copy-start.3 = (s32[2,256]{1,0:T(2,128)S(1)}, s32[2,256]{1,0:T(2,128)}, u32[]{:S(2)}) copy-start(s32[2,256]{1,0:T(2,128)} %band_ref.1) | copy-start | bytes 6148
  14.9 2.1 %collective-permute-start.4 = (bf16[3,128,128]{2,1,0:T(8,128)(2,1)S(1)}, bf16[3,128,128]{2,1,0:T(8,128)(2,1)S(1)}, u32[]{:S(2)}, u32[]{:S(2)}) collective-permute-start(bf16[3,128,128]{2,1,0:T(8,128)(2,1)S(1)} %get-tuple-element.35), channel_id=1, source_target_pairs={{0,4},{4,0},{8,12},{12,8},{16,20},{20,16},{24,28},{28,24},{1,5},{5... | collective-permute-start | bytes 294920 | tf_op jit(solution)/shard_map/ppermute | solution.py:304
  15.8 4.9 %collective-permute-start.7 = (bf16[3,128,128]{2,1,0:T(8,128)(2,1)S(1)}, bf16[3,128,128]{2,1,0:T(8,128)(2,1)S(1)}, u32[]{:S(2)}, u32[]{:S(2)}) collective-permute-start(bf16[3,128,128]{2,1,0:T(8,128)(2,1)S(1)} %reduce-precision_convert_fusion.2), channel_id=1, source_target_pairs={{0,8},{4,12},{8,0},{12,4},{16,24},{20,28},{24,16},{28,20},{1,9},{5... | collective-permute-start | bytes 294920 | tf_op jit(solution)/shard_map/ppermute | solution.py:304
  17.0 5.0 %collective-permute-start.9 = (bf16[3,128,128]{2,1,0:T(8,128)(2,1)S(1)}, bf16[3,128,128]{2,1,0:T(8,128)(2,1)S(1)}, u32[]{:S(2)}, u32[]{:S(2)}) collective-permute-start(bf16[3,128,128]{2,1,0:T(8,128)(2,1)S(1)} %reduce-precision_convert_fusion.3), channel_id=1, source_target_pairs={{0,16},{4,20},{8,24},{12,28},{16,0},{20,4},{24,8},{28,12},{1,17},{... | collective-permute-start | bytes 294920 | tf_op jit(solution)/shard_map/ppermute | solution.py:304
  17.8 5.0 %collective-permute-start.5 = (f32[8,128]{1,0:T(8,128)S(1)}, f32[8,128]{1,0:T(8,128)S(1)}, u32[]{:S(2)}, u32[]{:S(2)}) collective-permute-start(f32[8,128]{1,0:T(8,128)S(1)} %shard_map.82), channel_id=1, source_target_pairs={{0,2},{1,3},{2,0},{3,1},{4,6},{5,7},{6,4},{7,5},{8,10},{9,11},{10,... | collective-permute-start | bytes 12296 | tf_op jit(solution)/shard_map/ppermute | solution.py:304
  20.7 4.7 %collective-permute-start.8 = (bf16[3,128,128]{2,1,0:T(8,128)(2,1)S(1)}, bf16[3,128,128]{2,1,0:T(8,128)(2,1)S(1)}, u32[]{:S(2)}, u32[]{:S(2)}) collective-permute-start(bf16[3,128,128]{2,1,0:T(8,128)(2,1)S(1)} %reduce-precision_convert_fusion.1.main_one), channel_id=1, source_target_pairs={{0,16},{4,20},{8,24},{12,28},{16,0},{20,4},{24,8},{28,12},{1,17},{... | collective-permute-start | bytes 294920 | tf_op jit(solution)/shard_map/ppermute | solution.py:304
  22.0 4.7 %collective-permute-start.10 = (bf16[3,128,128]{2,1,0:T(8,128)(2,1)S(1)}, bf16[3,128,128]{2,1,0:T(8,128)(2,1)S(1)}, u32[]{:S(2)}, u32[]{:S(2)}) collective-permute-start(bf16[3,128,128]{2,1,0:T(8,128)(2,1)S(1)} %reduce-precision_convert_fusion.side_one), channel_id=1, source_target_pairs={{0,8},{4,12},{8,0},{12,4},{16,24},{20,28},{24,16},{28,20},{1,9},{5... | collective-permute-start | bytes 294920 | tf_op jit(solution)/shard_map/ppermute | solution.py:304
  27.0 1.2 %collective-permute-start.11 = (f32[8,128]{1,0:T(8,128)S(1)}, f32[8,128]{1,0:T(8,128)S(1)}, u32[]{:S(2)}, u32[]{:S(2)}) collective-permute-start(f32[8,128]{1,0:T(8,128)S(1)} %shard_map.83.own_ref), channel_id=1, source_target_pairs={{0,4},{4,0},{8,12},{12,8},{16,20},{20,16},{24,28},{28,24},{1,5},{5... | collective-permute-start | bytes 12296 | tf_op jit(solution)/shard_map/ppermute | solution.py:304
  28.2 5.4 %collective-permute-start.12 = (f32[8,128]{1,0:T(8,128)S(1)}, f32[8,128]{1,0:T(8,128)S(1)}, u32[]{:S(2)}, u32[]{:S(2)}) collective-permute-start(f32[8,128]{1,0:T(8,128)S(1)} %add.25), channel_id=1, source_target_pairs={{0,3},{1,2},{2,1},{3,0},{4,7},{5,6},{6,5},{7,4},{8,11},{9,10},{10,... | collective-permute-start | bytes 12296 | tf_op jit(solution)/shard_map/ppermute | solution.py:304
  30.0 4.5 %collective-permute-start.13 = (f32[8,128]{1,0:T(8,128)S(1)}, f32[8,128]{1,0:T(8,128)S(1)}, u32[]{:S(2)}, u32[]{:S(2)}) collective-permute-start(f32[8,128]{1,0:T(8,128)S(1)} %add.25), channel_id=1, source_target_pairs={{0,2},{1,3},{2,0},{3,1},{4,6},{5,7},{6,4},{7,5},{8,10},{9,11},{10,... | collective-permute-start | bytes 12296 | tf_op jit(solution)/shard_map/ppermute | solution.py:304
  30.3 4.2 %collective-permute-start.14 = (f32[8,128]{1,0:T(8,128)S(1)}, f32[8,128]{1,0:T(8,128)S(1)}, u32[]{:S(2)}, u32[]{:S(2)}) collective-permute-start(f32[8,128]{1,0:T(8,128)S(1)} %add.25), channel_id=1, source_target_pairs={{0,1},{1,0},{2,3},{3,2},{4,5},{5,4},{6,7},{7,6},{8,9},{9,8},{10,11... | collective-permute-start | bytes 12296 | tf_op jit(solution)/shard_map/ppermute | solution.py:304

commit v10 on v9

--- a/solution.py
+++ b/solution.py
@@ -304,6 +304,12 @@
     return lax.ppermute(x, axis, [(i, i ^ bit) for i in range(lax.axis_size(axis))])
 
 
+def upward(blocks, bit):
+    low = [i for i in range(blocks) if i < i ^ bit]
+    high = [i for i in range(blocks) if i > i ^ bit]
+    return {**{i: i ^ bit for i in low}, **dict(zip(high, low))}
+
+
 def bits_of(axis):
     return [1 << b for b in range(lax.axis_size(axis).bit_length() - 1)]
 
@@ -326,7 +332,7 @@
     inner_edge, outer_edge = edge_call(rim_kernel, (comps, RIM, modes), COST, eigvec)
     outer_edge, later = lax.optimization_barrier((outer_edge, freq_row))
     near_edge, far_edge = edge_call(halo_kernel, (comps, own + EXTRA, HALF), COST, eigvec, later)
-    far_edge, held = lax.optimization_barrier((far_edge, eigvec))
+    near_edge, held = lax.optimization_barrier((near_edge, eigvec))
     rim_two = lax.ppermute(outer_edge, "atom", outer)
     rim_one = lax.ppermute(inner_edge, "atom", inner)
     halo_one = lax.ppermute(near_edge, "mode", near)
@@ -370,8 +376,16 @@
     other = swap(summary, "atom", 1)
     diff, running = local_call(functools.partial(running_kernel, modes), (row, row), summary, other)
     total = summary + other
-    parts = [(bit, swap(total, "mode", bit)) for bit in reversed(range(1, blocks))]
-    earlier = sum(jnp.where((block ^ bit) < block, part, 0.0) for bit, part in parts)
+    odd = lax.rem(lax.axis_index("atom"), 2) == 1
+    held = jnp.zeros_like(total)
+    for high in range(blocks - 1, 1, -2):
+        routes = upward(blocks, high), upward(blocks, high - 1)
+        mixed = [(a * blocks + i, a * blocks + routes[a % 2][i]) for a in range(domains) for i in range(blocks)]
+        part = lax.ppermute(total, ("atom", "mode"), mixed)
+        source = block ^ jnp.where(odd, high - 1, high)
+        held = held + jnp.where(source < block, part, 0.0)
+    near_part = jnp.where((block & 1) != 0, swap(total, "mode", 1), 0.0)
+    earlier = (held + swap(held, "atom", 1)) + near_part
     conductivity = local_call(last_kernel, row, running, earlier[2:3])
     return diff.reshape(modes), conductivity.reshape(modes)
 

time: 35.3 us -> 34.1 us (0.966)
  waiting for transfers between devices: 8.29 us -> 7.28 us
    ppermute x0 -> x1, starting transfers between devices: none -> 2.41 us  [body(): part = lax.ppermute(total, ('atom', 'mode'), mixed)]
    ppermute x11 -> x10, waiting for transfers between devices: 8.28 us -> 5.96 us  [swap(): lax.ppermute(x, axis, [(i, i ^ bit) for i in range(lax.axis_size(axis))])]
    ppermute x0 -> x1, waiting for transfers between devices: none -> 1.31 us  [body(): part = lax.ppermute(total, ('atom', 'mode'), mixed)]
    ppermute x11 -> x10, starting transfers between devices: 10.1 us -> 8.86 us  [swap(): lax.ppermute(x, axis, [(i, i ^ bit) for i in range(lax.axis_size(axis))])]
    ppermute x1, starting transfers between devices: 2.68 us -> 1.64 us  [body(): halo_one = lax.ppermute(near_edge, 'mode', near)]
  transfers between devices with their start and end apart: 15 -> 15, of which waited for: 7 -> 6; matrix products, arithmetic and copies ran while one was open for 1% -> 1% of each run, Pallas kernels for 20% -> 21%
where the time goes in v10:
time: 34.1 us; the launch traced here: 33.9 us
  starting transfers between devices  16.6 us (49%)
  Pallas kernels  8.05 us (24%)
  waiting for transfers between devices  7.28 us (21%)
  local copies, waits for them, and re-layouts  1.02 us (3%)
  between operations  0.76 us (2%)
    ppermute x10, starting transfers between devices, swap(): lax.ppermute(x, axis, [(i, i ^ bit) for i in range(lax.axis_size(axis))])  8.86 us
    ppermute x10, waiting for transfers between devices, swap(): lax.ppermute(x, axis, [(i, i ^ bit) for i in range(lax.axis_size(axis))])  5.96 us
    pallas_call x1, Pallas kernels, own_image(): pl.pallas_call(functools.partial(coupling_kernel, atoms), out_shape=(jax....  4.52 us
    ppermute x1, starting transfers between devices, body(): rim_two = lax.ppermute(outer_edge, 'atom', outer)  3.4 us
    ppermute x1, starting transfers between devices, body(): part = lax.ppermute(total, ('atom', 'mode'), mixed)  2.41 us
    pallas_call x4, Pallas kernels, local_call(): pl.pallas_call(kernel, out_shape=out_shape, in_specs=[VMEM] * len(operand...  1.66 us
    ppermute x1, starting transfers between devices, body(): halo_one = lax.ppermute(near_edge, 'mode', near)  1.64 us
    pallas_call x2, Pallas kernels, pair_call(): pl.pallas_call(kernel, out_shape=tuple((jax.ShapeDtypeStruct(shape, kind)...  1.58 us
  transfers between devices with their start and end apart: 15, of which 6 were waited for; matrix products, arithmetic and copies ran while one was open for 1% of the time, Pallas kernels for 21%

profile of v10, /device:TPU:0, one launch (start us, length us, event | category | flops | bytes accessed | tf_op | source)
XLA Modules:
  0.0 33.9 jit_solution(13174134434354164735)
XLA Ops:
  0.6 0.0 copy-start
  0.6 1.0 %copy-done = bf16[3,256,256]{2,1,0:T(8,128)(2,1)S(1)} copy-done((bf16[3,256,256]{2,1,0:T(8,128)(2,1)S(1)}, bf16[3,256,256]{2,1,0:T(8,128)(2,1)}, u32[]{:S(2)}) %copy-start) | copy-done | bytes 393240
  1.6 0.2 shard_map.77
  1.8 3.4 %collective-permute-start.1 = (bf16[3,128,256]{2,1,0:T(8,128)(2,1)S(1)}, bf16[3,128,256]{2,1,0:T(8,128)(2,1)S(1)}, u32[]{:S(2)}, u32[]{:S(2)}) collective-permute-start(bf16[3,128,256]{2,1,0:T(8,128)(2,1)S(1)} %get-tuple-element.29), channel_id=1, source_target_pairs={{0,28},{4,8},{8,4},{12,16},{16,12},{20,24},{24,20},{28,0},{1,29},{... | collective-permute-start | bytes 589832 | tf_op jit(solution)/shard_map/ppermute | solution.py:336
  5.2 0.1 collective-permute-start
  5.3 0.0 copy-done.2
  5.3 0.1 shard_map.78
  5.4 1.6 %collective-permute-start.2 = (bf16[3,272,128]{2,1,0:T(8,128)(2,1)S(1)}, bf16[3,272,128]{2,1,0:T(8,128)(2,1)S(1)}, u32[]{:S(2)}, u32[]{:S(2)}) collective-permute-start(bf16[3,272,128]{2,1,0:T(8,128)(2,1)S(1)} %get-tuple-element.32), channel_id=1, source_target_pairs={{0,1},{1,0},{2,3},{3,2},{4,5},{5,4},{6,7},{7,6},{8,9},{9,8},{10,11... | collective-permute-start | bytes 626696 | tf_op jit(solution)/shard_map/ppermute | solution.py:338
  7.1 0.2 collective-permute-start.3
  7.3 0.0 copy-done.1
  7.3 0.0 copy-done.4
  7.3 0.0 copy-done.5
  7.3 0.0 copy-done.6
  7.3 4.5 %shard_map.79 = (f32[2,1152,256]{2,1,0:T(8,128)S(1)}, bf16[2,1152,384]{2,1,0:T(8,128)(2,1)S(1)}) custom-call(f32[3,3,16,256]{3,2,1,0:T(8,128)S(1)} %copy-done.4, f32[3,16,256]{2,1,0:T(8,128)S(1)} %copy-done.5, s32[16,256]{1,0:T(8,128)S(1)} %copy-done.6, bf16[3,256,256]{2,1,0:T(8,128)(2,1)S(1)} %copy-done.1), custom_call_target="tpu_custom_call" | custom-call | flops 4000000000 | bytes 6000000 | tf_op jit(solution)/shard_map/pallas_call | solution.py:125
  11.8 0.0 collective-permute-done.1.rim_two
  11.8 0.0 collective-permute-done.rim_one
  11.8 1.1 %shard_map.80 = (f32[3,128,128]{2,1,0:T(8,128)S(1)}, bf16[3,128,128]{2,1,0:T(8,128)(2,1)S(1)}, f32[2,3,128,128]{3,2,1,0:T(8,128)S(1)}, bf16[3,256,768]{2,1,0:T(8,128)(2,1)S(1)}) custom-call(f32[2,1152,256]{2,1,0:T(8,128)S(1)} %get-tuple-element.26.image_ref, bf16[2,1152,384]{2,1,0:T(8,128)(2,1)S(1)} %get-tuple-element.27.cpl_ref, ...), custom_call_target="tpu_custom_call" | custom-call | flops 1000000000 | bytes 1000000 | tf_op jit(solution)/shard_map/pallas_call | solution.py:196
  13.0 0.4 %collective-permute-start.6 = (bf16[3,128,128]{2,1,0:T(8,128)(2,1)S(1)}, bf16[3,128,128]{2,1,0:T(8,128)(2,1)S(1)}, u32[]{:S(2)}, u32[]{:S(2)}) collective-permute-start(bf16[3,128,128]{2,1,0:T(8,128)(2,1)S(1)} %get-tuple-element.38), channel_id=1, source_target_pairs={{0,4},{4,0},{8,12},{12,8},{16,20},{20,16},{24,28},{28,24},{1,5},{5... | collective-permute-start | bytes 294920 | tf_op jit(solution)/shard_map/ppermute | solution.py:304
  13.4 0.0 collective-permute-done.2.halo_one.halo_ref
  13.4 0.0 collective-permute-done.3.halo_two
  13.4 0.0 copy-start.3
  13.4 0.4 %shard_map.81 = (f32[3,128,128]{2,1,0:T(8,128)S(1)}, bf16[3,128,128]{2,1,0:T(8,128)(2,1)S(1)}) custom-call(bf16[3,256,768]{2,1,0:T(8,128)(2,1)S(1)} %get-tuple-element.30.flux_ref, f32[2,3,128,128]{3,2,1,0:T(8,128)S(1)} %get-tuple-element.31.cross_ref, bf16[3,272,128]{2,1,0:T(8,128)(2,1)S(1)} %collective-permute-done.2.halo_one.halo_ref, ...), custom_call_target="tpu_custom_call" | custom-call | flops 1000000000 | bytes 1000000 | tf_op jit(solution)/shard_map/pallas_call | solution.py:196
  13.8 0.3 collective-permute-start.4
  14.1 0.3 collective-permute-done.6
  14.4 1.2 %collective-permute-start.7 = (bf16[3,128,128]{2,1,0:T(8,128)(2,1)S(1)}, bf16[3,128,128]{2,1,0:T(8,128)(2,1)S(1)}, u32[]{:S(2)}, u32[]{:S(2)}) collective-permute-start(bf16[3,128,128]{2,1,0:T(8,128)(2,1)S(1)} %reduce-precision_convert_fusion.2), channel_id=1, source_target_pairs={{0,8},{4,12},{8,0},{12,4},{16,24},{20,28},{24,16},{28,20},{1,9},{5... | collective-permute-start | bytes 294920 | tf_op jit(solution)/shard_map/ppermute | solution.py:304
  15.6 0.0 collective-permute-done.4
  15.6 0.9 %collective-permute-start.9 = (bf16[3,128,128]{2,1,0:T(8,128)(2,1)S(1)}, bf16[3,128,128]{2,1,0:T(8,128)(2,1)S(1)}, u32[]{:S(2)}, u32[]{:S(2)}) collective-permute-start(bf16[3,128,128]{2,1,0:T(8,128)(2,1)S(1)} %reduce-precision_convert_fusion.3), channel_id=1, source_target_pairs={{0,16},{4,20},{8,24},{12,28},{16,0},{20,4},{24,8},{28,12},{1,17},{... | collective-permute-start | bytes 294920 | tf_op jit(solution)/shard_map/ppermute | solution.py:304
  16.5 0.1 shard_map.82
  16.6 3.1 %collective-permute-start.5 = (f32[8,128]{1,0:T(8,128)S(1)}, f32[8,128]{1,0:T(8,128)S(1)}, u32[]{:S(2)}, u32[]{:S(2)}) collective-permute-start(f32[8,128]{1,0:T(8,128)S(1)} %shard_map.82), channel_id=1, source_target_pairs={{0,2},{1,3},{2,0},{3,1},{4,6},{5,7},{6,4},{7,5},{8,10},{9,11},{10,... | collective-permute-start | bytes 12296 | tf_op jit(solution)/shard_map/ppermute | solution.py:304
  19.7 0.0 collective-permute-done.7
  19.7 1.3 %collective-permute-start.8 = (bf16[3,128,128]{2,1,0:T(8,128)(2,1)S(1)}, bf16[3,128,128]{2,1,0:T(8,128)(2,1)S(1)}, u32[]{:S(2)}, u32[]{:S(2)}) collective-permute-start(bf16[3,128,128]{2,1,0:T(8,128)(2,1)S(1)} %reduce-precision_convert_fusion.1.main_one), channel_id=1, source_target_pairs={{0,16},{4,20},{8,24},{12,28},{16,0},{20,4},{24,8},{28,12},{1,17},{... | collective-permute-start | bytes 294920 | tf_op jit(solution)/shard_map/ppermute | solution.py:304
  21.0 0.0 collective-permute-done.9
  21.1 0.9 %collective-permute-start.10 = (bf16[3,128,128]{2,1,0:T(8,128)(2,1)S(1)}, bf16[3,128,128]{2,1,0:T(8,128)(2,1)S(1)}, u32[]{:S(2)}, u32[]{:S(2)}) collective-permute-start(bf16[3,128,128]{2,1,0:T(8,128)(2,1)S(1)} %reduce-precision_convert_fusion.side_one), channel_id=1, source_target_pairs={{0,8},{4,12},{8,0},{12,4},{16,24},{20,28},{24,16},{28,20},{1,9},{5... | collective-permute-start | bytes 294920 | tf_op jit(solution)/shard_map/ppermute | solution.py:304
  22.0 0.0 collective-permute-done.5
  22.0 0.1 maximum_select_fusion.ends_ref
  22.1 2.3 %collective-permute-done.8.main_two = bf16[3,128,128]{2,1,0:T(8,128)(2,1)S(1)} collective-permute-done((bf16[3,128,128]{2,1,0:T(8,128)(2,1)S(1)}, bf16[3,128,128]{2,1,0:T(8,128)(2,1)S(1)}, u32[]{:S(2)}, u32[]{:S(2)}) %collective-permute-start.8) | collective-permute-done | bytes 98336 | tf_op jit(solution)/shard_map/ppermute | solution.py:304
  24.4 1.4 %collective-permute-done.10.side_two = bf16[3,128,128]{2,1,0:T(8,128)(2,1)S(1)} collective-permute-done((bf16[3,128,128]{2,1,0:T(8,128)(2,1)S(1)}, bf16[3,128,128]{2,1,0:T(8,128)(2,1)S(1)}, u32[]{:S(2)}, u32[]{:S(2)}) %collective-permute-start.10) | collective-permute-done | bytes 98336 | tf_op jit(solution)/shard_map/ppermute | solution.py:304
  25.8 0.3 shard_map.83.own_ref
  26.0 0.0 collective-permute-start.11
  26.1 1.2 %collective-permute-done.11.other_ref = f32[8,128]{1,0:T(8,128)S(1)} collective-permute-done((f32[8,128]{1,0:T(8,128)S(1)}, f32[8,128]{1,0:T(8,128)S(1)}, u32[]{:S(2)}, u32[]{:S(2)}) %collective-permute-start.11) | collective-permute-done | bytes 4128 | tf_op jit(solution)/shard_map/ppermute | solution.py:304
  27.2 2.4 %collective-permute-start.12 = (f32[8,128]{1,0:T(8,128)S(1)}, f32[8,128]{1,0:T(8,128)S(1)}, u32[]{:S(2)}, u32[]{:S(2)}) collective-permute-start(f32[8,128]{1,0:T(8,128)S(1)} %add.25), channel_id=1, source_target_pairs={{0,3},{1,2},{2,0},{3,1},{4,6},{5,7},{6,4},{7,5},{8,11},{9,10},{10,... | collective-permute-start | bytes 12296 | tf_op jit(solution)/shard_map/ppermute | solution.py:384
  29.6 0.8 %collective-permute-start.14 = (f32[8,128]{1,0:T(8,128)S(1)}, f32[8,128]{1,0:T(8,128)S(1)}, u32[]{:S(2)}, u32[]{:S(2)}) collective-permute-start(f32[8,128]{1,0:T(8,128)S(1)} %add.25), channel_id=1, source_target_pairs={{0,1},{1,0},{2,3},{3,2},{4,5},{5,4},{6,7},{7,6},{8,9},{9,8},{10,11... | collective-permute-start | bytes 12296 | tf_op jit(solution)/shard_map/ppermute | solution.py:304
  30.4 1.3 %collective-permute-done.12 = f32[8,128]{1,0:T(8,128)S(1)} collective-permute-done((f32[8,128]{1,0:T(8,128)S(1)}, f32[8,128]{1,0:T(8,128)S(1)}, u32[]{:S(2)}, u32[]{:S(2)}) %collective-permute-start.12) | collective-permute-done | bytes 4128 | tf_op jit(solution)/shard_map/ppermute | solution.py:384
  31.7 0.0 collective-permute-start.13
  31.7 0.7 %shard_map.84 = (f32[1,256]{1,0:T(1,128)}, f32[1,256]{1,0:T(1,128)S(1)}) custom-call(f32[8,128]{1,0:T(8,128)S(1)} %shard_map.83.own_ref, f32[8,128]{1,0:T(8,128)S(1)} %collective-permute-done.11.other_ref), custom_call_target="tpu_custom_call" | custom-call | flops 1000000 | bytes 1000000 | tf_op jit(solution)/shard_map/pallas_call | solution.py:278
  32.4 0.8 %collective-permute-done.14 = f32[8,128]{1,0:T(8,128)S(1)} collective-permute-done((f32[8,128]{1,0:T(8,128)S(1)}, f32[8,128]{1,0:T(8,128)S(1)}, u32[]{:S(2)}, u32[]{:S(2)}) %collective-permute-start.14) | collective-permute-done | bytes 4128 | tf_op jit(solution)/shard_map/ppermute | solution.py:304
  33.2 0.0 collective-permute-done.13
  33.3 0.6 %shard_map.85 = f32[1,256]{1,0:T(1,128)} custom-call(f32[1,256]{1,0:T(1,128)S(1)} %get-tuple-element.41.run_ref, f32[1,128]{1,0:T(1,128)S(1)} %slice.3.earlier_ref), custom_call_target="tpu_custom_call" | custom-call | flops 1000000 | bytes 1000000 | tf_op jit(solution)/shard_map/pallas_call | solution.py:278
  (15 shorter events, 0.1 us)
Async XLA Ops:
  0.6 1.0 %copy-start = (bf16[3,256,256]{2,1,0:T(8,128)(2,1)S(1)}, bf16[3,256,256]{2,1,0:T(8,128)(2,1)}, u32[]{:S(2)}) copy-start(bf16[3,256,256]{2,1,0:T(8,128)(2,1)} %own_ref.1) | copy-start | bytes 1179652
  1.6 3.7 %copy-start.2 = (f32[256]{0:T(256)S(1)}, f32[256]{0:T(256)}, u32[]{:S(2)}) copy-start(f32[256]{0:T(256)} %param.11) | copy-start | bytes 3076
  1.8 10.0 %collective-permute-start.1 = (bf16[3,128,256]{2,1,0:T(8,128)(2,1)S(1)}, bf16[3,128,256]{2,1,0:T(8,128)(2,1)S(1)}, u32[]{:S(2)}, u32[]{:S(2)}) collective-permute-start(bf16[3,128,256]{2,1,0:T(8,128)(2,1)S(1)} %get-tuple-element.29), channel_id=1, source_target_pairs={{0,28},{4,8},{8,4},{12,16},{16,12},{20,24},{24,20},{28,0},{1,29},{... | collective-permute-start | bytes 589832 | tf_op jit(solution)/shard_map/ppermute | solution.py:336
  5.2 2.1 %copy-start.1 = (bf16[3,256,256]{2,1,0:T(8,128)(2,1)S(1)}, bf16[3,256,256]{2,1,0:T(8,128)(2,1)}, u32[]{:S(2)}) copy-start(bf16[3,256,256]{2,1,0:T(8,128)(2,1)} %own_ref.1) | copy-start | bytes 1179652
  5.2 2.1 %copy-start.4 = (f32[3,3,16,256]{3,2,1,0:T(8,128)S(1)}, f32[3,3,16,256]{3,2,1,0:T(8,128)}, u32[]{:S(2)}) copy-start(f32[3,3,16,256]{3,2,1,0:T(8,128)} %force_ref.1) | copy-start | bytes 442372
  5.2 2.1 %copy-start.5 = (f32[3,16,256]{2,1,0:T(8,128)S(1)}, f32[3,16,256]{2,1,0:T(8,128)}, u32[]{:S(2)}) copy-start(f32[3,16,256]{2,1,0:T(8,128)} %bond_ref.1) | copy-start | bytes 147460
  5.2 2.1 %copy-start.6 = (s32[16,256]{1,0:T(8,128)S(1)}, s32[16,256]{1,0:T(8,128)}, u32[]{:S(2)}) copy-start(s32[16,256]{1,0:T(8,128)} %nbr_ref.1) | copy-start | bytes 49156
  5.2 6.6 %collective-permute-start = (bf16[3,128,256]{2,1,0:T(8,128)(2,1)S(1)}, bf16[3,128,256]{2,1,0:T(8,128)(2,1)S(1)}, u32[]{:S(2)}, u32[]{:S(2)}) collective-permute-start(bf16[3,128,256]{2,1,0:T(8,128)(2,1)S(1)} %get-tuple-element.28), channel_id=1, source_target_pairs={{0,4},{4,0},{8,12},{12,8},{16,20},{20,16},{24,28},{28,24},{1,5},{5... | collective-permute-start | bytes 589832 | tf_op jit(solution)/shard_map/ppermute | solution.py:337
  5.4 7.9 %collective-permute-start.2 = (bf16[3,272,128]{2,1,0:T(8,128)(2,1)S(1)}, bf16[3,272,128]{2,1,0:T(8,128)(2,1)S(1)}, u32[]{:S(2)}, u32[]{:S(2)}) collective-permute-start(bf16[3,272,128]{2,1,0:T(8,128)(2,1)S(1)} %get-tuple-element.32), channel_id=1, source_target_pairs={{0,1},{1,0},{2,3},{3,2},{4,5},{5,4},{6,7},{7,6},{8,9},{9,8},{10,11... | collective-permute-start | bytes 626696 | tf_op jit(solution)/shard_map/ppermute | solution.py:338
  7.1 6.3 %collective-permute-start.3 = (bf16[3,272,128]{2,1,0:T(8,128)(2,1)S(1)}, bf16[3,272,128]{2,1,0:T(8,128)(2,1)S(1)}, u32[]{:S(2)}, u32[]{:S(2)}) collective-permute-start(bf16[3,272,128]{2,1,0:T(8,128)(2,1)S(1)} %get-tuple-element.33), channel_id=1, source_target_pairs={{0,4},{1,2},{2,1},{3,7},{4,0},{5,6},{6,5},{7,3},{8,12},{9,10},{10,... | collective-permute-start | bytes 626696 | tf_op jit(solution)/shard_map/ppermute | solution.py:344
  13.0 1.4 %collective-permute-start.6 = (bf16[3,128,128]{2,1,0:T(8,128)(2,1)S(1)}, bf16[3,128,128]{2,1,0:T(8,128)(2,1)S(1)}, u32[]{:S(2)}, u32[]{:S(2)}) collective-permute-start(bf16[3,128,128]{2,1,0:T(8,128)(2,1)S(1)} %get-tuple-element.38), channel_id=1, source_target_pairs={{0,4},{4,0},{8,12},{12,8},{16,20},{20,16},{24,28},{28,24},{1,5},{5... | collective-permute-start | bytes 294920 | tf_op jit(solution)/shard_map/ppermute | solution.py:304
  13.4 12.4 %copy-start.3 = (s32[2,256]{1,0:T(2,128)S(1)}, s32[2,256]{1,0:T(2,128)}, u32[]{:S(2)}) copy-start(s32[2,256]{1,0:T(2,128)} %band_ref.1) | copy-start | bytes 6148
  13.8 1.8 %collective-permute-start.4 = (bf16[3,128,128]{2,1,0:T(8,128)(2,1)S(1)}, bf16[3,128,128]{2,1,0:T(8,128)(2,1)S(1)}, u32[]{:S(2)}, u32[]{:S(2)}) collective-permute-start(bf16[3,128,128]{2,1,0:T(8,128)(2,1)S(1)} %get-tuple-element.35), channel_id=1, source_target_pairs={{0,4},{4,0},{8,12},{12,8},{16,20},{20,16},{24,28},{28,24},{1,5},{5... | collective-permute-start | bytes 294920 | tf_op jit(solution)/shard_map/ppermute | solution.py:304
  14.4 5.3 %collective-permute-start.7 = (bf16[3,128,128]{2,1,0:T(8,128)(2,1)S(1)}, bf16[3,128,128]{2,1,0:T(8,128)(2,1)S(1)}, u32[]{:S(2)}, u32[]{:S(2)}) collective-permute-start(bf16[3,128,128]{2,1,0:T(8,128)(2,1)S(1)} %reduce-precision_convert_fusion.2), channel_id=1, source_target_pairs={{0,8},{4,12},{8,0},{12,4},{16,24},{20,28},{24,16},{28,20},{1,9},{5... | collective-permute-start | bytes 294920 | tf_op jit(solution)/shard_map/ppermute | solution.py:304
  15.6 5.4 %collective-permute-start.9 = (bf16[3,128,128]{2,1,0:T(8,128)(2,1)S(1)}, bf16[3,128,128]{2,1,0:T(8,128)(2,1)S(1)}, u32[]{:S(2)}, u32[]{:S(2)}) collective-permute-start(bf16[3,128,128]{2,1,0:T(8,128)(2,1)S(1)} %reduce-precision_convert_fusion.3), channel_id=1, source_target_pairs={{0,16},{4,20},{8,24},{12,28},{16,0},{20,4},{24,8},{28,12},{1,17},{... | collective-permute-start | bytes 294920 | tf_op jit(solution)/shard_map/ppermute | solution.py:304
  16.6 5.4 %collective-permute-start.5 = (f32[8,128]{1,0:T(8,128)S(1)}, f32[8,128]{1,0:T(8,128)S(1)}, u32[]{:S(2)}, u32[]{:S(2)}) collective-permute-start(f32[8,128]{1,0:T(8,128)S(1)} %shard_map.82), channel_id=1, source_target_pairs={{0,2},{1,3},{2,0},{3,1},{4,6},{5,7},{6,4},{7,5},{8,10},{9,11},{10,... | collective-permute-start | bytes 12296 | tf_op jit(solution)/shard_map/ppermute | solution.py:304
  19.7 4.7 %collective-permute-start.8 = (bf16[3,128,128]{2,1,0:T(8,128)(2,1)S(1)}, bf16[3,128,128]{2,1,0:T(8,128)(2,1)S(1)}, u32[]{:S(2)}, u32[]{:S(2)}) collective-permute-start(bf16[3,128,128]{2,1,0:T(8,128)(2,1)S(1)} %reduce-precision_convert_fusion.1.main_one), channel_id=1, source_target_pairs={{0,16},{4,20},{8,24},{12,28},{16,0},{20,4},{24,8},{28,12},{1,17},{... | collective-permute-start | bytes 294920 | tf_op jit(solution)/shard_map/ppermute | solution.py:304
  21.1 4.7 %collective-permute-start.10 = (bf16[3,128,128]{2,1,0:T(8,128)(2,1)S(1)}, bf16[3,128,128]{2,1,0:T(8,128)(2,1)S(1)}, u32[]{:S(2)}, u32[]{:S(2)}) collective-permute-start(bf16[3,128,128]{2,1,0:T(8,128)(2,1)S(1)} %reduce-precision_convert_fusion.side_one), channel_id=1, source_target_pairs={{0,8},{4,12},{8,0},{12,4},{16,24},{20,28},{24,16},{28,20},{1,9},{5... | collective-permute-start | bytes 294920 | tf_op jit(solution)/shard_map/ppermute | solution.py:304
  26.0 1.2 %collective-permute-start.11 = (f32[8,128]{1,0:T(8,128)S(1)}, f32[8,128]{1,0:T(8,128)S(1)}, u32[]{:S(2)}, u32[]{:S(2)}) collective-permute-start(f32[8,128]{1,0:T(8,128)S(1)} %shard_map.83.own_ref), channel_id=1, source_target_pairs={{0,4},{4,0},{8,12},{12,8},{16,20},{20,16},{24,28},{28,24},{1,5},{5... | collective-permute-start | bytes 12296 | tf_op jit(solution)/shard_map/ppermute | solution.py:304
  27.2 4.5 %collective-permute-start.12 = (f32[8,128]{1,0:T(8,128)S(1)}, f32[8,128]{1,0:T(8,128)S(1)}, u32[]{:S(2)}, u32[]{:S(2)}) collective-permute-start(f32[8,128]{1,0:T(8,128)S(1)} %add.25), channel_id=1, source_target_pairs={{0,3},{1,2},{2,0},{3,1},{4,6},{5,7},{6,4},{7,5},{8,11},{9,10},{10,... | collective-permute-start | bytes 12296 | tf_op jit(solution)/shard_map/ppermute | solution.py:384
  29.6 3.6 %collective-permute-start.14 = (f32[8,128]{1,0:T(8,128)S(1)}, f32[8,128]{1,0:T(8,128)S(1)}, u32[]{:S(2)}, u32[]{:S(2)}) collective-permute-start(f32[8,128]{1,0:T(8,128)S(1)} %add.25), channel_id=1, source_target_pairs={{0,1},{1,0},{2,3},{3,2},{4,5},{5,4},{6,7},{7,6},{8,9},{9,8},{10,11... | collective-permute-start | bytes 12296 | tf_op jit(solution)/shard_map/ppermute | solution.py:304
  31.7 1.5 %collective-permute-start.13 = (f32[8,128]{1,0:T(8,128)S(1)}, f32[8,128]{1,0:T(8,128)S(1)}, u32[]{:S(2)}, u32[]{:S(2)}) collective-permute-start(f32[8,128]{1,0:T(8,128)S(1)} %broadcast_select_fusion), channel_id=1, source_target_pairs={{0,4},{4,0},{8,12},{12,8},{16,20},{20,16},{24,28},{28,24},{1,5},{5... | collective-permute-start | bytes 12296 | tf_op jit(solution)/shard_map/ppermute | solution.py:304

commit v11 on v10

--- a/solution.py
+++ b/solution.py
@@ -45,17 +45,21 @@
     copies = []
     for place, (flag, ref) in enumerate(((1 - high, near_ref), (high, far_ref))):
         columns = pl.ds(pl.multiple_of(flag * (modes - HALF), HALF), HALF)
-        target = ref.at[:, pl.ds(0, own), :]
-        copies.append(pltpu.make_async_copy(eig_ref.at[:, :, columns], target, sems.at[place]))
+        for c in range(comps):
+            target = ref.at[pl.ds(c * own, own), :]
+            copies.append(pltpu.make_async_copy(eig_ref.at[c, :, columns], target, sems.at[place * comps + c]))
     for copy in copies:
         copy.start()
     freq = freq_ref[...]
-    rest = jnp.where(iota((EXTRA, HALF), 0) < EXTRA // 2, freq[:, 0:HALF], freq[:, modes - HALF : modes])
+    row = iota((EXTRA, HALF), 0)
+    rest = jnp.where(row < EXTRA // 2, freq[:, 0:HALF], freq[:, modes - HALF : modes])
+    tail = jnp.zeros((EXTRA, HALF), F32)
     for part in range(comps):
-        piece = rest.astype(BF16)
-        rest = rest - piece.astype(F32)
-        near_ref[part, own : own + EXTRA, :] = piece
-        far_ref[part, own : own + EXTRA, :] = piece
+        piece = rest.astype(BF16).astype(F32)
+        rest = rest - piece
+        tail = jnp.where(row % (EXTRA // 2) == part, piece, tail)
+    near_ref[comps * own : comps * own + EXTRA, :] = tail.astype(BF16)
+    far_ref[comps * own : comps * own + EXTRA, :] = tail.astype(BF16)
     for copy in copies:
         copy.wait()
 
@@ -66,7 +70,7 @@
         out_shape=(jax.ShapeDtypeStruct(shape, BF16),) * 2,
         in_specs=[VMEM] * len(operands),
         out_specs=(VMEM,) * 2,
-        scratch_shapes=[pltpu.SemaphoreType.DMA((2,))],
+        scratch_shapes=[pltpu.SemaphoreType.DMA((2 * operands[0].shape[0],))],
         compiler_params=pltpu.CompilerParams(vmem_limit_bytes=SMALL),
         cost_estimate=pl.CostEstimate(flops=cost, bytes_accessed=10**6, transcendentals=0),
     )(*operands)
@@ -174,8 +178,7 @@
     odd = lax.rem(lax.axis_index("atom"), 2) == 1
     high = lax.rem(lax.axis_index("mode"), 2) == 1
     flux = flux_ref[...].reshape(depth, wide)
-    first = halo_one[:, 0:own, :].reshape(depth, HALF)
-    second = halo_two[:, 0:own, :].reshape(depth, HALF)
+    first, second = halo_one[0:depth, :], halo_two[0:depth, :]
     before = jnp.where(high, first, second)
     after = jnp.where(high, second, first)
     low_flux = jnp.concatenate([flux[:, k * modes : k * modes + HALF] for k in range(comps)], axis=1)
@@ -203,29 +206,32 @@
     )(*operands)
 
 
-def halo_freq(halo_ref, own):
-    total = jnp.zeros((EXTRA, HALF), F32)
-    for part in reversed(range(halo_ref.shape[0])):
-        total = halo_ref[part, own : own + EXTRA, :].astype(F32) + total
-    return total[0:1], total[EXTRA // 2 : EXTRA // 2 + 1]
-
-
-def ends_kernel(own, freq_ref, halo_ref, out_ref):
+def halo_freq(halo_ref, comps):
+    tail = halo_ref[halo_ref.shape[0] - EXTRA :, :].astype(F32)
+    rows = []
+    for top in (0, EXTRA // 2):
+        total = jnp.zeros((1, HALF), F32)
+        for part in reversed(range(comps)):
+            total = tail[top + part : top + part + 1] + total
+        rows.append(total)
+    return rows
+
+
+def ends_kernel(comps, freq_ref, halo_ref, out_ref):
     modes = freq_ref.shape[1]
-    rows = (freq_ref[:, 0:HALF], freq_ref[:, modes - HALF : modes], *halo_freq(halo_ref, own))
+    rows = (freq_ref[:, 0:HALF], freq_ref[:, modes - HALF : modes], *halo_freq(halo_ref, comps))
     least = jnp.min(functools.reduce(jnp.minimum, rows), axis=1, keepdims=True)
     most = jnp.max(functools.reduce(jnp.maximum, rows), axis=1, keepdims=True)
     out_ref[...] = jnp.where(iota(out_ref.shape, 0) < 4, least, most)
 
 
-def weigh_kernel(count, own, freq_ref, ends_ref, band_ref, halo_one, halo_two, main_one, main_two, side_one, side_two, out_ref):
-    comps = main_one.shape[0]
+def weigh_kernel(count, comps, freq_ref, ends_ref, band_ref, halo_one, halo_two, main_one, main_two, side_one, side_two, out_ref):
     modes = freq_ref.shape[1]
     second = lax.rem(lax.axis_index("atom"), 2) == 1
     high = lax.rem(lax.axis_index("mode"), 2) == 1
     shift = jnp.where(second, HALF, 0)
     start = lax.axis_index("mode") * modes + shift
-    (one_first, one_last), (two_first, two_last) = halo_freq(halo_one, own), halo_freq(halo_two, own)
+    (one_first, one_last), (two_first, two_last) = halo_freq(halo_one, comps), halo_freq(halo_two, comps)
     one, two = jnp.where(high, one_last, one_first), jnp.where(high, two_first, two_last)
     outside = jnp.where(high == second, two, one)
     inside = jnp.where(second, freq_ref[:, 0:HALF], freq_ref[:, HALF:modes])
@@ -331,7 +337,7 @@
     far = [(i, i + 1 if i % 2 else i - 1) for i in range(1, blocks - 1)]
     inner_edge, outer_edge = edge_call(rim_kernel, (comps, RIM, modes), COST, eigvec)
     outer_edge, later = lax.optimization_barrier((outer_edge, freq_row))
-    near_edge, far_edge = edge_call(halo_kernel, (comps, own + EXTRA, HALF), COST, eigvec, later)
+    near_edge, far_edge = edge_call(halo_kernel, (comps * own + EXTRA, HALF), COST, eigvec, later)
     near_edge, held = lax.optimization_barrier((near_edge, eigvec))
     rim_two = lax.ppermute(outer_edge, "atom", outer)
     rim_one = lax.ppermute(inner_edge, "atom", inner)
@@ -359,7 +365,7 @@
     main = rounded_sum(keep_main, swap(send_main, "atom", 1))
     side = rounded_sum(keep_side, swap(send_side, "atom", 1))
     side, own_freq = lax.optimization_barrier((side, freq_row))
-    ends = local_call(functools.partial(ends_kernel, own), tile, own_freq, halo_one)
+    ends = local_call(functools.partial(ends_kernel, comps), tile, own_freq, halo_one)
     steps = bits_of("atom")[1:]
     for step, (one, two) in enumerate(zip(steps, reversed(steps))):
         main_other, side_other = swap(main, "atom", one), swap(side, "atom", two)
@@ -369,7 +375,7 @@
         other = swap(ends, "mode", bit)
         ends = jnp.where(iota((8, HALF), 0) < 4, jnp.minimum(ends, other), jnp.maximum(ends, other))
     summary = local_call(
-        functools.partial(weigh_kernel, count, own),
+        functools.partial(weigh_kernel, count, comps),
         tile, freq_row, ends, band, halo_one, halo_two, main, main_other, side, side_other,
     )
 

time: 34.1 us -> 34.1 us (level)
  no operation moved by 1% of the time
where the time goes in v11:
time: 34.1 us; the launch traced here: 33.9 us
  starting transfers between devices  16.4 us (48%)
  Pallas kernels  8.13 us (24%)
  waiting for transfers between devices  7.42 us (22%)
  local copies, waits for them, and re-layouts  1.02 us (3%)
  between operations  0.77 us (2%)
    ppermute x10, starting transfers between devices, swap(): lax.ppermute(x, axis, [(i, i ^ bit) for i in range(lax.axis_size(axis))])  8.56 us
    ppermute x10, waiting for transfers between devices, swap(): lax.ppermute(x, axis, [(i, i ^ bit) for i in range(lax.axis_size(axis))])  6.1 us
    pallas_call x1, Pallas kernels, own_image(): pl.pallas_call(functools.partial(coupling_kernel, atoms), out_shape=(jax....  4.52 us
    ppermute x1, starting transfers between devices, body(): rim_two = lax.ppermute(outer_edge, 'atom', outer)  3.4 us
    ppermute x1, starting transfers between devices, body(): part = lax.ppermute(total, ('atom', 'mode'), mixed)  2.53 us
    pallas_call x4, Pallas kernels, local_call(): pl.pallas_call(kernel, out_shape=out_shape, in_specs=[VMEM] * len(operand...  1.66 us
    ppermute x1, starting transfers between devices, body(): halo_one = lax.ppermute(near_edge, 'mode', near)  1.64 us
    pallas_call x2, Pallas kernels, pair_call(): pl.pallas_call(kernel, out_shape=tuple((jax.ShapeDtypeStruct(shape, kind)...  1.58 us
  transfers between devices with their start and end apart: 15, of which 6 were waited for; matrix products, arithmetic and copies ran while one was open for 1% of the time, Pallas kernels for 21%

profile of v11, /device:TPU:0, one launch (start us, length us, event | category | flops | bytes accessed | tf_op | source)
XLA Modules:
  0.0 33.9 jit_solution(37338538737807794)
XLA Ops:
  0.6 0.0 copy-start
  0.6 1.0 %copy-done = bf16[3,256,256]{2,1,0:T(8,128)(2,1)S(1)} copy-done((bf16[3,256,256]{2,1,0:T(8,128)(2,1)S(1)}, bf16[3,256,256]{2,1,0:T(8,128)(2,1)}, u32[]{:S(2)}) %copy-start) | copy-done | bytes 393240
  1.6 0.2 shard_map.77
  1.9 3.4 %collective-permute-start.1 = (bf16[3,128,256]{2,1,0:T(8,128)(2,1)S(1)}, bf16[3,128,256]{2,1,0:T(8,128)(2,1)S(1)}, u32[]{:S(2)}, u32[]{:S(2)}) collective-permute-start(bf16[3,128,256]{2,1,0:T(8,128)(2,1)S(1)} %get-tuple-element.29), channel_id=1, source_target_pairs={{0,28},{4,8},{8,4},{12,16},{16,12},{20,24},{24,20},{28,0},{1,29},{... | collective-permute-start | bytes 589832 | tf_op jit(solution)/shard_map/ppermute | solution.py:342
  5.3 0.1 collective-permute-start
  5.3 0.0 copy-done.2
  5.4 0.2 shard_map.78
  5.5 1.6 %collective-permute-start.2 = (bf16[784,128]{1,0:T(8,128)(2,1)S(1)}, bf16[784,128]{1,0:T(8,128)(2,1)S(1)}, u32[]{:S(2)}, u32[]{:S(2)}) collective-permute-start(bf16[784,128]{1,0:T(8,128)(2,1)S(1)} %get-tuple-element.32), channel_id=1, source_target_pairs={{0,1},{1,0},{2,3},{3,2},{4,5},{5,4},{6,7},{7,6},{8,9},{9,8},{10,11... | collective-permute-start | bytes 602120 | tf_op jit(solution)/shard_map/ppermute | solution.py:344
  7.2 0.2 collective-permute-start.3
  7.4 0.0 copy-done.1
  7.4 0.0 copy-done.4
  7.4 0.0 copy-done.5
  7.4 0.0 copy-done.6
  7.4 4.5 %shard_map.79 = (f32[2,1152,256]{2,1,0:T(8,128)S(1)}, bf16[2,1152,384]{2,1,0:T(8,128)(2,1)S(1)}) custom-call(f32[3,3,16,256]{3,2,1,0:T(8,128)S(1)} %copy-done.4, f32[3,16,256]{2,1,0:T(8,128)S(1)} %copy-done.5, s32[16,256]{1,0:T(8,128)S(1)} %copy-done.6, bf16[3,256,256]{2,1,0:T(8,128)(2,1)S(1)} %copy-done.1), custom_call_target="tpu_custom_call" | custom-call | flops 4000000000 | bytes 6000000 | tf_op jit(solution)/shard_map/pallas_call | solution.py:129
  11.9 0.0 collective-permute-done.1.rim_two
  11.9 0.0 collective-permute-done.rim_one
  11.9 1.2 %shard_map.80 = (f32[3,128,128]{2,1,0:T(8,128)S(1)}, bf16[3,128,128]{2,1,0:T(8,128)(2,1)S(1)}, f32[2,3,128,128]{3,2,1,0:T(8,128)S(1)}, bf16[3,256,768]{2,1,0:T(8,128)(2,1)S(1)}) custom-call(f32[2,1152,256]{2,1,0:T(8,128)S(1)} %get-tuple-element.26.image_ref, bf16[2,1152,384]{2,1,0:T(8,128)(2,1)S(1)} %get-tuple-element.27.cpl_ref, ...), custom_call_target="tpu_custom_call" | custom-call | flops 1000000000 | bytes 1000000 | tf_op jit(solution)/shard_map/pallas_call | solution.py:199
  13.1 0.4 %collective-permute-start.6 = (bf16[3,128,128]{2,1,0:T(8,128)(2,1)S(1)}, bf16[3,128,128]{2,1,0:T(8,128)(2,1)S(1)}, u32[]{:S(2)}, u32[]{:S(2)}) collective-permute-start(bf16[3,128,128]{2,1,0:T(8,128)(2,1)S(1)} %get-tuple-element.38), channel_id=1, source_target_pairs={{0,4},{4,0},{8,12},{12,8},{16,20},{20,16},{24,28},{28,24},{1,5},{5... | collective-permute-start | bytes 294920 | tf_op jit(solution)/shard_map/ppermute | solution.py:310
  13.5 0.0 collective-permute-done.2.halo_one.halo_ref
  13.5 0.0 collective-permute-done.3.halo_two
  13.5 0.0 copy-start.3
  13.5 0.4 %shard_map.81 = (f32[3,128,128]{2,1,0:T(8,128)S(1)}, bf16[3,128,128]{2,1,0:T(8,128)(2,1)S(1)}) custom-call(bf16[3,256,768]{2,1,0:T(8,128)(2,1)S(1)} %get-tuple-element.30.flux_ref, f32[2,3,128,128]{3,2,1,0:T(8,128)S(1)} %get-tuple-element.31.cross_ref, bf16[784,128]{1,0:T(8,128)(2,1)S(1)} %collective-permute-done.2.halo_one.halo_ref, ...), custom_call_target="tpu_custom_call" | custom-call | flops 1000000000 | bytes 1000000 | tf_op jit(solution)/shard_map/pallas_call | solution.py:199
  13.9 0.3 collective-permute-start.4
  14.2 0.3 collective-permute-done.6
  14.5 1.2 %collective-permute-start.7 = (bf16[3,128,128]{2,1,0:T(8,128)(2,1)S(1)}, bf16[3,128,128]{2,1,0:T(8,128)(2,1)S(1)}, u32[]{:S(2)}, u32[]{:S(2)}) collective-permute-start(bf16[3,128,128]{2,1,0:T(8,128)(2,1)S(1)} %reduce-precision_convert_fusion.2), channel_id=1, source_target_pairs={{0,8},{4,12},{8,0},{12,4},{16,24},{20,28},{24,16},{28,20},{1,9},{5... | collective-permute-start | bytes 294920 | tf_op jit(solution)/shard_map/ppermute | solution.py:310
  15.7 0.0 collective-permute-done.4
  15.7 0.9 %collective-permute-start.9 = (bf16[3,128,128]{2,1,0:T(8,128)(2,1)S(1)}, bf16[3,128,128]{2,1,0:T(8,128)(2,1)S(1)}, u32[]{:S(2)}, u32[]{:S(2)}) collective-permute-start(bf16[3,128,128]{2,1,0:T(8,128)(2,1)S(1)} %reduce-precision_convert_fusion.3), channel_id=1, source_target_pairs={{0,16},{4,20},{8,24},{12,28},{16,0},{20,4},{24,8},{28,12},{1,17},{... | collective-permute-start | bytes 294920 | tf_op jit(solution)/shard_map/ppermute | solution.py:310
  16.6 0.1 shard_map.82
  16.7 2.9 %collective-permute-start.5 = (f32[8,128]{1,0:T(8,128)S(1)}, f32[8,128]{1,0:T(8,128)S(1)}, u32[]{:S(2)}, u32[]{:S(2)}) collective-permute-start(f32[8,128]{1,0:T(8,128)S(1)} %shard_map.82), channel_id=1, source_target_pairs={{0,2},{1,3},{2,0},{3,1},{4,6},{5,7},{6,4},{7,5},{8,10},{9,11},{10,... | collective-permute-start | bytes 12296 | tf_op jit(solution)/shard_map/ppermute | solution.py:310
  19.6 0.0 collective-permute-done.7
  19.6 1.3 %collective-permute-start.8 = (bf16[3,128,128]{2,1,0:T(8,128)(2,1)S(1)}, bf16[3,128,128]{2,1,0:T(8,128)(2,1)S(1)}, u32[]{:S(2)}, u32[]{:S(2)}) collective-permute-start(bf16[3,128,128]{2,1,0:T(8,128)(2,1)S(1)} %reduce-precision_convert_fusion.1.main_one), channel_id=1, source_target_pairs={{0,16},{4,20},{8,24},{12,28},{16,0},{20,4},{24,8},{28,12},{1,17},{... | collective-permute-start | bytes 294920 | tf_op jit(solution)/shard_map/ppermute | solution.py:310
  21.0 0.0 collective-permute-done.9
  21.0 0.9 %collective-permute-start.10 = (bf16[3,128,128]{2,1,0:T(8,128)(2,1)S(1)}, bf16[3,128,128]{2,1,0:T(8,128)(2,1)S(1)}, u32[]{:S(2)}, u32[]{:S(2)}) collective-permute-start(bf16[3,128,128]{2,1,0:T(8,128)(2,1)S(1)} %reduce-precision_convert_fusion.side_one), channel_id=1, source_target_pairs={{0,8},{4,12},{8,0},{12,4},{16,24},{20,28},{24,16},{28,20},{1,9},{5... | collective-permute-start | bytes 294920 | tf_op jit(solution)/shard_map/ppermute | solution.py:310
  21.9 0.0 collective-permute-done.5
  21.9 0.1 maximum_select_fusion.ends_ref
  22.0 2.3 %collective-permute-done.8.main_two = bf16[3,128,128]{2,1,0:T(8,128)(2,1)S(1)} collective-permute-done((bf16[3,128,128]{2,1,0:T(8,128)(2,1)S(1)}, bf16[3,128,128]{2,1,0:T(8,128)(2,1)S(1)}, u32[]{:S(2)}, u32[]{:S(2)}) %collective-permute-start.8) | collective-permute-done | bytes 98336 | tf_op jit(solution)/shard_map/ppermute | solution.py:310
  24.3 1.4 %collective-permute-done.10.side_two = bf16[3,128,128]{2,1,0:T(8,128)(2,1)S(1)} collective-permute-done((bf16[3,128,128]{2,1,0:T(8,128)(2,1)S(1)}, bf16[3,128,128]{2,1,0:T(8,128)(2,1)S(1)}, u32[]{:S(2)}, u32[]{:S(2)}) %collective-permute-start.10) | collective-permute-done | bytes 98336 | tf_op jit(solution)/shard_map/ppermute | solution.py:310
  25.7 0.3 shard_map.83.own_ref
  26.0 0.0 collective-permute-start.11
  26.0 1.2 %collective-permute-done.11.other_ref = f32[8,128]{1,0:T(8,128)S(1)} collective-permute-done((f32[8,128]{1,0:T(8,128)S(1)}, f32[8,128]{1,0:T(8,128)S(1)}, u32[]{:S(2)}, u32[]{:S(2)}) %collective-permute-start.11) | collective-permute-done | bytes 4128 | tf_op jit(solution)/shard_map/ppermute | solution.py:310
  27.1 2.5 %collective-permute-start.12 = (f32[8,128]{1,0:T(8,128)S(1)}, f32[8,128]{1,0:T(8,128)S(1)}, u32[]{:S(2)}, u32[]{:S(2)}) collective-permute-start(f32[8,128]{1,0:T(8,128)S(1)} %add.25), channel_id=1, source_target_pairs={{0,3},{1,2},{2,0},{3,1},{4,6},{5,7},{6,4},{7,5},{8,11},{9,10},{10,... | collective-permute-start | bytes 12296 | tf_op jit(solution)/shard_map/ppermute | solution.py:390
  29.7 0.7 %collective-permute-start.14 = (f32[8,128]{1,0:T(8,128)S(1)}, f32[8,128]{1,0:T(8,128)S(1)}, u32[]{:S(2)}, u32[]{:S(2)}) collective-permute-start(f32[8,128]{1,0:T(8,128)S(1)} %add.25), channel_id=1, source_target_pairs={{0,1},{1,0},{2,3},{3,2},{4,5},{5,4},{6,7},{7,6},{8,9},{9,8},{10,11... | collective-permute-start | bytes 12296 | tf_op jit(solution)/shard_map/ppermute | solution.py:310
  30.3 1.3 %collective-permute-done.12 = f32[8,128]{1,0:T(8,128)S(1)} collective-permute-done((f32[8,128]{1,0:T(8,128)S(1)}, f32[8,128]{1,0:T(8,128)S(1)}, u32[]{:S(2)}, u32[]{:S(2)}) %collective-permute-start.12) | collective-permute-done | bytes 4128 | tf_op jit(solution)/shard_map/ppermute | solution.py:390
  31.6 0.0 collective-permute-start.13
  31.6 0.7 %shard_map.84 = (f32[1,256]{1,0:T(1,128)}, f32[1,256]{1,0:T(1,128)S(1)}) custom-call(f32[8,128]{1,0:T(8,128)S(1)} %shard_map.83.own_ref, f32[8,128]{1,0:T(8,128)S(1)} %collective-permute-done.11.other_ref), custom_call_target="tpu_custom_call" | custom-call | flops 1000000 | bytes 1000000 | tf_op jit(solution)/shard_map/pallas_call | solution.py:284
  32.3 1.0 %collective-permute-done.14 = f32[8,128]{1,0:T(8,128)S(1)} collective-permute-done((f32[8,128]{1,0:T(8,128)S(1)}, f32[8,128]{1,0:T(8,128)S(1)}, u32[]{:S(2)}, u32[]{:S(2)}) %collective-permute-start.14) | collective-permute-done | bytes 4128 | tf_op jit(solution)/shard_map/ppermute | solution.py:310
  33.3 0.0 collective-permute-done.13
  33.3 0.6 %shard_map.85 = f32[1,256]{1,0:T(1,128)} custom-call(f32[1,256]{1,0:T(1,128)S(1)} %get-tuple-element.41.run_ref, f32[1,128]{1,0:T(1,128)S(1)} %slice.3.earlier_ref), custom_call_target="tpu_custom_call" | custom-call | flops 1000000 | bytes 1000000 | tf_op jit(solution)/shard_map/pallas_call | solution.py:284
  (15 shorter events, 0.1 us)
Async XLA Ops:
  0.6 1.0 %copy-start = (bf16[3,256,256]{2,1,0:T(8,128)(2,1)S(1)}, bf16[3,256,256]{2,1,0:T(8,128)(2,1)}, u32[]{:S(2)}) copy-start(bf16[3,256,256]{2,1,0:T(8,128)(2,1)} %own_ref.1) | copy-start | bytes 1179652
  1.6 3.7 %copy-start.2 = (f32[256]{0:T(256)S(1)}, f32[256]{0:T(256)}, u32[]{:S(2)}) copy-start(f32[256]{0:T(256)} %param.11) | copy-start | bytes 3076
  1.9 10.0 %collective-permute-start.1 = (bf16[3,128,256]{2,1,0:T(8,128)(2,1)S(1)}, bf16[3,128,256]{2,1,0:T(8,128)(2,1)S(1)}, u32[]{:S(2)}, u32[]{:S(2)}) collective-permute-start(bf16[3,128,256]{2,1,0:T(8,128)(2,1)S(1)} %get-tuple-element.29), channel_id=1, source_target_pairs={{0,28},{4,8},{8,4},{12,16},{16,12},{20,24},{24,20},{28,0},{1,29},{... | collective-permute-start | bytes 589832 | tf_op jit(solution)/shard_map/ppermute | solution.py:342
  5.3 2.1 %copy-start.1 = (bf16[3,256,256]{2,1,0:T(8,128)(2,1)S(1)}, bf16[3,256,256]{2,1,0:T(8,128)(2,1)}, u32[]{:S(2)}) copy-start(bf16[3,256,256]{2,1,0:T(8,128)(2,1)} %own_ref.1) | copy-start | bytes 1179652
  5.3 2.1 %copy-start.4 = (f32[3,3,16,256]{3,2,1,0:T(8,128)S(1)}, f32[3,3,16,256]{3,2,1,0:T(8,128)}, u32[]{:S(2)}) copy-start(f32[3,3,16,256]{3,2,1,0:T(8,128)} %force_ref.1) | copy-start | bytes 442372
  5.3 2.1 %copy-start.5 = (f32[3,16,256]{2,1,0:T(8,128)S(1)}, f32[3,16,256]{2,1,0:T(8,128)}, u32[]{:S(2)}) copy-start(f32[3,16,256]{2,1,0:T(8,128)} %bond_ref.1) | copy-start | bytes 147460
  5.3 2.1 %copy-start.6 = (s32[16,256]{1,0:T(8,128)S(1)}, s32[16,256]{1,0:T(8,128)}, u32[]{:S(2)}) copy-start(s32[16,256]{1,0:T(8,128)} %nbr_ref.1) | copy-start | bytes 49156
  5.3 6.6 %collective-permute-start = (bf16[3,128,256]{2,1,0:T(8,128)(2,1)S(1)}, bf16[3,128,256]{2,1,0:T(8,128)(2,1)S(1)}, u32[]{:S(2)}, u32[]{:S(2)}) collective-permute-start(bf16[3,128,256]{2,1,0:T(8,128)(2,1)S(1)} %get-tuple-element.28), channel_id=1, source_target_pairs={{0,4},{4,0},{8,12},{12,8},{16,20},{20,16},{24,28},{28,24},{1,5},{5... | collective-permute-start | bytes 589832 | tf_op jit(solution)/shard_map/ppermute | solution.py:343
  5.5 7.9 %collective-permute-start.2 = (bf16[784,128]{1,0:T(8,128)(2,1)S(1)}, bf16[784,128]{1,0:T(8,128)(2,1)S(1)}, u32[]{:S(2)}, u32[]{:S(2)}) collective-permute-start(bf16[784,128]{1,0:T(8,128)(2,1)S(1)} %get-tuple-element.32), channel_id=1, source_target_pairs={{0,1},{1,0},{2,3},{3,2},{4,5},{5,4},{6,7},{7,6},{8,9},{9,8},{10,11... | collective-permute-start | bytes 602120 | tf_op jit(solution)/shard_map/ppermute | solution.py:344
  7.2 6.3 %collective-permute-start.3 = (bf16[784,128]{1,0:T(8,128)(2,1)S(1)}, bf16[784,128]{1,0:T(8,128)(2,1)S(1)}, u32[]{:S(2)}, u32[]{:S(2)}) collective-permute-start(bf16[784,128]{1,0:T(8,128)(2,1)S(1)} %get-tuple-element.33), channel_id=1, source_target_pairs={{0,4},{1,2},{2,1},{3,7},{4,0},{5,6},{6,5},{7,3},{8,12},{9,10},{10,... | collective-permute-start | bytes 602120 | tf_op jit(solution)/shard_map/ppermute | solution.py:350
  13.1 1.4 %collective-permute-start.6 = (bf16[3,128,128]{2,1,0:T(8,128)(2,1)S(1)}, bf16[3,128,128]{2,1,0:T(8,128)(2,1)S(1)}, u32[]{:S(2)}, u32[]{:S(2)}) collective-permute-start(bf16[3,128,128]{2,1,0:T(8,128)(2,1)S(1)} %get-tuple-element.38), channel_id=1, source_target_pairs={{0,4},{4,0},{8,12},{12,8},{16,20},{20,16},{24,28},{28,24},{1,5},{5... | collective-permute-start | bytes 294920 | tf_op jit(solution)/shard_map/ppermute | solution.py:310
  13.5 12.2 %copy-start.3 = (s32[2,256]{1,0:T(2,128)S(1)}, s32[2,256]{1,0:T(2,128)}, u32[]{:S(2)}) copy-start(s32[2,256]{1,0:T(2,128)} %band_ref.1) | copy-start | bytes 6148
  13.9 1.8 %collective-permute-start.4 = (bf16[3,128,128]{2,1,0:T(8,128)(2,1)S(1)}, bf16[3,128,128]{2,1,0:T(8,128)(2,1)S(1)}, u32[]{:S(2)}, u32[]{:S(2)}) collective-permute-start(bf16[3,128,128]{2,1,0:T(8,128)(2,1)S(1)} %get-tuple-element.35), channel_id=1, source_target_pairs={{0,4},{4,0},{8,12},{12,8},{16,20},{20,16},{24,28},{28,24},{1,5},{5... | collective-permute-start | bytes 294920 | tf_op jit(solution)/shard_map/ppermute | solution.py:310
  14.5 5.1 %collective-permute-start.7 = (bf16[3,128,128]{2,1,0:T(8,128)(2,1)S(1)}, bf16[3,128,128]{2,1,0:T(8,128)(2,1)S(1)}, u32[]{:S(2)}, u32[]{:S(2)}) collective-permute-start(bf16[3,128,128]{2,1,0:T(8,128)(2,1)S(1)} %reduce-precision_convert_fusion.2), channel_id=1, source_target_pairs={{0,8},{4,12},{8,0},{12,4},{16,24},{20,28},{24,16},{28,20},{1,9},{5... | collective-permute-start | bytes 294920 | tf_op jit(solution)/shard_map/ppermute | solution.py:310
  15.7 5.2 %collective-permute-start.9 = (bf16[3,128,128]{2,1,0:T(8,128)(2,1)S(1)}, bf16[3,128,128]{2,1,0:T(8,128)(2,1)S(1)}, u32[]{:S(2)}, u32[]{:S(2)}) collective-permute-start(bf16[3,128,128]{2,1,0:T(8,128)(2,1)S(1)} %reduce-precision_convert_fusion.3), channel_id=1, source_target_pairs={{0,16},{4,20},{8,24},{12,28},{16,0},{20,4},{24,8},{28,12},{1,17},{... | collective-permute-start | bytes 294920 | tf_op jit(solution)/shard_map/ppermute | solution.py:310
  16.7 5.3 %collective-permute-start.5 = (f32[8,128]{1,0:T(8,128)S(1)}, f32[8,128]{1,0:T(8,128)S(1)}, u32[]{:S(2)}, u32[]{:S(2)}) collective-permute-start(f32[8,128]{1,0:T(8,128)S(1)} %shard_map.82), channel_id=1, source_target_pairs={{0,2},{1,3},{2,0},{3,1},{4,6},{5,7},{6,4},{7,5},{8,10},{9,11},{10,... | collective-permute-start | bytes 12296 | tf_op jit(solution)/shard_map/ppermute | solution.py:310
  19.6 4.7 %collective-permute-start.8 = (bf16[3,128,128]{2,1,0:T(8,128)(2,1)S(1)}, bf16[3,128,128]{2,1,0:T(8,128)(2,1)S(1)}, u32[]{:S(2)}, u32[]{:S(2)}) collective-permute-start(bf16[3,128,128]{2,1,0:T(8,128)(2,1)S(1)} %reduce-precision_convert_fusion.1.main_one), channel_id=1, source_target_pairs={{0,16},{4,20},{8,24},{12,28},{16,0},{20,4},{24,8},{28,12},{1,17},{... | collective-permute-start | bytes 294920 | tf_op jit(solution)/shard_map/ppermute | solution.py:310
  21.0 4.7 %collective-permute-start.10 = (bf16[3,128,128]{2,1,0:T(8,128)(2,1)S(1)}, bf16[3,128,128]{2,1,0:T(8,128)(2,1)S(1)}, u32[]{:S(2)}, u32[]{:S(2)}) collective-permute-start(bf16[3,128,128]{2,1,0:T(8,128)(2,1)S(1)} %reduce-precision_convert_fusion.side_one), channel_id=1, source_target_pairs={{0,8},{4,12},{8,0},{12,4},{16,24},{20,28},{24,16},{28,20},{1,9},{5... | collective-permute-start | bytes 294920 | tf_op jit(solution)/shard_map/ppermute | solution.py:310
  26.0 1.2 %collective-permute-start.11 = (f32[8,128]{1,0:T(8,128)S(1)}, f32[8,128]{1,0:T(8,128)S(1)}, u32[]{:S(2)}, u32[]{:S(2)}) collective-permute-start(f32[8,128]{1,0:T(8,128)S(1)} %shard_map.83.own_ref), channel_id=1, source_target_pairs={{0,4},{4,0},{8,12},{12,8},{16,20},{20,16},{24,28},{28,24},{1,5},{5... | collective-permute-start | bytes 12296 | tf_op jit(solution)/shard_map/ppermute | solution.py:310
  27.1 4.5 %collective-permute-start.12 = (f32[8,128]{1,0:T(8,128)S(1)}, f32[8,128]{1,0:T(8,128)S(1)}, u32[]{:S(2)}, u32[]{:S(2)}) collective-permute-start(f32[8,128]{1,0:T(8,128)S(1)} %add.25), channel_id=1, source_target_pairs={{0,3},{1,2},{2,0},{3,1},{4,6},{5,7},{6,4},{7,5},{8,11},{9,10},{10,... | collective-permute-start | bytes 12296 | tf_op jit(solution)/shard_map/ppermute | solution.py:390
  29.7 3.6 %collective-permute-start.14 = (f32[8,128]{1,0:T(8,128)S(1)}, f32[8,128]{1,0:T(8,128)S(1)}, u32[]{:S(2)}, u32[]{:S(2)}) collective-permute-start(f32[8,128]{1,0:T(8,128)S(1)} %add.25), channel_id=1, source_target_pairs={{0,1},{1,0},{2,3},{3,2},{4,5},{5,4},{6,7},{7,6},{8,9},{9,8},{10,11... | collective-permute-start | bytes 12296 | tf_op jit(solution)/shard_map/ppermute | solution.py:310
  31.6 1.6 %collective-permute-start.13 = (f32[8,128]{1,0:T(8,128)S(1)}, f32[8,128]{1,0:T(8,128)S(1)}, u32[]{:S(2)}, u32[]{:S(2)}) collective-permute-start(f32[8,128]{1,0:T(8,128)S(1)} %broadcast_select_fusion), channel_id=1, source_target_pairs={{0,4},{4,0},{8,12},{12,8},{16,20},{20,16},{24,28},{28,24},{1,5},{5... | collective-permute-start | bytes 12296 | tf_op jit(solution)/shard_map/ppermute | solution.py:310

commit v12 on v11

--- a/solution.py
+++ b/solution.py
@@ -381,7 +381,7 @@
 
     other = swap(summary, "atom", 1)
     diff, running = local_call(functools.partial(running_kernel, modes), (row, row), summary, other)
-    total = summary + other
+    total = summary[2:3] + other[2:3]
     odd = lax.rem(lax.axis_index("atom"), 2) == 1
     held = jnp.zeros_like(total)
     for high in range(blocks - 1, 1, -2):
@@ -392,7 +392,7 @@
         held = held + jnp.where(source < block, part, 0.0)
     near_part = jnp.where((block & 1) != 0, swap(total, "mode", 1), 0.0)
     earlier = (held + swap(held, "atom", 1)) + near_part
-    conductivity = local_call(last_kernel, row, running, earlier[2:3])
+    conductivity = local_call(last_kernel, row, running, earlier)
     return diff.reshape(modes), conductivity.reshape(modes)
 
 

time: 34.1 us -> 34 us (level)
  no operation moved by 1% of the time
where the time goes in v12:
time: 34 us; the launch traced here: 33.9 us
  starting transfers between devices  16.4 us (48%)
  Pallas kernels  8.13 us (24%)
  waiting for transfers between devices  7.35 us (22%)
  local copies, waits for them, and re-layouts  1.02 us (3%)
  between operations  0.76 us (2%)
    ppermute x10, starting transfers between devices, swap(): lax.ppermute(x, axis, [(i, i ^ bit) for i in range(lax.axis_size(axis))])  8.56 us
    ppermute x10, waiting for transfers between devices, swap(): lax.ppermute(x, axis, [(i, i ^ bit) for i in range(lax.axis_size(axis))])  6.09 us
    pallas_call x1, Pallas kernels, own_image(): pl.pallas_call(functools.partial(coupling_kernel, atoms), out_shape=(jax....  4.52 us
    ppermute x1, starting transfers between devices, body(): rim_two = lax.ppermute(outer_edge, 'atom', outer)  3.4 us
    ppermute x1, starting transfers between devices, body(): part = lax.ppermute(total, ('atom', 'mode'), mixed)  2.53 us
    pallas_call x4, Pallas kernels, local_call(): pl.pallas_call(kernel, out_shape=out_shape, in_specs=[VMEM] * len(operand...  1.67 us
    ppermute x1, starting transfers between devices, body(): halo_one = lax.ppermute(near_edge, 'mode', near)  1.64 us
    pallas_call x2, Pallas kernels, pair_call(): pl.pallas_call(kernel, out_shape=tuple((jax.ShapeDtypeStruct(shape, kind)...  1.58 us
  transfers between devices with their start and end apart: 15, of which 6 were waited for; matrix products, arithmetic and copies ran while one was open for 1% of the time, Pallas kernels for 21%

profile of v12, /device:TPU:0, one launch (start us, length us, event | category | flops | bytes accessed | tf_op | source)
XLA Modules:
  0.0 33.9 jit_solution(4564205460983072365)
XLA Ops:
  0.6 0.0 copy-start
  0.6 1.0 %copy-done = bf16[3,256,256]{2,1,0:T(8,128)(2,1)S(1)} copy-done((bf16[3,256,256]{2,1,0:T(8,128)(2,1)S(1)}, bf16[3,256,256]{2,1,0:T(8,128)(2,1)}, u32[]{:S(2)}) %copy-start) | copy-done | bytes 393240
  1.6 0.2 shard_map.77
  1.9 3.4 %collective-permute-start.1 = (bf16[3,128,256]{2,1,0:T(8,128)(2,1)S(1)}, bf16[3,128,256]{2,1,0:T(8,128)(2,1)S(1)}, u32[]{:S(2)}, u32[]{:S(2)}) collective-permute-start(bf16[3,128,256]{2,1,0:T(8,128)(2,1)S(1)} %get-tuple-element.29), channel_id=1, source_target_pairs={{0,28},{4,8},{8,4},{12,16},{16,12},{20,24},{24,20},{28,0},{1,29},{... | collective-permute-start | bytes 589832 | tf_op jit(solution)/shard_map/ppermute | solution.py:342
  5.3 0.1 collective-permute-start
  5.3 0.0 copy-done.2
  5.4 0.2 shard_map.78
  5.5 1.6 %collective-permute-start.2 = (bf16[784,128]{1,0:T(8,128)(2,1)S(1)}, bf16[784,128]{1,0:T(8,128)(2,1)S(1)}, u32[]{:S(2)}, u32[]{:S(2)}) collective-permute-start(bf16[784,128]{1,0:T(8,128)(2,1)S(1)} %get-tuple-element.32), channel_id=1, source_target_pairs={{0,1},{1,0},{2,3},{3,2},{4,5},{5,4},{6,7},{7,6},{8,9},{9,8},{10,11... | collective-permute-start | bytes 602120 | tf_op jit(solution)/shard_map/ppermute | solution.py:344
  7.2 0.2 collective-permute-start.3
  7.4 0.0 copy-done.1
  7.4 0.0 copy-done.4
  7.4 0.0 copy-done.5
  7.4 0.0 copy-done.6
  7.4 4.5 %shard_map.79 = (f32[2,1152,256]{2,1,0:T(8,128)S(1)}, bf16[2,1152,384]{2,1,0:T(8,128)(2,1)S(1)}) custom-call(f32[3,3,16,256]{3,2,1,0:T(8,128)S(1)} %copy-done.4, f32[3,16,256]{2,1,0:T(8,128)S(1)} %copy-done.5, s32[16,256]{1,0:T(8,128)S(1)} %copy-done.6, bf16[3,256,256]{2,1,0:T(8,128)(2,1)S(1)} %copy-done.1), custom_call_target="tpu_custom_call" | custom-call | flops 4000000000 | bytes 6000000 | tf_op jit(solution)/shard_map/pallas_call | solution.py:129
  11.9 0.0 collective-permute-done.1.rim_two
  11.9 0.0 collective-permute-done.rim_one
  11.9 1.2 %shard_map.80 = (f32[3,128,128]{2,1,0:T(8,128)S(1)}, bf16[3,128,128]{2,1,0:T(8,128)(2,1)S(1)}, f32[2,3,128,128]{3,2,1,0:T(8,128)S(1)}, bf16[3,256,768]{2,1,0:T(8,128)(2,1)S(1)}) custom-call(f32[2,1152,256]{2,1,0:T(8,128)S(1)} %get-tuple-element.26.image_ref, bf16[2,1152,384]{2,1,0:T(8,128)(2,1)S(1)} %get-tuple-element.27.cpl_ref, ...), custom_call_target="tpu_custom_call" | custom-call | flops 1000000000 | bytes 1000000 | tf_op jit(solution)/shard_map/pallas_call | solution.py:199
  13.1 0.4 %collective-permute-start.6 = (bf16[3,128,128]{2,1,0:T(8,128)(2,1)S(1)}, bf16[3,128,128]{2,1,0:T(8,128)(2,1)S(1)}, u32[]{:S(2)}, u32[]{:S(2)}) collective-permute-start(bf16[3,128,128]{2,1,0:T(8,128)(2,1)S(1)} %get-tuple-element.38), channel_id=1, source_target_pairs={{0,4},{4,0},{8,12},{12,8},{16,20},{20,16},{24,28},{28,24},{1,5},{5... | collective-permute-start | bytes 294920 | tf_op jit(solution)/shard_map/ppermute | solution.py:310
  13.5 0.0 collective-permute-done.2.halo_one.halo_ref
  13.5 0.0 collective-permute-done.3.halo_two
  13.5 0.0 copy-start.3
  13.5 0.4 %shard_map.81 = (f32[3,128,128]{2,1,0:T(8,128)S(1)}, bf16[3,128,128]{2,1,0:T(8,128)(2,1)S(1)}) custom-call(bf16[3,256,768]{2,1,0:T(8,128)(2,1)S(1)} %get-tuple-element.30.flux_ref, f32[2,3,128,128]{3,2,1,0:T(8,128)S(1)} %get-tuple-element.31.cross_ref, bf16[784,128]{1,0:T(8,128)(2,1)S(1)} %collective-permute-done.2.halo_one.halo_ref, ...), custom_call_target="tpu_custom_call" | custom-call | flops 1000000000 | bytes 1000000 | tf_op jit(solution)/shard_map/pallas_call | solution.py:199
  13.9 0.3 collective-permute-start.4
  14.2 0.3 collective-permute-done.6
  14.5 1.2 %collective-permute-start.7 = (bf16[3,128,128]{2,1,0:T(8,128)(2,1)S(1)}, bf16[3,128,128]{2,1,0:T(8,128)(2,1)S(1)}, u32[]{:S(2)}, u32[]{:S(2)}) collective-permute-start(bf16[3,128,128]{2,1,0:T(8,128)(2,1)S(1)} %reduce-precision_convert_fusion.2), channel_id=1, source_target_pairs={{0,8},{4,12},{8,0},{12,4},{16,24},{20,28},{24,16},{28,20},{1,9},{5... | collective-permute-start | bytes 294920 | tf_op jit(solution)/shard_map/ppermute | solution.py:310
  15.7 0.0 collective-permute-done.4
  15.7 0.9 %collective-permute-start.9 = (bf16[3,128,128]{2,1,0:T(8,128)(2,1)S(1)}, bf16[3,128,128]{2,1,0:T(8,128)(2,1)S(1)}, u32[]{:S(2)}, u32[]{:S(2)}) collective-permute-start(bf16[3,128,128]{2,1,0:T(8,128)(2,1)S(1)} %reduce-precision_convert_fusion.3), channel_id=1, source_target_pairs={{0,16},{4,20},{8,24},{12,28},{16,0},{20,4},{24,8},{28,12},{1,17},{... | collective-permute-start | bytes 294920 | tf_op jit(solution)/shard_map/ppermute | solution.py:310
  16.6 0.1 shard_map.82
  16.7 2.9 %collective-permute-start.5 = (f32[8,128]{1,0:T(8,128)S(1)}, f32[8,128]{1,0:T(8,128)S(1)}, u32[]{:S(2)}, u32[]{:S(2)}) collective-permute-start(f32[8,128]{1,0:T(8,128)S(1)} %shard_map.82), channel_id=1, source_target_pairs={{0,2},{1,3},{2,0},{3,1},{4,6},{5,7},{6,4},{7,5},{8,10},{9,11},{10,... | collective-permute-start | bytes 12296 | tf_op jit(solution)/shard_map/ppermute | solution.py:310
  19.6 0.0 collective-permute-done.7
  19.6 1.3 %collective-permute-start.8 = (bf16[3,128,128]{2,1,0:T(8,128)(2,1)S(1)}, bf16[3,128,128]{2,1,0:T(8,128)(2,1)S(1)}, u32[]{:S(2)}, u32[]{:S(2)}) collective-permute-start(bf16[3,128,128]{2,1,0:T(8,128)(2,1)S(1)} %reduce-precision_convert_fusion.1.main_one), channel_id=1, source_target_pairs={{0,16},{4,20},{8,24},{12,28},{16,0},{20,4},{24,8},{28,12},{1,17},{... | collective-permute-start | bytes 294920 | tf_op jit(solution)/shard_map/ppermute | solution.py:310
  21.0 0.0 collective-permute-done.9
  21.0 0.9 %collective-permute-start.10 = (bf16[3,128,128]{2,1,0:T(8,128)(2,1)S(1)}, bf16[3,128,128]{2,1,0:T(8,128)(2,1)S(1)}, u32[]{:S(2)}, u32[]{:S(2)}) collective-permute-start(bf16[3,128,128]{2,1,0:T(8,128)(2,1)S(1)} %reduce-precision_convert_fusion.side_one), channel_id=1, source_target_pairs={{0,8},{4,12},{8,0},{12,4},{16,24},{20,28},{24,16},{28,20},{1,9},{5... | collective-permute-start | bytes 294920 | tf_op jit(solution)/shard_map/ppermute | solution.py:310
  21.9 0.0 collective-permute-done.5
  21.9 0.1 maximum_select_fusion.ends_ref
  22.0 2.3 %collective-permute-done.8.main_two = bf16[3,128,128]{2,1,0:T(8,128)(2,1)S(1)} collective-permute-done((bf16[3,128,128]{2,1,0:T(8,128)(2,1)S(1)}, bf16[3,128,128]{2,1,0:T(8,128)(2,1)S(1)}, u32[]{:S(2)}, u32[]{:S(2)}) %collective-permute-start.8) | collective-permute-done | bytes 98336 | tf_op jit(solution)/shard_map/ppermute | solution.py:310
  24.3 1.4 %collective-permute-done.10.side_two = bf16[3,128,128]{2,1,0:T(8,128)(2,1)S(1)} collective-permute-done((bf16[3,128,128]{2,1,0:T(8,128)(2,1)S(1)}, bf16[3,128,128]{2,1,0:T(8,128)(2,1)S(1)}, u32[]{:S(2)}, u32[]{:S(2)}) %collective-permute-start.10) | collective-permute-done | bytes 98336 | tf_op jit(solution)/shard_map/ppermute | solution.py:310
  25.7 0.3 shard_map.83.own_ref
  26.0 0.0 collective-permute-start.11
  26.0 1.2 %collective-permute-done.11.other_ref = f32[8,128]{1,0:T(8,128)S(1)} collective-permute-done((f32[8,128]{1,0:T(8,128)S(1)}, f32[8,128]{1,0:T(8,128)S(1)}, u32[]{:S(2)}, u32[]{:S(2)}) %collective-permute-start.11) | collective-permute-done | bytes 4128 | tf_op jit(solution)/shard_map/ppermute | solution.py:310
  27.1 2.5 %collective-permute-start.12 = (f32[1,128]{1,0:T(1,128)S(1)}, f32[1,128]{1,0:T(1,128)S(1)}, u32[]{:S(2)}, u32[]{:S(2)}) collective-permute-start(f32[1,128]{1,0:T(1,128)S(1)} %slice_add_fusion), channel_id=1, source_target_pairs={{0,3},{1,2},{2,0},{3,1},{4,6},{5,7},{6,4},{7,5},{8,11},{9,10},{10,... | collective-permute-start | bytes 1544 | tf_op jit(solution)/shard_map/ppermute | solution.py:390
  29.7 0.7 %collective-permute-start.14 = (f32[1,128]{1,0:T(1,128)S(1)}, f32[1,128]{1,0:T(1,128)S(1)}, u32[]{:S(2)}, u32[]{:S(2)}) collective-permute-start(f32[1,128]{1,0:T(1,128)S(1)} %slice_add_fusion), channel_id=1, source_target_pairs={{0,1},{1,0},{2,3},{3,2},{4,5},{5,4},{6,7},{7,6},{8,9},{9,8},{10,11... | collective-permute-start | bytes 1544 | tf_op jit(solution)/shard_map/ppermute | solution.py:310
  30.3 1.2 %collective-permute-done.12 = f32[1,128]{1,0:T(1,128)S(1)} collective-permute-done((f32[1,128]{1,0:T(1,128)S(1)}, f32[1,128]{1,0:T(1,128)S(1)}, u32[]{:S(2)}, u32[]{:S(2)}) %collective-permute-start.12) | collective-permute-done | bytes 544 | tf_op jit(solution)/shard_map/ppermute | solution.py:390
  31.6 0.0 collective-permute-start.13
  31.6 0.7 %shard_map.84 = (f32[1,256]{1,0:T(1,128)}, f32[1,256]{1,0:T(1,128)S(1)}) custom-call(f32[8,128]{1,0:T(8,128)S(1)} %shard_map.83.own_ref, f32[8,128]{1,0:T(8,128)S(1)} %collective-permute-done.11.other_ref), custom_call_target="tpu_custom_call" | custom-call | flops 1000000 | bytes 1000000 | tf_op jit(solution)/shard_map/pallas_call | solution.py:284
  32.2 1.0 %collective-permute-done.14 = f32[1,128]{1,0:T(1,128)S(1)} collective-permute-done((f32[1,128]{1,0:T(1,128)S(1)}, f32[1,128]{1,0:T(1,128)S(1)}, u32[]{:S(2)}, u32[]{:S(2)}) %collective-permute-start.14) | collective-permute-done | bytes 544 | tf_op jit(solution)/shard_map/ppermute | solution.py:310
  33.2 0.0 collective-permute-done.13
  33.2 0.6 %shard_map.85 = f32[1,256]{1,0:T(1,128)} custom-call(f32[1,256]{1,0:T(1,128)S(1)} %get-tuple-element.41.run_ref, f32[1,128]{1,0:T(1,128)S(1)} %fusion.earlier_ref), custom_call_target="tpu_custom_call" | custom-call | flops 1000000 | bytes 1000000 | tf_op jit(solution)/shard_map/pallas_call | solution.py:284
  (14 shorter events, 0.1 us)
Async XLA Ops:
  0.6 1.0 %copy-start = (bf16[3,256,256]{2,1,0:T(8,128)(2,1)S(1)}, bf16[3,256,256]{2,1,0:T(8,128)(2,1)}, u32[]{:S(2)}) copy-start(bf16[3,256,256]{2,1,0:T(8,128)(2,1)} %own_ref.1) | copy-start | bytes 1179652
  1.6 3.7 %copy-start.2 = (f32[256]{0:T(256)S(1)}, f32[256]{0:T(256)}, u32[]{:S(2)}) copy-start(f32[256]{0:T(256)} %param.11) | copy-start | bytes 3076
  1.9 10.0 %collective-permute-start.1 = (bf16[3,128,256]{2,1,0:T(8,128)(2,1)S(1)}, bf16[3,128,256]{2,1,0:T(8,128)(2,1)S(1)}, u32[]{:S(2)}, u32[]{:S(2)}) collective-permute-start(bf16[3,128,256]{2,1,0:T(8,128)(2,1)S(1)} %get-tuple-element.29), channel_id=1, source_target_pairs={{0,28},{4,8},{8,4},{12,16},{16,12},{20,24},{24,20},{28,0},{1,29},{... | collective-permute-start | bytes 589832 | tf_op jit(solution)/shard_map/ppermute | solution.py:342
  5.3 2.1 %copy-start.1 = (bf16[3,256,256]{2,1,0:T(8,128)(2,1)S(1)}, bf16[3,256,256]{2,1,0:T(8,128)(2,1)}, u32[]{:S(2)}) copy-start(bf16[3,256,256]{2,1,0:T(8,128)(2,1)} %own_ref.1) | copy-start | bytes 1179652
  5.3 2.1 %copy-start.4 = (f32[3,3,16,256]{3,2,1,0:T(8,128)S(1)}, f32[3,3,16,256]{3,2,1,0:T(8,128)}, u32[]{:S(2)}) copy-start(f32[3,3,16,256]{3,2,1,0:T(8,128)} %force_ref.1) | copy-start | bytes 442372
  5.3 2.1 %copy-start.5 = (f32[3,16,256]{2,1,0:T(8,128)S(1)}, f32[3,16,256]{2,1,0:T(8,128)}, u32[]{:S(2)}) copy-start(f32[3,16,256]{2,1,0:T(8,128)} %bond_ref.1) | copy-start | bytes 147460
  5.3 2.1 %copy-start.6 = (s32[16,256]{1,0:T(8,128)S(1)}, s32[16,256]{1,0:T(8,128)}, u32[]{:S(2)}) copy-start(s32[16,256]{1,0:T(8,128)} %nbr_ref.1) | copy-start | bytes 49156
  5.3 6.6 %collective-permute-start = (bf16[3,128,256]{2,1,0:T(8,128)(2,1)S(1)}, bf16[3,128,256]{2,1,0:T(8,128)(2,1)S(1)}, u32[]{:S(2)}, u32[]{:S(2)}) collective-permute-start(bf16[3,128,256]{2,1,0:T(8,128)(2,1)S(1)} %get-tuple-element.28), channel_id=1, source_target_pairs={{0,4},{4,0},{8,12},{12,8},{16,20},{20,16},{24,28},{28,24},{1,5},{5... | collective-permute-start | bytes 589832 | tf_op jit(solution)/shard_map/ppermute | solution.py:343
  5.5 7.9 %collective-permute-start.2 = (bf16[784,128]{1,0:T(8,128)(2,1)S(1)}, bf16[784,128]{1,0:T(8,128)(2,1)S(1)}, u32[]{:S(2)}, u32[]{:S(2)}) collective-permute-start(bf16[784,128]{1,0:T(8,128)(2,1)S(1)} %get-tuple-element.32), channel_id=1, source_target_pairs={{0,1},{1,0},{2,3},{3,2},{4,5},{5,4},{6,7},{7,6},{8,9},{9,8},{10,11... | collective-permute-start | bytes 602120 | tf_op jit(solution)/shard_map/ppermute | solution.py:344
  7.2 6.3 %collective-permute-start.3 = (bf16[784,128]{1,0:T(8,128)(2,1)S(1)}, bf16[784,128]{1,0:T(8,128)(2,1)S(1)}, u32[]{:S(2)}, u32[]{:S(2)}) collective-permute-start(bf16[784,128]{1,0:T(8,128)(2,1)S(1)} %get-tuple-element.33), channel_id=1, source_target_pairs={{0,4},{1,2},{2,1},{3,7},{4,0},{5,6},{6,5},{7,3},{8,12},{9,10},{10,... | collective-permute-start | bytes 602120 | tf_op jit(solution)/shard_map/ppermute | solution.py:350
  13.1 1.4 %collective-permute-start.6 = (bf16[3,128,128]{2,1,0:T(8,128)(2,1)S(1)}, bf16[3,128,128]{2,1,0:T(8,128)(2,1)S(1)}, u32[]{:S(2)}, u32[]{:S(2)}) collective-permute-start(bf16[3,128,128]{2,1,0:T(8,128)(2,1)S(1)} %get-tuple-element.38), channel_id=1, source_target_pairs={{0,4},{4,0},{8,12},{12,8},{16,20},{20,16},{24,28},{28,24},{1,5},{5... | collective-permute-start | bytes 294920 | tf_op jit(solution)/shard_map/ppermute | solution.py:310
  13.5 12.2 %copy-start.3 = (s32[2,256]{1,0:T(2,128)S(1)}, s32[2,256]{1,0:T(2,128)}, u32[]{:S(2)}) copy-start(s32[2,256]{1,0:T(2,128)} %band_ref.1) | copy-start | bytes 6148
  13.9 1.8 %collective-permute-start.4 = (bf16[3,128,128]{2,1,0:T(8,128)(2,1)S(1)}, bf16[3,128,128]{2,1,0:T(8,128)(2,1)S(1)}, u32[]{:S(2)}, u32[]{:S(2)}) collective-permute-start(bf16[3,128,128]{2,1,0:T(8,128)(2,1)S(1)} %get-tuple-element.35), channel_id=1, source_target_pairs={{0,4},{4,0},{8,12},{12,8},{16,20},{20,16},{24,28},{28,24},{1,5},{5... | collective-permute-start | bytes 294920 | tf_op jit(solution)/shard_map/ppermute | solution.py:310
  14.5 5.1 %collective-permute-start.7 = (bf16[3,128,128]{2,1,0:T(8,128)(2,1)S(1)}, bf16[3,128,128]{2,1,0:T(8,128)(2,1)S(1)}, u32[]{:S(2)}, u32[]{:S(2)}) collective-permute-start(bf16[3,128,128]{2,1,0:T(8,128)(2,1)S(1)} %reduce-precision_convert_fusion.2), channel_id=1, source_target_pairs={{0,8},{4,12},{8,0},{12,4},{16,24},{20,28},{24,16},{28,20},{1,9},{5... | collective-permute-start | bytes 294920 | tf_op jit(solution)/shard_map/ppermute | solution.py:310
  15.7 5.2 %collective-permute-start.9 = (bf16[3,128,128]{2,1,0:T(8,128)(2,1)S(1)}, bf16[3,128,128]{2,1,0:T(8,128)(2,1)S(1)}, u32[]{:S(2)}, u32[]{:S(2)}) collective-permute-start(bf16[3,128,128]{2,1,0:T(8,128)(2,1)S(1)} %reduce-precision_convert_fusion.3), channel_id=1, source_target_pairs={{0,16},{4,20},{8,24},{12,28},{16,0},{20,4},{24,8},{28,12},{1,17},{... | collective-permute-start | bytes 294920 | tf_op jit(solution)/shard_map/ppermute | solution.py:310
  16.7 5.3 %collective-permute-start.5 = (f32[8,128]{1,0:T(8,128)S(1)}, f32[8,128]{1,0:T(8,128)S(1)}, u32[]{:S(2)}, u32[]{:S(2)}) collective-permute-start(f32[8,128]{1,0:T(8,128)S(1)} %shard_map.82), channel_id=1, source_target_pairs={{0,2},{1,3},{2,0},{3,1},{4,6},{5,7},{6,4},{7,5},{8,10},{9,11},{10,... | collective-permute-start | bytes 12296 | tf_op jit(solution)/shard_map/ppermute | solution.py:310
  19.6 4.7 %collective-permute-start.8 = (bf16[3,128,128]{2,1,0:T(8,128)(2,1)S(1)}, bf16[3,128,128]{2,1,0:T(8,128)(2,1)S(1)}, u32[]{:S(2)}, u32[]{:S(2)}) collective-permute-start(bf16[3,128,128]{2,1,0:T(8,128)(2,1)S(1)} %reduce-precision_convert_fusion.1.main_one), channel_id=1, source_target_pairs={{0,16},{4,20},{8,24},{12,28},{16,0},{20,4},{24,8},{28,12},{1,17},{... | collective-permute-start | bytes 294920 | tf_op jit(solution)/shard_map/ppermute | solution.py:310
  21.0 4.7 %collective-permute-start.10 = (bf16[3,128,128]{2,1,0:T(8,128)(2,1)S(1)}, bf16[3,128,128]{2,1,0:T(8,128)(2,1)S(1)}, u32[]{:S(2)}, u32[]{:S(2)}) collective-permute-start(bf16[3,128,128]{2,1,0:T(8,128)(2,1)S(1)} %reduce-precision_convert_fusion.side_one), channel_id=1, source_target_pairs={{0,8},{4,12},{8,0},{12,4},{16,24},{20,28},{24,16},{28,20},{1,9},{5... | collective-permute-start | bytes 294920 | tf_op jit(solution)/shard_map/ppermute | solution.py:310
  26.0 1.2 %collective-permute-start.11 = (f32[8,128]{1,0:T(8,128)S(1)}, f32[8,128]{1,0:T(8,128)S(1)}, u32[]{:S(2)}, u32[]{:S(2)}) collective-permute-start(f32[8,128]{1,0:T(8,128)S(1)} %shard_map.83.own_ref), channel_id=1, source_target_pairs={{0,4},{4,0},{8,12},{12,8},{16,20},{20,16},{24,28},{28,24},{1,5},{5... | collective-permute-start | bytes 12296 | tf_op jit(solution)/shard_map/ppermute | solution.py:310
  27.1 4.4 %collective-permute-start.12 = (f32[1,128]{1,0:T(1,128)S(1)}, f32[1,128]{1,0:T(1,128)S(1)}, u32[]{:S(2)}, u32[]{:S(2)}) collective-permute-start(f32[1,128]{1,0:T(1,128)S(1)} %slice_add_fusion), channel_id=1, source_target_pairs={{0,3},{1,2},{2,0},{3,1},{4,6},{5,7},{6,4},{7,5},{8,11},{9,10},{10,... | collective-permute-start | bytes 1544 | tf_op jit(solution)/shard_map/ppermute | solution.py:390
  29.7 3.5 %collective-permute-start.14 = (f32[1,128]{1,0:T(1,128)S(1)}, f32[1,128]{1,0:T(1,128)S(1)}, u32[]{:S(2)}, u32[]{:S(2)}) collective-permute-start(f32[1,128]{1,0:T(1,128)S(1)} %slice_add_fusion), channel_id=1, source_target_pairs={{0,1},{1,0},{2,3},{3,2},{4,5},{5,4},{6,7},{7,6},{8,9},{9,8},{10,11... | collective-permute-start | bytes 1544 | tf_op jit(solution)/shard_map/ppermute | solution.py:310
  31.6 1.6 %collective-permute-start.13 = (f32[1,128]{1,0:T(1,128)S(1)}, f32[1,128]{1,0:T(1,128)S(1)}, u32[]{:S(2)}, u32[]{:S(2)}) collective-permute-start(f32[1,128]{1,0:T(1,128)S(1)} %broadcast_select_fusion.1), channel_id=1, source_target_pairs={{0,4},{4,0},{8,12},{12,8},{16,20},{20,16},{24,28},{28,24},{1,5},{5... | collective-permute-start | bytes 1544 | tf_op jit(solution)/shard_map/ppermute | solution.py:310
